TPU v7x, 768 devices: a whole 4x8x12 slice. The times are simulated.
768 devices in a mesh: section: 2 (over core), dp: 24 (over y_lo, z), mp: 16 (over y_hi, x).
Axes of the slice: x: 4, y: 8 (y_hi: 4, y_lo: 2; y = y_hi * 2 + y_lo), z: 12, core: 2. Of those that a mesh axis runs over, the one named last changes fastest.
Arguments:
- states: bfloat16 [2, 12288, 4096], P('section', 'dp', 'mp')
- proj_weights: bfloat16 [2, 2, 4096, 4096], P('section', None, None, 'mp'), may hold values from -0.09375 to 0.09375
- out_cotangent: bfloat16 [12288, 4096], P('dp', 'mp'), may hold values from -6 to 6
- enc_lengths: int32 [48], P('dp'), may hold values from 64 to 256
- dec_lengths: int32 [48], P('dp'), may hold values from 64 to 256
Outputs:
- state_grads: bfloat16 [2, 12288, 4096], P('section', 'dp', 'mp')
All inputs are finite; a program needn't handle non-finite values.
Results may differ from a plain program's by a relative error of at most 0.023.
The roundings to bfloat16 on the way count: a program that leaves them out, or rounds other values in their place, can miss the bound.
Values may be sent and summed in bfloat16 or wider, within the bound.
No kernel may reach another device: no remote copies, remote signals or barrier semaphores. Data moves between devices by JAX's collectives and lax.ppermute only.
A program may use at most 32 MiB of HBM per device.

v0:
```python
import jax
import jax.numpy as jnp
from jax import lax
from jax.sharding import PartitionSpec as P

HS = 256


def passed_along(block, axis, distance):
    devices = range(lax.axis_size(axis))
    route = [(i - distance, i) for i in devices if i - distance in devices]
    return lax.ppermute(block, axis, route)


def attend_local(queries, keys, values, out_grad, enc_lengths, dec_lengths):
    seq_count = enc_lengths.shape[0]
    span = queries.shape[0] // seq_count
    head_count = queries.shape[1] // HS
    shape4 = (seq_count, span, head_count, HS)
    q4 = queries.reshape(shape4)
    k4 = keys.reshape(shape4)
    v4 = values.reshape(shape4)
    g4 = out_grad.reshape(shape4)
    slots = jnp.arange(span, dtype=jnp.int32)
    key_live = slots[None, :] < enc_lengths[:, None]
    query_live = slots[None, :] < dec_lengths[:, None]
    g4 = jnp.where(query_live[:, :, None, None], g4, jnp.zeros_like(g4))
    scale = 1.0 / HS**0.5
    scores = jnp.einsum("sqhc,skhc->shqk", q4, k4, preferred_element_type=jnp.float32) * scale
    scores = jnp.where(key_live[:, None, None, :], scores, -1e30)
    top = jnp.max(scores, axis=-1, keepdims=True)
    expd = jnp.exp(scores - top)
    probs = expd / jnp.sum(expd, axis=-1, keepdims=True)
    probs_b = probs.astype(jnp.bfloat16)
    value_grad = jnp.einsum(
        "shqk,sqhc->skhc", probs_b, g4, preferred_element_type=jnp.float32
    ).astype(jnp.bfloat16)
    prob_grad = jnp.einsum("sqhc,skhc->shqk", g4, v4, preferred_element_type=jnp.float32)
    delta = jnp.sum(probs * prob_grad, axis=-1, keepdims=True)
    sg_b = (probs * (prob_grad - delta)).astype(jnp.bfloat16)
    query_grad = (
        jnp.einsum("shqk,skhc->sqhc", sg_b, k4, preferred_element_type=jnp.float32) * scale
    ).astype(jnp.bfloat16)
    key_grad = (
        jnp.einsum("shqk,sqhc->skhc", sg_b, q4, preferred_element_type=jnp.float32) * scale
    ).astype(jnp.bfloat16)
    flat = queries.shape
    return (query_grad.reshape(flat), key_grad.reshape(flat), value_grad.reshape(flat))


def local(states, proj_weights, out_cotangent, enc_lengths, dec_lengths):
    is_decoder = lax.axis_index("section") == 1
    own_rows = states[0]
    second_rows = jnp.where(is_decoder, out_cotangent, own_rows)
    w_first = proj_weights[0, 0]
    w_second = proj_weights[0, 1]
    full_own, full_second = (
        lax.all_gather(own_rows, "mp", axis=1, tiled=True),
        lax.all_gather(second_rows, "mp", axis=1, tiled=True),
    )
    first = jnp.dot(full_own, w_first, preferred_element_type=jnp.float32)
    other = jnp.dot(full_second, w_second, preferred_element_type=jnp.float32)
    first_b = first.astype(jnp.bfloat16)
    other_b = other.astype(jnp.bfloat16)
    keys, values = passed_along((first_b, other_b), "section", 1)

    def decoder_side(operands):
        return attend_local(
            operands[0], operands[1], operands[2], operands[3], enc_lengths, dec_lengths
        )

    def encoder_side(operands):
        blank = jnp.zeros_like(operands[0])
        return (blank, blank, blank)

    query_grad, key_grad, value_grad = lax.cond(
        is_decoder, decoder_side, encoder_side, (first_b, keys, values, other_b)
    )
    back_key, back_value = passed_along((key_grad, value_grad), "section", -1)
    lead_grad = jnp.where(is_decoder, query_grad, back_key)
    contract = (((1,), (1,)), ((), ()))

    def one_pair(_):
        return lax.dot_general(w_first, lead_grad, contract, preferred_element_type=jnp.float32)

    def two_pairs(_):
        return lax.dot_general(
            w_first, lead_grad, contract, preferred_element_type=jnp.float32
        ) + lax.dot_general(w_second, back_value, contract, preferred_element_type=jnp.float32)

    summed = lax.psum_scatter(
        lax.cond(is_decoder, one_pair, two_pairs, 0).astype(jnp.bfloat16),
        "mp",
        scatter_dimension=0,
        tiled=True,
    ).astype(jnp.float32)
    return summed.T.astype(jnp.bfloat16)[None]


def solution(mesh):
    placed = (
        P("section", "dp", "mp"),
        P("section", None, None, "mp"),
        P("dp", "mp"),
        P("dp"),
        P("dp"),
    )
    return jax.shard_map(
        local, mesh=mesh, in_specs=placed, out_specs=P("section", "dp", "mp"), check_vma=False
    )
```

profile of v0, /device:TPU:1, one launch (start us, length us, event | category | flops | bytes accessed | tf_op | source)
XLA Modules:
  0.0 344.2 jit_solution(13839723278208646301)
XLA Ops:
  6.5 1.8 bitcast_select_fusion
  8.3 0.0 all-gather.4.cloned.1.call-update
  8.3 0.0 all-gather.6.cloned.1.call-start
  8.4 0.7 all-gather.6.cloned.1.call-update
  9.1 0.0 reduce-scatter.2.cloned.1.call-start
  9.1 104.1 %all-gather.4.cloned.1.call-done = bf16[512,4096]{1,0:T(8,128)(2,1)} async-done(((bf16[512,256]{1,0:T(8,128)(2,1)}), bf16[512,4096]{1,0:T(8,128)(2,1)}) %all-gather.4.cloned.1.call-update) | async-done | bytes 4194320 | tf_op jit(solution)/shard_map/all_gather | solution.py:59
  113.2 4.1 %convolution_convert_fusion.1 = bf16[512,256]{1,0:T(8,128)(2,1)S(1)} fusion(bf16[512,4096]{1,0:T(8,128)(2,1)} %all-gather.4.cloned.1.call-done, bf16[1,2,4096,256]{3,2,1,0:T(8,128)(2,1)} %param.10), kind=kOutput, calls=%fused_computation.30 | convolution fusion | flops 1073872896 | bytes 6553600 | tf_op jit(solution)/shard_map/dot_general | solution.py:62
  117.3 0.0 copy-start
  117.3 0.0 copy-start.1
  117.3 1.3 collective-permute-start.1
  118.6 90.6 %all-gather.6.cloned.1.call-done = bf16[1,512,4096]{2,1,0:T(8,128)(2,1)} async-done(((bf16[1,512,256]{2,1,0:T(8,128)(2,1)}), bf16[1,512,4096]{2,1,0:T(8,128)(2,1)}) %all-gather.6.cloned.1.call-update) | async-done | bytes 4194320 | tf_op jit(solution)/shard_map/all_gather | solution.py:58
  209.2 4.1 %fusion.16 = bf16[512,256]{1,0:T(8,128)(2,1)S(1)} fusion(bf16[1,512,4096]{2,1,0:T(8,128)(2,1)} %all-gather.6.cloned.1.call-done, bf16[1,2,4096,256]{3,2,1,0:T(8,128)(2,1)} %param.10), kind=kOutput, calls=%fused_computation.29 | convolution fusion | flops 1073872896 | bytes 6553600 | tf_op jit(solution)/shard_map/dot_general | solution.py:61
  213.3 1.3 collective-permute-start
  214.7 2.1 collective-permute-done
  216.8 2.3 conditional.2
  216.8 0.1 iota_compare_fusion
  216.9 0.4 fusion.19
  217.2 0.6 convolution_convert_fusion
  217.8 0.4 multiply_reduce_fusion
  218.2 0.1 multiply_convert_fusion
  218.2 0.3 fusion.6
  218.5 0.3 fusion.7
  218.8 0.1 copy.14
  219.0 0.1 copy.16
  219.1 1.3 collective-permute-start.2
  220.4 1.3 collective-permute-start.3
  221.7 2.5 slice_bitcast_fusion
  224.3 3.3 conditional.3
  224.3 3.3 fusion.20
  227.6 6.4 %copy.17 = bf16[4096,512]{0,1:T(8,128)(2,1)} copy(bf16[4096,512]{1,0:T(8,128)(2,1)} %get-tuple-element.68) | data formatting | bytes 8388608 | tf_op jit(solution)/shard_map/cond | solution.py:92
  234.0 0.0 reduce-scatter.2.cloned.1.call-update
  234.0 103.7 %reduce-scatter.2.cloned.1.call-done = bf16[256,512]{0,1:T(8,128)(2,1)} async-done(((bf16[4096,512]{0,1:T(8,128)(2,1)}), bf16[256,512]{0,1:T(8,128)(2,1)}) %reduce-scatter.2.cloned.1.call-update) | async-done | bytes 262160 | tf_op jit(solution)/shard_map/reduce_scatter | solution.py:91
  (7 shorter events, 0.0 us)
Async XLA Ops:
  6.5 106.7 %all-gather.4.cloned.1.call-start = ((), (), s32[]{:S(2)}) async-start(), calls=%async_computation.1 | async-start | bytes 4456448 | tf_op jit(solution)/shard_map/all_gather | solution.py:59
  8.3 200.9 %all-gather.6.cloned.1.call-start = ((), (), s32[]{:S(2)}) async-start(), calls=%async_computation.3 | async-start | bytes 4456448 | tf_op jit(solution)/shard_map/all_gather | solution.py:58
  9.1 328.6 %reduce-scatter.2.cloned.1.call-start = ((), (), s32[]{:S(2)}) async-start(), calls=%async_computation.2 | async-start | bytes 4456448 | tf_op jit(solution)/shard_map/reduce_scatter | solution.py:91
  117.3 99.5 %copy-start = (s32[2]{0:T(128)S(1)}, s32[2]{0:T(128)}, u32[]{:S(2)}) copy-start(s32[2]{0:T(128)} %param.12) | copy-start | bytes 28
  117.3 99.4 %copy-start.1 = (s32[2]{0:T(128)S(1)}, s32[2]{0:T(128)}, u32[]{:S(2)}) copy-start(s32[2]{0:T(128)} %param.13) | copy-start | bytes 28
  117.3 97.3 %collective-permute-start.1 = (bf16[512,256]{1,0:T(8,128)(2,1)S(1)}, bf16[512,256]{1,0:T(8,128)(2,1)S(1)}, u32[]{:S(2)}, u32[]{:S(2)}) collective-permute-start(bf16[512,256]{1,0:T(8,128)(2,1)S(1)} %convolution_convert_fusion.1), channel_id=1, source_target_pairs={{0,384},{1,385},{2,386},{3,387},{4,388},{5,389},{6,390},{7,391},{8... | collective-permute-start | bytes 786440 | tf_op jit(solution)/shard_map/ppermute | solution.py:12
  213.3 3.4 collective-permute-start
  219.1 5.1 %collective-permute-start.2 = (bf16[512,256]{1,0:T(8,128)(2,1)S(1)}, bf16[512,256]{1,0:T(8,128)(2,1)S(1)}, u32[]{:S(2)}, u32[]{:S(2)}) collective-permute-start(bf16[512,256]{1,0:T(8,128)(2,1)S(1)} %get-tuple-element.48), channel_id=1, source_target_pairs={{384,0},{385,1},{386,2},{387,3},{388,4},{389,5},{390,6},{391,7},{3... | collective-permute-start | bytes 786440 | tf_op jit(solution)/shard_map/ppermute | solution.py:12
  220.4 3.9 %collective-permute-start.3 = (bf16[512,256]{1,0:T(8,128)(2,1)S(1)}, bf16[512,256]{1,0:T(8,128)(2,1)S(1)}, u32[]{:S(2)}, u32[]{:S(2)}) collective-permute-start(bf16[512,256]{1,0:T(8,128)(2,1)S(1)} %get-tuple-element.49), channel_id=1, source_target_pairs={{384,0},{385,1},{386,2},{387,3},{388,4},{389,5},{390,6},{391,7},{3... | collective-permute-start | bytes 786440 | tf_op jit(solution)/shard_map/ppermute | solution.py:12
Sparse Core Ops, SparseCore 0:
  10.9 102.2 all-gather.3
  116.8 92.4 all-gather.5
  234.1 103.5 reduce-scatter.1
where the time goes:
time: 345 us; the launch traced here: 344 us
  waiting for transfers between devices  301 us (87%)
  matrix products  13.3 us (4%)
  between operations  13.2 us (4%)
  local copies, waits for them, and re-layouts  9.17 us (3%)
  starting transfers between devices  5.28 us (2%)
    all_gather x1, waiting for transfers between devices, local(): lax.all_gather(second_rows, 'mp', axis=1, tiled=True)  104 us
    reduce_scatter x1, waiting for transfers between devices, local(): lax.psum_scatter(lax.cond(is_decoder, one_pair, two_pairs, 0).astype(jnp....  104 us
    all_gather x1, waiting for transfers between devices, local(): lax.all_gather(own_rows, 'mp', axis=1, tiled=True)  90.6 us
  transfers between devices with their start and end apart: 7, of which 4 were waited for; matrix products, arithmetic and copies ran while one was open for 3% of the time, Pallas kernels for 0%

commit v1 on v0

v1 whole, which is shorter than its diff:
```python
import jax
import jax.numpy as jnp
from jax import lax
from jax.experimental import pallas as pl
from jax.experimental.pallas import tpu as pltpu
from jax.sharding import PartitionSpec as P

HS = 256
SIDE = 4
F32 = jnp.float32
BF16 = jnp.bfloat16
SWAP = [(0, 1), (1, 0)]


def shift_x(block, step):
    route = [(y * SIDE + x, y * SIDE + (x + step) % SIDE) for y in range(SIDE) for x in range(SIDE)]
    return lax.ppermute(block, "mp", route)


def shift_y(block, step):
    route = [(y * SIDE + x, (y + step) % SIDE * SIDE + x) for y in range(SIDE) for x in range(SIDE)]
    return lax.ppermute(block, "mp", route)


def cat(*parts):
    return jnp.concatenate(parts, axis=0)


def project(blocks, places, sec, own_w, other_w, total):
    rows = 3 * HS
    count = len(places)
    scalars = jnp.stack([*places, sec]).astype(jnp.int32)
    first = total is None

    def body(scalar_ref, x_ref, u_ref, r_ref, *rest):
        out_ref = rest[-1]
        step = pl.program_id(0)
        shift = pl.multiple_of(scalar_ref[count] * HS, HS)

        @pl.when(step == 0)
        def _():
            if first:
                out_ref[...] = jnp.zeros_like(out_ref)
            else:
                out_ref[...] = rest[0][...]

        low = x_ref[pl.ds(shift, HS), :]
        mid = x_ref[pl.ds(shift + HS, HS), :]
        out_ref[0] += jnp.dot(x_ref[:HS, :], u_ref[0], preferred_element_type=F32)
        out_ref[1] += jnp.dot(low, u_ref[1], preferred_element_type=F32)
        out_ref[2] += jnp.dot(mid, r_ref[0], preferred_element_type=F32)
        out_ref[3] += jnp.dot(x_ref[2 * HS :, :], r_ref[1], preferred_element_type=F32)

    whole = pl.BlockSpec((4, HS, HS), lambda i, s: (0, 0, 0))
    weight = pl.BlockSpec((2, HS, HS), lambda i, s: (0, s[i], 0))
    return pl.pallas_call(
        body,
        out_shape=jax.ShapeDtypeStruct((4, HS, HS), F32),
        grid_spec=pltpu.PrefetchScalarGridSpec(
            num_scalar_prefetch=1,
            grid=(count,),
            in_specs=[pl.BlockSpec((rows, HS), lambda i, s: (i, 0)), weight, weight] + ([] if first else [whole]),
            out_specs=whole,
        ),
        cost_estimate=pl.CostEstimate(
            flops=count * 8 * HS**3, bytes_accessed=count * 7 * HS * HS * 2, transcendentals=0
        ),
    )(scalars, blocks, own_w, other_w, *([] if first else [total]))


def attend_and_spread(total, sec, enc_lengths, dec_lengths, own_w, other_w):
    scale = 1.0 / HS**0.5
    groups = own_w.shape[1] // HS
    scalars = jnp.stack([sec, enc_lengths[sec], dec_lengths[sec]]).astype(jnp.int32)

    def body(scalar_ref, t_ref, u_ref, r_ref, out_ref, g_ref):
        nt = (((1,), (1,)), ((), ()))
        tn = (((0,), (0,)), ((), ()))

        @pl.when(pl.program_id(0) == 0)
        def _():
            me = scalar_ref[0]
            keys = t_ref[2 * me].astype(BF16)
            values = t_ref[2 * me + 1].astype(BF16)
            queries = t_ref[2 - 2 * me].astype(BF16)
            out_grad = t_ref[3 - 2 * me]
            live_q = lax.broadcasted_iota(jnp.int32, (HS, HS), 0) < scalar_ref[2]
            live_k = lax.broadcasted_iota(jnp.int32, (HS, HS), 1) < scalar_ref[1]
            masked = jnp.where(live_q, out_grad, 0.0).astype(BF16)
            scores = lax.dot_general(queries, keys, nt, preferred_element_type=F32) * scale
            scores = jnp.where(live_k, scores, -1e30)
            top = jnp.max(scores, axis=-1, keepdims=True)
            expd = jnp.exp(scores - top)
            probs = expd / jnp.sum(expd, axis=-1, keepdims=True)
            value_grad = lax.dot_general(probs.astype(BF16), masked, tn, preferred_element_type=F32).astype(BF16)
            prob_grad = lax.dot_general(masked, values, nt, preferred_element_type=F32)
            delta = jnp.sum(probs * prob_grad, axis=-1, keepdims=True)
            sg = (probs * (prob_grad - delta)).astype(BF16)
            query_grad = (jnp.dot(sg, keys, preferred_element_type=F32) * scale).astype(BF16)
            key_grad = (lax.dot_general(sg, queries, tn, preferred_element_type=F32) * scale).astype(BF16)
            g_ref[2 * me] = key_grad
            g_ref[2 * me + 1] = value_grad
            g_ref[2 - 2 * me] = query_grad
            g_ref[3 - 2 * me] = jnp.zeros_like(query_grad)

        for slot, w_ref in ((0, u_ref), (1, r_ref)):
            term = lax.dot_general(g_ref[2 * slot], w_ref[0], nt, preferred_element_type=F32)
            term += lax.dot_general(g_ref[2 * slot + 1], w_ref[1], nt, preferred_element_type=F32)
            out_ref[slot, 0] = term.astype(BF16)

    weight = pl.BlockSpec((2, HS, HS), lambda i, s: (0, i, 0))
    return pl.pallas_call(
        body,
        out_shape=jax.ShapeDtypeStruct((2, groups, HS, HS), BF16),
        grid_spec=pltpu.PrefetchScalarGridSpec(
            num_scalar_prefetch=1,
            grid=(groups,),
            in_specs=[pl.BlockSpec((4, HS, HS), lambda i, s: (0, 0, 0)), weight, weight],
            out_specs=pl.BlockSpec((2, 1, HS, HS), lambda i, s: (0, i, 0, 0)),
            scratch_shapes=[pltpu.VMEM((4, HS, HS), BF16)],
        ),
        cost_estimate=pl.CostEstimate(
            flops=groups * 8 * HS**3, bytes_accessed=groups * 6 * HS * HS * 2, transcendentals=HS * HS
        ),
    )(scalars, total, own_w, other_w)


def local(states, proj_weights, out_cotangent, enc_lengths, dec_lengths):
    sec = lax.axis_index("section")
    me = lax.axis_index("mp")
    my_y, my_x = me // SIDE, me % SIDE

    def place(dy, dx):
        return (my_y + dy) % SIDE * SIDE + (my_x + dx) % SIDE

    own_w = proj_weights[0]
    rows = states[0].reshape(2, HS, HS)
    mine = lax.dynamic_index_in_dim(rows, sec, 0, keepdims=False)
    partner = lax.ppermute(lax.dynamic_index_in_dim(rows, 1 - sec, 0, keepdims=False), "section", SWAP)
    other_w = lax.ppermute(own_w, "section", SWAP)
    cotangent = lax.dynamic_slice_in_dim(out_cotangent, sec * HS, HS, 0)
    is_first = sec == 0
    c0 = cat(mine, jnp.where(is_first, partner, cotangent), jnp.where(is_first, cotangent, partner))
    n = c0.shape[0]
    h = n // 2

    up1, down1 = shift_y(c0, 1), shift_y(c0, -1)
    right0, left0 = shift_x(c0, 1), shift_x(c0, -1)
    right1 = shift_x(cat(right0[:h], up1, down1), 1)
    left1 = shift_x(cat(left0[h:], up1, down1), -1)
    up2, down2 = shift_y(up1[:h], 1), shift_y(down1[h:], -1)
    right2 = shift_x(cat(right1[h : 2 * h], right1[h + n : 2 * h + n], up2, down2), 1)
    left2 = shift_x(cat(left1[n : n + h], left1[2 * n : 2 * n + h], up2, down2), -1)
    right3, left3 = shift_x(right2[n : n + h], 1), shift_x(left2[n + h :], -1)

    total = project(
        cat(c0, up1, down1, right0, left0),
        [place(0, 0), place(-1, 0), place(1, 0), place(0, -1), place(0, 1)],
        sec, own_w, other_w, None,
    )
    total = project(
        cat(right1[h:], left1[h:], right1[:h], left1[:h], up2, down2),
        [place(-1, -1), place(1, -1), place(-1, 1), place(1, 1), place(0, 2), place(2, 0)],
        sec, own_w, other_w, total,
    )
    total = project(
        cat(right2[:h], left2[:h], right2[h:n], left2[h:n], right2[n:], left2[n:]),
        [place(-1, 2), place(1, 2), place(2, -1), place(2, 1)],
        sec, own_w, other_w, total,
    )
    total = project(cat(right3, left3), [place(2, 2)], sec, own_w, other_w, total)

    terms = attend_and_spread(total, sec, enc_lengths, dec_lengths, own_w, other_w)
    by_section = jnp.where(is_first, terms, terms[::-1])
    arrived = lax.all_to_all(by_section.reshape(32, HS, HS), ("section", "mp"), 0, 0, tiled=True)
    summed = jnp.sum(arrived.reshape(2, 16, HS, HS).astype(F32), axis=1)
    return summed.astype(BF16).reshape(1, 2 * HS, HS)


def solution(mesh):
    placed = (
        P("section", "dp", "mp"),
        P("section", None, None, "mp"),
        P("dp", "mp"),
        P("dp"),
        P("dp"),
    )
    return jax.shard_map(
        local, mesh=mesh, in_specs=placed, out_specs=P("section", "dp", "mp"), check_vma=False
    )
```

time: 345 us -> 266 us (0.77)
  waiting for transfers between devices: 301 us -> 40.8 us
  blocking collectives: 0 us -> 104 us
  starting transfers between devices: 5.28 us -> 53.1 us
  Pallas kernels: 0 us -> 37.5 us
  matrix products: 13.3 us -> 0 us
  between operations: 13.2 us -> 0.37 us
  other arithmetic: 1.94 us -> 14 us
  local copies, waits for them, and re-layouts: 9.17 us -> 14.4 us
    all_gather x2 -> x0, waiting for transfers between devices: 195 us -> none  [the longest x1 104 us: local(): lax.all_gather(second_rows, 'mp', axis=1, tiled=True)]
    all_to_all x0 -> x1, blocking collectives: none -> 104 us  [local(): lax.all_to_all(by_section.reshape(32, HS, HS), ('section', 'mp'), 0, 0, t...]
    reduce_scatter x1 -> x0, waiting for transfers between devices: 104 us -> none  [local(): lax.psum_scatter(lax.cond(is_decoder, one_pair, two_pairs, 0).astype(jnp....]
    ppermute x4 -> x14, starting transfers between devices: 5.2 us -> 53.1 us  [the longest x8 25.4 us: shift_x(): return lax.ppermute(block, 'mp', route)]
    ppermute x4 -> x14, waiting for transfers between devices: 2.12 us -> 40.8 us  [the longest x8 29.2 us: shift_x(): return lax.ppermute(block, 'mp', route)]
    pallas_call x0 -> x5, Pallas kernels: none -> 37.5 us  [the longest x4 22.2 us: project(): pl.pallas_call(body, out_shape=jax.ShapeDtypeStruct((4, HS, HS), F32), gr...]
    dot_general x7 -> x0, matrix products: 13 us -> none  [the longest x1 4.11 us: local(): other = jnp.dot(full_second, w_second, preferred_element_type=jnp.float32)]
    unnamed x4 -> x26, local copies, waits for them, and re-layouts: 0.01 us -> 9.37 us
  transfers between devices with their start and end apart: 7 -> 14, of which waited for: 4 -> 9; matrix products, arithmetic and copies ran while one was open for 3% -> 6% of each run, Pallas kernels for 0% -> 0%
where the time goes in v1:
time: 266 us; the launch traced here: 265 us
  blocking collectives  104 us (39%)
  starting transfers between devices  53.1 us (20%)
  waiting for transfers between devices  40.8 us (15%)
  Pallas kernels  37.5 us (14%)
  local copies, waits for them, and re-layouts  14.4 us (5%)
  other arithmetic  14 us (5%)
    all_to_all x1, blocking collectives, local(): lax.all_to_all(by_section.reshape(32, HS, HS), ('section', 'mp'), 0, 0, t...  104 us
    ppermute x8, waiting for transfers between devices, shift_x(): return lax.ppermute(block, 'mp', route)  29.2 us
    ppermute x8, starting transfers between devices, shift_x(): return lax.ppermute(block, 'mp', route)  25.4 us
    pallas_call x4, Pallas kernels, project(): pl.pallas_call(body, out_shape=jax.ShapeDtypeStruct((4, HS, HS), F32), gr...  22.2 us
    pallas_call x1, Pallas kernels, attend_and_spread(): pl.pallas_call(body, out_shape=jax.ShapeDtypeStruct((2, groups, HS, HS),...  15.3 us
    ppermute x1, starting transfers between devices, local(): lax.ppermute(lax.dynamic_index_in_dim(rows, 1 - sec, 0, keepdims=False),...  12.4 us
    ppermute x4, starting transfers between devices, shift_y(): return lax.ppermute(block, 'mp', route)  12.4 us
    ppermute x4, waiting for transfers between devices, shift_y(): return lax.ppermute(block, 'mp', route)  11.6 us
  transfers between devices with their start and end apart: 14, of which 9 were waited for; matrix products, arithmetic and copies ran while one was open for 6% of the time, Pallas kernels for 0%

profile of v1, /device:TPU:1, one launch (start us, length us, event | category | flops | bytes accessed | tf_op | source)
XLA Modules:
  0.0 264.6 jit_solution(4502032591186665893)
XLA Ops:
  0.9 12.4 %collective-permute-start = (bf16[256,256]{1,0:T(8,128)(2,1)S(1)}, bf16[256,256]{1,0:T(8,128)(2,1)S(1)}, u32[]{:S(2)}, u32[]{:S(2)}) collective-permute-start(bf16[256,256]{1,0:T(8,128)(2,1)S(1)} %dynamic-slice_bitcast_fusion), channel_id=1, source_target_pairs={{0,384},{384,0},{1,385},{385,1},{2,386},{386,2},{3,387},{387,3},{4... | collective-permute-start | bytes 393224 | tf_op jit(solution)/shard_map/ppermute | solution.py:139
  13.4 1.6 constant_dynamic-update-slice_fusion.8
  14.9 1.6 constant_dynamic-update-slice_fusion.7
  16.5 1.6 constant_dynamic-update-slice_fusion.6
  18.1 1.9 collective-permute-start.9
  20.1 3.4 %collective-permute-start.1 = (bf16[768,256]{1,0:T(8,128)(2,1)S(1)}, bf16[768,256]{1,0:T(8,128)(2,1)S(1)}, u32[]{:S(2)}, u32[]{:S(2)}) collective-permute-start(bf16[768,256]{1,0:T(8,128)(2,1)S(1)} %pad_maximum_fusion.8), channel_id=1, source_target_pairs={{0,1},{1,2},{2,3},{3,0},{4,5},{5,6},{6,7},{7,4},{8,9},{9,10},{10,1... | collective-permute-start | bytes 1179656 | tf_op jit(solution)/shard_map/ppermute | solution.py:17
  23.4 1.9 collective-permute-start.3
  25.4 4.3 %collective-permute-start.2 = (bf16[768,256]{1,0:T(8,128)(2,1)S(1)}, bf16[768,256]{1,0:T(8,128)(2,1)S(1)}, u32[]{:S(2)}, u32[]{:S(2)}) collective-permute-start(bf16[768,256]{1,0:T(8,128)(2,1)S(1)} %pad_maximum_fusion.8), channel_id=1, source_target_pairs={{0,4},{1,5},{2,6},{3,7},{4,8},{5,9},{6,10},{7,11},{8,12},{9,13},{1... | collective-permute-start | bytes 1179656 | tf_op jit(solution)/shard_map/ppermute | solution.py:22
  30.8 3.1 %collective-permute-done.1 = bf16[768,256]{1,0:T(8,128)(2,1)S(1)} collective-permute-done((bf16[768,256]{1,0:T(8,128)(2,1)S(1)}, bf16[768,256]{1,0:T(8,128)(2,1)S(1)}, u32[]{:S(2)}, u32[]{:S(2)}) %collective-permute-start.1) | collective-permute-done | bytes 393248 | tf_op jit(solution)/shard_map/ppermute | solution.py:17
  33.9 6.1 %collective-permute-done.3 = bf16[768,256]{1,0:T(8,128)(2,1)S(1)} collective-permute-done((bf16[768,256]{1,0:T(8,128)(2,1)S(1)}, bf16[768,256]{1,0:T(8,128)(2,1)S(1)}, u32[]{:S(2)}, u32[]{:S(2)}) %collective-permute-start.3) | collective-permute-done | bytes 393248 | tf_op jit(solution)/shard_map/ppermute | solution.py:22
  40.0 5.5 %collective-permute-done.2 = bf16[768,256]{1,0:T(8,128)(2,1)S(1)} collective-permute-done((bf16[768,256]{1,0:T(8,128)(2,1)S(1)}, bf16[768,256]{1,0:T(8,128)(2,1)S(1)}, u32[]{:S(2)}, u32[]{:S(2)}) %collective-permute-start.2) | collective-permute-done | bytes 393248 | tf_op jit(solution)/shard_map/ppermute | solution.py:22
  46.6 2.1 collective-permute-start.4
  48.8 4.4 %collective-permute-start.10 = (bf16[1920,256]{1,0:T(8,128)(2,1)}, bf16[1920,256]{1,0:T(8,128)(2,1)}, u32[]{:S(2)}, u32[]{:S(2)}) collective-permute-start(bf16[1920,256]{1,0:T(8,128)(2,1)} %get-tuple-element.22), channel_id=1, source_target_pairs={{0,3},{1,0},{2,1},{3,2},{4,7},{5,4},{6,5},{7,6},{8,11},{9,8},{10,9... | collective-permute-start | bytes 2949128 | tf_op jit(solution)/shard_map/ppermute | solution.py:17
  53.2 2.9 %collective-permute-start.13 = (bf16[2,4096,256]{2,1,0:T(8,128)(2,1)}, bf16[2,4096,256]{2,1,0:T(8,128)(2,1)}, u32[]{:S(2)}, u32[]{:S(2)}) collective-permute-start(bf16[2,4096,256]{2,1,0:T(8,128)(2,1)} %bitcast.5.u_ref), channel_id=1, source_target_pairs={{0,384},{384,0},{1,385},{385,1},{2,386},{386,2},{3,387},{387,3},{4... | collective-permute-start | bytes 12582920 | tf_op jit(solution)/shard_map/ppermute | solution.py:140
  60.0 1.9 collective-permute-start.6
  62.0 4.3 %collective-permute-start.5 = (bf16[384,256]{1,0:T(8,128)(2,1)S(1)}, bf16[384,256]{1,0:T(8,128)(2,1)S(1)}, u32[]{:S(2)}, u32[]{:S(2)}) collective-permute-start(bf16[384,256]{1,0:T(8,128)(2,1)S(1)} %slice.83), channel_id=1, source_target_pairs={{0,4},{1,5},{2,6},{3,7},{4,8},{5,9},{6,10},{7,11},{8,12},{9,13},{1... | collective-permute-start | bytes 589832 | tf_op jit(solution)/shard_map/ppermute | solution.py:22
  66.2 6.5 %collective-permute-done.4 = bf16[1920,256]{1,0:T(8,128)(2,1)} collective-permute-done((bf16[1920,256]{1,0:T(8,128)(2,1)S(1)}, bf16[1920,256]{1,0:T(8,128)(2,1)}, u32[]{:S(2)}, u32[]{:S(2)}) %collective-permute-start.4) | collective-permute-done | bytes 983072 | tf_op jit(solution)/shard_map/ppermute | solution.py:17
  77.6 3.7 %collective-permute-start.7 = (bf16[1536,256]{1,0:T(8,128)(2,1)S(1)}, bf16[1536,256]{1,0:T(8,128)(2,1)S(1)}, u32[]{:S(2)}, u32[]{:S(2)}) collective-permute-start(bf16[1536,256]{1,0:T(8,128)(2,1)S(1)} %get-tuple-element.23), channel_id=1, source_target_pairs={{0,1},{1,2},{2,3},{3,0},{4,5},{5,6},{6,7},{7,4},{8,9},{9,10},{10,1... | collective-permute-start | bytes 2359304 | tf_op jit(solution)/shard_map/ppermute | solution.py:17
  81.3 1.9 pad_add_fusion.scalar_ref
  83.9 3.4 %collective-permute-start.11 = (bf16[1536,256]{1,0:T(8,128)(2,1)S(1)}, bf16[1536,256]{1,0:T(8,128)(2,1)S(1)}, u32[]{:S(2)}, u32[]{:S(2)}) collective-permute-start(bf16[1536,256]{1,0:T(8,128)(2,1)S(1)} %get-tuple-element.24), channel_id=1, source_target_pairs={{0,3},{1,0},{2,1},{3,2},{4,7},{5,4},{6,5},{7,6},{8,11},{9,8},{10,9... | collective-permute-start | bytes 2359304 | tf_op jit(solution)/shard_map/ppermute | solution.py:17
  89.8 9.2 %collective-permute-done.7 = bf16[1536,256]{1,0:T(8,128)(2,1)S(1)} collective-permute-done((bf16[1536,256]{1,0:T(8,128)(2,1)S(1)}, bf16[1536,256]{1,0:T(8,128)(2,1)S(1)}, u32[]{:S(2)}, u32[]{:S(2)}) %collective-permute-start.7) | collective-permute-done | bytes 786464 | tf_op jit(solution)/shard_map/ppermute | solution.py:17
  99.0 4.2 %collective-permute-done.11 = bf16[1536,256]{1,0:T(8,128)(2,1)S(1)} collective-permute-done((bf16[1536,256]{1,0:T(8,128)(2,1)S(1)}, bf16[1536,256]{1,0:T(8,128)(2,1)S(1)}, u32[]{:S(2)}, u32[]{:S(2)}) %collective-permute-start.11) | collective-permute-done | bytes 786464 | tf_op jit(solution)/shard_map/ppermute | solution.py:17
  103.3 4.6 %collective-permute-start.12 = (bf16[384,256]{1,0:T(8,128)(2,1)S(1)}, bf16[384,256]{1,0:T(8,128)(2,1)S(1)}, u32[]{:S(2)}, u32[]{:S(2)}) collective-permute-start(bf16[384,256]{1,0:T(8,128)(2,1)S(1)} %get-tuple-element.18), channel_id=1, source_target_pairs={{0,3},{1,0},{2,1},{3,2},{4,7},{5,4},{6,5},{7,6},{8,11},{9,8},{10,9... | collective-permute-start | bytes 589832 | tf_op jit(solution)/shard_map/ppermute | solution.py:17
  107.9 1.9 collective-permute-start.8
  111.1 4.4 %collective-permute-done.8 = bf16[384,256]{1,0:T(8,128)(2,1)S(1)} collective-permute-done((bf16[384,256]{1,0:T(8,128)(2,1)S(1)}, bf16[384,256]{1,0:T(8,128)(2,1)S(1)}, u32[]{:S(2)}, u32[]{:S(2)}) %collective-permute-start.8) | collective-permute-done | bytes 196640 | tf_op jit(solution)/shard_map/ppermute | solution.py:17
  116.3 6.1 %shard_map.55.rest_0_ = f32[4,256,256]{2,1,0:T(8,128)} custom-call(s32[6]{0:T(128)} %stack.91.scalar_ref, bf16[3840,256]{1,0:T(8,128)(2,1)} %constant_dynamic-update-slice_fusion.2.x_ref, bf16[2,4096,256]{2,1,0:T(8,128)(2,1)} %bitcast.5.u_ref, bf16[2,4096,256]{2,1,0:T(8,128)(2,1)} %collective-permute-done.13.r_ref), custom_call_target="tpu_custom_call" | custom-call | flops 671088640 | bytes 4587520 | tf_op jit(solution)/shard_map/pallas_call | solution.py:56
  122.5 7.0 %shard_map.56.rest_0_ = f32[4,256,256]{2,1,0:T(8,128)} custom-call(s32[7]{0:T(128)} %stack.85.scalar_ref, bf16[4608,256]{1,0:T(8,128)(2,1)} %copy-done, bf16[2,4096,256]{2,1,0:T(8,128)(2,1)} %bitcast.5.u_ref, bf16[2,4096,256]{2,1,0:T(8,128)(2,1)} %collective-permute-done.13.r_ref, f32[4,256,256]{2,1,0:T(8,128)} %shard_map.55.rest_0_), custom_call_target="tpu_custom_call" | custom-call | flops 805306368 | bytes 5505024 | tf_op jit(solution)/shard_map/pallas_call | solution.py:56
  129.5 5.5 %shard_map.57.rest_0_ = f32[4,256,256]{2,1,0:T(8,128)} custom-call(s32[5]{0:T(128)} %stack.78.scalar_ref, bf16[3072,256]{1,0:T(8,128)(2,1)} %copy-done.1, bf16[2,4096,256]{2,1,0:T(8,128)(2,1)} %bitcast.5.u_ref, bf16[2,4096,256]{2,1,0:T(8,128)(2,1)} %collective-permute-done.13.r_ref, f32[4,256,256]{2,1,0:T(8,128)} %shard_map.56.rest_0_), custom_call_target="tpu_custom_call" | custom-call | flops 536870912 | bytes 3670016 | tf_op jit(solution)/shard_map/pallas_call | solution.py:56
  135.0 3.6 %shard_map.58.t_ref = f32[4,256,256]{2,1,0:T(8,128)} custom-call(s32[2]{0:T(128)} %pad_add_fusion.1.scalar_ref, bf16[768,256]{1,0:T(8,128)(2,1)} %pad_maximum_fusion.9.x_ref, bf16[2,4096,256]{2,1,0:T(8,128)(2,1)} %bitcast.5.u_ref, bf16[2,4096,256]{2,1,0:T(8,128)(2,1)} %collective-permute-done.13.r_ref, f32[4,256,256]{2,1,0:T(8,128)} %shard_map.57.rest_0_), custom_call_target="tpu_custom_call" | custom-call | flops 134217728 | bytes 917504 | tf_op jit(solution)/shard_map/pallas_call | solution.py:56
  138.5 15.3 %shard_map.59 = bf16[2,16,256,256]{3,2,1,0:T(8,128)(2,1)} custom-call(s32[3]{0:T(128)} %pad_add_fusion.scalar_ref, f32[4,256,256]{2,1,0:T(8,128)} %shard_map.58.t_ref, bf16[2,4096,256]{2,1,0:T(8,128)(2,1)} %bitcast.5.u_ref, bf16[2,4096,256]{2,1,0:T(8,128)(2,1)} %collective-permute-done.13.r_ref), custom_call_target="tpu_custom_call" | custom-call | flops 2147483648 | bytes 12582912 | tf_op jit(solution)/shard_map/pallas_call | solution.py:112
  153.9 5.0 %reverse_select_fusion = bf16[2,16,256,256]{3,2,1,0:T(8,128)(2,1)S(1)} fusion(bf16[2,16,256,256]{3,2,1,0:T(8,128)(2,1)} %shard_map.59, pred[]{:T(512)S(6)} %eq.37), kind=kLoop, calls=%fused_computation | loop fusion | flops 2097152 | bytes 8388609 | tf_op jit(solution)/shard_map/jit(_where)/select_n | solution.py:174
  158.8 104.5 %all_to_all.5 = bf16[32,256,256]{2,1,0:T(8,128)(2,1)S(1)} all-to-all(bf16[32,256,256]{2,1,0:T(8,128)(2,1)S(1)} %bitcast.28), channel_id=1, replica_groups=mesh['section'=2,'dp'=24,'mp'=16] {'section','mp'}, dimensions={0} | all-to-all | bytes 8388608 | tf_op jit(solution)/shard_map/all_to_all | solution.py:175
  (51 shorter events, 18.4 us)
Async XLA Ops:
  0.9 14.0 %collective-permute-start = (bf16[256,256]{1,0:T(8,128)(2,1)S(1)}, bf16[256,256]{1,0:T(8,128)(2,1)S(1)}, u32[]{:S(2)}, u32[]{:S(2)}) collective-permute-start(bf16[256,256]{1,0:T(8,128)(2,1)S(1)} %dynamic-slice_bitcast_fusion), channel_id=1, source_target_pairs={{0,384},{384,0},{1,385},{385,1},{2,386},{386,2},{3,387},{387,3},{4... | collective-permute-start | bytes 393224 | tf_op jit(solution)/shard_map/ppermute | solution.py:139
  18.1 12.6 %collective-permute-start.9 = (bf16[768,256]{1,0:T(8,128)(2,1)S(1)}, bf16[768,256]{1,0:T(8,128)(2,1)S(1)}, u32[]{:S(2)}, u32[]{:S(2)}) collective-permute-start(bf16[768,256]{1,0:T(8,128)(2,1)S(1)} %pad_maximum_fusion.8), channel_id=1, source_target_pairs={{0,3},{1,0},{2,1},{3,2},{4,7},{5,4},{6,5},{7,6},{8,11},{9,8},{10,9... | collective-permute-start | bytes 1179656 | tf_op jit(solution)/shard_map/ppermute | solution.py:17
  20.1 13.8 %collective-permute-start.1 = (bf16[768,256]{1,0:T(8,128)(2,1)S(1)}, bf16[768,256]{1,0:T(8,128)(2,1)S(1)}, u32[]{:S(2)}, u32[]{:S(2)}) collective-permute-start(bf16[768,256]{1,0:T(8,128)(2,1)S(1)} %pad_maximum_fusion.8), channel_id=1, source_target_pairs={{0,1},{1,2},{2,3},{3,0},{4,5},{5,6},{6,7},{7,4},{8,9},{9,10},{10,1... | collective-permute-start | bytes 1179656 | tf_op jit(solution)/shard_map/ppermute | solution.py:17
  23.4 16.6 %collective-permute-start.3 = (bf16[768,256]{1,0:T(8,128)(2,1)S(1)}, bf16[768,256]{1,0:T(8,128)(2,1)S(1)}, u32[]{:S(2)}, u32[]{:S(2)}) collective-permute-start(bf16[768,256]{1,0:T(8,128)(2,1)S(1)} %pad_maximum_fusion.8), channel_id=1, source_target_pairs={{0,12},{1,13},{2,14},{3,15},{4,0},{5,1},{6,2},{7,3},{8,4},{9,5},{1... | collective-permute-start | bytes 1179656 | tf_op jit(solution)/shard_map/ppermute | solution.py:22
  25.4 20.2 %collective-permute-start.2 = (bf16[768,256]{1,0:T(8,128)(2,1)S(1)}, bf16[768,256]{1,0:T(8,128)(2,1)S(1)}, u32[]{:S(2)}, u32[]{:S(2)}) collective-permute-start(bf16[768,256]{1,0:T(8,128)(2,1)S(1)} %pad_maximum_fusion.8), channel_id=1, source_target_pairs={{0,4},{1,5},{2,6},{3,7},{4,8},{5,9},{6,10},{7,11},{8,12},{9,13},{1... | collective-permute-start | bytes 1179656 | tf_op jit(solution)/shard_map/ppermute | solution.py:22
  30.8 26.0 %copy-start.4 = (s32[2]{0:T(128)S(1)}, s32[2]{0:T(128)}, u32[]{:S(2)}) copy-start(s32[2]{0:T(128)} %param.9) | copy-start | bytes 28
  30.8 26.6 %copy-start.5 = (s32[2]{0:T(128)S(1)}, s32[2]{0:T(128)}, u32[]{:S(2)}) copy-start(s32[2]{0:T(128)} %param.8) | copy-start | bytes 28
  33.9 6.1 %copy-start.2 = (bf16[768,256]{1,0:T(8,128)(2,1)}, bf16[768,256]{1,0:T(8,128)(2,1)S(1)}, u32[]{:S(2)}) copy-start(bf16[768,256]{1,0:T(8,128)(2,1)S(1)} %collective-permute-done.1) | copy-start | bytes 1179652
  46.6 26.1 %collective-permute-start.4 = (bf16[1920,256]{1,0:T(8,128)(2,1)S(1)}, bf16[1920,256]{1,0:T(8,128)(2,1)}, u32[]{:S(2)}, u32[]{:S(2)}) collective-permute-start(bf16[1920,256]{1,0:T(8,128)(2,1)S(1)} %get-tuple-element.21), channel_id=1, source_target_pairs={{0,1},{1,2},{2,3},{3,0},{4,5},{5,6},{6,7},{7,4},{8,9},{9,10},{10,1... | collective-permute-start | bytes 2949128 | tf_op jit(solution)/shard_map/ppermute | solution.py:17
  48.8 25.2 %collective-permute-start.10 = (bf16[1920,256]{1,0:T(8,128)(2,1)}, bf16[1920,256]{1,0:T(8,128)(2,1)}, u32[]{:S(2)}, u32[]{:S(2)}) collective-permute-start(bf16[1920,256]{1,0:T(8,128)(2,1)} %get-tuple-element.22), channel_id=1, source_target_pairs={{0,3},{1,0},{2,1},{3,2},{4,7},{5,4},{6,5},{7,6},{8,11},{9,8},{10,9... | collective-permute-start | bytes 2949128 | tf_op jit(solution)/shard_map/ppermute | solution.py:17
  53.2 63.2 %collective-permute-start.13 = (bf16[2,4096,256]{2,1,0:T(8,128)(2,1)}, bf16[2,4096,256]{2,1,0:T(8,128)(2,1)}, u32[]{:S(2)}, u32[]{:S(2)}) collective-permute-start(bf16[2,4096,256]{2,1,0:T(8,128)(2,1)} %bitcast.5.u_ref), channel_id=1, source_target_pairs={{0,384},{384,0},{1,385},{385,1},{2,386},{386,2},{3,387},{387,3},{4... | collective-permute-start | bytes 12582920 | tf_op jit(solution)/shard_map/ppermute | solution.py:140
  60.0 17.4 %collective-permute-start.6 = (bf16[384,256]{1,0:T(8,128)(2,1)S(1)}, bf16[384,256]{1,0:T(8,128)(2,1)S(1)}, u32[]{:S(2)}, u32[]{:S(2)}) collective-permute-start(bf16[384,256]{1,0:T(8,128)(2,1)S(1)} %slice.84), channel_id=1, source_target_pairs={{0,12},{1,13},{2,14},{3,15},{4,0},{5,1},{6,2},{7,3},{8,4},{9,5},{1... | collective-permute-start | bytes 589832 | tf_op jit(solution)/shard_map/ppermute | solution.py:22
  62.0 15.5 %collective-permute-start.5 = (bf16[384,256]{1,0:T(8,128)(2,1)S(1)}, bf16[384,256]{1,0:T(8,128)(2,1)S(1)}, u32[]{:S(2)}, u32[]{:S(2)}) collective-permute-start(bf16[384,256]{1,0:T(8,128)(2,1)S(1)} %slice.83), channel_id=1, source_target_pairs={{0,4},{1,5},{2,6},{3,7},{4,8},{5,9},{6,10},{7,11},{8,12},{9,13},{1... | collective-permute-start | bytes 589832 | tf_op jit(solution)/shard_map/ppermute | solution.py:22
  77.5 10.7 %copy-start.3 = (bf16[768,256]{1,0:T(8,128)(2,1)S(1)}, bf16[768,256]{1,0:T(8,128)(2,1)}, u32[]{:S(2)}) copy-start(bf16[768,256]{1,0:T(8,128)(2,1)} %copy-done.2) | copy-start | bytes 1179652
  77.6 21.4 %collective-permute-start.7 = (bf16[1536,256]{1,0:T(8,128)(2,1)S(1)}, bf16[1536,256]{1,0:T(8,128)(2,1)S(1)}, u32[]{:S(2)}, u32[]{:S(2)}) collective-permute-start(bf16[1536,256]{1,0:T(8,128)(2,1)S(1)} %get-tuple-element.23), channel_id=1, source_target_pairs={{0,1},{1,2},{2,3},{3,0},{4,5},{5,6},{6,7},{7,4},{8,9},{9,10},{10,1... | collective-permute-start | bytes 2359304 | tf_op jit(solution)/shard_map/ppermute | solution.py:17
  83.9 19.3 %collective-permute-start.11 = (bf16[1536,256]{1,0:T(8,128)(2,1)S(1)}, bf16[1536,256]{1,0:T(8,128)(2,1)S(1)}, u32[]{:S(2)}, u32[]{:S(2)}) collective-permute-start(bf16[1536,256]{1,0:T(8,128)(2,1)S(1)} %get-tuple-element.24), channel_id=1, source_target_pairs={{0,3},{1,0},{2,1},{3,2},{4,7},{5,4},{6,5},{7,6},{8,11},{9,8},{10,9... | collective-permute-start | bytes 2359304 | tf_op jit(solution)/shard_map/ppermute | solution.py:17
  89.8 20.1 %copy-start = (bf16[4608,256]{1,0:T(8,128)(2,1)}, bf16[4608,256]{1,0:T(8,128)(2,1)S(1)}, u32[]{:S(2)}) copy-start(bf16[4608,256]{1,0:T(8,128)(2,1)S(1)} %constant_dynamic-update-slice_fusion.x_ref) | copy-start | bytes 7077892
  103.3 7.2 %collective-permute-start.12 = (bf16[384,256]{1,0:T(8,128)(2,1)S(1)}, bf16[384,256]{1,0:T(8,128)(2,1)S(1)}, u32[]{:S(2)}, u32[]{:S(2)}) collective-permute-start(bf16[384,256]{1,0:T(8,128)(2,1)S(1)} %get-tuple-element.18), channel_id=1, source_target_pairs={{0,3},{1,0},{2,1},{3,2},{4,7},{5,4},{6,5},{7,6},{8,11},{9,8},{10,9... | collective-permute-start | bytes 589832 | tf_op jit(solution)/shard_map/ppermute | solution.py:17
  107.9 7.6 %collective-permute-start.8 = (bf16[384,256]{1,0:T(8,128)(2,1)S(1)}, bf16[384,256]{1,0:T(8,128)(2,1)S(1)}, u32[]{:S(2)}, u32[]{:S(2)}) collective-permute-start(bf16[384,256]{1,0:T(8,128)(2,1)S(1)} %get-tuple-element.20), channel_id=1, source_target_pairs={{0,1},{1,2},{2,3},{3,0},{4,5},{5,6},{6,7},{7,4},{8,9},{9,10},{10,1... | collective-permute-start | bytes 589832 | tf_op jit(solution)/shard_map/ppermute | solution.py:17
  109.9 1.2 copy-start.1

commit v2 on v1

v2 whole, which is shorter than its diff:
```python
import jax
import jax.numpy as jnp
from jax import lax
from jax.experimental import pallas as pl
from jax.experimental.pallas import tpu as pltpu
from jax.sharding import PartitionSpec as P

HS = 256
SIDE = 4
F32 = jnp.float32
BF16 = jnp.bfloat16
SWAP = [(0, 1), (1, 0)]
NT = (((1,), (1,)), ((), ()))
TN = (((0,), (0,)), ((), ()))


def shift_x(block, step):
    route = [(y * SIDE + x, y * SIDE + (x + step) % SIDE) for y in range(SIDE) for x in range(SIDE)]
    return lax.ppermute(block, "mp", route)


def shift_y(block, step):
    route = [(y * SIDE + x, (y + step) % SIDE * SIDE + x) for y in range(SIDE) for x in range(SIDE)]
    return lax.ppermute(block, "mp", route)


def cat(*parts):
    return jnp.concatenate(parts, axis=0)


def project(blocks, places, sec, own_w, other_w, total):
    rows = 3 * HS
    count = len(places)
    scalars = jnp.stack([*places, sec]).astype(jnp.int32)
    first = total is None

    def body(scalar_ref, x_ref, u_ref, r_ref, *rest):
        out_ref = rest[-1]
        step = pl.program_id(0)
        shift = pl.multiple_of(scalar_ref[count] * HS, HS)

        @pl.when(step == 0)
        def _():
            if first:
                out_ref[...] = jnp.zeros_like(out_ref)
            else:
                out_ref[...] = rest[0][...]

        low = x_ref[pl.ds(shift, HS), :]
        mid = x_ref[pl.ds(shift + HS, HS), :]
        out_ref[0] += jnp.dot(x_ref[:HS, :], u_ref[0], preferred_element_type=F32)
        out_ref[1] += jnp.dot(low, u_ref[1], preferred_element_type=F32)
        out_ref[2] += jnp.dot(mid, r_ref[0], preferred_element_type=F32)
        out_ref[3] += jnp.dot(x_ref[2 * HS :, :], r_ref[1], preferred_element_type=F32)

    whole = pl.BlockSpec((4, HS, HS), lambda i, s: (0, 0, 0))
    weight = pl.BlockSpec((2, HS, HS), lambda i, s: (0, s[i], 0))
    return pl.pallas_call(
        body,
        out_shape=jax.ShapeDtypeStruct((4, HS, HS), F32),
        grid_spec=pltpu.PrefetchScalarGridSpec(
            num_scalar_prefetch=1,
            grid=(count,),
            in_specs=[pl.BlockSpec((rows, HS), lambda i, s: (i, 0)), weight, weight] + ([] if first else [whole]),
            out_specs=whole,
        ),
        cost_estimate=pl.CostEstimate(
            flops=count * 8 * HS**3, bytes_accessed=count * 7 * HS * HS * 2, transcendentals=0
        ),
    )(scalars, blocks, own_w, other_w, *([] if first else [total]))


def attend_and_spread(total, places, sec, enc_lengths, dec_lengths, own_w, other_w):
    scale = 1.0 / HS**0.5
    count = len(places)
    scalars = jnp.stack([*places, sec, enc_lengths[sec], dec_lengths[sec]]).astype(jnp.int32)

    def body(scalar_ref, t_ref, u_ref, r_ref, out_ref, g_ref):
        @pl.when(pl.program_id(0) == 0)
        def _():
            me = scalar_ref[count]
            keys = t_ref[2 * me].astype(BF16)
            values = t_ref[2 * me + 1].astype(BF16)
            queries = t_ref[2 - 2 * me].astype(BF16)
            out_grad = t_ref[3 - 2 * me]
            live_q = lax.broadcasted_iota(jnp.int32, (HS, HS), 0) < scalar_ref[count + 2]
            live_k = lax.broadcasted_iota(jnp.int32, (HS, HS), 1) < scalar_ref[count + 1]
            masked = jnp.where(live_q, out_grad, 0.0).astype(BF16)
            scores = lax.dot_general(queries, keys, NT, preferred_element_type=F32) * scale
            scores = jnp.where(live_k, scores, -1e30)
            top = jnp.max(scores, axis=-1, keepdims=True)
            expd = jnp.exp(scores - top)
            probs = expd / jnp.sum(expd, axis=-1, keepdims=True)
            value_grad = lax.dot_general(probs.astype(BF16), masked, TN, preferred_element_type=F32).astype(BF16)
            prob_grad = lax.dot_general(masked, values, NT, preferred_element_type=F32)
            delta = jnp.sum(probs * prob_grad, axis=-1, keepdims=True)
            sg = (probs * (prob_grad - delta)).astype(BF16)
            query_grad = (jnp.dot(sg, keys, preferred_element_type=F32) * scale).astype(BF16)
            key_grad = (lax.dot_general(sg, queries, TN, preferred_element_type=F32) * scale).astype(BF16)
            g_ref[2 * me] = key_grad
            g_ref[2 * me + 1] = value_grad
            g_ref[2 - 2 * me] = query_grad
            g_ref[3 - 2 * me] = jnp.zeros_like(query_grad)

        one_block(g_ref, u_ref, r_ref, out_ref)

    whole = pl.BlockSpec((4, HS, HS), lambda i, s: (0, 0, 0))
    weight = pl.BlockSpec((2, HS, HS), lambda i, s: (0, s[i], 0))
    return pl.pallas_call(
        body,
        out_shape=(
            jax.ShapeDtypeStruct((count, 2 * HS, HS), BF16),
            jax.ShapeDtypeStruct((4, HS, HS), BF16),
        ),
        grid_spec=pltpu.PrefetchScalarGridSpec(
            num_scalar_prefetch=1,
            grid=(count,),
            in_specs=[whole, weight, weight],
            out_specs=(pl.BlockSpec((1, 2 * HS, HS), lambda i, s: (i, 0, 0)), whole),
        ),
        cost_estimate=spread_cost(count),
    )(scalars, total, own_w, other_w)


def one_block(g_ref, u_ref, r_ref, out_ref):
    for slot, w_ref in ((0, u_ref), (1, r_ref)):
        term = lax.dot_general(g_ref[2 * slot], w_ref[0], NT, preferred_element_type=F32)
        term += lax.dot_general(g_ref[2 * slot + 1], w_ref[1], NT, preferred_element_type=F32)
        out_ref[0, slot * HS : (slot + 1) * HS, :] = term.astype(BF16)


def spread_cost(count):
    return pl.CostEstimate(flops=count * 8 * HS**3, bytes_accessed=count * 12 * HS * HS, transcendentals=HS * HS)


def spread(grads, places, own_w, other_w):
    count = len(places)

    def body(scalar_ref, g_ref, u_ref, r_ref, out_ref):
        one_block(g_ref, u_ref, r_ref, out_ref)

    weight = pl.BlockSpec((2, HS, HS), lambda i, s: (0, s[i], 0))
    return pl.pallas_call(
        body,
        out_shape=jax.ShapeDtypeStruct((count, 2 * HS, HS), BF16),
        grid_spec=pltpu.PrefetchScalarGridSpec(
            num_scalar_prefetch=1,
            grid=(count,),
            in_specs=[pl.BlockSpec((4, HS, HS), lambda i, s: (0, 0, 0)), weight, weight],
            out_specs=pl.BlockSpec((1, 2 * HS, HS), lambda i, s: (i, 0, 0)),
        ),
        cost_estimate=spread_cost(count),
    )(jnp.stack(places).astype(jnp.int32), grads, own_w, other_w)


def plus(*parts):
    return sum(p.astype(F32) for p in parts).astype(BF16)


def local(states, proj_weights, out_cotangent, enc_lengths, dec_lengths):
    sec = lax.axis_index("section")
    me = lax.axis_index("mp")
    my_y, my_x = me // SIDE, me % SIDE

    def place(dy, dx):
        return (my_y + dy) % SIDE * SIDE + (my_x + dx) % SIDE

    own_w = proj_weights[0]
    rows = states[0].reshape(2, HS, HS)
    mine = lax.dynamic_index_in_dim(rows, sec, 0, keepdims=False)
    partner = lax.ppermute(lax.dynamic_index_in_dim(rows, 1 - sec, 0, keepdims=False), "section", SWAP)
    other_w = lax.ppermute(own_w, "section", SWAP)
    cotangent = lax.dynamic_slice_in_dim(out_cotangent, sec * HS, HS, 0)
    is_first = sec == 0
    c0 = cat(mine, jnp.where(is_first, partner, cotangent), jnp.where(is_first, cotangent, partner))
    n = c0.shape[0]
    h = n // 2

    up1, down1 = shift_y(c0, 1), shift_y(c0, -1)
    right0, left0, across0 = shift_x(c0, 1), shift_x(c0, -1), shift_x(c0, 2)
    pair = cat(up1, down1)
    right1, left1 = shift_x(pair, 1), shift_x(pair, -1)
    up2, down2 = shift_y(up1[:h], 1), shift_y(down1[h:], -1)
    total = project(
        cat(c0, pair, right0, left0, across0),
        [place(0, 0), place(-1, 0), place(1, 0), place(0, -1), place(0, 1), place(0, 2)],
        sec, own_w, other_w, None,
    )
    right1, left1, up2, down2, total = lax.optimization_barrier((right1, left1, up2, down2, total))
    last = cat(up2, down2)
    right2 = shift_x(cat(right1[:h], right1[n : n + h], last), 1)
    left2 = shift_x(cat(left1[h:n], left1[n + h :], last), -1)
    across2 = shift_x(last, 2)
    total = project(
        cat(right1, left1, last),
        [place(-1, -1), place(1, -1), place(-1, 1), place(1, 1), place(2, 0)],
        sec, own_w, other_w, total,
    )
    right2, left2, across2, total = lax.optimization_barrier((right2, left2, across2, total))
    total = project(
        cat(right2[:h], left2[:h], right2[h:n], left2[h:n], right2[n:], left2[n:], across2),
        [place(-1, 2), place(1, 2), place(2, -1), place(2, 1), place(2, 2)],
        sec, own_w, other_w, total,
    )

    n, h = 2 * HS, HS
    early = [(2, 1), (2, -1), (2, 2), (1, 2), (-1, 2)]
    late = [(1, 1), (1, -1), (-1, 1), (-1, -1), (0, 2), (2, 0), (1, 0), (-1, 0), (0, 1), (0, -1), (0, 0)]
    terms, grads = attend_and_spread(
        total, [place(*p) for p in early], sec, enc_lengths, dec_lengths, own_w, other_w
    )
    t = {p: terms[i] for i, p in enumerate(early)}
    right_a = shift_x(cat(t[2, 1], t[1, 2][:h], t[-1, 2][:h]), 1)
    left_a = shift_x(cat(t[2, -1], t[1, 2][h:], t[-1, 2][h:]), -1)
    across_a = shift_x(t[2, 2], 2)
    terms = spread(grads, [place(*p) for p in late], own_w, other_w)
    t |= {p: terms[i] for i, p in enumerate(late)}

    far = plus(t[2, 0], right_a[:n], left_a[:n], across_a)
    up_b, down_b = shift_y(far[:h], 1), shift_y(far[h:], -1)
    right_b = shift_x(
        cat(
            plus(t[1, 1][:h], right_a[n : n + h]), t[1, 1][h:],
            plus(t[-1, 1][:h], right_a[n + h :]), t[-1, 1][h:],
            t[0, 2][:h],
        ),
        1,
    )
    left_b = shift_x(
        cat(
            t[1, -1][:h], plus(t[1, -1][h:], left_a[n : n + h]),
            t[-1, -1][:h], plus(t[-1, -1][h:], left_a[n + h :]),
            t[0, 2][h:],
        ),
        -1,
    )
    up_c = shift_y(
        cat(
            plus(t[1, 0][:h], right_b[:h], left_b[:h], up_b),
            plus(t[1, 0][h:], right_b[h:n], left_b[h:n]),
        ),
        1,
    )
    down_c = shift_y(
        cat(
            plus(t[-1, 0][:h], right_b[n : n + h], left_b[n : n + h]),
            plus(t[-1, 0][h:], right_b[n + h : 2 * n], left_b[n + h : 2 * n], down_b),
        ),
        -1,
    )
    right_c = shift_x(cat(plus(t[0, 1][:h], right_b[2 * n :]), t[0, 1][h:]), 1)
    left_c = shift_x(cat(t[0, -1][:h], plus(t[0, -1][h:], left_b[2 * n :])), -1)
    swapped = lax.ppermute(plus(t[0, 0][h:], right_c[h:], left_c[h:], up_c[h:], down_c[h:]), "section", SWAP)
    kept = plus(t[0, 0][:h], right_c[:h], left_c[:h], up_c[:h], down_c[:h])
    return jnp.where(is_first, cat(kept, swapped), cat(swapped, kept))[None]


def solution(mesh):
    placed = (
        P("section", "dp", "mp"),
        P("section", None, None, "mp"),
        P("dp", "mp"),
        P("dp"),
        P("dp"),
    )
    return jax.shard_map(
        local, mesh=mesh, in_specs=placed, out_specs=P("section", "dp", "mp"), check_vma=False
    )
```

time: 266 us -> 232 us (0.87)
  blocking collectives: 104 us -> 0 us
  starting transfers between devices: 53.1 us -> 109 us
  local copies, waits for them, and re-layouts: 14.4 us -> 28.4 us
    all_to_all x1 -> x0, blocking collectives: 104 us -> none  [local(): lax.all_to_all(by_section.reshape(32, HS, HS), ('section', 'mp'), 0, 0, t...]
    ppermute x8 -> x15, starting transfers between devices: 25.4 us -> 49.2 us  [shift_x(): return lax.ppermute(block, 'mp', route)]
    ppermute x0 -> x1, starting transfers between devices: none -> 17 us  [local(): lax.ppermute(plus(t[0, 0][h:], right_c[h:], left_c[h:], up_c[h:], down_c[...]
    ppermute x4 -> x8, starting transfers between devices: 12.4 us -> 28.8 us  [shift_y(): return lax.ppermute(block, 'mp', route)]
    ppermute x8 -> x15, waiting for transfers between devices: 29.2 us -> 18 us  [shift_x(): return lax.ppermute(block, 'mp', route)]
    ppermute x1, starting transfers between devices: 12.4 us -> 1.92 us  [local(): lax.ppermute(lax.dynamic_index_in_dim(rows, 1 - sec, 0, keepdims=False),...]
    ppermute x1, starting transfers between devices: 2.94 us -> 12.4 us  [local(): other_w = lax.ppermute(own_w, 'section', SWAP)]
    ppermute x4 -> x8, waiting for transfers between devices: 11.6 us -> 19.8 us  [shift_y(): return lax.ppermute(block, 'mp', route)]
  transfers between devices with their start and end apart: 14 -> 26, of which waited for: 9 -> 10; matrix products, arithmetic and copies ran while one was open for 6% -> 11% of each run, Pallas kernels for 0% -> 10%
where the time goes in v2:
time: 232 us; the launch traced here: 230 us
  starting transfers between devices  109 us (47%)
  waiting for transfers between devices  41.9 us (18%)
  Pallas kernels  37.4 us (16%)
  local copies, waits for them, and re-layouts  28.4 us (12%)
  other arithmetic  11.9 us (5%)
    ppermute x15, starting transfers between devices, shift_x(): return lax.ppermute(block, 'mp', route)  49.2 us
    ppermute x8, starting transfers between devices, shift_y(): return lax.ppermute(block, 'mp', route)  28.8 us
    ppermute x8, waiting for transfers between devices, shift_y(): return lax.ppermute(block, 'mp', route)  19.8 us
    pallas_call x3, Pallas kernels, project(): pl.pallas_call(body, out_shape=jax.ShapeDtypeStruct((4, HS, HS), F32), gr...  19.7 us
    ppermute x15, waiting for transfers between devices, shift_x(): return lax.ppermute(block, 'mp', route)  18 us
    ppermute x1, starting transfers between devices, local(): lax.ppermute(plus(t[0, 0][h:], right_c[h:], left_c[h:], up_c[h:], down_c[...  17 us
    unnamed x27, local copies, waits for them, and re-layouts  13.3 us
    ppermute x1, starting transfers between devices, local(): other_w = lax.ppermute(own_w, 'section', SWAP)  12.4 us
  transfers between devices with their start and end apart: 26, of which 10 were waited for; matrix products, arithmetic and copies ran while one was open for 11% of the time, Pallas kernels for 10%

profile of v2, /device:TPU:1, one launch (start us, length us, event | category | flops | bytes accessed | tf_op | source)
XLA Modules:
  0.0 229.7 jit_solution(1805628870965429047)
XLA Ops:
  0.0 12.4 %collective-permute-start.10 = (bf16[2,4096,256]{2,1,0:T(8,128)(2,1)}, bf16[2,4096,256]{2,1,0:T(8,128)(2,1)}, u32[]{:S(2)}, u32[]{:S(2)}) collective-permute-start(bf16[2,4096,256]{2,1,0:T(8,128)(2,1)} %bitcast.134), channel_id=1, source_target_pairs={{0,384},{384,0},{1,385},{385,1},{2,386},{386,2},{3,387},{387,3},{4... | collective-permute-start | bytes 12582920 | tf_op jit(solution)/shard_map/ppermute | solution.py:172
  16.2 3.2 %collective-permute-done = bf16[256,256]{1,0:T(8,128)(2,1)S(1)} collective-permute-done((bf16[256,256]{1,0:T(8,128)(2,1)S(1)}, bf16[256,256]{1,0:T(8,128)(2,1)S(1)}, u32[]{:S(2)}, u32[]{:S(2)}) %collective-permute-start) | collective-permute-done | bytes 131104 | tf_op jit(solution)/shard_map/ppermute | solution.py:171
  24.0 5.5 %collective-permute-start.2 = (bf16[768,256]{1,0:T(8,128)(2,1)}, bf16[768,256]{1,0:T(8,128)(2,1)S(1)}, u32[]{:S(2)}, u32[]{:S(2)}) collective-permute-start(bf16[768,256]{1,0:T(8,128)(2,1)} %pad_maximum_fusion.7), channel_id=1, source_target_pairs={{0,12},{1,13},{2,14},{3,15},{4,0},{5,1},{6,2},{7,3},{8,4},{9,5},{1... | collective-permute-start | bytes 1179656 | tf_op jit(solution)/shard_map/ppermute | solution.py:24
  29.4 1.9 collective-permute-start.7
  31.4 9.1 %collective-permute-done.1 = bf16[768,256]{1,0:T(8,128)(2,1)S(1)} collective-permute-done((bf16[768,256]{1,0:T(8,128)(2,1)}, bf16[768,256]{1,0:T(8,128)(2,1)S(1)}, u32[]{:S(2)}, u32[]{:S(2)}) %collective-permute-start.1) | collective-permute-done | bytes 393248 | tf_op jit(solution)/shard_map/ppermute | solution.py:24
  42.2 3.8 %collective-permute-start.4 = (bf16[1536,256]{1,0:T(8,128)(2,1)}, bf16[1536,256]{1,0:T(8,128)(2,1)S(1)}, u32[]{:S(2)}, u32[]{:S(2)}) collective-permute-start(bf16[1536,256]{1,0:T(8,128)(2,1)} %get-tuple-element.67), channel_id=1, source_target_pairs={{0,3},{1,0},{2,1},{3,2},{4,7},{5,4},{6,5},{7,6},{8,11},{9,8},{10,9... | collective-permute-start | bytes 2359304 | tf_op jit(solution)/shard_map/ppermute | solution.py:19
  46.1 1.9 collective-permute-start.3
  48.0 4.6 %collective-permute-start.8 = (bf16[768,256]{1,0:T(8,128)(2,1)}, bf16[768,256]{1,0:T(8,128)(2,1)}, u32[]{:S(2)}, u32[]{:S(2)}) collective-permute-start(bf16[768,256]{1,0:T(8,128)(2,1)} %pad_maximum_fusion.7), channel_id=1, source_target_pairs={{0,3},{1,0},{2,1},{3,2},{4,7},{5,4},{6,5},{7,6},{8,11},{9,8},{10,9... | collective-permute-start | bytes 1179656 | tf_op jit(solution)/shard_map/ppermute | solution.py:19
  52.6 1.9 collective-permute-start.9
  58.6 12.9 %collective-permute-done.8 = bf16[768,256]{1,0:T(8,128)(2,1)} collective-permute-done((bf16[768,256]{1,0:T(8,128)(2,1)}, bf16[768,256]{1,0:T(8,128)(2,1)}, u32[]{:S(2)}, u32[]{:S(2)}) %collective-permute-start.8) | collective-permute-done | bytes 393248 | tf_op jit(solution)/shard_map/ppermute | solution.py:19
  71.5 2.7 %collective-permute-start.6 = (bf16[384,256]{1,0:T(8,128)(2,1)}, bf16[384,256]{1,0:T(8,128)(2,1)S(1)}, u32[]{:S(2)}, u32[]{:S(2)}) collective-permute-start(bf16[384,256]{1,0:T(8,128)(2,1)} %slice.361), channel_id=1, source_target_pairs={{0,12},{1,13},{2,14},{3,15},{4,0},{5,1},{6,2},{7,3},{8,4},{9,5},{1... | collective-permute-start | bytes 589832 | tf_op jit(solution)/shard_map/ppermute | solution.py:24
  75.3 3.4 %collective-permute-start.5 = (bf16[384,256]{1,0:T(8,128)(2,1)}, bf16[384,256]{1,0:T(8,128)(2,1)S(1)}, u32[]{:S(2)}, u32[]{:S(2)}) collective-permute-start(bf16[384,256]{1,0:T(8,128)(2,1)} %slice.360), channel_id=1, source_target_pairs={{0,4},{1,5},{2,6},{3,7},{4,8},{5,9},{6,10},{7,11},{8,12},{9,13},{1... | collective-permute-start | bytes 589832 | tf_op jit(solution)/shard_map/ppermute | solution.py:24
  81.2 6.6 %shard_map.55.rest_0_ = f32[4,256,256]{2,1,0:T(8,128)} custom-call(s32[7]{0:T(128)} %stack.105.scalar_ref, bf16[4608,256]{1,0:T(8,128)(2,1)} %copy-done.1, bf16[2,4096,256]{2,1,0:T(8,128)(2,1)} %bitcast.135, bf16[2,4096,256]{2,1,0:T(8,128)(2,1)} %collective-permute-done.10.r_ref), custom_call_target="tpu_custom_call" | custom-call | flops 805306368 | bytes 5505024 | tf_op jit(solution)/shard_map/pallas_call | solution.py:58
  89.1 9.3 %collective-permute-start.12 = (bf16[1536,256]{1,0:T(8,128)(2,1)S(1)}, bf16[1536,256]{1,0:T(8,128)(2,1)S(1)}, u32[]{:S(2)}, u32[]{:S(2)}) collective-permute-start(bf16[1536,256]{1,0:T(8,128)(2,1)S(1)} %get-tuple-element.64), channel_id=1, source_target_pairs={{0,3},{1,0},{2,1},{3,2},{4,7},{5,4},{6,5},{7,6},{8,11},{9,8},{10,9... | collective-permute-start | bytes 2359304 | tf_op jit(solution)/shard_map/ppermute | solution.py:19
  98.4 1.9 collective-permute-start.11
  105.4 3.1 %collective-permute-start.13 = (bf16[768,256]{1,0:T(8,128)(2,1)}, bf16[768,256]{1,0:T(8,128)(2,1)}, u32[]{:S(2)}, u32[]{:S(2)}) collective-permute-start(bf16[768,256]{1,0:T(8,128)(2,1)} %pad_maximum_fusion.8), channel_id=1, source_target_pairs={{0,2},{1,3},{2,0},{3,1},{4,6},{5,7},{6,4},{7,5},{8,10},{9,11},{10,... | collective-permute-start | bytes 1179656 | tf_op jit(solution)/shard_map/ppermute | solution.py:19
  108.5 2.6 %pad_maximum_fusion.x_ref = bf16[3840,256]{1,0:T(8,128)(2,1)} fusion(bf16[384,256]{1,0:T(8,128)(2,1)S(1)} %collective-permute-done.6, bf16[384,256]{1,0:T(8,128)(2,1)S(1)} %collective-permute-done.5, bf16[1536,256]{1,0:T(8,128)(2,1)S(1)} %collective-permute-done.4, bf16[1536,256]{1,0:T(8,128)(2,1)} %collective-permute-done.3), kind=kLoop, calls=%fused_computation | loop fusion | flops 7864320 | bytes 3932160 | tf_op jit(solution)/shard_map/concatenate | solution.py:28
  111.1 6.6 %shard_map.56.rest_0_ = f32[4,256,256]{2,1,0:T(8,128)} custom-call(s32[6]{0:T(128)} %stack.106.scalar_ref, bf16[3840,256]{1,0:T(8,128)(2,1)} %pad_maximum_fusion.x_ref, bf16[2,4096,256]{2,1,0:T(8,128)(2,1)} %bitcast.136, bf16[2,4096,256]{2,1,0:T(8,128)(2,1)} %collective-permute-done.10.r_ref, f32[4,256,256]{2,1,0:T(8,128)} %shard_map.55.rest_0_), custom_call_target="tpu_custom_call" | custom-call | flops 671088640 | bytes 4587520 | tf_op jit(solution)/shard_map/pallas_call | solution.py:58
  117.7 3.7 %collective-permute-done.13 = bf16[768,256]{1,0:T(8,128)(2,1)} collective-permute-done((bf16[768,256]{1,0:T(8,128)(2,1)}, bf16[768,256]{1,0:T(8,128)(2,1)}, u32[]{:S(2)}, u32[]{:S(2)}) %collective-permute-start.13) | collective-permute-done | bytes 393248 | tf_op jit(solution)/shard_map/ppermute | solution.py:19
  129.6 6.5 %shard_map.57.t_ref = f32[4,256,256]{2,1,0:T(8,128)} custom-call(s32[6]{0:T(128)} %stack.104.scalar_ref, bf16[3840,256]{1,0:T(8,128)(2,1)} %copy-done.2, bf16[2,4096,256]{2,1,0:T(8,128)(2,1)} %bitcast.137, bf16[2,4096,256]{2,1,0:T(8,128)(2,1)} %collective-permute-done.10.r_ref, f32[4,256,256]{2,1,0:T(8,128)} %shard_map.56.rest_0_), custom_call_target="tpu_custom_call" | custom-call | flops 671088640 | bytes 4587520 | tf_op jit(solution)/shard_map/pallas_call | solution.py:58
  136.1 7.2 %shard_map.58 = (bf16[5,512,256]{2,1,0:T(8,128)(2,1)}, bf16[4,256,256]{2,1,0:T(8,128)(2,1)}) custom-call(s32[8]{0:T(128)} %stack.103.scalar_ref, f32[4,256,256]{2,1,0:T(8,128)} %shard_map.57.t_ref, bf16[2,4096,256]{2,1,0:T(8,128)(2,1)} %bitcast.138, bf16[2,4096,256]{2,1,0:T(8,128)(2,1)} %collective-permute-done.10.r_ref), custom_call_target="tpu_custom_call" | custom-call | flops 671088640 | bytes 3932160 | tf_op jit(solution)/shard_map/pallas_call | solution.py:109
  145.6 1.9 collective-permute-start.14
  147.6 4.6 %collective-permute-start.17 = (bf16[1024,256]{1,0:T(8,128)(2,1)S(1)}, bf16[1024,256]{1,0:T(8,128)(2,1)S(1)}, u32[]{:S(2)}, u32[]{:S(2)}) collective-permute-start(bf16[1024,256]{1,0:T(8,128)(2,1)S(1)} %pad_maximum_fusion.6), channel_id=1, source_target_pairs={{0,3},{1,0},{2,1},{3,2},{4,7},{5,4},{6,5},{7,6},{8,11},{9,8},{10,9... | collective-permute-start | bytes 1572872 | tf_op jit(solution)/shard_map/ppermute | solution.py:19
  152.8 2.5 %collective-permute-start.20 = (bf16[512,256]{1,0:T(8,128)(2,1)S(1)}, bf16[512,256]{1,0:T(8,128)(2,1)S(1)}, u32[]{:S(2)}, u32[]{:S(2)}) collective-permute-start(bf16[512,256]{1,0:T(8,128)(2,1)S(1)} %get-tuple-element.54), channel_id=1, source_target_pairs={{0,2},{1,3},{2,0},{3,1},{4,6},{5,7},{6,4},{7,5},{8,10},{9,11},{10,... | collective-permute-start | bytes 786440 | tf_op jit(solution)/shard_map/ppermute | solution.py:19
  155.3 10.5 %shard_map.59 = bf16[11,512,256]{2,1,0:T(8,128)(2,1)} custom-call(s32[11]{0:T(128)} %stack.96.scalar_ref, bf16[4,256,256]{2,1,0:T(8,128)(2,1)} %get-tuple-element.25.g_ref, bf16[2,4096,256]{2,1,0:T(8,128)(2,1)} %bitcast.139, bf16[2,4096,256]{2,1,0:T(8,128)(2,1)} %collective-permute-done.10.r_ref), custom_call_target="tpu_custom_call" | custom-call | flops 1476395008 | bytes 8650752 | tf_op jit(solution)/shard_map/pallas_call | solution.py:143
  172.9 4.6 %collective-permute-start.18 = (bf16[1280,256]{1,0:T(8,128)(2,1)S(1)}, bf16[1280,256]{1,0:T(8,128)(2,1)S(1)}, u32[]{:S(2)}, u32[]{:S(2)}) collective-permute-start(bf16[1280,256]{1,0:T(8,128)(2,1)S(1)} %get-tuple-element.44), channel_id=1, source_target_pairs={{0,3},{1,0},{2,1},{3,2},{4,7},{5,4},{6,5},{7,6},{8,11},{9,8},{10,9... | collective-permute-start | bytes 1966088 | tf_op jit(solution)/shard_map/ppermute | solution.py:19
  179.6 5.5 %collective-permute-start.23 = (bf16[256,256]{1,0:T(8,128)(2,1)S(1)}, bf16[256,256]{1,0:T(8,128)(2,1)S(1)}, u32[]{:S(2)}, u32[]{:S(2)}) collective-permute-start(bf16[256,256]{1,0:T(8,128)(2,1)S(1)} %get-tuple-element.71), channel_id=1, source_target_pairs={{0,12},{1,13},{2,14},{3,15},{4,0},{5,1},{6,2},{7,3},{8,4},{9,5},{1... | collective-permute-start | bytes 393224 | tf_op jit(solution)/shard_map/ppermute | solution.py:24
  187.3 6.0 %collective-permute-start.24 = (bf16[512,256]{1,0:T(8,128)(2,1)S(1)}, bf16[512,256]{1,0:T(8,128)(2,1)S(1)}, u32[]{:S(2)}, u32[]{:S(2)}) collective-permute-start(bf16[512,256]{1,0:T(8,128)(2,1)S(1)} %pad_maximum_fusion.12), channel_id=1, source_target_pairs={{0,12},{1,13},{2,14},{3,15},{4,0},{5,1},{6,2},{7,3},{8,4},{9,5},{1... | collective-permute-start | bytes 786440 | tf_op jit(solution)/shard_map/ppermute | solution.py:24
  193.4 1.9 collective-permute-start.19
  195.3 3.4 %collective-permute-start.16 = (bf16[512,256]{1,0:T(8,128)(2,1)S(1)}, bf16[512,256]{1,0:T(8,128)(2,1)S(1)}, u32[]{:S(2)}, u32[]{:S(2)}) collective-permute-start(bf16[512,256]{1,0:T(8,128)(2,1)S(1)} %pad_maximum_fusion.9), channel_id=1, source_target_pairs={{0,1},{1,2},{2,3},{3,0},{4,5},{5,6},{6,7},{7,4},{8,9},{9,10},{10,1... | collective-permute-start | bytes 786440 | tf_op jit(solution)/shard_map/ppermute | solution.py:19
  203.6 7.1 %collective-permute-done.22 = bf16[512,256]{1,0:T(8,128)(2,1)S(1)} collective-permute-done((bf16[512,256]{1,0:T(8,128)(2,1)S(1)}, bf16[512,256]{1,0:T(8,128)(2,1)S(1)}, u32[]{:S(2)}, u32[]{:S(2)}) %collective-permute-start.22) | collective-permute-done | bytes 262176 | tf_op jit(solution)/shard_map/ppermute | solution.py:24
  210.9 17.0 %collective-permute-start.25 = (bf16[256,256]{1,0:T(8,128)(2,1)S(1)}, bf16[256,256]{1,0:T(8,128)(2,1)S(1)}, u32[]{:S(2)}, u32[]{:S(2)}) collective-permute-start(bf16[256,256]{1,0:T(8,128)(2,1)S(1)} %get-tuple-element.38), channel_id=1, source_target_pairs={{0,384},{384,0},{1,385},{385,1},{2,386},{386,2},{3,387},{387,3},{4... | collective-permute-start | bytes 393224 | tf_op jit(solution)/shard_map/ppermute | solution.py:253
  (90 shorter events, 53.2 us)
Async XLA Ops:
  0.0 79.8 %collective-permute-start.10 = (bf16[2,4096,256]{2,1,0:T(8,128)(2,1)}, bf16[2,4096,256]{2,1,0:T(8,128)(2,1)}, u32[]{:S(2)}, u32[]{:S(2)}) collective-permute-start(bf16[2,4096,256]{2,1,0:T(8,128)(2,1)} %bitcast.134), channel_id=1, source_target_pairs={{0,384},{384,0},{1,385},{385,1},{2,386},{386,2},{3,387},{387,3},{4... | collective-permute-start | bytes 12582920 | tf_op jit(solution)/shard_map/ppermute | solution.py:172
  13.4 6.0 %collective-permute-start = (bf16[256,256]{1,0:T(8,128)(2,1)S(1)}, bf16[256,256]{1,0:T(8,128)(2,1)S(1)}, u32[]{:S(2)}, u32[]{:S(2)}) collective-permute-start(bf16[256,256]{1,0:T(8,128)(2,1)S(1)} %dynamic-slice_bitcast_fusion), channel_id=1, source_target_pairs={{0,384},{384,0},{1,385},{385,1},{2,386},{386,2},{3,387},{387,3},{4... | collective-permute-start | bytes 393224 | tf_op jit(solution)/shard_map/ppermute | solution.py:171
  22.0 18.4 %collective-permute-start.1 = (bf16[768,256]{1,0:T(8,128)(2,1)}, bf16[768,256]{1,0:T(8,128)(2,1)S(1)}, u32[]{:S(2)}, u32[]{:S(2)}) collective-permute-start(bf16[768,256]{1,0:T(8,128)(2,1)} %pad_maximum_fusion.7), channel_id=1, source_target_pairs={{0,4},{1,5},{2,6},{3,7},{4,8},{5,9},{6,10},{7,11},{8,12},{9,13},{1... | collective-permute-start | bytes 1179656 | tf_op jit(solution)/shard_map/ppermute | solution.py:24
  24.0 17.4 %collective-permute-start.2 = (bf16[768,256]{1,0:T(8,128)(2,1)}, bf16[768,256]{1,0:T(8,128)(2,1)S(1)}, u32[]{:S(2)}, u32[]{:S(2)}) collective-permute-start(bf16[768,256]{1,0:T(8,128)(2,1)} %pad_maximum_fusion.7), channel_id=1, source_target_pairs={{0,12},{1,13},{2,14},{3,15},{4,0},{5,1},{6,2},{7,3},{8,4},{9,5},{1... | collective-permute-start | bytes 1179656 | tf_op jit(solution)/shard_map/ppermute | solution.py:24
  29.4 23.1 %collective-permute-start.7 = (bf16[768,256]{1,0:T(8,128)(2,1)}, bf16[768,256]{1,0:T(8,128)(2,1)}, u32[]{:S(2)}, u32[]{:S(2)}) collective-permute-start(bf16[768,256]{1,0:T(8,128)(2,1)} %pad_maximum_fusion.7), channel_id=1, source_target_pairs={{0,1},{1,2},{2,3},{3,0},{4,5},{5,6},{6,7},{7,4},{8,9},{9,10},{10,1... | collective-permute-start | bytes 1179656 | tf_op jit(solution)/shard_map/ppermute | solution.py:19
  42.2 45.6 %collective-permute-start.4 = (bf16[1536,256]{1,0:T(8,128)(2,1)}, bf16[1536,256]{1,0:T(8,128)(2,1)S(1)}, u32[]{:S(2)}, u32[]{:S(2)}) collective-permute-start(bf16[1536,256]{1,0:T(8,128)(2,1)} %get-tuple-element.67), channel_id=1, source_target_pairs={{0,3},{1,0},{2,1},{3,2},{4,7},{5,4},{6,5},{7,6},{8,11},{9,8},{10,9... | collective-permute-start | bytes 2359304 | tf_op jit(solution)/shard_map/ppermute | solution.py:19
  46.1 41.8 %collective-permute-start.3 = (bf16[1536,256]{1,0:T(8,128)(2,1)}, bf16[1536,256]{1,0:T(8,128)(2,1)}, u32[]{:S(2)}, u32[]{:S(2)}) collective-permute-start(bf16[1536,256]{1,0:T(8,128)(2,1)} %get-tuple-element.67), channel_id=1, source_target_pairs={{0,1},{1,2},{2,3},{3,0},{4,5},{5,6},{6,7},{7,4},{8,9},{9,10},{10,1... | collective-permute-start | bytes 2359304 | tf_op jit(solution)/shard_map/ppermute | solution.py:19
  48.0 23.5 %collective-permute-start.8 = (bf16[768,256]{1,0:T(8,128)(2,1)}, bf16[768,256]{1,0:T(8,128)(2,1)}, u32[]{:S(2)}, u32[]{:S(2)}) collective-permute-start(bf16[768,256]{1,0:T(8,128)(2,1)} %pad_maximum_fusion.7), channel_id=1, source_target_pairs={{0,3},{1,0},{2,1},{3,2},{4,7},{5,4},{6,5},{7,6},{8,11},{9,8},{10,9... | collective-permute-start | bytes 1179656 | tf_op jit(solution)/shard_map/ppermute | solution.py:19
  52.6 22.7 %collective-permute-start.9 = (bf16[768,256]{1,0:T(8,128)(2,1)}, bf16[768,256]{1,0:T(8,128)(2,1)}, u32[]{:S(2)}, u32[]{:S(2)}) collective-permute-start(bf16[768,256]{1,0:T(8,128)(2,1)} %pad_maximum_fusion.7), channel_id=1, source_target_pairs={{0,2},{1,3},{2,0},{3,1},{4,6},{5,7},{6,4},{7,5},{8,10},{9,11},{10,... | collective-permute-start | bytes 1179656 | tf_op jit(solution)/shard_map/ppermute | solution.py:19
  71.5 16.3 %collective-permute-start.6 = (bf16[384,256]{1,0:T(8,128)(2,1)}, bf16[384,256]{1,0:T(8,128)(2,1)S(1)}, u32[]{:S(2)}, u32[]{:S(2)}) collective-permute-start(bf16[384,256]{1,0:T(8,128)(2,1)} %slice.361), channel_id=1, source_target_pairs={{0,12},{1,13},{2,14},{3,15},{4,0},{5,1},{6,2},{7,3},{8,4},{9,5},{1... | collective-permute-start | bytes 589832 | tf_op jit(solution)/shard_map/ppermute | solution.py:24
  75.3 12.6 %collective-permute-start.5 = (bf16[384,256]{1,0:T(8,128)(2,1)}, bf16[384,256]{1,0:T(8,128)(2,1)S(1)}, u32[]{:S(2)}, u32[]{:S(2)}) collective-permute-start(bf16[384,256]{1,0:T(8,128)(2,1)} %slice.360), channel_id=1, source_target_pairs={{0,4},{1,5},{2,6},{3,7},{4,8},{5,9},{6,10},{7,11},{8,12},{9,13},{1... | collective-permute-start | bytes 589832 | tf_op jit(solution)/shard_map/ppermute | solution.py:24
  79.8 1.5 copy-start.1
  87.9 12.6 %copy-start.6 = (s32[2]{0:T(128)S(1)}, s32[2]{0:T(128)}, u32[]{:S(2)}) copy-start(s32[2]{0:T(128)} %param.9) | copy-start | bytes 28
  87.9 13.2 %copy-start.7 = (s32[2]{0:T(128)S(1)}, s32[2]{0:T(128)}, u32[]{:S(2)}) copy-start(s32[2]{0:T(128)} %param.8) | copy-start | bytes 28
  89.1 32.3 %collective-permute-start.12 = (bf16[1536,256]{1,0:T(8,128)(2,1)S(1)}, bf16[1536,256]{1,0:T(8,128)(2,1)S(1)}, u32[]{:S(2)}, u32[]{:S(2)}) collective-permute-start(bf16[1536,256]{1,0:T(8,128)(2,1)S(1)} %get-tuple-element.64), channel_id=1, source_target_pairs={{0,3},{1,0},{2,1},{3,2},{4,7},{5,4},{6,5},{7,6},{8,11},{9,8},{10,9... | collective-permute-start | bytes 2359304 | tf_op jit(solution)/shard_map/ppermute | solution.py:19
  98.4 23.8 %collective-permute-start.11 = (bf16[1536,256]{1,0:T(8,128)(2,1)S(1)}, bf16[1536,256]{1,0:T(8,128)(2,1)}, u32[]{:S(2)}, u32[]{:S(2)}) collective-permute-start(bf16[1536,256]{1,0:T(8,128)(2,1)S(1)} %get-tuple-element.65), channel_id=1, source_target_pairs={{0,1},{1,2},{2,3},{3,0},{4,5},{5,6},{6,7},{7,4},{8,9},{9,10},{10,1... | collective-permute-start | bytes 2359304 | tf_op jit(solution)/shard_map/ppermute | solution.py:19
  105.4 15.9 %collective-permute-start.13 = (bf16[768,256]{1,0:T(8,128)(2,1)}, bf16[768,256]{1,0:T(8,128)(2,1)}, u32[]{:S(2)}, u32[]{:S(2)}) collective-permute-start(bf16[768,256]{1,0:T(8,128)(2,1)} %pad_maximum_fusion.8), channel_id=1, source_target_pairs={{0,2},{1,3},{2,0},{3,1},{4,6},{5,7},{6,4},{7,5},{8,10},{9,11},{10,... | collective-permute-start | bytes 1179656 | tf_op jit(solution)/shard_map/ppermute | solution.py:19
  122.3 4.9 %copy-start.5 = (bf16[1536,256]{1,0:T(8,128)(2,1)S(1)}, bf16[1536,256]{1,0:T(8,128)(2,1)}, u32[]{:S(2)}) copy-start(bf16[1536,256]{1,0:T(8,128)(2,1)} %copy-done.4) | copy-start | bytes 2359300
  128.2 1.3 copy-start.2
  145.6 20.1 %collective-permute-start.14 = (bf16[1024,256]{1,0:T(8,128)(2,1)S(1)}, bf16[1024,256]{1,0:T(8,128)(2,1)S(1)}, u32[]{:S(2)}, u32[]{:S(2)}) collective-permute-start(bf16[1024,256]{1,0:T(8,128)(2,1)S(1)} %pad_maximum_fusion.5), channel_id=1, source_target_pairs={{0,1},{1,2},{2,3},{3,0},{4,5},{5,6},{6,7},{7,4},{8,9},{9,10},{10,1... | collective-permute-start | bytes 1572872 | tf_op jit(solution)/shard_map/ppermute | solution.py:19
  147.6 19.3 %collective-permute-start.17 = (bf16[1024,256]{1,0:T(8,128)(2,1)S(1)}, bf16[1024,256]{1,0:T(8,128)(2,1)S(1)}, u32[]{:S(2)}, u32[]{:S(2)}) collective-permute-start(bf16[1024,256]{1,0:T(8,128)(2,1)S(1)} %pad_maximum_fusion.6), channel_id=1, source_target_pairs={{0,3},{1,0},{2,1},{3,2},{4,7},{5,4},{6,5},{7,6},{8,11},{9,8},{10,9... | collective-permute-start | bytes 1572872 | tf_op jit(solution)/shard_map/ppermute | solution.py:19
  152.8 24.7 %collective-permute-start.20 = (bf16[512,256]{1,0:T(8,128)(2,1)S(1)}, bf16[512,256]{1,0:T(8,128)(2,1)S(1)}, u32[]{:S(2)}, u32[]{:S(2)}) collective-permute-start(bf16[512,256]{1,0:T(8,128)(2,1)S(1)} %get-tuple-element.54), channel_id=1, source_target_pairs={{0,2},{1,3},{2,0},{3,1},{4,6},{5,7},{6,4},{7,5},{8,10},{9,11},{10,... | collective-permute-start | bytes 786440 | tf_op jit(solution)/shard_map/ppermute | solution.py:19
  165.8 11.7 %copy-start = (bf16[11,512,256]{2,1,0:T(8,128)(2,1)S(1)}, bf16[11,512,256]{2,1,0:T(8,128)(2,1)}, u32[]{:S(2)}) copy-start(bf16[11,512,256]{2,1,0:T(8,128)(2,1)} %shard_map.59) | copy-start | bytes 8650756
  170.9 16.0 %collective-permute-start.15 = (bf16[1280,256]{1,0:T(8,128)(2,1)S(1)}, bf16[1280,256]{1,0:T(8,128)(2,1)S(1)}, u32[]{:S(2)}, u32[]{:S(2)}) collective-permute-start(bf16[1280,256]{1,0:T(8,128)(2,1)S(1)} %get-tuple-element.43), channel_id=1, source_target_pairs={{0,1},{1,2},{2,3},{3,0},{4,5},{5,6},{6,7},{7,4},{8,9},{9,10},{10,1... | collective-permute-start | bytes 1966088 | tf_op jit(solution)/shard_map/ppermute | solution.py:19
  172.9 14.1 %collective-permute-start.18 = (bf16[1280,256]{1,0:T(8,128)(2,1)S(1)}, bf16[1280,256]{1,0:T(8,128)(2,1)S(1)}, u32[]{:S(2)}, u32[]{:S(2)}) collective-permute-start(bf16[1280,256]{1,0:T(8,128)(2,1)S(1)} %get-tuple-element.44), channel_id=1, source_target_pairs={{0,3},{1,0},{2,1},{3,2},{4,7},{5,4},{6,5},{7,6},{8,11},{9,8},{10,9... | collective-permute-start | bytes 1966088 | tf_op jit(solution)/shard_map/ppermute | solution.py:19
  177.6 7.9 %collective-permute-start.21 = (bf16[256,256]{1,0:T(8,128)(2,1)S(1)}, bf16[256,256]{1,0:T(8,128)(2,1)S(1)}, u32[]{:S(2)}, u32[]{:S(2)}) collective-permute-start(bf16[256,256]{1,0:T(8,128)(2,1)S(1)} %get-tuple-element.70), channel_id=1, source_target_pairs={{0,4},{1,5},{2,6},{3,7},{4,8},{5,9},{6,10},{7,11},{8,12},{9,13},{1... | collective-permute-start | bytes 393224 | tf_op jit(solution)/shard_map/ppermute | solution.py:24
  179.6 7.4 %collective-permute-start.23 = (bf16[256,256]{1,0:T(8,128)(2,1)S(1)}, bf16[256,256]{1,0:T(8,128)(2,1)S(1)}, u32[]{:S(2)}, u32[]{:S(2)}) collective-permute-start(bf16[256,256]{1,0:T(8,128)(2,1)S(1)} %get-tuple-element.71), channel_id=1, source_target_pairs={{0,12},{1,13},{2,14},{3,15},{4,0},{5,1},{6,2},{7,3},{8,4},{9,5},{1... | collective-permute-start | bytes 393224 | tf_op jit(solution)/shard_map/ppermute | solution.py:24
  187.3 14.9 %collective-permute-start.24 = (bf16[512,256]{1,0:T(8,128)(2,1)S(1)}, bf16[512,256]{1,0:T(8,128)(2,1)S(1)}, u32[]{:S(2)}, u32[]{:S(2)}) collective-permute-start(bf16[512,256]{1,0:T(8,128)(2,1)S(1)} %pad_maximum_fusion.12), channel_id=1, source_target_pairs={{0,12},{1,13},{2,14},{3,15},{4,0},{5,1},{6,2},{7,3},{8,4},{9,5},{1... | collective-permute-start | bytes 786440 | tf_op jit(solution)/shard_map/ppermute | solution.py:24
  193.4 8.9 %collective-permute-start.19 = (bf16[512,256]{1,0:T(8,128)(2,1)S(1)}, bf16[512,256]{1,0:T(8,128)(2,1)S(1)}, u32[]{:S(2)}, u32[]{:S(2)}) collective-permute-start(bf16[512,256]{1,0:T(8,128)(2,1)S(1)} %pad_maximum_fusion.10), channel_id=1, source_target_pairs={{0,3},{1,0},{2,1},{3,2},{4,7},{5,4},{6,5},{7,6},{8,11},{9,8},{10,9... | collective-permute-start | bytes 786440 | tf_op jit(solution)/shard_map/ppermute | solution.py:19
  195.3 8.3 %collective-permute-start.16 = (bf16[512,256]{1,0:T(8,128)(2,1)S(1)}, bf16[512,256]{1,0:T(8,128)(2,1)S(1)}, u32[]{:S(2)}, u32[]{:S(2)}) collective-permute-start(bf16[512,256]{1,0:T(8,128)(2,1)S(1)} %pad_maximum_fusion.9), channel_id=1, source_target_pairs={{0,1},{1,2},{2,3},{3,0},{4,5},{5,6},{6,7},{7,4},{8,9},{9,10},{10,1... | collective-permute-start | bytes 786440 | tf_op jit(solution)/shard_map/ppermute | solution.py:19
  198.7 12.1 %collective-permute-start.22 = (bf16[512,256]{1,0:T(8,128)(2,1)S(1)}, bf16[512,256]{1,0:T(8,128)(2,1)S(1)}, u32[]{:S(2)}, u32[]{:S(2)}) collective-permute-start(bf16[512,256]{1,0:T(8,128)(2,1)S(1)} %pad_maximum_fusion.11), channel_id=1, source_target_pairs={{0,4},{1,5},{2,6},{3,7},{4,8},{5,9},{6,10},{7,11},{8,12},{9,13},{1... | collective-permute-start | bytes 786440 | tf_op jit(solution)/shard_map/ppermute | solution.py:24
  210.9 18.0 %collective-permute-start.25 = (bf16[256,256]{1,0:T(8,128)(2,1)S(1)}, bf16[256,256]{1,0:T(8,128)(2,1)S(1)}, u32[]{:S(2)}, u32[]{:S(2)}) collective-permute-start(bf16[256,256]{1,0:T(8,128)(2,1)S(1)} %get-tuple-element.38), channel_id=1, source_target_pairs={{0,384},{384,0},{1,385},{385,1},{2,386},{386,2},{3,387},{387,3},{4... | collective-permute-start | bytes 393224 | tf_op jit(solution)/shard_map/ppermute | solution.py:253
  (2 other events, 1.8 us)

commit v3 on v0

v3 whole, which is shorter than its diff:
```python
import jax
import jax.numpy as jnp
from jax import lax
from jax.experimental import pallas as pl
from jax.experimental.pallas import tpu as pltpu
from jax.sharding import PartitionSpec as P

HS = 256
SIDE = 4
ROWS = 3 * HS
HALF = ROWS // 2
N = 2 * HS
F32 = jnp.float32
BF16 = jnp.bfloat16
SWAP = [(0, 1), (1, 0)]
NT = (((1,), (1,)), ((), ()))
TN = (((0,), (0,)), ((), ()))
VMEM = pl.BlockSpec(memory_space=pltpu.VMEM)
SMEM = pl.BlockSpec(memory_space=pltpu.SMEM)


def shift_x(block, step):
    route = [(y * SIDE + x, y * SIDE + (x + step) % SIDE) for y in range(SIDE) for x in range(SIDE)]
    return lax.ppermute(block, "mp", route)


def shift_y(block, step):
    route = [(y * SIDE + x, (y + step) % SIDE * SIDE + x) for y in range(SIDE) for x in range(SIDE)]
    return lax.ppermute(block, "mp", route)


def call(body, inputs, rows, flops=0, out_dtype=BF16, shapes=None):
    shapes = shapes or [(r, HS) for r in rows]
    out = [jax.ShapeDtypeStruct(s, out_dtype) for s in shapes]
    moved = sum(a.size * a.dtype.itemsize for a in inputs[1:])
    return pl.pallas_call(
        body,
        out_shape=out,
        in_specs=[SMEM] + [VMEM] * (len(inputs) - 1),
        out_specs=[VMEM] * len(out),
        cost_estimate=pl.CostEstimate(flops=flops, bytes_accessed=moved, transcendentals=0),
    )(*inputs)


def assemble(table, own, cotangent, partner):
    def body(table_ref, own_ref, cot_ref, partner_ref, out_ref):
        sec = table_ref[0]
        here = pl.ds(pl.multiple_of(sec * HS, HS), HS)
        out_ref[:HS, :] = own_ref[here, :]
        out_ref[pl.ds(pl.multiple_of((2 - sec) * HS, HS), HS), :] = cot_ref[here, :]
        out_ref[pl.ds(pl.multiple_of((1 + sec) * HS, HS), HS), :] = partner_ref[here, :]

    return call(body, [table, own, cotangent, partner], [ROWS])[0]


def rows_of(refs, block, low, high):
    parts, at = [], 0
    for which, first, count in block:
        a, b = max(low, at), min(high, at + count)
        if a < b:
            parts.append(refs[which][first + a - at : first + b - at, :])
        at += count
    return parts[0] if len(parts) == 1 else jnp.concatenate(parts, axis=0)


def project(table, pieces, blocks, own_w, other_w, total):
    def body(table_ref, u_ref, r_ref, *rest):
        refs, out_ref = rest[: len(pieces)], rest[-1]
        core0 = table_ref[0] == 0
        sums = [None if total is None else rest[-2][j] for j in range(4)]
        for entry, block in blocks:
            feats = pl.ds(pl.multiple_of(table_ref[entry] * HS, HS), HS)
            p0 = rows_of(refs, block, 0, HS)
            p1 = rows_of(refs, block, HS, 2 * HS)
            p2 = rows_of(refs, block, 2 * HS, 3 * HS)
            for j, (rows, weight) in enumerate((
                (p0, u_ref[0, feats, :]),
                (jnp.where(core0, p0, p1), u_ref[1, feats, :]),
                (jnp.where(core0, p1, p2), r_ref[0, feats, :]),
                (p2, r_ref[1, feats, :]),
            )):
                term = jnp.dot(rows, weight, preferred_element_type=F32)
                sums[j] = term if sums[j] is None else sums[j] + term
        for j in range(4):
            out_ref[j] = sums[j]

    inputs = [table, own_w, other_w, *pieces] + ([] if total is None else [total])
    flops = len(blocks) * 8 * HS**3
    return call(body, inputs, None, flops, F32, [(4, HS, HS)])[0]


def term_of(g_ref, u_ref, r_ref, index, slot):
    w_ref = (u_ref, r_ref)[slot]
    feats = pl.ds(pl.multiple_of(index * HS, HS), HS)
    term = lax.dot_general(g_ref[2 * slot], w_ref[0, feats, :], NT, preferred_element_type=F32)
    term += lax.dot_general(g_ref[2 * slot + 1], w_ref[1, feats, :], NT, preferred_element_type=F32)
    return term.astype(BF16)


def write_terms(table_ref, g_ref, u_ref, r_ref, wanted):
    for entry, *slots in wanted:
        for slot, (out_ref, row) in enumerate(slots):
            out_ref[row : row + HS, :] = term_of(g_ref, u_ref, r_ref, table_ref[entry], slot)


def attend(table, total, own_w, other_w, at):
    scale = 1.0 / HS**0.5

    def body(table_ref, t_ref, u_ref, r_ref, right_ref, left_ref, across_ref, g_ref):
        me = table_ref[0]
        keys = t_ref[2 * me].astype(BF16)
        values = t_ref[2 * me + 1].astype(BF16)
        queries = t_ref[2 - 2 * me].astype(BF16)
        out_grad = t_ref[3 - 2 * me]
        live_q = lax.broadcasted_iota(jnp.int32, (HS, HS), 0) < table_ref[2]
        live_k = lax.broadcasted_iota(jnp.int32, (HS, HS), 1) < table_ref[1]
        masked = jnp.where(live_q, out_grad, 0.0).astype(BF16)
        scores = lax.dot_general(queries, keys, NT, preferred_element_type=F32) * scale
        scores = jnp.where(live_k, scores, -1e30)
        top = jnp.max(scores, axis=-1, keepdims=True)
        expd = jnp.exp(scores - top)
        probs = expd / jnp.sum(expd, axis=-1, keepdims=True)
        value_grad = lax.dot_general(probs.astype(BF16), masked, TN, preferred_element_type=F32).astype(BF16)
        prob_grad = lax.dot_general(masked, values, NT, preferred_element_type=F32)
        delta = jnp.sum(probs * prob_grad, axis=-1, keepdims=True)
        sg = (probs * (prob_grad - delta)).astype(BF16)
        query_grad = (jnp.dot(sg, keys, preferred_element_type=F32) * scale).astype(BF16)
        key_grad = (lax.dot_general(sg, queries, TN, preferred_element_type=F32) * scale).astype(BF16)
        g_ref[2 * me] = key_grad
        g_ref[2 * me + 1] = value_grad
        g_ref[2 - 2 * me] = query_grad
        g_ref[3 - 2 * me] = jnp.zeros_like(query_grad)
        write_terms(table_ref, g_ref, u_ref, r_ref, [
            (at[2, 1], (right_ref, 0), (right_ref, HS)),
            (at[1, 2], (right_ref, N), (left_ref, N)),
            (at[-1, 2], (right_ref, N + HS), (left_ref, N + HS)),
            (at[2, -1], (left_ref, 0), (left_ref, HS)),
            (at[2, 2], (across_ref, 0), (across_ref, HS)),
        ])

    shapes = [(2 * N, HS), (2 * N, HS), (N, HS), (4, HS, HS)]
    return call(body, [table, total, own_w, other_w], None, 60 * HS**3, BF16, shapes)


def spread(table, grads, own_w, other_w, at):
    def body(table_ref, g_ref, u_ref, r_ref, far, right, left, up, down, right_c, left_c, here):
        write_terms(table_ref, g_ref, u_ref, r_ref, [
            (at[2, 0], (far, 0), (far, HS)),
            (at[1, 1], (right, 0), (right, HS)),
            (at[-1, 1], (right, N), (right, N + HS)),
            (at[1, -1], (left, 0), (left, HS)),
            (at[-1, -1], (left, N), (left, N + HS)),
            (at[0, 2], (right, 2 * N), (left, 2 * N)),
            (at[1, 0], (up, 0), (up, HS)),
            (at[-1, 0], (down, 0), (down, HS)),
            (at[0, 1], (right_c, 0), (right_c, HS)),
            (at[0, -1], (left_c, 0), (left_c, HS)),
            (at[0, 0], (here, 0), (here, HS)),
        ])

    rows = [N, 2 * N + HS, 2 * N + HS, N, N, N, N, N]
    return call(body, [table, grads, own_w, other_w], rows, 88 * HS**3)


def add_rows(table, sources, rows, recipe):
    def body(table_ref, *refs):
        ins, outs = refs[: len(sources)], refs[len(sources) :]
        for out, row, parts in recipe:
            value = ins[parts[0][0]][parts[0][1] : parts[0][1] + HS, :]
            if len(parts) > 1:
                value = value.astype(F32)
                for source, first in parts[1:]:
                    value += ins[source][first : first + HS, :].astype(F32)
            outs[out][row : row + HS, :] = value.astype(BF16)

    return call(body, [table, *sources], rows)


def local(states, proj_weights, out_cotangent, enc_lengths, dec_lengths):
    sec = lax.axis_index("section")
    me = lax.axis_index("mp")
    my_y, my_x = me // SIDE, me % SIDE
    offsets = [(dy, dx) for dy in (0, 1, 2, -1) for dx in (0, 1, 2, -1)]
    at = {offset: 3 + i for i, offset in enumerate(offsets)}
    dy, dx = (jnp.array(v, jnp.int32) for v in zip(*offsets, strict=True))
    places = (my_y + dy) % SIDE * SIDE + (my_x + dx) % SIDE
    lengths = jnp.stack([enc_lengths, dec_lengths], axis=1)[sec]
    table = jnp.concatenate([sec[None], lengths, places]).astype(jnp.int32)

    own = states[0]
    partner = lax.ppermute(own, "section", SWAP)
    own_w, partner = lax.optimization_barrier((proj_weights[0], partner))
    other_w = lax.ppermute(own_w, "section", SWAP)
    c0 = assemble(table, own, out_cotangent, partner)

    up1, down1 = shift_y(c0, 1), shift_y(c0, -1)
    right0, left0, across0 = shift_x(c0, 1), shift_x(c0, -1), shift_x(c0, 2)
    c0, up1, down1, right0, left0, across0 = lax.optimization_barrier((c0, up1, down1, right0, left0, across0))

    pair = jnp.concatenate([up1, down1], axis=0)
    right1, left1 = shift_x(pair, 1), shift_x(pair, -1)
    up2, down2 = shift_y(up1[:HALF], 1), shift_y(down1[HALF:], -1)
    total = project(
        table, [c0, pair, right0, left0, across0],
        [
            (at[0, 0], [(0, 0, ROWS)]), (at[-1, 0], [(1, 0, ROWS)]), (at[1, 0], [(1, ROWS, ROWS)]),
            (at[0, -1], [(2, 0, ROWS)]), (at[0, 1], [(3, 0, ROWS)]), (at[0, 2], [(4, 0, ROWS)]),
        ],
        own_w, other_w, None,
    )
    right1, left1, up2, down2, total = lax.optimization_barrier((right1, left1, up2, down2, total))

    last = jnp.concatenate([up2, down2], axis=0)
    right2 = shift_x(jnp.concatenate([right1[:HALF], right1[ROWS : ROWS + HALF], last], axis=0), 1)
    left2 = shift_x(jnp.concatenate([left1[HALF:ROWS], left1[ROWS + HALF :], last], axis=0), -1)
    across2 = shift_x(last, 2)
    total = project(
        table, [right1, left1, last],
        [
            (at[-1, -1], [(0, 0, ROWS)]), (at[1, -1], [(0, ROWS, ROWS)]),
            (at[-1, 1], [(1, 0, ROWS)]), (at[1, 1], [(1, ROWS, ROWS)]), (at[2, 0], [(2, 0, ROWS)]),
        ],
        own_w, other_w, total,
    )
    right2, left2, across2, total = lax.optimization_barrier((right2, left2, across2, total))
    total = project(
        table, [right2, left2, across2],
        [
            (at[-1, 2], [(0, 0, HALF), (1, 0, HALF)]), (at[1, 2], [(0, HALF, HALF), (1, HALF, HALF)]),
            (at[2, -1], [(0, ROWS, ROWS)]), (at[2, 1], [(1, ROWS, ROWS)]), (at[2, 2], [(2, 0, ROWS)]),
        ],
        own_w, other_w, total,
    )

    right_a, left_a, across_a, grads = attend(table, total, own_w, other_w, at)
    right_a, left_a, across_a = shift_x(right_a, 1), shift_x(left_a, -1), shift_x(across_a, 2)
    far, right_b, left_b, up_c, down_c, right_c, left_c, here = spread(table, grads, own_w, other_w, at)
    far, right_b, left_b = add_rows(
        table, [far, right_b, left_b, right_a, left_a, across_a], [N, 2 * N + HS, 2 * N + HS],
        [
            (0, 0, [(0, 0), (3, 0), (4, 0), (5, 0)]), (0, HS, [(0, HS), (3, HS), (4, HS), (5, HS)]),
            (1, 0, [(1, 0), (3, N)]), (1, HS, [(1, HS)]),
            (1, N, [(1, N), (3, N + HS)]), (1, N + HS, [(1, N + HS)]), (1, 2 * N, [(1, 2 * N)]),
            (2, 0, [(2, 0)]), (2, HS, [(2, HS), (4, N)]),
            (2, N, [(2, N)]), (2, N + HS, [(2, N + HS), (4, N + HS)]), (2, 2 * N, [(2, 2 * N)]),
        ],
    )
    up_b, down_b = shift_y(far[:HS], 1), shift_y(far[HS:], -1)
    right_b, left_b = shift_x(right_b, 1), shift_x(left_b, -1)
    up_c, down_c, right_c, left_c = add_rows(
        table, [up_c, down_c, right_c, left_c, right_b, left_b, up_b, down_b], [N] * 4,
        [
            (0, 0, [(0, 0), (4, 0), (5, 0), (6, 0)]), (0, HS, [(0, HS), (4, HS), (5, HS)]),
            (1, 0, [(1, 0), (4, N), (5, N)]), (1, HS, [(1, HS), (4, N + HS), (5, N + HS), (7, 0)]),
            (2, 0, [(2, 0), (4, 2 * N)]), (2, HS, [(2, HS)]),
            (3, 0, [(3, 0)]), (3, HS, [(3, HS), (5, 2 * N)]),
        ],
    )
    up_c, down_c, right_c, left_c = shift_y(up_c, 1), shift_y(down_c, -1), shift_x(right_c, 1), shift_x(left_c, -1)
    kept, sent = add_rows(
        table, [here, up_c, down_c, right_c, left_c], [HS, HS],
        [(0, 0, [(i, 0) for i in range(5)]), (1, 0, [(i, HS) for i in range(5)])],
    )
    swapped = lax.ppermute(sent, "section", SWAP)
    first = sec == 0
    return jnp.where(first, jnp.concatenate([kept, swapped]), jnp.concatenate([swapped, kept]))[None]


def solution(mesh):
    placed = (
        P("section", "dp", "mp"),
        P("section", None, None, "mp"),
        P("dp", "mp"),
        P("dp"),
        P("dp"),
    )
    return jax.shard_map(
        local, mesh=mesh, in_specs=placed, out_specs=P("section", "dp", "mp"), check_vma=False
    )
```

time: 345 us -> 201 us (0.58)
  waiting for transfers between devices: 301 us -> 42.8 us
  starting transfers between devices: 5.28 us -> 101 us
  Pallas kernels: 0 us -> 40.7 us
  matrix products: 13.3 us -> 0 us
  between operations: 13.2 us -> 0.46 us
    all_gather x2 -> x0, waiting for transfers between devices: 195 us -> none  [the longest x1 104 us: local(): lax.all_gather(second_rows, 'mp', axis=1, tiled=True)]
    reduce_scatter x1 -> x0, waiting for transfers between devices: 104 us -> none  [local(): lax.psum_scatter(lax.cond(is_decoder, one_pair, two_pairs, 0).astype(jnp....]
    ppermute x4 -> x26, starting transfers between devices: 5.2 us -> 101 us  [the longest x15 48.7 us: shift_x(): return lax.ppermute(block, 'mp', route)]
    ppermute x4 -> x26, waiting for transfers between devices: 2.12 us -> 42.8 us  [the longest x15 31 us: shift_x(): return lax.ppermute(block, 'mp', route)]
    pallas_call x0 -> x9, Pallas kernels: none -> 40.7 us  [call(): pl.pallas_call(body, out_shape=out, in_specs=[SMEM] + [VMEM] * (len(input...]
    dot_general x7 -> x0, matrix products: 13 us -> none  [the longest x1 4.11 us: local(): other = jnp.dot(full_second, w_second, preferred_element_type=jnp.float32)]
    unnamed x4 -> x46, local copies, waits for them, and re-layouts: 0.01 us -> 6.73 us
    cond x1 -> x0, local copies, waits for them, and re-layouts: 6.39 us -> none  [local(): lax.cond(is_decoder, one_pair, two_pairs, 0).astype(jnp.bfloat16)]
  transfers between devices with their start and end apart: 7 -> 26, of which waited for: 4 -> 13; matrix products, arithmetic and copies ran while one was open for 3% -> 3% of each run, Pallas kernels for 0% -> 10%
where the time goes in v3:
time: 201 us; the launch traced here: 200 us
  starting transfers between devices  101 us (50%)
  waiting for transfers between devices  42.8 us (21%)
  Pallas kernels  40.7 us (20%)
  local copies, waits for them, and re-layouts  10.3 us (5%)
  other arithmetic  3.88 us (2%)
    ppermute x15, starting transfers between devices, shift_x(): return lax.ppermute(block, 'mp', route)  48.7 us
    pallas_call x9, Pallas kernels, call(): pl.pallas_call(body, out_shape=out, in_specs=[SMEM] + [VMEM] * (len(input...  40.7 us
    ppermute x15, waiting for transfers between devices, shift_x(): return lax.ppermute(block, 'mp', route)  31 us
    ppermute x8, starting transfers between devices, shift_y(): return lax.ppermute(block, 'mp', route)  28.3 us
    ppermute x1, starting transfers between devices, local(): partner = lax.ppermute(own, 'section', SWAP)  12.4 us
    ppermute x1, starting transfers between devices, local(): swapped = lax.ppermute(sent, 'section', SWAP)  9.78 us
    ppermute x8, waiting for transfers between devices, shift_y(): return lax.ppermute(block, 'mp', route)  9.32 us
    unnamed x46, local copies, waits for them, and re-layouts  6.73 us
  transfers between devices with their start and end apart: 26, of which 13 were waited for; matrix products, arithmetic and copies ran while one was open for 3% of the time, Pallas kernels for 10%

profile of v3, /device:TPU:1, one launch (start us, length us, event | category | flops | bytes accessed | tf_op | source)
XLA Modules:
  0.0 199.6 jit_solution(11852964273353448568)
XLA Ops:
  0.0 12.4 %collective-permute-start = (bf16[512,256]{1,0:T(8,128)(2,1)}, bf16[512,256]{1,0:T(8,128)(2,1)S(1)}, u32[]{:S(2)}, u32[]{:S(2)}) collective-permute-start(bf16[512,256]{1,0:T(8,128)(2,1)} %bitcast.13), channel_id=1, source_target_pairs={{0,384},{384,0},{1,385},{385,1},{2,386},{386,2},{3,387},{387,3},{4... | collective-permute-start | bytes 786440 | tf_op jit(solution)/shard_map/ppermute | solution.py:191
  13.8 2.3 %collective-permute-start.1 = (bf16[2,4096,256]{2,1,0:T(8,128)(2,1)}, bf16[2,4096,256]{2,1,0:T(8,128)(2,1)}, u32[]{:S(2)}, u32[]{:S(2)}) collective-permute-start(bf16[2,4096,256]{2,1,0:T(8,128)(2,1)} %bitcast.7), channel_id=1, source_target_pairs={{0,384},{384,0},{1,385},{385,1},{2,386},{386,2},{3,387},{387,3},{4... | collective-permute-start | bytes 12582920 | tf_op jit(solution)/shard_map/ppermute | solution.py:193
  22.1 5.5 %collective-permute-start.3 = (bf16[768,256]{1,0:T(8,128)(2,1)}, bf16[768,256]{1,0:T(8,128)(2,1)S(1)}, u32[]{:S(2)}, u32[]{:S(2)}) collective-permute-start(bf16[768,256]{1,0:T(8,128)(2,1)} %shard_map.73.rest_0_), channel_id=1, source_target_pairs={{0,12},{1,13},{2,14},{3,15},{4,0},{5,1},{6,2},{7,3},{8,4},{9,5},{1... | collective-permute-start | bytes 1179656 | tf_op jit(solution)/shard_map/ppermute | solution.py:29
  29.5 4.6 %collective-permute-start.5 = (bf16[768,256]{1,0:T(8,128)(2,1)}, bf16[768,256]{1,0:T(8,128)(2,1)S(1)}, u32[]{:S(2)}, u32[]{:S(2)}) collective-permute-start(bf16[768,256]{1,0:T(8,128)(2,1)} %shard_map.73.rest_0_), channel_id=1, source_target_pairs={{0,3},{1,0},{2,1},{3,2},{4,7},{5,4},{6,5},{7,6},{8,11},{9,8},{10,9... | collective-permute-start | bytes 1179656 | tf_op jit(solution)/shard_map/ppermute | solution.py:24
  34.1 4.5 %collective-permute-done.2 = bf16[768,256]{1,0:T(8,128)(2,1)S(1)} collective-permute-done((bf16[768,256]{1,0:T(8,128)(2,1)}, bf16[768,256]{1,0:T(8,128)(2,1)S(1)}, u32[]{:S(2)}, u32[]{:S(2)}) %collective-permute-start.2) | collective-permute-done | bytes 393248 | tf_op jit(solution)/shard_map/ppermute | solution.py:29
  42.5 10.1 %collective-permute-done.6.rest_4_ = bf16[768,256]{1,0:T(8,128)(2,1)} collective-permute-done((bf16[768,256]{1,0:T(8,128)(2,1)}, bf16[768,256]{1,0:T(8,128)(2,1)}, u32[]{:S(2)}, u32[]{:S(2)}) %collective-permute-start.6) | collective-permute-done | bytes 393248 | tf_op jit(solution)/shard_map/ppermute | solution.py:24
  54.6 4.6 %collective-permute-start.8 = (bf16[1536,256]{1,0:T(8,128)(2,1)S(1)}, bf16[1536,256]{1,0:T(8,128)(2,1)S(1)}, u32[]{:S(2)}, u32[]{:S(2)}) collective-permute-start(bf16[1536,256]{1,0:T(8,128)(2,1)S(1)} %constant_dynamic-update-slice_fusion.rest_1_), channel_id=1, source_target_pairs={{0,3},{1,0},{2,1},{3,2},{4,7},{5,4},{6,5},{7,6},{8,11},{9,8},{10,9... | collective-permute-start | bytes 2359304 | tf_op jit(solution)/shard_map/ppermute | solution.py:24
  62.5 4.3 %collective-permute-start.9 = (bf16[384,256]{1,0:T(8,128)(2,1)}, bf16[384,256]{1,0:T(8,128)(2,1)S(1)}, u32[]{:S(2)}, u32[]{:S(2)}) collective-permute-start(bf16[384,256]{1,0:T(8,128)(2,1)} %slice.24), channel_id=1, source_target_pairs={{0,4},{1,5},{2,6},{3,7},{4,8},{5,9},{6,10},{7,11},{8,12},{9,13},{1... | collective-permute-start | bytes 589832 | tf_op jit(solution)/shard_map/ppermute | solution.py:29
  66.8 6.0 %shard_map.74.rest_3_ = f32[4,256,256]{2,1,0:T(8,128)} custom-call(s32[19]{0:T(128)} %pad_add_fusion.1.table_ref, bf16[2,4096,256]{2,1,0:T(8,128)(2,1)} %bitcast.8, bf16[2,4096,256]{2,1,0:T(8,128)(2,1)} %collective-permute-done.1.r_ref, bf16[768,256]{1,0:T(8,128)(2,1)} %shard_map.73.rest_0_, bf16[1536,256]{1,0:T(8,128)(2,1)} %copy-done, ...), custom_call_target="tpu_custom_call" | custom-call | flops 805306368 | bytes 10747904 | tf_op jit(solution)/shard_map/pallas_call | solution.py:36
  78.0 4.6 %collective-permute-start.12 = (bf16[1536,256]{1,0:T(8,128)(2,1)S(1)}, bf16[1536,256]{1,0:T(8,128)(2,1)S(1)}, u32[]{:S(2)}, u32[]{:S(2)}) collective-permute-start(bf16[1536,256]{1,0:T(8,128)(2,1)S(1)} %get-tuple-element.85), channel_id=1, source_target_pairs={{0,3},{1,0},{2,1},{3,2},{4,7},{5,4},{6,5},{7,6},{8,11},{9,8},{10,9... | collective-permute-start | bytes 2359304 | tf_op jit(solution)/shard_map/ppermute | solution.py:24
  84.5 3.1 %collective-permute-start.13 = (bf16[768,256]{1,0:T(8,128)(2,1)S(1)}, bf16[768,256]{1,0:T(8,128)(2,1)}, u32[]{:S(2)}, u32[]{:S(2)}) collective-permute-start(bf16[768,256]{1,0:T(8,128)(2,1)S(1)} %constant_dynamic-update-slice_fusion.2.rest_2_), channel_id=1, source_target_pairs={{0,2},{1,3},{2,0},{3,1},{4,6},{5,7},{6,4},{7,5},{8,10},{9,11},{10,... | collective-permute-start | bytes 1179656 | tf_op jit(solution)/shard_map/ppermute | solution.py:24
  87.6 6.1 %shard_map.75.rest_3_ = f32[4,256,256]{2,1,0:T(8,128)} custom-call(s32[19]{0:T(128)} %pad_add_fusion.1.table_ref, bf16[2,4096,256]{2,1,0:T(8,128)(2,1)} %bitcast.9, bf16[2,4096,256]{2,1,0:T(8,128)(2,1)} %collective-permute-done.1.r_ref, bf16[1536,256]{1,0:T(8,128)(2,1)} %copy-done.1, bf16[1536,256]{1,0:T(8,128)(2,1)} %copy-done.2, ...), custom_call_target="tpu_custom_call" | custom-call | flops 671088640 | bytes 11403264 | tf_op jit(solution)/shard_map/pallas_call | solution.py:36
  93.7 11.7 %collective-permute-done.13.rest_2_ = bf16[768,256]{1,0:T(8,128)(2,1)} collective-permute-done((bf16[768,256]{1,0:T(8,128)(2,1)S(1)}, bf16[768,256]{1,0:T(8,128)(2,1)}, u32[]{:S(2)}, u32[]{:S(2)}) %collective-permute-start.13) | collective-permute-done | bytes 393248 | tf_op jit(solution)/shard_map/ppermute | solution.py:24
  107.3 6.1 %shard_map.76.t_ref = f32[4,256,256]{2,1,0:T(8,128)} custom-call(s32[19]{0:T(128)} %pad_add_fusion.1.table_ref, bf16[2,4096,256]{2,1,0:T(8,128)(2,1)} %bitcast.10, bf16[2,4096,256]{2,1,0:T(8,128)(2,1)} %collective-permute-done.1.r_ref, bf16[1536,256]{1,0:T(8,128)(2,1)} %copy-done.4, bf16[1536,256]{1,0:T(8,128)(2,1)} %copy-done.5, ...), custom_call_target="tpu_custom_call" | custom-call | flops 671088640 | bytes 11403264 | tf_op jit(solution)/shard_map/pallas_call | solution.py:36
  113.4 6.4 %shard_map.77 = (bf16[1024,256]{1,0:T(8,128)(2,1)}, bf16[1024,256]{1,0:T(8,128)(2,1)}, bf16[512,256]{1,0:T(8,128)(2,1)}, bf16[4,256,256]{2,1,0:T(8,128)(2,1)}) custom-call(s32[19]{0:T(128)} %pad_add_fusion.1.table_ref, f32[4,256,256]{2,1,0:T(8,128)} %shard_map.76.t_ref, bf16[2,4096,256]{2,1,0:T(8,128)(2,1)} %bitcast.11, ...), custom_call_target="tpu_custom_call" | custom-call | flops 1006632960 | bytes 9437184 | tf_op jit(solution)/shard_map/pallas_call | solution.py:36
  119.8 4.4 %collective-permute-start.14 = (bf16[1024,256]{1,0:T(8,128)(2,1)}, bf16[1024,256]{1,0:T(8,128)(2,1)S(1)}, u32[]{:S(2)}, u32[]{:S(2)}) collective-permute-start(bf16[1024,256]{1,0:T(8,128)(2,1)} %get-tuple-element.69), channel_id=1, source_target_pairs={{0,1},{1,2},{2,3},{3,0},{4,5},{5,6},{6,7},{7,4},{8,9},{9,10},{10,1... | collective-permute-start | bytes 1572872 | tf_op jit(solution)/shard_map/ppermute | solution.py:24
  126.3 3.5 %collective-permute-start.16 = (bf16[512,256]{1,0:T(8,128)(2,1)}, bf16[512,256]{1,0:T(8,128)(2,1)S(1)}, u32[]{:S(2)}, u32[]{:S(2)}) collective-permute-start(bf16[512,256]{1,0:T(8,128)(2,1)} %get-tuple-element.71), channel_id=1, source_target_pairs={{0,2},{1,3},{2,0},{3,1},{4,6},{5,7},{6,4},{7,5},{8,10},{9,11},{10,... | collective-permute-start | bytes 786440 | tf_op jit(solution)/shard_map/ppermute | solution.py:24
  129.9 6.3 %shard_map.78 = (bf16[512,256]{1,0:T(8,128)(2,1)}, bf16[1280,256]{1,0:T(8,128)(2,1)}, bf16[1280,256]{1,0:T(8,128)(2,1)}, bf16[512,256]{1,0:T(8,128)(2,1)}, bf16[...) custom-call(s32[19]{0:T(128)} %pad_add_fusion.1.table_ref, ...), custom_call_target="tpu_custom_call" | custom-call | flops 1476395008 | bytes 8912896 | tf_op jit(solution)/shard_map/pallas_call | solution.py:36
  136.1 3.5 %collective-permute-done.16.refs_5_ = bf16[512,256]{1,0:T(8,128)(2,1)S(1)} collective-permute-done((bf16[512,256]{1,0:T(8,128)(2,1)}, bf16[512,256]{1,0:T(8,128)(2,1)S(1)}, u32[]{:S(2)}, u32[]{:S(2)}) %collective-permute-start.16) | collective-permute-done | bytes 262176 | tf_op jit(solution)/shard_map/ppermute | solution.py:24
  140.7 3.0 %shard_map.79 = (bf16[512,256]{1,0:T(8,128)(2,1)}, bf16[1280,256]{1,0:T(8,128)(2,1)}, bf16[1280,256]{1,0:T(8,128)(2,1)}) custom-call(s32[19]{0:T(128)} %pad_add_fusion.1.table_ref, bf16[512,256]{1,0:T(8,128)(2,1)} %get-tuple-element.66.refs_0_, bf16[1280,256]{1,0:T(8,128)(2,1)} %get-tuple-element.67.refs_1_, bf16[1280,256]{1,0:T(8,128)(2,1)} %get-tuple-element.68.refs_2_, ...), custom_call_target="tpu_custom_call" | custom-call | bytes 2883584 | tf_op jit(solution)/shard_map/pallas_call | solution.py:36
  143.7 4.4 %collective-permute-start.17 = (bf16[1280,256]{1,0:T(8,128)(2,1)}, bf16[1280,256]{1,0:T(8,128)(2,1)S(1)}, u32[]{:S(2)}, u32[]{:S(2)}) collective-permute-start(bf16[1280,256]{1,0:T(8,128)(2,1)} %get-tuple-element.72), channel_id=1, source_target_pairs={{0,1},{1,2},{2,3},{3,0},{4,5},{5,6},{6,7},{7,4},{8,9},{9,10},{10,1... | collective-permute-start | bytes 1966088 | tf_op jit(solution)/shard_map/ppermute | solution.py:24
  148.1 3.3 %collective-permute-start.18 = (bf16[1280,256]{1,0:T(8,128)(2,1)}, bf16[1280,256]{1,0:T(8,128)(2,1)S(1)}, u32[]{:S(2)}, u32[]{:S(2)}) collective-permute-start(bf16[1280,256]{1,0:T(8,128)(2,1)} %get-tuple-element.73), channel_id=1, source_target_pairs={{0,3},{1,0},{2,1},{3,2},{4,7},{5,4},{6,5},{7,6},{8,11},{9,8},{10,9... | collective-permute-start | bytes 1966088 | tf_op jit(solution)/shard_map/ppermute | solution.py:24
  152.4 3.2 %collective-permute-start.19 = (bf16[256,256]{1,0:T(8,128)(2,1)S(1)}, bf16[256,256]{1,0:T(8,128)(2,1)S(1)}, u32[]{:S(2)}, u32[]{:S(2)}) collective-permute-start(bf16[256,256]{1,0:T(8,128)(2,1)S(1)} %get-tuple-element.88), channel_id=1, source_target_pairs={{0,4},{1,5},{2,6},{3,7},{4,8},{5,9},{6,10},{7,11},{8,12},{9,13},{1... | collective-permute-start | bytes 393224 | tf_op jit(solution)/shard_map/ppermute | solution.py:29
  155.6 4.2 %collective-permute-start.20 = (bf16[256,256]{1,0:T(8,128)(2,1)S(1)}, bf16[256,256]{1,0:T(8,128)(2,1)S(1)}, u32[]{:S(2)}, u32[]{:S(2)}) collective-permute-start(bf16[256,256]{1,0:T(8,128)(2,1)S(1)} %get-tuple-element.87), channel_id=1, source_target_pairs={{0,12},{1,13},{2,14},{3,15},{4,0},{5,1},{6,2},{7,3},{8,4},{9,5},{1... | collective-permute-start | bytes 393224 | tf_op jit(solution)/shard_map/ppermute | solution.py:29
  163.7 2.8 %shard_map.80 = (bf16[512,256]{1,0:T(8,128)(2,1)}, bf16[512,256]{1,0:T(8,128)(2,1)}, bf16[512,256]{1,0:T(8,128)(2,1)}, bf16[512,256]{1,0:T(8,128)(2,1)}) custom-call(s32[19]{0:T(128)} %pad_add_fusion.1.table_ref, bf16[512,256]{1,0:T(8,128)(2,1)} %get-tuple-element.62.refs_0_, bf16[512,256]{1,0:T(8,128)(2,1)} %get-tuple-element.63.refs_1_, ...), custom_call_target="tpu_custom_call" | custom-call | bytes 2621440 | tf_op jit(solution)/shard_map/pallas_call | solution.py:36
  166.4 3.3 %collective-permute-start.21 = (bf16[512,256]{1,0:T(8,128)(2,1)}, bf16[512,256]{1,0:T(8,128)(2,1)S(1)}, u32[]{:S(2)}, u32[]{:S(2)}) collective-permute-start(bf16[512,256]{1,0:T(8,128)(2,1)} %get-tuple-element.75), channel_id=1, source_target_pairs={{0,4},{1,5},{2,6},{3,7},{4,8},{5,9},{6,10},{7,11},{8,12},{9,13},{1... | collective-permute-start | bytes 786440 | tf_op jit(solution)/shard_map/ppermute | solution.py:29
  169.7 4.1 %collective-permute-start.22 = (bf16[512,256]{1,0:T(8,128)(2,1)}, bf16[512,256]{1,0:T(8,128)(2,1)S(1)}, u32[]{:S(2)}, u32[]{:S(2)}) collective-permute-start(bf16[512,256]{1,0:T(8,128)(2,1)} %get-tuple-element.76), channel_id=1, source_target_pairs={{0,12},{1,13},{2,14},{3,15},{4,0},{5,1},{6,2},{7,3},{8,4},{9,5},{1... | collective-permute-start | bytes 786440 | tf_op jit(solution)/shard_map/ppermute | solution.py:29
  173.8 2.7 %collective-permute-start.23 = (bf16[512,256]{1,0:T(8,128)(2,1)}, bf16[512,256]{1,0:T(8,128)(2,1)S(1)}, u32[]{:S(2)}, u32[]{:S(2)}) collective-permute-start(bf16[512,256]{1,0:T(8,128)(2,1)} %get-tuple-element.77), channel_id=1, source_target_pairs={{0,1},{1,2},{2,3},{3,0},{4,5},{5,6},{6,7},{7,4},{8,9},{9,10},{10,1... | collective-permute-start | bytes 786440 | tf_op jit(solution)/shard_map/ppermute | solution.py:24
  176.5 3.8 %collective-permute-start.24 = (bf16[512,256]{1,0:T(8,128)(2,1)}, bf16[512,256]{1,0:T(8,128)(2,1)S(1)}, u32[]{:S(2)}, u32[]{:S(2)}) collective-permute-start(bf16[512,256]{1,0:T(8,128)(2,1)} %get-tuple-element.78), channel_id=1, source_target_pairs={{0,3},{1,0},{2,1},{3,2},{4,7},{5,4},{6,5},{7,6},{8,11},{9,8},{10,9... | collective-permute-start | bytes 786440 | tf_op jit(solution)/shard_map/ppermute | solution.py:24
  180.4 2.3 %collective-permute-done.23.refs_3_ = bf16[512,256]{1,0:T(8,128)(2,1)S(1)} collective-permute-done((bf16[512,256]{1,0:T(8,128)(2,1)}, bf16[512,256]{1,0:T(8,128)(2,1)S(1)}, u32[]{:S(2)}, u32[]{:S(2)}) %collective-permute-start.23) | collective-permute-done | bytes 262176 | tf_op jit(solution)/shard_map/ppermute | solution.py:24
  184.8 2.1 %shard_map.81 = (bf16[256,256]{1,0:T(8,128)(2,1)}, bf16[256,256]{1,0:T(8,128)(2,1)}) custom-call(s32[19]{0:T(128)} %pad_add_fusion.1.table_ref, bf16[512,256]{1,0:T(8,128)(2,1)} %get-tuple-element.61.refs_0_, bf16[512,256]{1,0:T(8,128)(2,1)} %copy-done.14, bf16[512,256]{1,0:T(8,128)(2,1)} %copy-done.15, bf16[512,256]{1,0:T(8,128)(2,1)} %copy-done.17, ...), custom_call_target="tpu_custom_call" | custom-call | bytes 1310720 | tf_op jit(solution)/shard_map/pallas_call | solution.py:36
  186.9 9.8 %collective-permute-start.25 = (bf16[256,256]{1,0:T(8,128)(2,1)}, bf16[256,256]{1,0:T(8,128)(2,1)S(1)}, u32[]{:S(2)}, u32[]{:S(2)}) collective-permute-start(bf16[256,256]{1,0:T(8,128)(2,1)} %get-tuple-element.80), channel_id=1, source_target_pairs={{0,384},{384,0},{1,385},{385,1},{2,386},{386,2},{3,387},{387,3},{4... | collective-permute-start | bytes 393224 | tf_op jit(solution)/shard_map/ppermute | solution.py:264
  (87 shorter events, 40.4 us)
Async XLA Ops:
  0.0 13.8 %collective-permute-start = (bf16[512,256]{1,0:T(8,128)(2,1)}, bf16[512,256]{1,0:T(8,128)(2,1)S(1)}, u32[]{:S(2)}, u32[]{:S(2)}) collective-permute-start(bf16[512,256]{1,0:T(8,128)(2,1)} %bitcast.13), channel_id=1, source_target_pairs={{0,384},{384,0},{1,385},{385,1},{2,386},{386,2},{3,387},{387,3},{4... | collective-permute-start | bytes 786440 | tf_op jit(solution)/shard_map/ppermute | solution.py:191
  13.8 4.5 %copy-start.19 = (bf16[512,256]{1,0:T(8,128)(2,1)}, bf16[512,256]{1,0:T(8,128)(2,1)S(1)}, u32[]{:S(2)}) copy-start(bf16[512,256]{1,0:T(8,128)(2,1)S(1)} %collective-permute-done.partner_ref) | copy-start | bytes 786436
  13.8 53.0 %collective-permute-start.1 = (bf16[2,4096,256]{2,1,0:T(8,128)(2,1)}, bf16[2,4096,256]{2,1,0:T(8,128)(2,1)}, u32[]{:S(2)}, u32[]{:S(2)}) collective-permute-start(bf16[2,4096,256]{2,1,0:T(8,128)(2,1)} %bitcast.7), channel_id=1, source_target_pairs={{0,384},{384,0},{1,385},{385,1},{2,386},{386,2},{3,387},{387,3},{4... | collective-permute-start | bytes 12582920 | tf_op jit(solution)/shard_map/ppermute | solution.py:193
  20.2 18.4 %collective-permute-start.2 = (bf16[768,256]{1,0:T(8,128)(2,1)}, bf16[768,256]{1,0:T(8,128)(2,1)S(1)}, u32[]{:S(2)}, u32[]{:S(2)}) collective-permute-start(bf16[768,256]{1,0:T(8,128)(2,1)} %shard_map.73.rest_0_), channel_id=1, source_target_pairs={{0,4},{1,5},{2,6},{3,7},{4,8},{5,9},{6,10},{7,11},{8,12},{9,13},{1... | collective-permute-start | bytes 1179656 | tf_op jit(solution)/shard_map/ppermute | solution.py:29
  22.1 18.4 %collective-permute-start.3 = (bf16[768,256]{1,0:T(8,128)(2,1)}, bf16[768,256]{1,0:T(8,128)(2,1)S(1)}, u32[]{:S(2)}, u32[]{:S(2)}) collective-permute-start(bf16[768,256]{1,0:T(8,128)(2,1)} %shard_map.73.rest_0_), channel_id=1, source_target_pairs={{0,12},{1,13},{2,14},{3,15},{4,0},{5,1},{6,2},{7,3},{8,4},{9,5},{1... | collective-permute-start | bytes 1179656 | tf_op jit(solution)/shard_map/ppermute | solution.py:29
  27.6 13.3 %collective-permute-start.4 = (bf16[768,256]{1,0:T(8,128)(2,1)}, bf16[768,256]{1,0:T(8,128)(2,1)S(1)}, u32[]{:S(2)}, u32[]{:S(2)}) collective-permute-start(bf16[768,256]{1,0:T(8,128)(2,1)} %shard_map.73.rest_0_), channel_id=1, source_target_pairs={{0,1},{1,2},{2,3},{3,0},{4,5},{5,6},{6,7},{7,4},{8,9},{9,10},{10,1... | collective-permute-start | bytes 1179656 | tf_op jit(solution)/shard_map/ppermute | solution.py:24
  29.5 13.0 %collective-permute-start.5 = (bf16[768,256]{1,0:T(8,128)(2,1)}, bf16[768,256]{1,0:T(8,128)(2,1)S(1)}, u32[]{:S(2)}, u32[]{:S(2)}) collective-permute-start(bf16[768,256]{1,0:T(8,128)(2,1)} %shard_map.73.rest_0_), channel_id=1, source_target_pairs={{0,3},{1,0},{2,1},{3,2},{4,7},{5,4},{6,5},{7,6},{8,11},{9,8},{10,9... | collective-permute-start | bytes 1179656 | tf_op jit(solution)/shard_map/ppermute | solution.py:24
  38.6 13.9 %collective-permute-start.6 = (bf16[768,256]{1,0:T(8,128)(2,1)}, bf16[768,256]{1,0:T(8,128)(2,1)}, u32[]{:S(2)}, u32[]{:S(2)}) collective-permute-start(bf16[768,256]{1,0:T(8,128)(2,1)} %shard_map.73.rest_0_), channel_id=1, source_target_pairs={{0,2},{1,3},{2,0},{3,1},{4,6},{5,7},{6,4},{7,5},{8,10},{9,11},{10,... | collective-permute-start | bytes 1179656 | tf_op jit(solution)/shard_map/ppermute | solution.py:24
  40.9 25.9 %copy-start.12 = (bf16[768,256]{1,0:T(8,128)(2,1)}, bf16[768,256]{1,0:T(8,128)(2,1)S(1)}, u32[]{:S(2)}) copy-start(bf16[768,256]{1,0:T(8,128)(2,1)S(1)} %collective-permute-done.4.rest_2_) | copy-start | bytes 1179652
  42.5 24.3 %copy-start.13 = (bf16[768,256]{1,0:T(8,128)(2,1)}, bf16[768,256]{1,0:T(8,128)(2,1)S(1)}, u32[]{:S(2)}) copy-start(bf16[768,256]{1,0:T(8,128)(2,1)S(1)} %collective-permute-done.5.rest_3_) | copy-start | bytes 1179652
  52.6 14.1 %copy-start = (bf16[1536,256]{1,0:T(8,128)(2,1)}, bf16[1536,256]{1,0:T(8,128)(2,1)S(1)}, u32[]{:S(2)}) copy-start(bf16[1536,256]{1,0:T(8,128)(2,1)S(1)} %constant_dynamic-update-slice_fusion.rest_1_) | copy-start | bytes 2359300
  52.7 22.2 %collective-permute-start.7 = (bf16[1536,256]{1,0:T(8,128)(2,1)S(1)}, bf16[1536,256]{1,0:T(8,128)(2,1)S(1)}, u32[]{:S(2)}, u32[]{:S(2)}) collective-permute-start(bf16[1536,256]{1,0:T(8,128)(2,1)S(1)} %constant_dynamic-update-slice_fusion.rest_1_), channel_id=1, source_target_pairs={{0,1},{1,2},{2,3},{3,0},{4,5},{5,6},{6,7},{7,4},{8,9},{9,10},{10,1... | collective-permute-start | bytes 2359304 | tf_op jit(solution)/shard_map/ppermute | solution.py:24
  54.6 20.3 %collective-permute-start.8 = (bf16[1536,256]{1,0:T(8,128)(2,1)S(1)}, bf16[1536,256]{1,0:T(8,128)(2,1)S(1)}, u32[]{:S(2)}, u32[]{:S(2)}) collective-permute-start(bf16[1536,256]{1,0:T(8,128)(2,1)S(1)} %constant_dynamic-update-slice_fusion.rest_1_), channel_id=1, source_target_pairs={{0,3},{1,0},{2,1},{3,2},{4,7},{5,4},{6,5},{7,6},{8,11},{9,8},{10,9... | collective-permute-start | bytes 2359304 | tf_op jit(solution)/shard_map/ppermute | solution.py:24
  60.6 12.2 %collective-permute-start.10 = (bf16[384,256]{1,0:T(8,128)(2,1)}, bf16[384,256]{1,0:T(8,128)(2,1)S(1)}, u32[]{:S(2)}, u32[]{:S(2)}) collective-permute-start(bf16[384,256]{1,0:T(8,128)(2,1)} %slice.25), channel_id=1, source_target_pairs={{0,12},{1,13},{2,14},{3,15},{4,0},{5,1},{6,2},{7,3},{8,4},{9,5},{1... | collective-permute-start | bytes 589832 | tf_op jit(solution)/shard_map/ppermute | solution.py:29
  62.5 12.4 %collective-permute-start.9 = (bf16[384,256]{1,0:T(8,128)(2,1)}, bf16[384,256]{1,0:T(8,128)(2,1)S(1)}, u32[]{:S(2)}, u32[]{:S(2)}) collective-permute-start(bf16[384,256]{1,0:T(8,128)(2,1)} %slice.24), channel_id=1, source_target_pairs={{0,4},{1,5},{2,6},{3,7},{4,8},{5,9},{6,10},{7,11},{8,12},{9,13},{1... | collective-permute-start | bytes 589832 | tf_op jit(solution)/shard_map/ppermute | solution.py:29
  76.1 29.4 %collective-permute-start.11 = (bf16[1536,256]{1,0:T(8,128)(2,1)S(1)}, bf16[1536,256]{1,0:T(8,128)(2,1)S(1)}, u32[]{:S(2)}, u32[]{:S(2)}) collective-permute-start(bf16[1536,256]{1,0:T(8,128)(2,1)S(1)} %get-tuple-element.86), channel_id=1, source_target_pairs={{0,1},{1,2},{2,3},{3,0},{4,5},{5,6},{6,7},{7,4},{8,9},{9,10},{10,1... | collective-permute-start | bytes 2359304 | tf_op jit(solution)/shard_map/ppermute | solution.py:24
  78.0 27.4 %collective-permute-start.12 = (bf16[1536,256]{1,0:T(8,128)(2,1)S(1)}, bf16[1536,256]{1,0:T(8,128)(2,1)S(1)}, u32[]{:S(2)}, u32[]{:S(2)}) collective-permute-start(bf16[1536,256]{1,0:T(8,128)(2,1)S(1)} %get-tuple-element.85), channel_id=1, source_target_pairs={{0,3},{1,0},{2,1},{3,2},{4,7},{5,4},{6,5},{7,6},{8,11},{9,8},{10,9... | collective-permute-start | bytes 2359304 | tf_op jit(solution)/shard_map/ppermute | solution.py:24
  84.5 20.9 %collective-permute-start.13 = (bf16[768,256]{1,0:T(8,128)(2,1)S(1)}, bf16[768,256]{1,0:T(8,128)(2,1)}, u32[]{:S(2)}, u32[]{:S(2)}) collective-permute-start(bf16[768,256]{1,0:T(8,128)(2,1)S(1)} %constant_dynamic-update-slice_fusion.2.rest_2_), channel_id=1, source_target_pairs={{0,2},{1,3},{2,0},{3,1},{4,6},{5,7},{6,4},{7,5},{8,10},{9,11},{10,... | collective-permute-start | bytes 1179656 | tf_op jit(solution)/shard_map/ppermute | solution.py:24
  119.8 19.8 %collective-permute-start.14 = (bf16[1024,256]{1,0:T(8,128)(2,1)}, bf16[1024,256]{1,0:T(8,128)(2,1)S(1)}, u32[]{:S(2)}, u32[]{:S(2)}) collective-permute-start(bf16[1024,256]{1,0:T(8,128)(2,1)} %get-tuple-element.69), channel_id=1, source_target_pairs={{0,1},{1,2},{2,3},{3,0},{4,5},{5,6},{6,7},{7,4},{8,9},{9,10},{10,1... | collective-permute-start | bytes 1572872 | tf_op jit(solution)/shard_map/ppermute | solution.py:24
  124.2 15.4 %collective-permute-start.15 = (bf16[1024,256]{1,0:T(8,128)(2,1)}, bf16[1024,256]{1,0:T(8,128)(2,1)S(1)}, u32[]{:S(2)}, u32[]{:S(2)}) collective-permute-start(bf16[1024,256]{1,0:T(8,128)(2,1)} %get-tuple-element.70), channel_id=1, source_target_pairs={{0,3},{1,0},{2,1},{3,2},{4,7},{5,4},{6,5},{7,6},{8,11},{9,8},{10,9... | collective-permute-start | bytes 1572872 | tf_op jit(solution)/shard_map/ppermute | solution.py:24
  126.3 13.3 %collective-permute-start.16 = (bf16[512,256]{1,0:T(8,128)(2,1)}, bf16[512,256]{1,0:T(8,128)(2,1)S(1)}, u32[]{:S(2)}, u32[]{:S(2)}) collective-permute-start(bf16[512,256]{1,0:T(8,128)(2,1)} %get-tuple-element.71), channel_id=1, source_target_pairs={{0,2},{1,3},{2,0},{3,1},{4,6},{5,7},{6,4},{7,5},{8,10},{9,11},{10,... | collective-permute-start | bytes 786440 | tf_op jit(solution)/shard_map/ppermute | solution.py:24
  143.7 18.9 %collective-permute-start.17 = (bf16[1280,256]{1,0:T(8,128)(2,1)}, bf16[1280,256]{1,0:T(8,128)(2,1)S(1)}, u32[]{:S(2)}, u32[]{:S(2)}) collective-permute-start(bf16[1280,256]{1,0:T(8,128)(2,1)} %get-tuple-element.72), channel_id=1, source_target_pairs={{0,1},{1,2},{2,3},{3,0},{4,5},{5,6},{6,7},{7,4},{8,9},{9,10},{10,1... | collective-permute-start | bytes 1966088 | tf_op jit(solution)/shard_map/ppermute | solution.py:24
  148.1 14.5 %collective-permute-start.18 = (bf16[1280,256]{1,0:T(8,128)(2,1)}, bf16[1280,256]{1,0:T(8,128)(2,1)S(1)}, u32[]{:S(2)}, u32[]{:S(2)}) collective-permute-start(bf16[1280,256]{1,0:T(8,128)(2,1)} %get-tuple-element.73), channel_id=1, source_target_pairs={{0,3},{1,0},{2,1},{3,2},{4,7},{5,4},{6,5},{7,6},{8,11},{9,8},{10,9... | collective-permute-start | bytes 1966088 | tf_op jit(solution)/shard_map/ppermute | solution.py:24
  152.4 9.3 %collective-permute-start.19 = (bf16[256,256]{1,0:T(8,128)(2,1)S(1)}, bf16[256,256]{1,0:T(8,128)(2,1)S(1)}, u32[]{:S(2)}, u32[]{:S(2)}) collective-permute-start(bf16[256,256]{1,0:T(8,128)(2,1)S(1)} %get-tuple-element.88), channel_id=1, source_target_pairs={{0,4},{1,5},{2,6},{3,7},{4,8},{5,9},{6,10},{7,11},{8,12},{9,13},{1... | collective-permute-start | bytes 393224 | tf_op jit(solution)/shard_map/ppermute | solution.py:29
  155.6 6.9 %collective-permute-start.20 = (bf16[256,256]{1,0:T(8,128)(2,1)S(1)}, bf16[256,256]{1,0:T(8,128)(2,1)S(1)}, u32[]{:S(2)}, u32[]{:S(2)}) collective-permute-start(bf16[256,256]{1,0:T(8,128)(2,1)S(1)} %get-tuple-element.87), channel_id=1, source_target_pairs={{0,12},{1,13},{2,14},{3,15},{4,0},{5,1},{6,2},{7,3},{8,4},{9,5},{1... | collective-permute-start | bytes 393224 | tf_op jit(solution)/shard_map/ppermute | solution.py:29
  166.4 13.9 %collective-permute-start.21 = (bf16[512,256]{1,0:T(8,128)(2,1)}, bf16[512,256]{1,0:T(8,128)(2,1)S(1)}, u32[]{:S(2)}, u32[]{:S(2)}) collective-permute-start(bf16[512,256]{1,0:T(8,128)(2,1)} %get-tuple-element.75), channel_id=1, source_target_pairs={{0,4},{1,5},{2,6},{3,7},{4,8},{5,9},{6,10},{7,11},{8,12},{9,13},{1... | collective-permute-start | bytes 786440 | tf_op jit(solution)/shard_map/ppermute | solution.py:29
  169.7 10.6 %collective-permute-start.22 = (bf16[512,256]{1,0:T(8,128)(2,1)}, bf16[512,256]{1,0:T(8,128)(2,1)S(1)}, u32[]{:S(2)}, u32[]{:S(2)}) collective-permute-start(bf16[512,256]{1,0:T(8,128)(2,1)} %get-tuple-element.76), channel_id=1, source_target_pairs={{0,12},{1,13},{2,14},{3,15},{4,0},{5,1},{6,2},{7,3},{8,4},{9,5},{1... | collective-permute-start | bytes 786440 | tf_op jit(solution)/shard_map/ppermute | solution.py:29
  173.8 8.8 %collective-permute-start.23 = (bf16[512,256]{1,0:T(8,128)(2,1)}, bf16[512,256]{1,0:T(8,128)(2,1)S(1)}, u32[]{:S(2)}, u32[]{:S(2)}) collective-permute-start(bf16[512,256]{1,0:T(8,128)(2,1)} %get-tuple-element.77), channel_id=1, source_target_pairs={{0,1},{1,2},{2,3},{3,0},{4,5},{5,6},{6,7},{7,4},{8,9},{9,10},{10,1... | collective-permute-start | bytes 786440 | tf_op jit(solution)/shard_map/ppermute | solution.py:24
  176.5 7.6 %collective-permute-start.24 = (bf16[512,256]{1,0:T(8,128)(2,1)}, bf16[512,256]{1,0:T(8,128)(2,1)S(1)}, u32[]{:S(2)}, u32[]{:S(2)}) collective-permute-start(bf16[512,256]{1,0:T(8,128)(2,1)} %get-tuple-element.78), channel_id=1, source_target_pairs={{0,3},{1,0},{2,1},{3,2},{4,7},{5,4},{6,5},{7,6},{8,11},{9,8},{10,9... | collective-permute-start | bytes 786440 | tf_op jit(solution)/shard_map/ppermute | solution.py:24
  180.4 3.8 %copy-start.14 = (bf16[512,256]{1,0:T(8,128)(2,1)}, bf16[512,256]{1,0:T(8,128)(2,1)S(1)}, u32[]{:S(2)}) copy-start(bf16[512,256]{1,0:T(8,128)(2,1)S(1)} %collective-permute-done.21.refs_1_) | copy-start | bytes 786436
  180.4 3.8 %copy-start.15 = (bf16[512,256]{1,0:T(8,128)(2,1)}, bf16[512,256]{1,0:T(8,128)(2,1)S(1)}, u32[]{:S(2)}) copy-start(bf16[512,256]{1,0:T(8,128)(2,1)S(1)} %collective-permute-done.22.refs_2_) | copy-start | bytes 786436
  186.9 11.0 %collective-permute-start.25 = (bf16[256,256]{1,0:T(8,128)(2,1)}, bf16[256,256]{1,0:T(8,128)(2,1)S(1)}, u32[]{:S(2)}, u32[]{:S(2)}) collective-permute-start(bf16[256,256]{1,0:T(8,128)(2,1)} %get-tuple-element.80), channel_id=1, source_target_pairs={{0,384},{384,0},{1,385},{385,1},{2,386},{386,2},{3,387},{387,3},{4... | collective-permute-start | bytes 393224 | tf_op jit(solution)/shard_map/ppermute | solution.py:264
  (16 other events, 20.8 us)

commit v4 on v3

v4 whole, which is shorter than its diff:
```python
import jax
import jax.numpy as jnp
from jax import lax
from jax.experimental import pallas as pl
from jax.experimental.pallas import tpu as pltpu
from jax.sharding import PartitionSpec as P

HS = 256
SIDE = 4
ROWS = 3 * HS
HALF = ROWS // 2
N = 2 * HS
F32 = jnp.float32
BF16 = jnp.bfloat16
SWAP = [(0, 1), (1, 0)]
NT = (((1,), (1,)), ((), ()))
TN = (((0,), (0,)), ((), ()))
VMEM = pl.BlockSpec(memory_space=pltpu.VMEM)
SMEM = pl.BlockSpec(memory_space=pltpu.SMEM)
VMEM_LIMIT = 20 * 2**20


def shift_x(block, step):
    route = [(y * SIDE + x, y * SIDE + (x + step) % SIDE) for y in range(SIDE) for x in range(SIDE)]
    return lax.ppermute(block, "mp", route)


def shift_y(block, step):
    route = [(y * SIDE + x, (y + step) % SIDE * SIDE + x) for y in range(SIDE) for x in range(SIDE)]
    return lax.ppermute(block, "mp", route)


def call(body, inputs, shapes, flops=0, out_dtype=BF16, scalars=0):
    out = [jax.ShapeDtypeStruct(s, out_dtype) for s in shapes]
    moved = sum(a.size * a.dtype.itemsize for a in inputs)
    return pl.pallas_call(
        body,
        out_shape=out,
        in_specs=[SMEM] * scalars + [VMEM] * (len(inputs) - scalars),
        out_specs=[VMEM] * len(out),
        compiler_params=pltpu.CompilerParams(vmem_limit_bytes=VMEM_LIMIT),
        cost_estimate=pl.CostEstimate(flops=flops, bytes_accessed=moved, transcendentals=0),
    )(*inputs)


def feature_rows(offset):
    me = lax.axis_index("mp")
    y = lax.rem(lax.div(me, SIDE) + offset[0] + SIDE, SIDE)
    x = lax.rem(lax.rem(me, SIDE) + offset[1] + SIDE, SIDE)
    return pl.ds(pl.multiple_of((y * SIDE + x) * HS, HS), HS)


def slot_rows(index):
    return pl.ds(pl.multiple_of(index * HS, HS), HS)


def assemble(own, cotangent, partner):
    def body(own_ref, cot_ref, partner_ref, out_ref):
        sec = lax.axis_index("section")
        here = slot_rows(sec)
        out_ref[:HS, :] = own_ref[here, :]
        out_ref[slot_rows(2 - sec), :] = cot_ref[here, :]
        out_ref[slot_rows(1 + sec), :] = partner_ref[here, :]

    return call(body, [own, cotangent, partner], [(ROWS, HS)])[0]


def rows_of(refs, block, low, high):
    parts, at = [], 0
    for which, first, count in block:
        a, b = max(low, at), min(high, at + count)
        if a < b:
            parts.append(refs[which][first + a - at : first + b - at, :])
        at += count
    return parts[0] if len(parts) == 1 else jnp.concatenate(parts, axis=0)


def project(pieces, blocks, own_w, other_w, total):
    def body(u_ref, r_ref, *rest):
        refs, out_ref = rest[: len(pieces)], rest[-1]
        core0 = lax.axis_index("section") == 0
        feats = [feature_rows(offset) for offset, _ in blocks]
        parts = [
            jnp.concatenate([rows_of(refs, block, k * HS, (k + 1) * HS) for _, block in blocks], axis=1)
            for k in range(3)
        ]
        lhs = (parts[0], jnp.where(core0, parts[0], parts[1]), jnp.where(core0, parts[1], parts[2]), parts[2])
        for j in range(4):
            w_ref = (u_ref, r_ref)[j // 2]
            weight = jnp.concatenate([w_ref[j % 2, f, :] for f in feats], axis=0)
            term = jnp.dot(lhs[j], weight, preferred_element_type=F32)
            out_ref[j] = term if total is None else rest[-2][j] + term

    inputs = [own_w, other_w, *pieces] + ([] if total is None else [total])
    return call(body, inputs, [(4, HS, HS)], len(blocks) * 8 * HS**3, F32)[0]


def write_terms(g_ref, u_ref, r_ref, wanted):
    for offset, *slots in wanted:
        feats = feature_rows(offset)
        for slot, (out_ref, row) in enumerate(slots):
            w_ref = (u_ref, r_ref)[slot]
            term = lax.dot_general(g_ref[2 * slot], w_ref[0, feats, :], NT, preferred_element_type=F32)
            term += lax.dot_general(g_ref[2 * slot + 1], w_ref[1, feats, :], NT, preferred_element_type=F32)
            out_ref[row : row + HS, :] = term.astype(BF16)


def attend(enc_lengths, dec_lengths, total, own_w, other_w):
    scale = 1.0 / HS**0.5

    def body(enc_ref, dec_ref, t_ref, u_ref, r_ref, right_ref, left_ref, across_ref, g_ref):
        me = lax.axis_index("section")
        keys = t_ref[2 * me].astype(BF16)
        values = t_ref[2 * me + 1].astype(BF16)
        queries = t_ref[2 - 2 * me].astype(BF16)
        out_grad = t_ref[3 - 2 * me]
        live_q = lax.broadcasted_iota(jnp.int32, (HS, HS), 0) < dec_ref[me]
        live_k = lax.broadcasted_iota(jnp.int32, (HS, HS), 1) < enc_ref[me]
        masked = jnp.where(live_q, out_grad, 0.0).astype(BF16)
        scores = lax.dot_general(queries, keys, NT, preferred_element_type=F32) * scale
        scores = jnp.where(live_k, scores, -1e30)
        top = jnp.max(scores, axis=-1, keepdims=True)
        expd = jnp.exp(scores - top)
        probs = expd / jnp.sum(expd, axis=-1, keepdims=True)
        value_grad = lax.dot_general(probs.astype(BF16), masked, TN, preferred_element_type=F32).astype(BF16)
        prob_grad = lax.dot_general(masked, values, NT, preferred_element_type=F32)
        delta = jnp.sum(probs * prob_grad, axis=-1, keepdims=True)
        sg = (probs * (prob_grad - delta)).astype(BF16)
        query_grad = (jnp.dot(sg, keys, preferred_element_type=F32) * scale).astype(BF16)
        key_grad = (lax.dot_general(sg, queries, TN, preferred_element_type=F32) * scale).astype(BF16)
        g_ref[2 * me] = key_grad
        g_ref[2 * me + 1] = value_grad
        g_ref[2 - 2 * me] = query_grad
        g_ref[3 - 2 * me] = jnp.zeros_like(query_grad)
        write_terms(g_ref, u_ref, r_ref, [
            ((2, 1), (right_ref, 0), (right_ref, HS)),
            ((1, 2), (right_ref, N), (left_ref, N)),
            ((-1, 2), (right_ref, N + HS), (left_ref, N + HS)),
            ((2, -1), (left_ref, 0), (left_ref, HS)),
            ((2, 2), (across_ref, 0), (across_ref, HS)),
        ])

    shapes = [(2 * N, HS), (2 * N, HS), (N, HS), (4, HS, HS)]
    return call(body, [enc_lengths, dec_lengths, total, own_w, other_w], shapes, 60 * HS**3, BF16, 2)


def spread(grads, own_w, other_w):
    def body(g_ref, u_ref, r_ref, far, right, left, up, down, right_c, left_c, here):
        write_terms(g_ref, u_ref, r_ref, [
            ((2, 0), (far, 0), (far, HS)),
            ((1, 1), (right, 0), (right, HS)),
            ((-1, 1), (right, N), (right, N + HS)),
            ((1, -1), (left, 0), (left, HS)),
            ((-1, -1), (left, N), (left, N + HS)),
            ((0, 2), (right, 2 * N), (left, 2 * N)),
            ((1, 0), (up, 0), (up, HS)),
            ((-1, 0), (down, 0), (down, HS)),
            ((0, 1), (right_c, 0), (right_c, HS)),
            ((0, -1), (left_c, 0), (left_c, HS)),
            ((0, 0), (here, 0), (here, HS)),
        ])

    rows = [N, 2 * N + HS, 2 * N + HS, N, N, N, N, N]
    return call(body, [grads, own_w, other_w], [(r, HS) for r in rows], 88 * HS**3)


def add_rows(sources, rows, recipe):
    def body(*refs):
        ins, outs = refs[: len(sources)], refs[len(sources) :]
        for out, row, parts in recipe:
            value = ins[parts[0][0]][parts[0][1] : parts[0][1] + HS, :]
            if len(parts) > 1:
                value = value.astype(F32)
                for source, first in parts[1:]:
                    value += ins[source][first : first + HS, :].astype(F32)
            outs[out][row : row + HS, :] = value.astype(BF16)

    return call(body, list(sources), [(r, HS) for r in rows])


def finish(here, arrived, swapped):
    def body(here_ref, *rest):
        sec = lax.axis_index("section")
        value = here_ref[:HS, :].astype(F32)
        for ref in rest[:4]:
            value += ref[:HS, :].astype(F32)
        rest[-1][slot_rows(sec), :] = value.astype(BF16)
        rest[-1][slot_rows(1 - sec), :] = rest[4][...]

    return call(body, [here, *arrived, swapped], [(N, HS)])[0]


def local(states, proj_weights, out_cotangent, enc_lengths, dec_lengths):
    own = states[0]
    partner = lax.ppermute(own, "section", SWAP)
    c0 = assemble(own, out_cotangent, partner)

    up1, down1 = shift_y(c0, 1), shift_y(c0, -1)
    right0, left0, across0 = shift_x(c0, 1), shift_x(c0, -1), shift_x(c0, 2)
    own_w, right0 = lax.optimization_barrier((proj_weights[0], right0))
    other_w = lax.ppermute(own_w, "section", SWAP)
    c0, up1, down1, right0, left0, across0 = lax.optimization_barrier((c0, up1, down1, right0, left0, across0))

    pair = jnp.concatenate([up1, down1], axis=0)
    right1, left1 = shift_x(pair, 1), shift_x(pair, -1)
    up2, down2 = shift_y(up1[:HALF], 1), shift_y(down1[HALF:], -1)
    total = project(
        [c0, pair, right0, left0, across0],
        [
            ((0, 0), [(0, 0, ROWS)]), ((-1, 0), [(1, 0, ROWS)]), ((1, 0), [(1, ROWS, ROWS)]),
            ((0, -1), [(2, 0, ROWS)]), ((0, 1), [(3, 0, ROWS)]), ((0, 2), [(4, 0, ROWS)]),
        ],
        own_w, other_w, None,
    )
    right1, left1, up2, down2, total = lax.optimization_barrier((right1, left1, up2, down2, total))

    last = jnp.concatenate([up2, down2], axis=0)
    right2 = shift_x(jnp.concatenate([right1[:HALF], right1[ROWS : ROWS + HALF], last], axis=0), 1)
    left2 = shift_x(jnp.concatenate([left1[HALF:ROWS], left1[ROWS + HALF :], last], axis=0), -1)
    across2 = shift_x(last, 2)
    total = project(
        [right1, left1, last],
        [
            ((-1, -1), [(0, 0, ROWS)]), ((1, -1), [(0, ROWS, ROWS)]),
            ((-1, 1), [(1, 0, ROWS)]), ((1, 1), [(1, ROWS, ROWS)]), ((2, 0), [(2, 0, ROWS)]),
        ],
        own_w, other_w, total,
    )
    right2, left2, across2, total = lax.optimization_barrier((right2, left2, across2, total))
    total = project(
        [right2, left2, across2],
        [
            ((-1, 2), [(0, 0, HALF), (1, 0, HALF)]), ((1, 2), [(0, HALF, HALF), (1, HALF, HALF)]),
            ((2, -1), [(0, ROWS, ROWS)]), ((2, 1), [(1, ROWS, ROWS)]), ((2, 2), [(2, 0, ROWS)]),
        ],
        own_w, other_w, total,
    )

    right_a, left_a, across_a, grads = attend(enc_lengths, dec_lengths, total, own_w, other_w)
    right_a, left_a, across_a = shift_x(right_a, 1), shift_x(left_a, -1), shift_x(across_a, 2)
    far, right_b, left_b, up_c, down_c, right_c, left_c, here = spread(grads, own_w, other_w)
    far, right_b, left_b = add_rows(
        [far, right_b, left_b, right_a, left_a, across_a], [N, 2 * N + HS, 2 * N + HS],
        [
            (0, 0, [(0, 0), (3, 0), (4, 0), (5, 0)]), (0, HS, [(0, HS), (3, HS), (4, HS), (5, HS)]),
            (1, 0, [(1, 0), (3, N)]), (1, HS, [(1, HS)]),
            (1, N, [(1, N), (3, N + HS)]), (1, N + HS, [(1, N + HS)]), (1, 2 * N, [(1, 2 * N)]),
            (2, 0, [(2, 0)]), (2, HS, [(2, HS), (4, N)]),
            (2, N, [(2, N)]), (2, N + HS, [(2, N + HS), (4, N + HS)]), (2, 2 * N, [(2, 2 * N)]),
        ],
    )
    up_b, down_b = shift_y(far[:HS], 1), shift_y(far[HS:], -1)
    right_b, left_b = shift_x(right_b, 1), shift_x(left_b, -1)
    up_c, down_c, right_c, left_c = add_rows(
        [up_c, down_c, right_c, left_c, right_b, left_b, up_b, down_b], [N] * 4,
        [
            (0, 0, [(0, 0), (4, 0), (5, 0), (6, 0)]), (0, HS, [(0, HS), (4, HS), (5, HS)]),
            (1, 0, [(1, 0), (4, N), (5, N)]), (1, HS, [(1, HS), (4, N + HS), (5, N + HS), (7, 0)]),
            (2, 0, [(2, 0), (4, 2 * N)]), (2, HS, [(2, HS)]),
            (3, 0, [(3, 0)]), (3, HS, [(3, HS), (5, 2 * N)]),
        ],
    )
    up_c, down_c, right_c, left_c = shift_y(up_c, 1), shift_y(down_c, -1), shift_x(right_c, 1), shift_x(left_c, -1)
    arrived = [up_c, down_c, right_c, left_c]
    sent = add_rows([here, *arrived], [HS], [(0, 0, [(i, HS) for i in range(5)])])[0]
    swapped = lax.ppermute(sent, "section", SWAP)
    return finish(here, arrived, swapped)[None]


def solution(mesh):
    placed = (
        P("section", "dp", "mp"),
        P("section", None, None, "mp"),
        P("dp", "mp"),
        P("dp"),
        P("dp"),
    )
    return jax.shard_map(
        local, mesh=mesh, in_specs=placed, out_specs=P("section", "dp", "mp"), check_vma=False
    )
```

time: 201 us -> 185 us (0.920)
  Pallas kernels: 40.7 us -> 8.16 us
  waiting for transfers between devices: 42.8 us -> 62.4 us
  starting transfers between devices: 101 us -> 109 us
  local copies, waits for them, and re-layouts: 10.3 us -> 4.28 us
  other arithmetic: 3.88 us -> 0.1 us
    pallas_call x9 -> x10, Pallas kernels: 40.7 us -> 8.16 us  [call(): pl.pallas_call(body, out_shape=out, in_specs=[SMEM] * scalars + [VMEM] *...]
    ppermute x15, waiting for transfers between devices: 31 us -> 49.2 us  [shift_x(): return lax.ppermute(block, 'mp', route)]
    ppermute x15, starting transfers between devices: 48.7 us -> 53.1 us  [shift_x(): return lax.ppermute(block, 'mp', route)]
    unnamed x46 -> x12, local copies, waits for them, and re-layouts: 6.73 us -> 4.14 us
  transfers between devices with their start and end apart: 26 -> 26, of which waited for: 13 -> 16; matrix products, arithmetic and copies ran while one was open for 3% -> 0% of each run, Pallas kernels for 10% -> 2%
where the time goes in v4:
time: 185 us; the launch traced here: 184 us
  starting transfers between devices  109 us (59%)
  waiting for transfers between devices  62.4 us (34%)
  Pallas kernels  8.16 us (4%)
  local copies, waits for them, and re-layouts  4.28 us (2%)
    ppermute x15, starting transfers between devices, shift_x(): return lax.ppermute(block, 'mp', route)  53.1 us
    ppermute x15, waiting for transfers between devices, shift_x(): return lax.ppermute(block, 'mp', route)  49.2 us
    ppermute x8, starting transfers between devices, shift_y(): return lax.ppermute(block, 'mp', route)  28.5 us
    ppermute x1, starting transfers between devices, local(): partner = lax.ppermute(own, 'section', SWAP)  12.4 us
    ppermute x1, starting transfers between devices, local(): swapped = lax.ppermute(sent, 'section', SWAP)  11.5 us
    ppermute x8, waiting for transfers between devices, shift_y(): return lax.ppermute(block, 'mp', route)  10.8 us
    pallas_call x10, Pallas kernels, call(): pl.pallas_call(body, out_shape=out, in_specs=[SMEM] * scalars + [VMEM] *...  8.16 us
    unnamed x12, local copies, waits for them, and re-layouts  4.14 us
  transfers between devices with their start and end apart: 26, of which 16 were waited for; matrix products, arithmetic and copies ran while one was open for 0% of the time, Pallas kernels for 2%

profile of v4, /device:TPU:1, one launch (start us, length us, event | category | flops | bytes accessed | tf_op | source)
XLA Modules:
  0.0 183.9 jit_solution(1425654922822053443)
XLA Ops:
  0.0 12.4 %collective-permute-start = (bf16[512,256]{1,0:T(8,128)(2,1)}, bf16[512,256]{1,0:T(8,128)(2,1)S(1)}, u32[]{:S(2)}, u32[]{:S(2)}) collective-permute-start(bf16[512,256]{1,0:T(8,128)(2,1)} %bitcast.9), channel_id=1, source_target_pairs={{0,384},{384,0},{1,385},{385,1},{2,386},{386,2},{3,387},{387,3},{4... | collective-permute-start | bytes 786440 | tf_op jit(solution)/shard_map/ppermute | solution.py:195
  17.6 11.5 %collective-permute-done.1.rest_2_ = bf16[768,256]{1,0:T(8,128)(2,1)S(1)} collective-permute-done((bf16[768,256]{1,0:T(8,128)(2,1)S(1)}, bf16[768,256]{1,0:T(8,128)(2,1)S(1)}, u32[]{:S(2)}, u32[]{:S(2)}) %collective-permute-start.1) | collective-permute-done | bytes 393248 | tf_op jit(solution)/shard_map/ppermute | solution.py:25
  29.1 3.1 %collective-permute-start.2 = (bf16[2,4096,256]{2,1,0:T(8,128)(2,1)}, bf16[2,4096,256]{2,1,0:T(8,128)(2,1)S(1)}, u32[]{:S(2)}, u32[]{:S(2)}) collective-permute-start(bf16[2,4096,256]{2,1,0:T(8,128)(2,1)} %bitcast.3), channel_id=1, source_target_pairs={{0,384},{384,0},{1,385},{385,1},{2,386},{386,2},{3,387},{387,3},{4... | collective-permute-start | bytes 12582920 | tf_op jit(solution)/shard_map/ppermute | solution.py:201
  34.2 5.5 %collective-permute-start.4 = (bf16[768,256]{1,0:T(8,128)(2,1)S(1)}, bf16[768,256]{1,0:T(8,128)(2,1)S(1)}, u32[]{:S(2)}, u32[]{:S(2)}) collective-permute-start(bf16[768,256]{1,0:T(8,128)(2,1)S(1)} %shard_map.55.rest_0_), channel_id=1, source_target_pairs={{0,12},{1,13},{2,14},{3,15},{4,0},{5,1},{6,2},{7,3},{8,4},{9,5},{1... | collective-permute-start | bytes 1179656 | tf_op jit(solution)/shard_map/ppermute | solution.py:30
  41.6 2.5 %collective-permute-start.6 = (bf16[768,256]{1,0:T(8,128)(2,1)S(1)}, bf16[768,256]{1,0:T(8,128)(2,1)S(1)}, u32[]{:S(2)}, u32[]{:S(2)}) collective-permute-start(bf16[768,256]{1,0:T(8,128)(2,1)S(1)} %shard_map.55.rest_0_), channel_id=1, source_target_pairs={{0,2},{1,3},{2,0},{3,1},{4,6},{5,7},{6,4},{7,5},{8,10},{9,11},{10,... | collective-permute-start | bytes 1179656 | tf_op jit(solution)/shard_map/ppermute | solution.py:25
  44.1 6.4 %collective-permute-done.3 = bf16[768,256]{1,0:T(8,128)(2,1)S(1)} collective-permute-done((bf16[768,256]{1,0:T(8,128)(2,1)S(1)}, bf16[768,256]{1,0:T(8,128)(2,1)S(1)}, u32[]{:S(2)}, u32[]{:S(2)}) %collective-permute-start.3) | collective-permute-done | bytes 393248 | tf_op jit(solution)/shard_map/ppermute | solution.py:30
  51.6 3.4 %collective-permute-done.6.rest_4_ = bf16[768,256]{1,0:T(8,128)(2,1)S(1)} collective-permute-done((bf16[768,256]{1,0:T(8,128)(2,1)S(1)}, bf16[768,256]{1,0:T(8,128)(2,1)S(1)}, u32[]{:S(2)}, u32[]{:S(2)}) %collective-permute-start.6) | collective-permute-done | bytes 393248 | tf_op jit(solution)/shard_map/ppermute | solution.py:25
  55.1 6.2 %collective-permute-start.7 = (bf16[1536,256]{1,0:T(8,128)(2,1)S(1)}, bf16[1536,256]{1,0:T(8,128)(2,1)S(1)}, u32[]{:S(2)}, u32[]{:S(2)}) collective-permute-start(bf16[1536,256]{1,0:T(8,128)(2,1)S(1)} %constant_dynamic-update-slice_fusion.rest_1_), channel_id=1, source_target_pairs={{0,1},{1,2},{2,3},{3,0},{4,5},{5,6},{6,7},{7,4},{8,9},{9,10},{10,1... | collective-permute-start | bytes 2359304 | tf_op jit(solution)/shard_map/ppermute | solution.py:25
  61.3 5.0 %collective-permute-start.8 = (bf16[1536,256]{1,0:T(8,128)(2,1)S(1)}, bf16[1536,256]{1,0:T(8,128)(2,1)S(1)}, u32[]{:S(2)}, u32[]{:S(2)}) collective-permute-start(bf16[1536,256]{1,0:T(8,128)(2,1)S(1)} %constant_dynamic-update-slice_fusion.rest_1_), channel_id=1, source_target_pairs={{0,3},{1,0},{2,1},{3,2},{4,7},{5,4},{6,5},{7,6},{8,11},{9,8},{10,9... | collective-permute-start | bytes 2359304 | tf_op jit(solution)/shard_map/ppermute | solution.py:25
  66.4 2.2 %collective-permute-start.10 = (bf16[384,256]{1,0:T(8,128)(2,1)S(1)}, bf16[384,256]{1,0:T(8,128)(2,1)S(1)}, u32[]{:S(2)}, u32[]{:S(2)}) collective-permute-start(bf16[384,256]{1,0:T(8,128)(2,1)S(1)} %slice.25), channel_id=1, source_target_pairs={{0,12},{1,13},{2,14},{3,15},{4,0},{5,1},{6,2},{7,3},{8,4},{9,5},{1... | collective-permute-start | bytes 589832 | tf_op jit(solution)/shard_map/ppermute | solution.py:30
  68.7 3.9 %collective-permute-start.9 = (bf16[384,256]{1,0:T(8,128)(2,1)S(1)}, bf16[384,256]{1,0:T(8,128)(2,1)S(1)}, u32[]{:S(2)}, u32[]{:S(2)}) collective-permute-start(bf16[384,256]{1,0:T(8,128)(2,1)S(1)} %slice.24), channel_id=1, source_target_pairs={{0,4},{1,5},{2,6},{3,7},{4,8},{5,9},{6,10},{7,11},{8,12},{9,13},{1... | collective-permute-start | bytes 589832 | tf_op jit(solution)/shard_map/ppermute | solution.py:30
  72.6 2.2 %copy-done = bf16[1,2,4096,256]{3,2,1,0:T(8,128)(2,1)S(1)} copy-done((bf16[1,2,4096,256]{3,2,1,0:T(8,128)(2,1)S(1)}, bf16[1,2,4096,256]{3,2,1,0:T(8,128)(2,1)}, u32[]{:S(2)}) %copy-start) | copy-done | bytes 4194328
  77.2 3.7 %collective-permute-done.7.rest_0_ = bf16[1536,256]{1,0:T(8,128)(2,1)S(1)} collective-permute-done((bf16[1536,256]{1,0:T(8,128)(2,1)S(1)}, bf16[1536,256]{1,0:T(8,128)(2,1)S(1)}, u32[]{:S(2)}, u32[]{:S(2)}) %collective-permute-start.7) | collective-permute-done | bytes 786464 | tf_op jit(solution)/shard_map/ppermute | solution.py:25
  81.9 3.5 %collective-permute-start.11 = (bf16[1536,256]{1,0:T(8,128)(2,1)S(1)}, bf16[1536,256]{1,0:T(8,128)(2,1)S(1)}, u32[]{:S(2)}, u32[]{:S(2)}) collective-permute-start(bf16[1536,256]{1,0:T(8,128)(2,1)S(1)} %get-tuple-element.82), channel_id=1, source_target_pairs={{0,1},{1,2},{2,3},{3,0},{4,5},{5,6},{6,7},{7,4},{8,9},{9,10},{10,1... | collective-permute-start | bytes 2359304 | tf_op jit(solution)/shard_map/ppermute | solution.py:25
  85.4 3.7 %collective-permute-start.12 = (bf16[1536,256]{1,0:T(8,128)(2,1)S(1)}, bf16[1536,256]{1,0:T(8,128)(2,1)S(1)}, u32[]{:S(2)}, u32[]{:S(2)}) collective-permute-start(bf16[1536,256]{1,0:T(8,128)(2,1)S(1)} %get-tuple-element.81), channel_id=1, source_target_pairs={{0,3},{1,0},{2,1},{3,2},{4,7},{5,4},{6,5},{7,6},{8,11},{9,8},{10,9... | collective-permute-start | bytes 2359304 | tf_op jit(solution)/shard_map/ppermute | solution.py:25
  89.2 3.1 %collective-permute-start.13 = (bf16[768,256]{1,0:T(8,128)(2,1)S(1)}, bf16[768,256]{1,0:T(8,128)(2,1)S(1)}, u32[]{:S(2)}, u32[]{:S(2)}) collective-permute-start(bf16[768,256]{1,0:T(8,128)(2,1)S(1)} %constant_dynamic-update-slice_fusion.2.rest_2_), channel_id=1, source_target_pairs={{0,2},{1,3},{2,0},{3,1},{4,6},{5,7},{6,4},{7,5},{8,10},{9,11},{10,... | collective-permute-start | bytes 1179656 | tf_op jit(solution)/shard_map/ppermute | solution.py:25
  93.2 18.8 %collective-permute-done.13.rest_2_ = bf16[768,256]{1,0:T(8,128)(2,1)S(1)} collective-permute-done((bf16[768,256]{1,0:T(8,128)(2,1)S(1)}, bf16[768,256]{1,0:T(8,128)(2,1)S(1)}, u32[]{:S(2)}, u32[]{:S(2)}) %collective-permute-start.13) | collective-permute-done | bytes 393248 | tf_op jit(solution)/shard_map/ppermute | solution.py:25
  112.9 2.3 %shard_map.59 = (bf16[1024,256]{1,0:T(8,128)(2,1)S(1)}, bf16[1024,256]{1,0:T(8,128)(2,1)S(1)}, bf16[512,256]{1,0:T(8,128)(2,1)S(1)}, bf16[4,256,256]{2,1,0:T(8,128)(2,1)S(1)}) custom-call(s32[2]{0:T(128)S(1)} %copy-done.3, s32[2]{0:T(128)S(1)} %copy-done.4, f32[4,256,256]{2,1,0:T(8,128)S(1)} %shard_map.58.t_ref, bf16[2,4096,256]{2,1,0:T(8,128)(2,1)S(1)} %bitcast.7, ...), custom_call_target="tpu_custom_call" | custom-call | flops 1006632960 | bytes 9437200 | tf_op jit(solution)/shard_map/pallas_call | solution.py:36
  115.3 4.4 %collective-permute-start.14 = (bf16[1024,256]{1,0:T(8,128)(2,1)S(1)}, bf16[1024,256]{1,0:T(8,128)(2,1)S(1)}, u32[]{:S(2)}, u32[]{:S(2)}) collective-permute-start(bf16[1024,256]{1,0:T(8,128)(2,1)S(1)} %get-tuple-element.67), channel_id=1, source_target_pairs={{0,1},{1,2},{2,3},{3,0},{4,5},{5,6},{6,7},{7,4},{8,9},{9,10},{10,1... | collective-permute-start | bytes 1572872 | tf_op jit(solution)/shard_map/ppermute | solution.py:25
  119.7 2.1 %collective-permute-start.15 = (bf16[1024,256]{1,0:T(8,128)(2,1)S(1)}, bf16[1024,256]{1,0:T(8,128)(2,1)S(1)}, u32[]{:S(2)}, u32[]{:S(2)}) collective-permute-start(bf16[1024,256]{1,0:T(8,128)(2,1)S(1)} %get-tuple-element.68), channel_id=1, source_target_pairs={{0,3},{1,0},{2,1},{3,2},{4,7},{5,4},{6,5},{7,6},{8,11},{9,8},{10,9... | collective-permute-start | bytes 1572872 | tf_op jit(solution)/shard_map/ppermute | solution.py:25
  121.8 3.5 %collective-permute-start.16 = (bf16[512,256]{1,0:T(8,128)(2,1)S(1)}, bf16[512,256]{1,0:T(8,128)(2,1)S(1)}, u32[]{:S(2)}, u32[]{:S(2)}) collective-permute-start(bf16[512,256]{1,0:T(8,128)(2,1)S(1)} %get-tuple-element.69), channel_id=1, source_target_pairs={{0,2},{1,3},{2,0},{3,1},{4,6},{5,7},{6,4},{7,5},{8,10},{9,11},{10,... | collective-permute-start | bytes 786440 | tf_op jit(solution)/shard_map/ppermute | solution.py:25
  127.0 7.0 %collective-permute-done.16.refs_5_ = bf16[512,256]{1,0:T(8,128)(2,1)S(1)} collective-permute-done((bf16[512,256]{1,0:T(8,128)(2,1)S(1)}, bf16[512,256]{1,0:T(8,128)(2,1)S(1)}, u32[]{:S(2)}, u32[]{:S(2)}) %collective-permute-start.16) | collective-permute-done | bytes 262176 | tf_op jit(solution)/shard_map/ppermute | solution.py:25
  134.3 4.4 %collective-permute-start.17 = (bf16[1280,256]{1,0:T(8,128)(2,1)S(1)}, bf16[1280,256]{1,0:T(8,128)(2,1)S(1)}, u32[]{:S(2)}, u32[]{:S(2)}) collective-permute-start(bf16[1280,256]{1,0:T(8,128)(2,1)S(1)} %get-tuple-element.70), channel_id=1, source_target_pairs={{0,1},{1,2},{2,3},{3,0},{4,5},{5,6},{6,7},{7,4},{8,9},{9,10},{10,1... | collective-permute-start | bytes 1966088 | tf_op jit(solution)/shard_map/ppermute | solution.py:25
  138.7 4.3 %collective-permute-start.18 = (bf16[1280,256]{1,0:T(8,128)(2,1)S(1)}, bf16[1280,256]{1,0:T(8,128)(2,1)S(1)}, u32[]{:S(2)}, u32[]{:S(2)}) collective-permute-start(bf16[1280,256]{1,0:T(8,128)(2,1)S(1)} %get-tuple-element.71), channel_id=1, source_target_pairs={{0,3},{1,0},{2,1},{3,2},{4,7},{5,4},{6,5},{7,6},{8,11},{9,8},{10,9... | collective-permute-start | bytes 1966088 | tf_op jit(solution)/shard_map/ppermute | solution.py:25
  143.0 2.0 %collective-permute-start.19 = (bf16[256,256]{1,0:T(8,128)(2,1)S(1)}, bf16[256,256]{1,0:T(8,128)(2,1)S(1)}, u32[]{:S(2)}, u32[]{:S(2)}) collective-permute-start(bf16[256,256]{1,0:T(8,128)(2,1)S(1)} %get-tuple-element.84), channel_id=1, source_target_pairs={{0,4},{1,5},{2,6},{3,7},{4,8},{5,9},{6,10},{7,11},{8,12},{9,13},{1... | collective-permute-start | bytes 393224 | tf_op jit(solution)/shard_map/ppermute | solution.py:30
  145.0 5.4 %collective-permute-start.20 = (bf16[256,256]{1,0:T(8,128)(2,1)S(1)}, bf16[256,256]{1,0:T(8,128)(2,1)S(1)}, u32[]{:S(2)}, u32[]{:S(2)}) collective-permute-start(bf16[256,256]{1,0:T(8,128)(2,1)S(1)} %get-tuple-element.83), channel_id=1, source_target_pairs={{0,12},{1,13},{2,14},{3,15},{4,0},{5,1},{6,2},{7,3},{8,4},{9,5},{1... | collective-permute-start | bytes 393224 | tf_op jit(solution)/shard_map/ppermute | solution.py:30
  153.0 2.2 %collective-permute-start.21 = (bf16[512,256]{1,0:T(8,128)(2,1)S(1)}, bf16[512,256]{1,0:T(8,128)(2,1)S(1)}, u32[]{:S(2)}, u32[]{:S(2)}) collective-permute-start(bf16[512,256]{1,0:T(8,128)(2,1)S(1)} %get-tuple-element.73), channel_id=1, source_target_pairs={{0,4},{1,5},{2,6},{3,7},{4,8},{5,9},{6,10},{7,11},{8,12},{9,13},{1... | collective-permute-start | bytes 786440 | tf_op jit(solution)/shard_map/ppermute | solution.py:30
  155.1 5.3 %collective-permute-start.22 = (bf16[512,256]{1,0:T(8,128)(2,1)S(1)}, bf16[512,256]{1,0:T(8,128)(2,1)S(1)}, u32[]{:S(2)}, u32[]{:S(2)}) collective-permute-start(bf16[512,256]{1,0:T(8,128)(2,1)S(1)} %get-tuple-element.74), channel_id=1, source_target_pairs={{0,12},{1,13},{2,14},{3,15},{4,0},{5,1},{6,2},{7,3},{8,4},{9,5},{1... | collective-permute-start | bytes 786440 | tf_op jit(solution)/shard_map/ppermute | solution.py:30
  160.5 2.6 %collective-permute-start.23 = (bf16[512,256]{1,0:T(8,128)(2,1)S(1)}, bf16[512,256]{1,0:T(8,128)(2,1)S(1)}, u32[]{:S(2)}, u32[]{:S(2)}) collective-permute-start(bf16[512,256]{1,0:T(8,128)(2,1)S(1)} %get-tuple-element.75), channel_id=1, source_target_pairs={{0,1},{1,2},{2,3},{3,0},{4,5},{5,6},{6,7},{7,4},{8,9},{9,10},{10,1... | collective-permute-start | bytes 786440 | tf_op jit(solution)/shard_map/ppermute | solution.py:25
  163.1 3.9 %collective-permute-start.24 = (bf16[512,256]{1,0:T(8,128)(2,1)S(1)}, bf16[512,256]{1,0:T(8,128)(2,1)S(1)}, u32[]{:S(2)}, u32[]{:S(2)}) collective-permute-start(bf16[512,256]{1,0:T(8,128)(2,1)S(1)} %get-tuple-element.76), channel_id=1, source_target_pairs={{0,3},{1,0},{2,1},{3,2},{4,7},{5,4},{6,5},{7,6},{8,11},{9,8},{10,9... | collective-permute-start | bytes 786440 | tf_op jit(solution)/shard_map/ppermute | solution.py:25
  167.0 2.1 %collective-permute-done.23.refs_3_.rest_2_ = bf16[512,256]{1,0:T(8,128)(2,1)S(1)} collective-permute-done((bf16[512,256]{1,0:T(8,128)(2,1)S(1)}, bf16[512,256]{1,0:T(8,128)(2,1)S(1)}, u32[]{:S(2)}, u32[]{:S(2)}) %collective-permute-start.23) | collective-permute-done | bytes 262176 | tf_op jit(solution)/shard_map/ppermute | solution.py:25
  170.6 11.5 %collective-permute-start.25 = (bf16[256,256]{1,0:T(8,128)(2,1)S(1)}, bf16[256,256]{1,0:T(8,128)(2,1)S(1)}, u32[]{:S(2)}, u32[]{:S(2)}) collective-permute-start(bf16[256,256]{1,0:T(8,128)(2,1)S(1)} %shard_map.63), channel_id=1, source_target_pairs={{0,384},{384,0},{1,385},{385,1},{2,386},{386,2},{3,387},{387,3},{4... | collective-permute-start | bytes 393224 | tf_op jit(solution)/shard_map/ppermute | solution.py:266
  (49 shorter events, 23.2 us)
Async XLA Ops:
  0.0 13.8 %collective-permute-start = (bf16[512,256]{1,0:T(8,128)(2,1)}, bf16[512,256]{1,0:T(8,128)(2,1)S(1)}, u32[]{:S(2)}, u32[]{:S(2)}) collective-permute-start(bf16[512,256]{1,0:T(8,128)(2,1)} %bitcast.9), channel_id=1, source_target_pairs={{0,384},{384,0},{1,385},{385,1},{2,386},{386,2},{3,387},{387,3},{4... | collective-permute-start | bytes 786440 | tf_op jit(solution)/shard_map/ppermute | solution.py:195
  13.8 0.9 copy-start.1
  14.7 0.9 copy-start.2
  15.7 13.4 %collective-permute-start.1 = (bf16[768,256]{1,0:T(8,128)(2,1)S(1)}, bf16[768,256]{1,0:T(8,128)(2,1)S(1)}, u32[]{:S(2)}, u32[]{:S(2)}) collective-permute-start(bf16[768,256]{1,0:T(8,128)(2,1)S(1)} %shard_map.55.rest_0_), channel_id=1, source_target_pairs={{0,1},{1,2},{2,3},{3,0},{4,5},{5,6},{6,7},{7,4},{8,9},{9,10},{10,1... | collective-permute-start | bytes 1179656 | tf_op jit(solution)/shard_map/ppermute | solution.py:25
  29.1 43.5 %collective-permute-start.2 = (bf16[2,4096,256]{2,1,0:T(8,128)(2,1)}, bf16[2,4096,256]{2,1,0:T(8,128)(2,1)S(1)}, u32[]{:S(2)}, u32[]{:S(2)}) collective-permute-start(bf16[2,4096,256]{2,1,0:T(8,128)(2,1)} %bitcast.3), channel_id=1, source_target_pairs={{0,384},{384,0},{1,385},{385,1},{2,386},{386,2},{3,387},{387,3},{4... | collective-permute-start | bytes 12582920 | tf_op jit(solution)/shard_map/ppermute | solution.py:201
  32.2 18.3 %collective-permute-start.3 = (bf16[768,256]{1,0:T(8,128)(2,1)S(1)}, bf16[768,256]{1,0:T(8,128)(2,1)S(1)}, u32[]{:S(2)}, u32[]{:S(2)}) collective-permute-start(bf16[768,256]{1,0:T(8,128)(2,1)S(1)} %shard_map.55.rest_0_), channel_id=1, source_target_pairs={{0,4},{1,5},{2,6},{3,7},{4,8},{5,9},{6,10},{7,11},{8,12},{9,13},{1... | collective-permute-start | bytes 1179656 | tf_op jit(solution)/shard_map/ppermute | solution.py:30
  34.2 17.1 %collective-permute-start.4 = (bf16[768,256]{1,0:T(8,128)(2,1)S(1)}, bf16[768,256]{1,0:T(8,128)(2,1)S(1)}, u32[]{:S(2)}, u32[]{:S(2)}) collective-permute-start(bf16[768,256]{1,0:T(8,128)(2,1)S(1)} %shard_map.55.rest_0_), channel_id=1, source_target_pairs={{0,12},{1,13},{2,14},{3,15},{4,0},{5,1},{6,2},{7,3},{8,4},{9,5},{1... | collective-permute-start | bytes 1179656 | tf_op jit(solution)/shard_map/ppermute | solution.py:30
  39.7 12.0 %collective-permute-start.5 = (bf16[768,256]{1,0:T(8,128)(2,1)S(1)}, bf16[768,256]{1,0:T(8,128)(2,1)S(1)}, u32[]{:S(2)}, u32[]{:S(2)}) collective-permute-start(bf16[768,256]{1,0:T(8,128)(2,1)S(1)} %shard_map.55.rest_0_), channel_id=1, source_target_pairs={{0,3},{1,0},{2,1},{3,2},{4,7},{5,4},{6,5},{7,6},{8,11},{9,8},{10,9... | collective-permute-start | bytes 1179656 | tf_op jit(solution)/shard_map/ppermute | solution.py:25
  41.6 13.5 %collective-permute-start.6 = (bf16[768,256]{1,0:T(8,128)(2,1)S(1)}, bf16[768,256]{1,0:T(8,128)(2,1)S(1)}, u32[]{:S(2)}, u32[]{:S(2)}) collective-permute-start(bf16[768,256]{1,0:T(8,128)(2,1)S(1)} %shard_map.55.rest_0_), channel_id=1, source_target_pairs={{0,2},{1,3},{2,0},{3,1},{4,6},{5,7},{6,4},{7,5},{8,10},{9,11},{10,... | collective-permute-start | bytes 1179656 | tf_op jit(solution)/shard_map/ppermute | solution.py:25
  55.1 25.7 %collective-permute-start.7 = (bf16[1536,256]{1,0:T(8,128)(2,1)S(1)}, bf16[1536,256]{1,0:T(8,128)(2,1)S(1)}, u32[]{:S(2)}, u32[]{:S(2)}) collective-permute-start(bf16[1536,256]{1,0:T(8,128)(2,1)S(1)} %constant_dynamic-update-slice_fusion.rest_1_), channel_id=1, source_target_pairs={{0,1},{1,2},{2,3},{3,0},{4,5},{5,6},{6,7},{7,4},{8,9},{9,10},{10,1... | collective-permute-start | bytes 2359304 | tf_op jit(solution)/shard_map/ppermute | solution.py:25
  61.3 20.4 %collective-permute-start.8 = (bf16[1536,256]{1,0:T(8,128)(2,1)S(1)}, bf16[1536,256]{1,0:T(8,128)(2,1)S(1)}, u32[]{:S(2)}, u32[]{:S(2)}) collective-permute-start(bf16[1536,256]{1,0:T(8,128)(2,1)S(1)} %constant_dynamic-update-slice_fusion.rest_1_), channel_id=1, source_target_pairs={{0,3},{1,0},{2,1},{3,2},{4,7},{5,4},{6,5},{7,6},{8,11},{9,8},{10,9... | collective-permute-start | bytes 2359304 | tf_op jit(solution)/shard_map/ppermute | solution.py:25
  66.4 9.4 %collective-permute-start.10 = (bf16[384,256]{1,0:T(8,128)(2,1)S(1)}, bf16[384,256]{1,0:T(8,128)(2,1)S(1)}, u32[]{:S(2)}, u32[]{:S(2)}) collective-permute-start(bf16[384,256]{1,0:T(8,128)(2,1)S(1)} %slice.25), channel_id=1, source_target_pairs={{0,12},{1,13},{2,14},{3,15},{4,0},{5,1},{6,2},{7,3},{8,4},{9,5},{1... | collective-permute-start | bytes 589832 | tf_op jit(solution)/shard_map/ppermute | solution.py:30
  68.7 8.5 %collective-permute-start.9 = (bf16[384,256]{1,0:T(8,128)(2,1)S(1)}, bf16[384,256]{1,0:T(8,128)(2,1)S(1)}, u32[]{:S(2)}, u32[]{:S(2)}) collective-permute-start(bf16[384,256]{1,0:T(8,128)(2,1)S(1)} %slice.24), channel_id=1, source_target_pairs={{0,4},{1,5},{2,6},{3,7},{4,8},{5,9},{6,10},{7,11},{8,12},{9,13},{1... | collective-permute-start | bytes 589832 | tf_op jit(solution)/shard_map/ppermute | solution.py:30
  72.6 2.2 %copy-start = (bf16[1,2,4096,256]{3,2,1,0:T(8,128)(2,1)S(1)}, bf16[1,2,4096,256]{3,2,1,0:T(8,128)(2,1)}, u32[]{:S(2)}) copy-start(bf16[1,2,4096,256]{3,2,1,0:T(8,128)(2,1)} %param.6) | copy-start | bytes 12582916
  81.9 30.1 %collective-permute-start.11 = (bf16[1536,256]{1,0:T(8,128)(2,1)S(1)}, bf16[1536,256]{1,0:T(8,128)(2,1)S(1)}, u32[]{:S(2)}, u32[]{:S(2)}) collective-permute-start(bf16[1536,256]{1,0:T(8,128)(2,1)S(1)} %get-tuple-element.82), channel_id=1, source_target_pairs={{0,1},{1,2},{2,3},{3,0},{4,5},{5,6},{6,7},{7,4},{8,9},{9,10},{10,1... | collective-permute-start | bytes 2359304 | tf_op jit(solution)/shard_map/ppermute | solution.py:25
  85.4 26.6 %collective-permute-start.12 = (bf16[1536,256]{1,0:T(8,128)(2,1)S(1)}, bf16[1536,256]{1,0:T(8,128)(2,1)S(1)}, u32[]{:S(2)}, u32[]{:S(2)}) collective-permute-start(bf16[1536,256]{1,0:T(8,128)(2,1)S(1)} %get-tuple-element.81), channel_id=1, source_target_pairs={{0,3},{1,0},{2,1},{3,2},{4,7},{5,4},{6,5},{7,6},{8,11},{9,8},{10,9... | collective-permute-start | bytes 2359304 | tf_op jit(solution)/shard_map/ppermute | solution.py:25
  89.2 22.8 %collective-permute-start.13 = (bf16[768,256]{1,0:T(8,128)(2,1)S(1)}, bf16[768,256]{1,0:T(8,128)(2,1)S(1)}, u32[]{:S(2)}, u32[]{:S(2)}) collective-permute-start(bf16[768,256]{1,0:T(8,128)(2,1)S(1)} %constant_dynamic-update-slice_fusion.2.rest_2_), channel_id=1, source_target_pairs={{0,2},{1,3},{2,0},{3,1},{4,6},{5,7},{6,4},{7,5},{8,10},{9,11},{10,... | collective-permute-start | bytes 1179656 | tf_op jit(solution)/shard_map/ppermute | solution.py:25
  93.2 19.7 %copy-start.3 = (s32[2]{0:T(128)S(1)}, s32[2]{0:T(128)}, u32[]{:S(2)}) copy-start(s32[2]{0:T(128)} %enc_ref.1) | copy-start | bytes 28
  93.2 19.7 %copy-start.4 = (s32[2]{0:T(128)S(1)}, s32[2]{0:T(128)}, u32[]{:S(2)}) copy-start(s32[2]{0:T(128)} %dec_ref.1) | copy-start | bytes 28
  115.3 18.7 %collective-permute-start.14 = (bf16[1024,256]{1,0:T(8,128)(2,1)S(1)}, bf16[1024,256]{1,0:T(8,128)(2,1)S(1)}, u32[]{:S(2)}, u32[]{:S(2)}) collective-permute-start(bf16[1024,256]{1,0:T(8,128)(2,1)S(1)} %get-tuple-element.67), channel_id=1, source_target_pairs={{0,1},{1,2},{2,3},{3,0},{4,5},{5,6},{6,7},{7,4},{8,9},{9,10},{10,1... | collective-permute-start | bytes 1572872 | tf_op jit(solution)/shard_map/ppermute | solution.py:25
  119.7 14.3 %collective-permute-start.15 = (bf16[1024,256]{1,0:T(8,128)(2,1)S(1)}, bf16[1024,256]{1,0:T(8,128)(2,1)S(1)}, u32[]{:S(2)}, u32[]{:S(2)}) collective-permute-start(bf16[1024,256]{1,0:T(8,128)(2,1)S(1)} %get-tuple-element.68), channel_id=1, source_target_pairs={{0,3},{1,0},{2,1},{3,2},{4,7},{5,4},{6,5},{7,6},{8,11},{9,8},{10,9... | collective-permute-start | bytes 1572872 | tf_op jit(solution)/shard_map/ppermute | solution.py:25
  121.8 12.2 %collective-permute-start.16 = (bf16[512,256]{1,0:T(8,128)(2,1)S(1)}, bf16[512,256]{1,0:T(8,128)(2,1)S(1)}, u32[]{:S(2)}, u32[]{:S(2)}) collective-permute-start(bf16[512,256]{1,0:T(8,128)(2,1)S(1)} %get-tuple-element.69), channel_id=1, source_target_pairs={{0,2},{1,3},{2,0},{3,1},{4,6},{5,7},{6,4},{7,5},{8,10},{9,11},{10,... | collective-permute-start | bytes 786440 | tf_op jit(solution)/shard_map/ppermute | solution.py:25
  134.3 18.4 %collective-permute-start.17 = (bf16[1280,256]{1,0:T(8,128)(2,1)S(1)}, bf16[1280,256]{1,0:T(8,128)(2,1)S(1)}, u32[]{:S(2)}, u32[]{:S(2)}) collective-permute-start(bf16[1280,256]{1,0:T(8,128)(2,1)S(1)} %get-tuple-element.70), channel_id=1, source_target_pairs={{0,1},{1,2},{2,3},{3,0},{4,5},{5,6},{6,7},{7,4},{8,9},{9,10},{10,1... | collective-permute-start | bytes 1966088 | tf_op jit(solution)/shard_map/ppermute | solution.py:25
  138.7 14.0 %collective-permute-start.18 = (bf16[1280,256]{1,0:T(8,128)(2,1)S(1)}, bf16[1280,256]{1,0:T(8,128)(2,1)S(1)}, u32[]{:S(2)}, u32[]{:S(2)}) collective-permute-start(bf16[1280,256]{1,0:T(8,128)(2,1)S(1)} %get-tuple-element.71), channel_id=1, source_target_pairs={{0,3},{1,0},{2,1},{3,2},{4,7},{5,4},{6,5},{7,6},{8,11},{9,8},{10,9... | collective-permute-start | bytes 1966088 | tf_op jit(solution)/shard_map/ppermute | solution.py:25
  143.0 7.8 %collective-permute-start.19 = (bf16[256,256]{1,0:T(8,128)(2,1)S(1)}, bf16[256,256]{1,0:T(8,128)(2,1)S(1)}, u32[]{:S(2)}, u32[]{:S(2)}) collective-permute-start(bf16[256,256]{1,0:T(8,128)(2,1)S(1)} %get-tuple-element.84), channel_id=1, source_target_pairs={{0,4},{1,5},{2,6},{3,7},{4,8},{5,9},{6,10},{7,11},{8,12},{9,13},{1... | collective-permute-start | bytes 393224 | tf_op jit(solution)/shard_map/ppermute | solution.py:30
  145.0 7.7 %collective-permute-start.20 = (bf16[256,256]{1,0:T(8,128)(2,1)S(1)}, bf16[256,256]{1,0:T(8,128)(2,1)S(1)}, u32[]{:S(2)}, u32[]{:S(2)}) collective-permute-start(bf16[256,256]{1,0:T(8,128)(2,1)S(1)} %get-tuple-element.83), channel_id=1, source_target_pairs={{0,12},{1,13},{2,14},{3,15},{4,0},{5,1},{6,2},{7,3},{8,4},{9,5},{1... | collective-permute-start | bytes 393224 | tf_op jit(solution)/shard_map/ppermute | solution.py:30
  153.0 14.0 %collective-permute-start.21 = (bf16[512,256]{1,0:T(8,128)(2,1)S(1)}, bf16[512,256]{1,0:T(8,128)(2,1)S(1)}, u32[]{:S(2)}, u32[]{:S(2)}) collective-permute-start(bf16[512,256]{1,0:T(8,128)(2,1)S(1)} %get-tuple-element.73), channel_id=1, source_target_pairs={{0,4},{1,5},{2,6},{3,7},{4,8},{5,9},{6,10},{7,11},{8,12},{9,13},{1... | collective-permute-start | bytes 786440 | tf_op jit(solution)/shard_map/ppermute | solution.py:30
  155.1 11.9 %collective-permute-start.22 = (bf16[512,256]{1,0:T(8,128)(2,1)S(1)}, bf16[512,256]{1,0:T(8,128)(2,1)S(1)}, u32[]{:S(2)}, u32[]{:S(2)}) collective-permute-start(bf16[512,256]{1,0:T(8,128)(2,1)S(1)} %get-tuple-element.74), channel_id=1, source_target_pairs={{0,12},{1,13},{2,14},{3,15},{4,0},{5,1},{6,2},{7,3},{8,4},{9,5},{1... | collective-permute-start | bytes 786440 | tf_op jit(solution)/shard_map/ppermute | solution.py:30
  160.5 8.6 %collective-permute-start.23 = (bf16[512,256]{1,0:T(8,128)(2,1)S(1)}, bf16[512,256]{1,0:T(8,128)(2,1)S(1)}, u32[]{:S(2)}, u32[]{:S(2)}) collective-permute-start(bf16[512,256]{1,0:T(8,128)(2,1)S(1)} %get-tuple-element.75), channel_id=1, source_target_pairs={{0,1},{1,2},{2,3},{3,0},{4,5},{5,6},{6,7},{7,4},{8,9},{9,10},{10,1... | collective-permute-start | bytes 786440 | tf_op jit(solution)/shard_map/ppermute | solution.py:25
  163.1 7.4 %collective-permute-start.24 = (bf16[512,256]{1,0:T(8,128)(2,1)S(1)}, bf16[512,256]{1,0:T(8,128)(2,1)S(1)}, u32[]{:S(2)}, u32[]{:S(2)}) collective-permute-start(bf16[512,256]{1,0:T(8,128)(2,1)S(1)} %get-tuple-element.76), channel_id=1, source_target_pairs={{0,3},{1,0},{2,1},{3,2},{4,7},{5,4},{6,5},{7,6},{8,11},{9,8},{10,9... | collective-permute-start | bytes 786440 | tf_op jit(solution)/shard_map/ppermute | solution.py:25
  170.6 12.5 %collective-permute-start.25 = (bf16[256,256]{1,0:T(8,128)(2,1)S(1)}, bf16[256,256]{1,0:T(8,128)(2,1)S(1)}, u32[]{:S(2)}, u32[]{:S(2)}) collective-permute-start(bf16[256,256]{1,0:T(8,128)(2,1)S(1)} %shard_map.63), channel_id=1, source_target_pairs={{0,384},{384,0},{1,385},{385,1},{2,386},{386,2},{3,387},{387,3},{4... | collective-permute-start | bytes 393224 | tf_op jit(solution)/shard_map/ppermute | solution.py:266

commit v5 on v4

--- a/solution.py
+++ b/solution.py
@@ -182,10 +182,10 @@
     def body(here_ref, *rest):
         sec = lax.axis_index("section")
         value = here_ref[:HS, :].astype(F32)
-        for ref in rest[:4]:
+        for ref in rest[: len(arrived)]:
             value += ref[:HS, :].astype(F32)
         rest[-1][slot_rows(sec), :] = value.astype(BF16)
-        rest[-1][slot_rows(1 - sec), :] = rest[4][...]
+        rest[-1][slot_rows(1 - sec), :] = rest[len(arrived)][...]
 
     return call(body, [here, *arrived, swapped], [(N, HS)])[0]
 
@@ -197,13 +197,14 @@
 
     up1, down1 = shift_y(c0, 1), shift_y(c0, -1)
     right0, left0, across0 = shift_x(c0, 1), shift_x(c0, -1), shift_x(c0, 2)
-    own_w, right0 = lax.optimization_barrier((proj_weights[0], right0))
+    c0, up1, down1, right0, left0, across0, own_w = lax.optimization_barrier(
+        (c0, up1, down1, right0, left0, across0, proj_weights[0])
+    )
     other_w = lax.ppermute(own_w, "section", SWAP)
-    c0, up1, down1, right0, left0, across0 = lax.optimization_barrier((c0, up1, down1, right0, left0, across0))
 
     pair = jnp.concatenate([up1, down1], axis=0)
     right1, left1 = shift_x(pair, 1), shift_x(pair, -1)
-    up2, down2 = shift_y(up1[:HALF], 1), shift_y(down1[HALF:], -1)
+    last = shift_y(c0, 2)
     total = project(
         [c0, pair, right0, left0, across0],
         [
@@ -212,9 +213,8 @@
         ],
         own_w, other_w, None,
     )
-    right1, left1, up2, down2, total = lax.optimization_barrier((right1, left1, up2, down2, total))
-
-    last = jnp.concatenate([up2, down2], axis=0)
+    right1, left1, last, total = lax.optimization_barrier((right1, left1, last, total))
+
     right2 = shift_x(jnp.concatenate([right1[:HALF], right1[ROWS : ROWS + HALF], last], axis=0), 1)
     left2 = shift_x(jnp.concatenate([left1[HALF:ROWS], left1[ROWS + HALF :], last], axis=0), -1)
     across2 = shift_x(last, 2)
@@ -249,20 +249,20 @@
             (2, N, [(2, N)]), (2, N + HS, [(2, N + HS), (4, N + HS)]), (2, 2 * N, [(2, 2 * N)]),
         ],
     )
-    up_b, down_b = shift_y(far[:HS], 1), shift_y(far[HS:], -1)
+    far = shift_y(far, 2)
     right_b, left_b = shift_x(right_b, 1), shift_x(left_b, -1)
     up_c, down_c, right_c, left_c = add_rows(
-        [up_c, down_c, right_c, left_c, right_b, left_b, up_b, down_b], [N] * 4,
-        [
-            (0, 0, [(0, 0), (4, 0), (5, 0), (6, 0)]), (0, HS, [(0, HS), (4, HS), (5, HS)]),
-            (1, 0, [(1, 0), (4, N), (5, N)]), (1, HS, [(1, HS), (4, N + HS), (5, N + HS), (7, 0)]),
+        [up_c, down_c, right_c, left_c, right_b, left_b], [N] * 4,
+        [
+            (0, 0, [(0, 0), (4, 0), (5, 0)]), (0, HS, [(0, HS), (4, HS), (5, HS)]),
+            (1, 0, [(1, 0), (4, N), (5, N)]), (1, HS, [(1, HS), (4, N + HS), (5, N + HS)]),
             (2, 0, [(2, 0), (4, 2 * N)]), (2, HS, [(2, HS)]),
             (3, 0, [(3, 0)]), (3, HS, [(3, HS), (5, 2 * N)]),
         ],
     )
     up_c, down_c, right_c, left_c = shift_y(up_c, 1), shift_y(down_c, -1), shift_x(right_c, 1), shift_x(left_c, -1)
-    arrived = [up_c, down_c, right_c, left_c]
-    sent = add_rows([here, *arrived], [HS], [(0, 0, [(i, HS) for i in range(5)])])[0]
+    arrived = [far, up_c, down_c, right_c, left_c]
+    sent = add_rows([here, *arrived], [HS], [(0, 0, [(i, HS) for i in range(6)])])[0]
     swapped = lax.ppermute(sent, "section", SWAP)
     return finish(here, arrived, swapped)[None]
 

time: 185 us -> 182 us (0.984)
  starting transfers between devices: 109 us -> 94 us
  waiting for transfers between devices: 62.4 us -> 74.6 us
    ppermute x8 -> x6, waiting for transfers between devices: 10.8 us -> 27.6 us  [shift_y(): return lax.ppermute(block, 'mp', route)]
    ppermute x8 -> x6, starting transfers between devices: 28.5 us -> 19.4 us  [shift_y(): return lax.ppermute(block, 'mp', route)]
    ppermute x15, waiting for transfers between devices: 49.2 us -> 44.7 us  [shift_x(): return lax.ppermute(block, 'mp', route)]
    ppermute x1, starting transfers between devices: 11.5 us -> 7.32 us  [local(): swapped = lax.ppermute(sent, 'section', SWAP)]
    ppermute x15, starting transfers between devices: 53.1 us -> 49.9 us  [shift_x(): return lax.ppermute(block, 'mp', route)]
    unnamed x12 -> x11, local copies, waits for them, and re-layouts: 4.14 us -> 4.12 us
  transfers between devices with their start and end apart: 26 -> 24, of which waited for: 16 -> 11; matrix products, arithmetic and copies ran while one was open for 0% -> 0% of each run, Pallas kernels for 2% -> 2%
where the time goes in v5:
time: 182 us; the launch traced here: 181 us
  starting transfers between devices  94 us (52%)
  waiting for transfers between devices  74.6 us (41%)
  Pallas kernels  8.16 us (4%)
  local copies, waits for them, and re-layouts  4.2 us (2%)
    ppermute x15, starting transfers between devices, shift_x(): return lax.ppermute(block, 'mp', route)  49.9 us
    ppermute x15, waiting for transfers between devices, shift_x(): return lax.ppermute(block, 'mp', route)  44.7 us
    ppermute x6, waiting for transfers between devices, shift_y(): return lax.ppermute(block, 'mp', route)  27.6 us
    ppermute x6, starting transfers between devices, shift_y(): return lax.ppermute(block, 'mp', route)  19.4 us
    ppermute x1, starting transfers between devices, local(): partner = lax.ppermute(own, 'section', SWAP)  12.4 us
    pallas_call x10, Pallas kernels, call(): pl.pallas_call(body, out_shape=out, in_specs=[SMEM] * scalars + [VMEM] *...  8.16 us
    ppermute x1, starting transfers between devices, local(): swapped = lax.ppermute(sent, 'section', SWAP)  7.32 us
    ppermute x1, starting transfers between devices, local(): other_w = lax.ppermute(own_w, 'section', SWAP)  4.93 us
  transfers between devices with their start and end apart: 24, of which 11 were waited for; matrix products, arithmetic and copies ran while one was open for 0% of the time, Pallas kernels for 2%

profile of v5, /device:TPU:1, one launch (start us, length us, event | category | flops | bytes accessed | tf_op | source)
XLA Modules:
  0.0 181.4 jit_solution(1518329611876504255)
XLA Ops:
  0.0 12.4 %collective-permute-start = (bf16[512,256]{1,0:T(8,128)(2,1)}, bf16[512,256]{1,0:T(8,128)(2,1)S(1)}, u32[]{:S(2)}, u32[]{:S(2)}) collective-permute-start(bf16[512,256]{1,0:T(8,128)(2,1)} %bitcast.9), channel_id=1, source_target_pairs={{0,384},{384,0},{1,385},{385,1},{2,386},{386,2},{3,387},{387,3},{4... | collective-permute-start | bytes 786440 | tf_op jit(solution)/shard_map/ppermute | solution.py:195
  15.7 1.9 %collective-permute-start.1 = (bf16[768,256]{1,0:T(8,128)(2,1)S(1)}, bf16[768,256]{1,0:T(8,128)(2,1)S(1)}, u32[]{:S(2)}, u32[]{:S(2)}) collective-permute-start(bf16[768,256]{1,0:T(8,128)(2,1)S(1)} %shard_map.55.rest_0_), channel_id=1, source_target_pairs={{0,4},{1,5},{2,6},{3,7},{4,8},{5,9},{6,10},{7,11},{8,12},{9,13},{1... | collective-permute-start | bytes 1179656 | tf_op jit(solution)/shard_map/ppermute | solution.py:30
  17.6 5.5 %collective-permute-start.2 = (bf16[768,256]{1,0:T(8,128)(2,1)S(1)}, bf16[768,256]{1,0:T(8,128)(2,1)S(1)}, u32[]{:S(2)}, u32[]{:S(2)}) collective-permute-start(bf16[768,256]{1,0:T(8,128)(2,1)S(1)} %shard_map.55.rest_0_), channel_id=1, source_target_pairs={{0,12},{1,13},{2,14},{3,15},{4,0},{5,1},{6,2},{7,3},{8,4},{9,5},{1... | collective-permute-start | bytes 1179656 | tf_op jit(solution)/shard_map/ppermute | solution.py:30
  23.1 1.9 %collective-permute-start.3 = (bf16[768,256]{1,0:T(8,128)(2,1)S(1)}, bf16[768,256]{1,0:T(8,128)(2,1)S(1)}, u32[]{:S(2)}, u32[]{:S(2)}) collective-permute-start(bf16[768,256]{1,0:T(8,128)(2,1)S(1)} %shard_map.55.rest_0_), channel_id=1, source_target_pairs={{0,1},{1,2},{2,3},{3,0},{4,5},{5,6},{6,7},{7,4},{8,9},{9,10},{10,1... | collective-permute-start | bytes 1179656 | tf_op jit(solution)/shard_map/ppermute | solution.py:25
  25.0 4.6 %collective-permute-start.4 = (bf16[768,256]{1,0:T(8,128)(2,1)S(1)}, bf16[768,256]{1,0:T(8,128)(2,1)S(1)}, u32[]{:S(2)}, u32[]{:S(2)}) collective-permute-start(bf16[768,256]{1,0:T(8,128)(2,1)S(1)} %shard_map.55.rest_0_), channel_id=1, source_target_pairs={{0,3},{1,0},{2,1},{3,2},{4,7},{5,4},{6,5},{7,6},{8,11},{9,8},{10,9... | collective-permute-start | bytes 1179656 | tf_op jit(solution)/shard_map/ppermute | solution.py:25
  29.6 1.9 %collective-permute-start.5 = (bf16[768,256]{1,0:T(8,128)(2,1)S(1)}, bf16[768,256]{1,0:T(8,128)(2,1)S(1)}, u32[]{:S(2)}, u32[]{:S(2)}) collective-permute-start(bf16[768,256]{1,0:T(8,128)(2,1)S(1)} %shard_map.55.rest_0_), channel_id=1, source_target_pairs={{0,2},{1,3},{2,0},{3,1},{4,6},{5,7},{6,4},{7,5},{8,10},{9,11},{10,... | collective-permute-start | bytes 1179656 | tf_op jit(solution)/shard_map/ppermute | solution.py:25
  31.5 2.4 %collective-permute-done.1 = bf16[768,256]{1,0:T(8,128)(2,1)S(1)} collective-permute-done((bf16[768,256]{1,0:T(8,128)(2,1)S(1)}, bf16[768,256]{1,0:T(8,128)(2,1)S(1)}, u32[]{:S(2)}, u32[]{:S(2)}) %collective-permute-start.1) | collective-permute-done | bytes 393248 | tf_op jit(solution)/shard_map/ppermute | solution.py:30
  34.7 9.6 %collective-permute-done.3.rest_2_ = bf16[768,256]{1,0:T(8,128)(2,1)S(1)} collective-permute-done((bf16[768,256]{1,0:T(8,128)(2,1)S(1)}, bf16[768,256]{1,0:T(8,128)(2,1)S(1)}, u32[]{:S(2)}, u32[]{:S(2)}) %collective-permute-start.3) | collective-permute-done | bytes 393248 | tf_op jit(solution)/shard_map/ppermute | solution.py:25
  44.3 4.9 %collective-permute-start.6 = (bf16[2,4096,256]{2,1,0:T(8,128)(2,1)}, bf16[2,4096,256]{2,1,0:T(8,128)(2,1)S(1)}, u32[]{:S(2)}, u32[]{:S(2)}) collective-permute-start(bf16[2,4096,256]{2,1,0:T(8,128)(2,1)} %bitcast.3), channel_id=1, source_target_pairs={{0,384},{384,0},{1,385},{385,1},{2,386},{386,2},{3,387},{387,3},{4... | collective-permute-start | bytes 12582920 | tf_op jit(solution)/shard_map/ppermute | solution.py:203
  49.3 3.2 %collective-permute-start.7 = (bf16[1536,256]{1,0:T(8,128)(2,1)S(1)}, bf16[1536,256]{1,0:T(8,128)(2,1)S(1)}, u32[]{:S(2)}, u32[]{:S(2)}) collective-permute-start(bf16[1536,256]{1,0:T(8,128)(2,1)S(1)} %constant_dynamic-update-slice_fusion.rest_1_), channel_id=1, source_target_pairs={{0,1},{1,2},{2,3},{3,0},{4,5},{5,6},{6,7},{7,4},{8,9},{9,10},{10,1... | collective-permute-start | bytes 2359304 | tf_op jit(solution)/shard_map/ppermute | solution.py:25
  52.6 4.0 %collective-permute-start.8 = (bf16[1536,256]{1,0:T(8,128)(2,1)S(1)}, bf16[1536,256]{1,0:T(8,128)(2,1)S(1)}, u32[]{:S(2)}, u32[]{:S(2)}) collective-permute-start(bf16[1536,256]{1,0:T(8,128)(2,1)S(1)} %constant_dynamic-update-slice_fusion.rest_1_), channel_id=1, source_target_pairs={{0,3},{1,0},{2,1},{3,2},{4,7},{5,4},{6,5},{7,6},{8,11},{9,8},{10,9... | collective-permute-start | bytes 2359304 | tf_op jit(solution)/shard_map/ppermute | solution.py:25
  56.6 1.9 %collective-permute-start.9 = (bf16[768,256]{1,0:T(8,128)(2,1)S(1)}, bf16[768,256]{1,0:T(8,128)(2,1)S(1)}, u32[]{:S(2)}, u32[]{:S(2)}) collective-permute-start(bf16[768,256]{1,0:T(8,128)(2,1)S(1)} %shard_map.55.rest_0_), channel_id=1, source_target_pairs={{0,8},{1,9},{2,10},{3,11},{4,12},{5,13},{6,14},{7,15},{8,0},{9,1},... | collective-permute-start | bytes 1179656 | tf_op jit(solution)/shard_map/ppermute | solution.py:30
  58.5 2.2 %copy-done = bf16[1,2,4096,256]{3,2,1,0:T(8,128)(2,1)S(1)} copy-done((bf16[1,2,4096,256]{3,2,1,0:T(8,128)(2,1)S(1)}, bf16[1,2,4096,256]{3,2,1,0:T(8,128)(2,1)}, u32[]{:S(2)}) %copy-start) | copy-done | bytes 4194328
  61.7 19.6 %collective-permute-done.9.rest_2_ = bf16[768,256]{1,0:T(8,128)(2,1)S(1)} collective-permute-done((bf16[768,256]{1,0:T(8,128)(2,1)S(1)}, bf16[768,256]{1,0:T(8,128)(2,1)S(1)}, u32[]{:S(2)}, u32[]{:S(2)}) %collective-permute-start.9) | collective-permute-done | bytes 393248 | tf_op jit(solution)/shard_map/ppermute | solution.py:30
  83.4 4.6 %collective-permute-start.11 = (bf16[1536,256]{1,0:T(8,128)(2,1)S(1)}, bf16[1536,256]{1,0:T(8,128)(2,1)S(1)}, u32[]{:S(2)}, u32[]{:S(2)}) collective-permute-start(bf16[1536,256]{1,0:T(8,128)(2,1)S(1)} %get-tuple-element.77), channel_id=1, source_target_pairs={{0,3},{1,0},{2,1},{3,2},{4,7},{5,4},{6,5},{7,6},{8,11},{9,8},{10,9... | collective-permute-start | bytes 2359304 | tf_op jit(solution)/shard_map/ppermute | solution.py:25
  88.0 1.9 %collective-permute-start.12 = (bf16[768,256]{1,0:T(8,128)(2,1)S(1)}, bf16[768,256]{1,0:T(8,128)(2,1)S(1)}, u32[]{:S(2)}, u32[]{:S(2)}) collective-permute-start(bf16[768,256]{1,0:T(8,128)(2,1)S(1)} %collective-permute-done.9.rest_2_), channel_id=1, source_target_pairs={{0,2},{1,3},{2,0},{3,1},{4,6},{5,7},{6,4},{7,5},{8,10},{9,11},{10,... | collective-permute-start | bytes 1179656 | tf_op jit(solution)/shard_map/ppermute | solution.py:25
  90.8 19.5 %collective-permute-done.12.rest_2_ = bf16[768,256]{1,0:T(8,128)(2,1)S(1)} collective-permute-done((bf16[768,256]{1,0:T(8,128)(2,1)S(1)}, bf16[768,256]{1,0:T(8,128)(2,1)S(1)}, u32[]{:S(2)}, u32[]{:S(2)}) %collective-permute-start.12) | collective-permute-done | bytes 393248 | tf_op jit(solution)/shard_map/ppermute | solution.py:25
  111.2 2.3 %shard_map.59 = (bf16[1024,256]{1,0:T(8,128)(2,1)S(1)}, bf16[1024,256]{1,0:T(8,128)(2,1)S(1)}, bf16[512,256]{1,0:T(8,128)(2,1)S(1)}, bf16[4,256,256]{2,1,0:T(8,128)(2,1)S(1)}) custom-call(s32[2]{0:T(128)S(1)} %copy-done.3, s32[2]{0:T(128)S(1)} %copy-done.4, f32[4,256,256]{2,1,0:T(8,128)S(1)} %shard_map.58.t_ref, bf16[2,4096,256]{2,1,0:T(8,128)(2,1)S(1)} %bitcast.7, ...), custom_call_target="tpu_custom_call" | custom-call | flops 1006632960 | bytes 9437200 | tf_op jit(solution)/shard_map/pallas_call | solution.py:36
  113.5 4.5 %collective-permute-start.13 = (bf16[1024,256]{1,0:T(8,128)(2,1)S(1)}, bf16[1024,256]{1,0:T(8,128)(2,1)S(1)}, u32[]{:S(2)}, u32[]{:S(2)}) collective-permute-start(bf16[1024,256]{1,0:T(8,128)(2,1)S(1)} %get-tuple-element.59), channel_id=1, source_target_pairs={{0,1},{1,2},{2,3},{3,0},{4,5},{5,6},{6,7},{7,4},{8,9},{9,10},{10,1... | collective-permute-start | bytes 1572872 | tf_op jit(solution)/shard_map/ppermute | solution.py:25
  118.1 3.1 %collective-permute-start.14 = (bf16[1024,256]{1,0:T(8,128)(2,1)S(1)}, bf16[1024,256]{1,0:T(8,128)(2,1)S(1)}, u32[]{:S(2)}, u32[]{:S(2)}) collective-permute-start(bf16[1024,256]{1,0:T(8,128)(2,1)S(1)} %get-tuple-element.60), channel_id=1, source_target_pairs={{0,3},{1,0},{2,1},{3,2},{4,7},{5,4},{6,5},{7,6},{8,11},{9,8},{10,9... | collective-permute-start | bytes 1572872 | tf_op jit(solution)/shard_map/ppermute | solution.py:25
  121.2 3.1 %collective-permute-start.15 = (bf16[512,256]{1,0:T(8,128)(2,1)S(1)}, bf16[512,256]{1,0:T(8,128)(2,1)S(1)}, u32[]{:S(2)}, u32[]{:S(2)}) collective-permute-start(bf16[512,256]{1,0:T(8,128)(2,1)S(1)} %get-tuple-element.61), channel_id=1, source_target_pairs={{0,2},{1,3},{2,0},{3,1},{4,6},{5,7},{6,4},{7,5},{8,10},{9,11},{10,... | collective-permute-start | bytes 786440 | tf_op jit(solution)/shard_map/ppermute | solution.py:25
  126.0 8.2 %collective-permute-done.15.refs_5_ = bf16[512,256]{1,0:T(8,128)(2,1)S(1)} collective-permute-done((bf16[512,256]{1,0:T(8,128)(2,1)S(1)}, bf16[512,256]{1,0:T(8,128)(2,1)S(1)}, u32[]{:S(2)}, u32[]{:S(2)}) %collective-permute-start.15) | collective-permute-done | bytes 262176 | tf_op jit(solution)/shard_map/ppermute | solution.py:25
  134.5 4.4 %collective-permute-start.17 = (bf16[1280,256]{1,0:T(8,128)(2,1)S(1)}, bf16[1280,256]{1,0:T(8,128)(2,1)S(1)}, u32[]{:S(2)}, u32[]{:S(2)}) collective-permute-start(bf16[1280,256]{1,0:T(8,128)(2,1)S(1)} %get-tuple-element.67), channel_id=1, source_target_pairs={{0,1},{1,2},{2,3},{3,0},{4,5},{5,6},{6,7},{7,4},{8,9},{9,10},{10,1... | collective-permute-start | bytes 1966088 | tf_op jit(solution)/shard_map/ppermute | solution.py:25
  138.9 3.5 %collective-permute-start.18 = (bf16[1280,256]{1,0:T(8,128)(2,1)S(1)}, bf16[1280,256]{1,0:T(8,128)(2,1)S(1)}, u32[]{:S(2)}, u32[]{:S(2)}) collective-permute-start(bf16[1280,256]{1,0:T(8,128)(2,1)S(1)} %get-tuple-element.68), channel_id=1, source_target_pairs={{0,3},{1,0},{2,1},{3,2},{4,7},{5,4},{6,5},{7,6},{8,11},{9,8},{10,9... | collective-permute-start | bytes 1966088 | tf_op jit(solution)/shard_map/ppermute | solution.py:25
  142.4 2.7 %collective-permute-start.16 = (bf16[512,256]{1,0:T(8,128)(2,1)S(1)}, bf16[512,256]{1,0:T(8,128)(2,1)S(1)}, u32[]{:S(2)}, u32[]{:S(2)}) collective-permute-start(bf16[512,256]{1,0:T(8,128)(2,1)S(1)} %get-tuple-element.62), channel_id=1, source_target_pairs={{0,8},{1,9},{2,10},{3,11},{4,12},{5,13},{6,14},{7,15},{8,0},{9,1},... | collective-permute-start | bytes 786440 | tf_op jit(solution)/shard_map/ppermute | solution.py:30
  145.1 6.3 %collective-permute-done.17.refs_4_ = bf16[1280,256]{1,0:T(8,128)(2,1)S(1)} collective-permute-done((bf16[1280,256]{1,0:T(8,128)(2,1)S(1)}, bf16[1280,256]{1,0:T(8,128)(2,1)S(1)}, u32[]{:S(2)}, u32[]{:S(2)}) %collective-permute-start.17) | collective-permute-done | bytes 655392 | tf_op jit(solution)/shard_map/ppermute | solution.py:25
  152.6 1.9 %collective-permute-start.19 = (bf16[512,256]{1,0:T(8,128)(2,1)S(1)}, bf16[512,256]{1,0:T(8,128)(2,1)S(1)}, u32[]{:S(2)}, u32[]{:S(2)}) collective-permute-start(bf16[512,256]{1,0:T(8,128)(2,1)S(1)} %get-tuple-element.69), channel_id=1, source_target_pairs={{0,4},{1,5},{2,6},{3,7},{4,8},{5,9},{6,10},{7,11},{8,12},{9,13},{1... | collective-permute-start | bytes 786440 | tf_op jit(solution)/shard_map/ppermute | solution.py:30
  154.6 5.5 %collective-permute-start.20 = (bf16[512,256]{1,0:T(8,128)(2,1)S(1)}, bf16[512,256]{1,0:T(8,128)(2,1)S(1)}, u32[]{:S(2)}, u32[]{:S(2)}) collective-permute-start(bf16[512,256]{1,0:T(8,128)(2,1)S(1)} %get-tuple-element.70), channel_id=1, source_target_pairs={{0,12},{1,13},{2,14},{3,15},{4,0},{5,1},{6,2},{7,3},{8,4},{9,5},{1... | collective-permute-start | bytes 786440 | tf_op jit(solution)/shard_map/ppermute | solution.py:30
  160.0 3.5 %collective-permute-start.21 = (bf16[512,256]{1,0:T(8,128)(2,1)S(1)}, bf16[512,256]{1,0:T(8,128)(2,1)S(1)}, u32[]{:S(2)}, u32[]{:S(2)}) collective-permute-start(bf16[512,256]{1,0:T(8,128)(2,1)S(1)} %get-tuple-element.71), channel_id=1, source_target_pairs={{0,1},{1,2},{2,3},{3,0},{4,5},{5,6},{6,7},{7,4},{8,9},{9,10},{10,1... | collective-permute-start | bytes 786440 | tf_op jit(solution)/shard_map/ppermute | solution.py:25
  163.6 3.7 %collective-permute-start.22 = (bf16[512,256]{1,0:T(8,128)(2,1)S(1)}, bf16[512,256]{1,0:T(8,128)(2,1)S(1)}, u32[]{:S(2)}, u32[]{:S(2)}) collective-permute-start(bf16[512,256]{1,0:T(8,128)(2,1)S(1)} %get-tuple-element.72), channel_id=1, source_target_pairs={{0,3},{1,0},{2,1},{3,2},{4,7},{5,4},{6,5},{7,6},{8,11},{9,8},{10,9... | collective-permute-start | bytes 786440 | tf_op jit(solution)/shard_map/ppermute | solution.py:25
  167.3 4.9 %collective-permute-done.19.refs_2_.rest_1_ = bf16[512,256]{1,0:T(8,128)(2,1)S(1)} collective-permute-done((bf16[512,256]{1,0:T(8,128)(2,1)S(1)}, bf16[512,256]{1,0:T(8,128)(2,1)S(1)}, u32[]{:S(2)}, u32[]{:S(2)}) %collective-permute-start.19) | collective-permute-done | bytes 262176 | tf_op jit(solution)/shard_map/ppermute | solution.py:30
  172.3 7.3 %collective-permute-start.23 = (bf16[256,256]{1,0:T(8,128)(2,1)S(1)}, bf16[256,256]{1,0:T(8,128)(2,1)S(1)}, u32[]{:S(2)}, u32[]{:S(2)}) collective-permute-start(bf16[256,256]{1,0:T(8,128)(2,1)S(1)} %shard_map.63), channel_id=1, source_target_pairs={{0,384},{384,0},{1,385},{385,1},{2,386},{386,2},{3,387},{387,3},{4... | collective-permute-start | bytes 393224 | tf_op jit(solution)/shard_map/ppermute | solution.py:266
  (40 shorter events, 13.9 us)
Async XLA Ops:
  0.0 13.8 %collective-permute-start = (bf16[512,256]{1,0:T(8,128)(2,1)}, bf16[512,256]{1,0:T(8,128)(2,1)S(1)}, u32[]{:S(2)}, u32[]{:S(2)}) collective-permute-start(bf16[512,256]{1,0:T(8,128)(2,1)} %bitcast.9), channel_id=1, source_target_pairs={{0,384},{384,0},{1,385},{385,1},{2,386},{386,2},{3,387},{387,3},{4... | collective-permute-start | bytes 786440 | tf_op jit(solution)/shard_map/ppermute | solution.py:195
  13.8 0.9 copy-start.1
  14.7 0.9 copy-start.2
  15.7 18.2 %collective-permute-start.1 = (bf16[768,256]{1,0:T(8,128)(2,1)S(1)}, bf16[768,256]{1,0:T(8,128)(2,1)S(1)}, u32[]{:S(2)}, u32[]{:S(2)}) collective-permute-start(bf16[768,256]{1,0:T(8,128)(2,1)S(1)} %shard_map.55.rest_0_), channel_id=1, source_target_pairs={{0,4},{1,5},{2,6},{3,7},{4,8},{5,9},{6,10},{7,11},{8,12},{9,13},{1... | collective-permute-start | bytes 1179656 | tf_op jit(solution)/shard_map/ppermute | solution.py:30
  17.6 17.1 %collective-permute-start.2 = (bf16[768,256]{1,0:T(8,128)(2,1)S(1)}, bf16[768,256]{1,0:T(8,128)(2,1)S(1)}, u32[]{:S(2)}, u32[]{:S(2)}) collective-permute-start(bf16[768,256]{1,0:T(8,128)(2,1)S(1)} %shard_map.55.rest_0_), channel_id=1, source_target_pairs={{0,12},{1,13},{2,14},{3,15},{4,0},{5,1},{6,2},{7,3},{8,4},{9,5},{1... | collective-permute-start | bytes 1179656 | tf_op jit(solution)/shard_map/ppermute | solution.py:30
  23.1 21.2 %collective-permute-start.3 = (bf16[768,256]{1,0:T(8,128)(2,1)S(1)}, bf16[768,256]{1,0:T(8,128)(2,1)S(1)}, u32[]{:S(2)}, u32[]{:S(2)}) collective-permute-start(bf16[768,256]{1,0:T(8,128)(2,1)S(1)} %shard_map.55.rest_0_), channel_id=1, source_target_pairs={{0,1},{1,2},{2,3},{3,0},{4,5},{5,6},{6,7},{7,4},{8,9},{9,10},{10,1... | collective-permute-start | bytes 1179656 | tf_op jit(solution)/shard_map/ppermute | solution.py:25
  25.0 19.3 %collective-permute-start.4 = (bf16[768,256]{1,0:T(8,128)(2,1)S(1)}, bf16[768,256]{1,0:T(8,128)(2,1)S(1)}, u32[]{:S(2)}, u32[]{:S(2)}) collective-permute-start(bf16[768,256]{1,0:T(8,128)(2,1)S(1)} %shard_map.55.rest_0_), channel_id=1, source_target_pairs={{0,3},{1,0},{2,1},{3,2},{4,7},{5,4},{6,5},{7,6},{8,11},{9,8},{10,9... | collective-permute-start | bytes 1179656 | tf_op jit(solution)/shard_map/ppermute | solution.py:25
  29.6 14.7 %collective-permute-start.5 = (bf16[768,256]{1,0:T(8,128)(2,1)S(1)}, bf16[768,256]{1,0:T(8,128)(2,1)S(1)}, u32[]{:S(2)}, u32[]{:S(2)}) collective-permute-start(bf16[768,256]{1,0:T(8,128)(2,1)S(1)} %shard_map.55.rest_0_), channel_id=1, source_target_pairs={{0,2},{1,3},{2,0},{3,1},{4,6},{5,7},{6,4},{7,5},{8,10},{9,11},{10,... | collective-permute-start | bytes 1179656 | tf_op jit(solution)/shard_map/ppermute | solution.py:25
  44.3 14.2 %collective-permute-start.6 = (bf16[2,4096,256]{2,1,0:T(8,128)(2,1)}, bf16[2,4096,256]{2,1,0:T(8,128)(2,1)S(1)}, u32[]{:S(2)}, u32[]{:S(2)}) collective-permute-start(bf16[2,4096,256]{2,1,0:T(8,128)(2,1)} %bitcast.3), channel_id=1, source_target_pairs={{0,384},{384,0},{1,385},{385,1},{2,386},{386,2},{3,387},{387,3},{4... | collective-permute-start | bytes 12582920 | tf_op jit(solution)/shard_map/ppermute | solution.py:203
  49.3 32.0 %collective-permute-start.7 = (bf16[1536,256]{1,0:T(8,128)(2,1)S(1)}, bf16[1536,256]{1,0:T(8,128)(2,1)S(1)}, u32[]{:S(2)}, u32[]{:S(2)}) collective-permute-start(bf16[1536,256]{1,0:T(8,128)(2,1)S(1)} %constant_dynamic-update-slice_fusion.rest_1_), channel_id=1, source_target_pairs={{0,1},{1,2},{2,3},{3,0},{4,5},{5,6},{6,7},{7,4},{8,9},{9,10},{10,1... | collective-permute-start | bytes 2359304 | tf_op jit(solution)/shard_map/ppermute | solution.py:25
  52.6 28.7 %collective-permute-start.8 = (bf16[1536,256]{1,0:T(8,128)(2,1)S(1)}, bf16[1536,256]{1,0:T(8,128)(2,1)S(1)}, u32[]{:S(2)}, u32[]{:S(2)}) collective-permute-start(bf16[1536,256]{1,0:T(8,128)(2,1)S(1)} %constant_dynamic-update-slice_fusion.rest_1_), channel_id=1, source_target_pairs={{0,3},{1,0},{2,1},{3,2},{4,7},{5,4},{6,5},{7,6},{8,11},{9,8},{10,9... | collective-permute-start | bytes 2359304 | tf_op jit(solution)/shard_map/ppermute | solution.py:25
  56.6 24.7 %collective-permute-start.9 = (bf16[768,256]{1,0:T(8,128)(2,1)S(1)}, bf16[768,256]{1,0:T(8,128)(2,1)S(1)}, u32[]{:S(2)}, u32[]{:S(2)}) collective-permute-start(bf16[768,256]{1,0:T(8,128)(2,1)S(1)} %shard_map.55.rest_0_), channel_id=1, source_target_pairs={{0,8},{1,9},{2,10},{3,11},{4,12},{5,13},{6,14},{7,15},{8,0},{9,1},... | collective-permute-start | bytes 1179656 | tf_op jit(solution)/shard_map/ppermute | solution.py:30
  58.5 2.2 %copy-start = (bf16[1,2,4096,256]{3,2,1,0:T(8,128)(2,1)S(1)}, bf16[1,2,4096,256]{3,2,1,0:T(8,128)(2,1)}, u32[]{:S(2)}) copy-start(bf16[1,2,4096,256]{3,2,1,0:T(8,128)(2,1)} %param.6) | copy-start | bytes 12582916
  81.5 28.9 %collective-permute-start.10 = (bf16[1536,256]{1,0:T(8,128)(2,1)S(1)}, bf16[1536,256]{1,0:T(8,128)(2,1)S(1)}, u32[]{:S(2)}, u32[]{:S(2)}) collective-permute-start(bf16[1536,256]{1,0:T(8,128)(2,1)S(1)} %get-tuple-element.78), channel_id=1, source_target_pairs={{0,1},{1,2},{2,3},{3,0},{4,5},{5,6},{6,7},{7,4},{8,9},{9,10},{10,1... | collective-permute-start | bytes 2359304 | tf_op jit(solution)/shard_map/ppermute | solution.py:25
  83.4 26.9 %collective-permute-start.11 = (bf16[1536,256]{1,0:T(8,128)(2,1)S(1)}, bf16[1536,256]{1,0:T(8,128)(2,1)S(1)}, u32[]{:S(2)}, u32[]{:S(2)}) collective-permute-start(bf16[1536,256]{1,0:T(8,128)(2,1)S(1)} %get-tuple-element.77), channel_id=1, source_target_pairs={{0,3},{1,0},{2,1},{3,2},{4,7},{5,4},{6,5},{7,6},{8,11},{9,8},{10,9... | collective-permute-start | bytes 2359304 | tf_op jit(solution)/shard_map/ppermute | solution.py:25
  88.0 22.3 %collective-permute-start.12 = (bf16[768,256]{1,0:T(8,128)(2,1)S(1)}, bf16[768,256]{1,0:T(8,128)(2,1)S(1)}, u32[]{:S(2)}, u32[]{:S(2)}) collective-permute-start(bf16[768,256]{1,0:T(8,128)(2,1)S(1)} %collective-permute-done.9.rest_2_), channel_id=1, source_target_pairs={{0,2},{1,3},{2,0},{3,1},{4,6},{5,7},{6,4},{7,5},{8,10},{9,11},{10,... | collective-permute-start | bytes 1179656 | tf_op jit(solution)/shard_map/ppermute | solution.py:25
  90.8 20.4 %copy-start.3 = (s32[2]{0:T(128)S(1)}, s32[2]{0:T(128)}, u32[]{:S(2)}) copy-start(s32[2]{0:T(128)} %enc_ref.1) | copy-start | bytes 28
  90.8 20.4 %copy-start.4 = (s32[2]{0:T(128)S(1)}, s32[2]{0:T(128)}, u32[]{:S(2)}) copy-start(s32[2]{0:T(128)} %dec_ref.1) | copy-start | bytes 28
  113.5 20.7 %collective-permute-start.13 = (bf16[1024,256]{1,0:T(8,128)(2,1)S(1)}, bf16[1024,256]{1,0:T(8,128)(2,1)S(1)}, u32[]{:S(2)}, u32[]{:S(2)}) collective-permute-start(bf16[1024,256]{1,0:T(8,128)(2,1)S(1)} %get-tuple-element.59), channel_id=1, source_target_pairs={{0,1},{1,2},{2,3},{3,0},{4,5},{5,6},{6,7},{7,4},{8,9},{9,10},{10,1... | collective-permute-start | bytes 1572872 | tf_op jit(solution)/shard_map/ppermute | solution.py:25
  118.1 16.2 %collective-permute-start.14 = (bf16[1024,256]{1,0:T(8,128)(2,1)S(1)}, bf16[1024,256]{1,0:T(8,128)(2,1)S(1)}, u32[]{:S(2)}, u32[]{:S(2)}) collective-permute-start(bf16[1024,256]{1,0:T(8,128)(2,1)S(1)} %get-tuple-element.60), channel_id=1, source_target_pairs={{0,3},{1,0},{2,1},{3,2},{4,7},{5,4},{6,5},{7,6},{8,11},{9,8},{10,9... | collective-permute-start | bytes 1572872 | tf_op jit(solution)/shard_map/ppermute | solution.py:25
  121.2 13.1 %collective-permute-start.15 = (bf16[512,256]{1,0:T(8,128)(2,1)S(1)}, bf16[512,256]{1,0:T(8,128)(2,1)S(1)}, u32[]{:S(2)}, u32[]{:S(2)}) collective-permute-start(bf16[512,256]{1,0:T(8,128)(2,1)S(1)} %get-tuple-element.61), channel_id=1, source_target_pairs={{0,2},{1,3},{2,0},{3,1},{4,6},{5,7},{6,4},{7,5},{8,10},{9,11},{10,... | collective-permute-start | bytes 786440 | tf_op jit(solution)/shard_map/ppermute | solution.py:25
  134.5 17.0 %collective-permute-start.17 = (bf16[1280,256]{1,0:T(8,128)(2,1)S(1)}, bf16[1280,256]{1,0:T(8,128)(2,1)S(1)}, u32[]{:S(2)}, u32[]{:S(2)}) collective-permute-start(bf16[1280,256]{1,0:T(8,128)(2,1)S(1)} %get-tuple-element.67), channel_id=1, source_target_pairs={{0,1},{1,2},{2,3},{3,0},{4,5},{5,6},{6,7},{7,4},{8,9},{9,10},{10,1... | collective-permute-start | bytes 1966088 | tf_op jit(solution)/shard_map/ppermute | solution.py:25
  138.9 13.5 %collective-permute-start.18 = (bf16[1280,256]{1,0:T(8,128)(2,1)S(1)}, bf16[1280,256]{1,0:T(8,128)(2,1)S(1)}, u32[]{:S(2)}, u32[]{:S(2)}) collective-permute-start(bf16[1280,256]{1,0:T(8,128)(2,1)S(1)} %get-tuple-element.68), channel_id=1, source_target_pairs={{0,3},{1,0},{2,1},{3,2},{4,7},{5,4},{6,5},{7,6},{8,11},{9,8},{10,9... | collective-permute-start | bytes 1966088 | tf_op jit(solution)/shard_map/ppermute | solution.py:25
  142.4 24.9 %collective-permute-start.16 = (bf16[512,256]{1,0:T(8,128)(2,1)S(1)}, bf16[512,256]{1,0:T(8,128)(2,1)S(1)}, u32[]{:S(2)}, u32[]{:S(2)}) collective-permute-start(bf16[512,256]{1,0:T(8,128)(2,1)S(1)} %get-tuple-element.62), channel_id=1, source_target_pairs={{0,8},{1,9},{2,10},{3,11},{4,12},{5,13},{6,14},{7,15},{8,0},{9,1},... | collective-permute-start | bytes 786440 | tf_op jit(solution)/shard_map/ppermute | solution.py:30
  152.6 19.5 %collective-permute-start.19 = (bf16[512,256]{1,0:T(8,128)(2,1)S(1)}, bf16[512,256]{1,0:T(8,128)(2,1)S(1)}, u32[]{:S(2)}, u32[]{:S(2)}) collective-permute-start(bf16[512,256]{1,0:T(8,128)(2,1)S(1)} %get-tuple-element.69), channel_id=1, source_target_pairs={{0,4},{1,5},{2,6},{3,7},{4,8},{5,9},{6,10},{7,11},{8,12},{9,13},{1... | collective-permute-start | bytes 786440 | tf_op jit(solution)/shard_map/ppermute | solution.py:30
  154.6 17.6 %collective-permute-start.20 = (bf16[512,256]{1,0:T(8,128)(2,1)S(1)}, bf16[512,256]{1,0:T(8,128)(2,1)S(1)}, u32[]{:S(2)}, u32[]{:S(2)}) collective-permute-start(bf16[512,256]{1,0:T(8,128)(2,1)S(1)} %get-tuple-element.70), channel_id=1, source_target_pairs={{0,12},{1,13},{2,14},{3,15},{4,0},{5,1},{6,2},{7,3},{8,4},{9,5},{1... | collective-permute-start | bytes 786440 | tf_op jit(solution)/shard_map/ppermute | solution.py:30
  160.0 12.1 %collective-permute-start.21 = (bf16[512,256]{1,0:T(8,128)(2,1)S(1)}, bf16[512,256]{1,0:T(8,128)(2,1)S(1)}, u32[]{:S(2)}, u32[]{:S(2)}) collective-permute-start(bf16[512,256]{1,0:T(8,128)(2,1)S(1)} %get-tuple-element.71), channel_id=1, source_target_pairs={{0,1},{1,2},{2,3},{3,0},{4,5},{5,6},{6,7},{7,4},{8,9},{9,10},{10,1... | collective-permute-start | bytes 786440 | tf_op jit(solution)/shard_map/ppermute | solution.py:25
  163.6 8.6 %collective-permute-start.22 = (bf16[512,256]{1,0:T(8,128)(2,1)S(1)}, bf16[512,256]{1,0:T(8,128)(2,1)S(1)}, u32[]{:S(2)}, u32[]{:S(2)}) collective-permute-start(bf16[512,256]{1,0:T(8,128)(2,1)S(1)} %get-tuple-element.72), channel_id=1, source_target_pairs={{0,3},{1,0},{2,1},{3,2},{4,7},{5,4},{6,5},{7,6},{8,11},{9,8},{10,9... | collective-permute-start | bytes 786440 | tf_op jit(solution)/shard_map/ppermute | solution.py:25
  172.3 8.3 %collective-permute-start.23 = (bf16[256,256]{1,0:T(8,128)(2,1)S(1)}, bf16[256,256]{1,0:T(8,128)(2,1)S(1)}, u32[]{:S(2)}, u32[]{:S(2)}) collective-permute-start(bf16[256,256]{1,0:T(8,128)(2,1)S(1)} %shard_map.63), channel_id=1, source_target_pairs={{0,384},{384,0},{1,385},{385,1},{2,386},{386,2},{3,387},{387,3},{4... | collective-permute-start | bytes 393224 | tf_op jit(solution)/shard_map/ppermute | solution.py:266

commit v6 on v5

--- a/solution.py
+++ b/solution.py
@@ -30,6 +30,10 @@
     return lax.ppermute(block, "mp", route)
 
 
+def join(*parts):
+    return jnp.concatenate(parts, axis=0)
+
+
 def call(body, inputs, shapes, flops=0, out_dtype=BF16, scalars=0):
     out = [jax.ShapeDtypeStruct(s, out_dtype) for s in shapes]
     moved = sum(a.size * a.dtype.itemsize for a in inputs)
@@ -55,14 +59,27 @@
 
 
 def assemble(own, cotangent, partner):
-    def body(own_ref, cot_ref, partner_ref, out_ref):
+    def body(own_ref, cot_ref, partner_ref, out_ref, sems):
         sec = lax.axis_index("section")
         here = slot_rows(sec)
-        out_ref[:HS, :] = own_ref[here, :]
-        out_ref[slot_rows(2 - sec), :] = cot_ref[here, :]
+        copies = [
+            pltpu.make_async_copy(own_ref.at[here, :], out_ref.at[pl.ds(0, HS), :], sems.at[0]),
+            pltpu.make_async_copy(cot_ref.at[here, :], out_ref.at[slot_rows(2 - sec), :], sems.at[1]),
+        ]
+        for copy in copies:
+            copy.start()
         out_ref[slot_rows(1 + sec), :] = partner_ref[here, :]
-
-    return call(body, [own, cotangent, partner], [(ROWS, HS)])[0]
+        for copy in copies:
+            copy.wait()
+
+    return pl.pallas_call(
+        body,
+        out_shape=jax.ShapeDtypeStruct((ROWS, HS), BF16),
+        in_specs=[pl.BlockSpec(memory_space=pltpu.HBM)] * 2 + [VMEM],
+        out_specs=VMEM,
+        scratch_shapes=[pltpu.SemaphoreType.DMA((2,))],
+        compiler_params=pltpu.CompilerParams(vmem_limit_bytes=VMEM_LIMIT),
+    )(own, cotangent, partner)
 
 
 def rows_of(refs, block, low, high):
@@ -196,33 +213,36 @@
     c0 = assemble(own, out_cotangent, partner)
 
     up1, down1 = shift_y(c0, 1), shift_y(c0, -1)
-    right0, left0, across0 = shift_x(c0, 1), shift_x(c0, -1), shift_x(c0, 2)
-    c0, up1, down1, right0, left0, across0, own_w = lax.optimization_barrier(
-        (c0, up1, down1, right0, left0, across0, proj_weights[0])
+    right0, left0 = shift_x(c0, 1), shift_x(c0, -1)
+    c0, up1, down1, right0, left0, own_w = lax.optimization_barrier(
+        (c0, up1, down1, right0, left0, proj_weights[0])
     )
     other_w = lax.ppermute(own_w, "section", SWAP)
 
-    pair = jnp.concatenate([up1, down1], axis=0)
-    right1, left1 = shift_x(pair, 1), shift_x(pair, -1)
-    last = shift_y(c0, 2)
+    right1 = shift_x(join(right0[:HALF], up1, down1[:HALF]), 1)
+    left1 = shift_x(join(left0[HALF:], up1[HALF:], down1), -1)
+    up2 = shift_y(join(up1[:HALF], left0[:HALF]), 1)
+    down2 = shift_y(join(down1[HALF:], right0[HALF:]), -1)
     total = project(
-        [c0, pair, right0, left0, across0],
-        [
-            ((0, 0), [(0, 0, ROWS)]), ((-1, 0), [(1, 0, ROWS)]), ((1, 0), [(1, ROWS, ROWS)]),
-            ((0, -1), [(2, 0, ROWS)]), ((0, 1), [(3, 0, ROWS)]), ((0, 2), [(4, 0, ROWS)]),
+        [c0, up1, down1, right0, left0],
+        [
+            ((0, 0), [(0, 0, ROWS)]), ((-1, 0), [(1, 0, ROWS)]), ((1, 0), [(2, 0, ROWS)]),
+            ((0, -1), [(3, 0, ROWS)]), ((0, 1), [(4, 0, ROWS)]),
         ],
         own_w, other_w, None,
     )
-    right1, left1, last, total = lax.optimization_barrier((right1, left1, last, total))
-
-    right2 = shift_x(jnp.concatenate([right1[:HALF], right1[ROWS : ROWS + HALF], last], axis=0), 1)
-    left2 = shift_x(jnp.concatenate([left1[HALF:ROWS], left1[ROWS + HALF :], last], axis=0), -1)
+    right1, left1, up2, down2, total = lax.optimization_barrier((right1, left1, up2, down2, total))
+
+    last = join(up2[:HALF], down2[:HALF])
+    right2 = shift_x(join(right1[HALF:ROWS], right1[ROWS + HALF :], last), 1)
+    left2 = shift_x(join(left1[HALF:ROWS], left1[ROWS + HALF :], last), -1)
     across2 = shift_x(last, 2)
     total = project(
-        [right1, left1, last],
-        [
-            ((-1, -1), [(0, 0, ROWS)]), ((1, -1), [(0, ROWS, ROWS)]),
-            ((-1, 1), [(1, 0, ROWS)]), ((1, 1), [(1, ROWS, ROWS)]), ((2, 0), [(2, 0, ROWS)]),
+        [right1, left1, up2, down2],
+        [
+            ((-1, -1), [(0, HALF, ROWS)]), ((1, -1), [(0, HALF + ROWS, HALF), (3, HALF, HALF)]),
+            ((-1, 1), [(2, HALF, HALF), (1, HALF, HALF)]), ((1, 1), [(1, ROWS, ROWS)]),
+            ((0, 2), [(0, 0, HALF), (1, 0, HALF)]), ((2, 0), [(2, 0, HALF), (3, 0, HALF)]),
         ],
         own_w, other_w, total,
     )

time: 182 us -> 175 us (0.962)
  waiting for transfers between devices: 74.6 us -> 67 us
  local copies, waits for them, and re-layouts: 4.2 us -> 2.11 us
    ppermute x6 -> x7, waiting for transfers between devices: 27.6 us -> 19.3 us  [shift_y(): return lax.ppermute(block, 'mp', route)]
    ppermute x6 -> x7, starting transfers between devices: 19.4 us -> 24.2 us  [shift_y(): return lax.ppermute(block, 'mp', route)]
    ppermute x15 -> x14, starting transfers between devices: 49.9 us -> 47.6 us  [shift_x(): return lax.ppermute(block, 'mp', route)]
    unnamed x11 -> x10, local copies, waits for them, and re-layouts: 4.12 us -> 1.92 us
    ppermute x15 -> x14, waiting for transfers between devices: 44.7 us -> 45.3 us  [shift_x(): return lax.ppermute(block, 'mp', route)]
    pallas_call x10 -> x9, Pallas kernels: 8.16 us -> 8.15 us  [call(): pl.pallas_call(body, out_shape=out, in_specs=[SMEM] * scalars + [VMEM] *...]
  transfers between devices with their start and end apart: 24 -> 24, of which waited for: 11 -> 15; matrix products, arithmetic and copies ran while one was open for 0% -> 0% of each run, Pallas kernels for 2% -> 2%
where the time goes in v6:
time: 175 us; the launch traced here: 174 us
  starting transfers between devices  95.7 us (55%)
  waiting for transfers between devices  67 us (38%)
  Pallas kernels  8.48 us (5%)
  local copies, waits for them, and re-layouts  2.11 us (1%)
    ppermute x14, starting transfers between devices, shift_x(): return lax.ppermute(block, 'mp', route)  47.6 us
    ppermute x14, waiting for transfers between devices, shift_x(): return lax.ppermute(block, 'mp', route)  45.3 us
    ppermute x7, starting transfers between devices, shift_y(): return lax.ppermute(block, 'mp', route)  24.2 us
    ppermute x7, waiting for transfers between devices, shift_y(): return lax.ppermute(block, 'mp', route)  19.3 us
    ppermute x1, starting transfers between devices, local(): partner = lax.ppermute(own, 'section', SWAP)  12.4 us
    pallas_call x9, Pallas kernels, call(): pl.pallas_call(body, out_shape=out, in_specs=[SMEM] * scalars + [VMEM] *...  8.15 us
    ppermute x1, starting transfers between devices, local(): swapped = lax.ppermute(sent, 'section', SWAP)  7.41 us
    ppermute x1, starting transfers between devices, local(): other_w = lax.ppermute(own_w, 'section', SWAP)  4.04 us
  transfers between devices with their start and end apart: 24, of which 15 were waited for; matrix products, arithmetic and copies ran while one was open for 0% of the time, Pallas kernels for 2%

profile of v6, /device:TPU:1, one launch (start us, length us, event | category | flops | bytes accessed | tf_op | source)
XLA Modules:
  0.0 174.0 jit_solution(4544055702505953706)
XLA Ops:
  0.0 12.4 %collective-permute-start = (bf16[512,256]{1,0:T(8,128)(2,1)}, bf16[512,256]{1,0:T(8,128)(2,1)S(1)}, u32[]{:S(2)}, u32[]{:S(2)}) collective-permute-start(bf16[512,256]{1,0:T(8,128)(2,1)} %bitcast.9), channel_id=1, source_target_pairs={{0,384},{384,0},{1,385},{385,1},{2,386},{386,2},{3,387},{387,3},{4... | collective-permute-start | bytes 786440 | tf_op jit(solution)/shard_map/ppermute | solution.py:212
  16.0 1.9 %collective-permute-start.1 = (bf16[768,256]{1,0:T(8,128)(2,1)S(1)}, bf16[768,256]{1,0:T(8,128)(2,1)S(1)}, u32[]{:S(2)}, u32[]{:S(2)}) collective-permute-start(bf16[768,256]{1,0:T(8,128)(2,1)S(1)} %shard_map.55.rest_0_), channel_id=1, source_target_pairs={{0,4},{1,5},{2,6},{3,7},{4,8},{5,9},{6,10},{7,11},{8,12},{9,13},{1... | collective-permute-start | bytes 1179656 | tf_op jit(solution)/shard_map/ppermute | solution.py:30
  17.9 5.5 %collective-permute-start.2 = (bf16[768,256]{1,0:T(8,128)(2,1)S(1)}, bf16[768,256]{1,0:T(8,128)(2,1)S(1)}, u32[]{:S(2)}, u32[]{:S(2)}) collective-permute-start(bf16[768,256]{1,0:T(8,128)(2,1)S(1)} %shard_map.55.rest_0_), channel_id=1, source_target_pairs={{0,12},{1,13},{2,14},{3,15},{4,0},{5,1},{6,2},{7,3},{8,4},{9,5},{1... | collective-permute-start | bytes 1179656 | tf_op jit(solution)/shard_map/ppermute | solution.py:30
  23.4 1.9 %collective-permute-start.3 = (bf16[768,256]{1,0:T(8,128)(2,1)S(1)}, bf16[768,256]{1,0:T(8,128)(2,1)S(1)}, u32[]{:S(2)}, u32[]{:S(2)}) collective-permute-start(bf16[768,256]{1,0:T(8,128)(2,1)S(1)} %shard_map.55.rest_0_), channel_id=1, source_target_pairs={{0,1},{1,2},{2,3},{3,0},{4,5},{5,6},{6,7},{7,4},{8,9},{9,10},{10,1... | collective-permute-start | bytes 1179656 | tf_op jit(solution)/shard_map/ppermute | solution.py:25
  25.4 4.6 %collective-permute-start.4 = (bf16[768,256]{1,0:T(8,128)(2,1)S(1)}, bf16[768,256]{1,0:T(8,128)(2,1)S(1)}, u32[]{:S(2)}, u32[]{:S(2)}) collective-permute-start(bf16[768,256]{1,0:T(8,128)(2,1)S(1)} %shard_map.55.rest_0_), channel_id=1, source_target_pairs={{0,3},{1,0},{2,1},{3,2},{4,7},{5,4},{6,5},{7,6},{8,11},{9,8},{10,9... | collective-permute-start | bytes 1179656 | tf_op jit(solution)/shard_map/ppermute | solution.py:25
  29.9 4.3 %collective-permute-done.1.rest_1_ = bf16[768,256]{1,0:T(8,128)(2,1)S(1)} collective-permute-done((bf16[768,256]{1,0:T(8,128)(2,1)S(1)}, bf16[768,256]{1,0:T(8,128)(2,1)S(1)}, u32[]{:S(2)}, u32[]{:S(2)}) %collective-permute-start.1) | collective-permute-done | bytes 393248 | tf_op jit(solution)/shard_map/ppermute | solution.py:30
  37.1 4.0 %collective-permute-start.5 = (bf16[2,4096,256]{2,1,0:T(8,128)(2,1)}, bf16[2,4096,256]{2,1,0:T(8,128)(2,1)S(1)}, u32[]{:S(2)}, u32[]{:S(2)}) collective-permute-start(bf16[2,4096,256]{2,1,0:T(8,128)(2,1)} %bitcast.3), channel_id=1, source_target_pairs={{0,384},{384,0},{1,385},{385,1},{2,386},{386,2},{3,387},{387,3},{4... | collective-permute-start | bytes 12582920 | tf_op jit(solution)/shard_map/ppermute | solution.py:220
  41.3 5.3 %collective-permute-start.7 = (bf16[1536,256]{1,0:T(8,128)(2,1)S(1)}, bf16[1536,256]{1,0:T(8,128)(2,1)S(1)}, u32[]{:S(2)}, u32[]{:S(2)}) collective-permute-start(bf16[1536,256]{1,0:T(8,128)(2,1)S(1)} %pad_maximum_fusion.5), channel_id=1, source_target_pairs={{0,3},{1,0},{2,1},{3,2},{4,7},{5,4},{6,5},{7,6},{8,11},{9,8},{10,9... | collective-permute-start | bytes 2359304 | tf_op jit(solution)/shard_map/ppermute | solution.py:25
  46.7 2.2 %collective-permute-start.6 = (bf16[1536,256]{1,0:T(8,128)(2,1)S(1)}, bf16[1536,256]{1,0:T(8,128)(2,1)S(1)}, u32[]{:S(2)}, u32[]{:S(2)}) collective-permute-start(bf16[1536,256]{1,0:T(8,128)(2,1)S(1)} %pad_maximum_fusion.4), channel_id=1, source_target_pairs={{0,1},{1,2},{2,3},{3,0},{4,5},{5,6},{6,7},{7,4},{8,9},{9,10},{10,1... | collective-permute-start | bytes 2359304 | tf_op jit(solution)/shard_map/ppermute | solution.py:25
  49.0 1.9 %collective-permute-start.8 = (bf16[768,256]{1,0:T(8,128)(2,1)S(1)}, bf16[768,256]{1,0:T(8,128)(2,1)S(1)}, u32[]{:S(2)}, u32[]{:S(2)}) collective-permute-start(bf16[768,256]{1,0:T(8,128)(2,1)S(1)} %pad_maximum_fusion.6), channel_id=1, source_target_pairs={{0,4},{1,5},{2,6},{3,7},{4,8},{5,9},{6,10},{7,11},{8,12},{9,13},{1... | collective-permute-start | bytes 1179656 | tf_op jit(solution)/shard_map/ppermute | solution.py:30
  50.9 5.5 %collective-permute-start.9 = (bf16[768,256]{1,0:T(8,128)(2,1)S(1)}, bf16[768,256]{1,0:T(8,128)(2,1)S(1)}, u32[]{:S(2)}, u32[]{:S(2)}) collective-permute-start(bf16[768,256]{1,0:T(8,128)(2,1)S(1)} %pad_maximum_fusion.7), channel_id=1, source_target_pairs={{0,12},{1,13},{2,14},{3,15},{4,0},{5,1},{6,2},{7,3},{8,4},{9,5},{1... | collective-permute-start | bytes 1179656 | tf_op jit(solution)/shard_map/ppermute | solution.py:30
  57.3 9.1 %collective-permute-done.8.rest_2_ = bf16[768,256]{1,0:T(8,128)(2,1)S(1)} collective-permute-done((bf16[768,256]{1,0:T(8,128)(2,1)S(1)}, bf16[768,256]{1,0:T(8,128)(2,1)S(1)}, u32[]{:S(2)}, u32[]{:S(2)}) %collective-permute-start.8) | collective-permute-done | bytes 393248 | tf_op jit(solution)/shard_map/ppermute | solution.py:30
  66.4 4.0 %collective-permute-done.9.rest_3_ = bf16[768,256]{1,0:T(8,128)(2,1)S(1)} collective-permute-done((bf16[768,256]{1,0:T(8,128)(2,1)S(1)}, bf16[768,256]{1,0:T(8,128)(2,1)S(1)}, u32[]{:S(2)}, u32[]{:S(2)}) %collective-permute-start.9) | collective-permute-done | bytes 393248 | tf_op jit(solution)/shard_map/ppermute | solution.py:30
  70.6 1.9 %collective-permute-start.10 = (bf16[1536,256]{1,0:T(8,128)(2,1)S(1)}, bf16[1536,256]{1,0:T(8,128)(2,1)S(1)}, u32[]{:S(2)}, u32[]{:S(2)}) collective-permute-start(bf16[1536,256]{1,0:T(8,128)(2,1)S(1)} %get-tuple-element.78), channel_id=1, source_target_pairs={{0,1},{1,2},{2,3},{3,0},{4,5},{5,6},{6,7},{7,4},{8,9},{9,10},{10,1... | collective-permute-start | bytes 2359304 | tf_op jit(solution)/shard_map/ppermute | solution.py:25
  72.6 4.6 %collective-permute-start.11 = (bf16[1536,256]{1,0:T(8,128)(2,1)S(1)}, bf16[1536,256]{1,0:T(8,128)(2,1)S(1)}, u32[]{:S(2)}, u32[]{:S(2)}) collective-permute-start(bf16[1536,256]{1,0:T(8,128)(2,1)S(1)} %get-tuple-element.77), channel_id=1, source_target_pairs={{0,3},{1,0},{2,1},{3,2},{4,7},{5,4},{6,5},{7,6},{8,11},{9,8},{10,9... | collective-permute-start | bytes 2359304 | tf_op jit(solution)/shard_map/ppermute | solution.py:25
  77.2 3.1 %collective-permute-start.12 = (bf16[768,256]{1,0:T(8,128)(2,1)S(1)}, bf16[768,256]{1,0:T(8,128)(2,1)S(1)}, u32[]{:S(2)}, u32[]{:S(2)}) collective-permute-start(bf16[768,256]{1,0:T(8,128)(2,1)S(1)} %pad_maximum_fusion.8), channel_id=1, source_target_pairs={{0,2},{1,3},{2,0},{3,1},{4,6},{5,7},{6,4},{7,5},{8,10},{9,11},{10,... | collective-permute-start | bytes 1179656 | tf_op jit(solution)/shard_map/ppermute | solution.py:25
  81.3 20.6 %collective-permute-done.12.rest_2_ = bf16[768,256]{1,0:T(8,128)(2,1)S(1)} collective-permute-done((bf16[768,256]{1,0:T(8,128)(2,1)S(1)}, bf16[768,256]{1,0:T(8,128)(2,1)S(1)}, u32[]{:S(2)}, u32[]{:S(2)}) %collective-permute-start.12) | collective-permute-done | bytes 393248 | tf_op jit(solution)/shard_map/ppermute | solution.py:25
  102.8 2.3 %shard_map.59 = (bf16[1024,256]{1,0:T(8,128)(2,1)S(1)}, bf16[1024,256]{1,0:T(8,128)(2,1)S(1)}, bf16[512,256]{1,0:T(8,128)(2,1)S(1)}, bf16[4,256,256]{2,1,0:T(8,128)(2,1)S(1)}) custom-call(s32[2]{0:T(128)S(1)} %copy-done.3, s32[2]{0:T(128)S(1)} %copy-done.4, f32[4,256,256]{2,1,0:T(8,128)S(1)} %shard_map.58.t_ref, bf16[2,4096,256]{2,1,0:T(8,128)(2,1)S(1)} %bitcast.7, ...), custom_call_target="tpu_custom_call" | custom-call | flops 1006632960 | bytes 9437200 | tf_op jit(solution)/shard_map/pallas_call | solution.py:40
  105.1 4.4 %collective-permute-start.13 = (bf16[1024,256]{1,0:T(8,128)(2,1)S(1)}, bf16[1024,256]{1,0:T(8,128)(2,1)S(1)}, u32[]{:S(2)}, u32[]{:S(2)}) collective-permute-start(bf16[1024,256]{1,0:T(8,128)(2,1)S(1)} %get-tuple-element.59), channel_id=1, source_target_pairs={{0,1},{1,2},{2,3},{3,0},{4,5},{5,6},{6,7},{7,4},{8,9},{9,10},{10,1... | collective-permute-start | bytes 1572872 | tf_op jit(solution)/shard_map/ppermute | solution.py:25
  109.5 2.5 %collective-permute-start.14 = (bf16[1024,256]{1,0:T(8,128)(2,1)S(1)}, bf16[1024,256]{1,0:T(8,128)(2,1)S(1)}, u32[]{:S(2)}, u32[]{:S(2)}) collective-permute-start(bf16[1024,256]{1,0:T(8,128)(2,1)S(1)} %get-tuple-element.60), channel_id=1, source_target_pairs={{0,3},{1,0},{2,1},{3,2},{4,7},{5,4},{6,5},{7,6},{8,11},{9,8},{10,9... | collective-permute-start | bytes 1572872 | tf_op jit(solution)/shard_map/ppermute | solution.py:25
  112.1 3.1 %collective-permute-start.15 = (bf16[512,256]{1,0:T(8,128)(2,1)S(1)}, bf16[512,256]{1,0:T(8,128)(2,1)S(1)}, u32[]{:S(2)}, u32[]{:S(2)}) collective-permute-start(bf16[512,256]{1,0:T(8,128)(2,1)S(1)} %get-tuple-element.61), channel_id=1, source_target_pairs={{0,2},{1,3},{2,0},{3,1},{4,6},{5,7},{6,4},{7,5},{8,10},{9,11},{10,... | collective-permute-start | bytes 786440 | tf_op jit(solution)/shard_map/ppermute | solution.py:25
  115.2 1.7 shard_map.60
  116.9 10.3 %collective-permute-done.15.refs_5_ = bf16[512,256]{1,0:T(8,128)(2,1)S(1)} collective-permute-done((bf16[512,256]{1,0:T(8,128)(2,1)S(1)}, bf16[512,256]{1,0:T(8,128)(2,1)S(1)}, u32[]{:S(2)}, u32[]{:S(2)}) %collective-permute-start.15) | collective-permute-done | bytes 262176 | tf_op jit(solution)/shard_map/ppermute | solution.py:25
  127.5 4.4 %collective-permute-start.17 = (bf16[1280,256]{1,0:T(8,128)(2,1)S(1)}, bf16[1280,256]{1,0:T(8,128)(2,1)S(1)}, u32[]{:S(2)}, u32[]{:S(2)}) collective-permute-start(bf16[1280,256]{1,0:T(8,128)(2,1)S(1)} %get-tuple-element.67), channel_id=1, source_target_pairs={{0,1},{1,2},{2,3},{3,0},{4,5},{5,6},{6,7},{7,4},{8,9},{9,10},{10,1... | collective-permute-start | bytes 1966088 | tf_op jit(solution)/shard_map/ppermute | solution.py:25
  131.9 3.1 %collective-permute-start.18 = (bf16[1280,256]{1,0:T(8,128)(2,1)S(1)}, bf16[1280,256]{1,0:T(8,128)(2,1)S(1)}, u32[]{:S(2)}, u32[]{:S(2)}) collective-permute-start(bf16[1280,256]{1,0:T(8,128)(2,1)S(1)} %get-tuple-element.68), channel_id=1, source_target_pairs={{0,3},{1,0},{2,1},{3,2},{4,7},{5,4},{6,5},{7,6},{8,11},{9,8},{10,9... | collective-permute-start | bytes 1966088 | tf_op jit(solution)/shard_map/ppermute | solution.py:25
  135.0 2.1 %collective-permute-start.16 = (bf16[512,256]{1,0:T(8,128)(2,1)S(1)}, bf16[512,256]{1,0:T(8,128)(2,1)S(1)}, u32[]{:S(2)}, u32[]{:S(2)}) collective-permute-start(bf16[512,256]{1,0:T(8,128)(2,1)S(1)} %get-tuple-element.62), channel_id=1, source_target_pairs={{0,8},{1,9},{2,10},{3,11},{4,12},{5,13},{6,14},{7,15},{8,0},{9,1},... | collective-permute-start | bytes 786440 | tf_op jit(solution)/shard_map/ppermute | solution.py:30
  137.1 8.1 %collective-permute-done.17.refs_4_ = bf16[1280,256]{1,0:T(8,128)(2,1)S(1)} collective-permute-done((bf16[1280,256]{1,0:T(8,128)(2,1)S(1)}, bf16[1280,256]{1,0:T(8,128)(2,1)S(1)}, u32[]{:S(2)}, u32[]{:S(2)}) %collective-permute-start.17) | collective-permute-done | bytes 655392 | tf_op jit(solution)/shard_map/ppermute | solution.py:25
  147.1 2.3 %collective-permute-start.19 = (bf16[512,256]{1,0:T(8,128)(2,1)S(1)}, bf16[512,256]{1,0:T(8,128)(2,1)S(1)}, u32[]{:S(2)}, u32[]{:S(2)}) collective-permute-start(bf16[512,256]{1,0:T(8,128)(2,1)S(1)} %get-tuple-element.69), channel_id=1, source_target_pairs={{0,4},{1,5},{2,6},{3,7},{4,8},{5,9},{6,10},{7,11},{8,12},{9,13},{1... | collective-permute-start | bytes 786440 | tf_op jit(solution)/shard_map/ppermute | solution.py:30
  149.4 5.1 %collective-permute-start.20 = (bf16[512,256]{1,0:T(8,128)(2,1)S(1)}, bf16[512,256]{1,0:T(8,128)(2,1)S(1)}, u32[]{:S(2)}, u32[]{:S(2)}) collective-permute-start(bf16[512,256]{1,0:T(8,128)(2,1)S(1)} %get-tuple-element.70), channel_id=1, source_target_pairs={{0,12},{1,13},{2,14},{3,15},{4,0},{5,1},{6,2},{7,3},{8,4},{9,5},{1... | collective-permute-start | bytes 786440 | tf_op jit(solution)/shard_map/ppermute | solution.py:30
  154.5 2.8 %collective-permute-start.21 = (bf16[512,256]{1,0:T(8,128)(2,1)S(1)}, bf16[512,256]{1,0:T(8,128)(2,1)S(1)}, u32[]{:S(2)}, u32[]{:S(2)}) collective-permute-start(bf16[512,256]{1,0:T(8,128)(2,1)S(1)} %get-tuple-element.71), channel_id=1, source_target_pairs={{0,1},{1,2},{2,3},{3,0},{4,5},{5,6},{6,7},{7,4},{8,9},{9,10},{10,1... | collective-permute-start | bytes 786440 | tf_op jit(solution)/shard_map/ppermute | solution.py:25
  157.3 3.7 %collective-permute-start.22 = (bf16[512,256]{1,0:T(8,128)(2,1)S(1)}, bf16[512,256]{1,0:T(8,128)(2,1)S(1)}, u32[]{:S(2)}, u32[]{:S(2)}) collective-permute-start(bf16[512,256]{1,0:T(8,128)(2,1)S(1)} %get-tuple-element.72), channel_id=1, source_target_pairs={{0,3},{1,0},{2,1},{3,2},{4,7},{5,4},{6,5},{7,6},{8,11},{9,8},{10,9... | collective-permute-start | bytes 786440 | tf_op jit(solution)/shard_map/ppermute | solution.py:25
  164.8 7.4 %collective-permute-start.23 = (bf16[256,256]{1,0:T(8,128)(2,1)S(1)}, bf16[256,256]{1,0:T(8,128)(2,1)S(1)}, u32[]{:S(2)}, u32[]{:S(2)}) collective-permute-start(bf16[256,256]{1,0:T(8,128)(2,1)S(1)} %shard_map.63), channel_id=1, source_target_pairs={{0,384},{384,0},{1,385},{385,1},{2,386},{386,2},{3,387},{387,3},{4... | collective-permute-start | bytes 393224 | tf_op jit(solution)/shard_map/ppermute | solution.py:286
  (48 shorter events, 17.3 us)
Async XLA Ops:
  0.0 13.8 %collective-permute-start = (bf16[512,256]{1,0:T(8,128)(2,1)}, bf16[512,256]{1,0:T(8,128)(2,1)S(1)}, u32[]{:S(2)}, u32[]{:S(2)}) collective-permute-start(bf16[512,256]{1,0:T(8,128)(2,1)} %bitcast.9), channel_id=1, source_target_pairs={{0,384},{384,0},{1,385},{385,1},{2,386},{386,2},{3,387},{387,3},{4... | collective-permute-start | bytes 786440 | tf_op jit(solution)/shard_map/ppermute | solution.py:212
  13.8 0.9 copy-start.1
  14.7 0.9 copy-start.2
  16.0 18.2 %collective-permute-start.1 = (bf16[768,256]{1,0:T(8,128)(2,1)S(1)}, bf16[768,256]{1,0:T(8,128)(2,1)S(1)}, u32[]{:S(2)}, u32[]{:S(2)}) collective-permute-start(bf16[768,256]{1,0:T(8,128)(2,1)S(1)} %shard_map.55.rest_0_), channel_id=1, source_target_pairs={{0,4},{1,5},{2,6},{3,7},{4,8},{5,9},{6,10},{7,11},{8,12},{9,13},{1... | collective-permute-start | bytes 1179656 | tf_op jit(solution)/shard_map/ppermute | solution.py:30
  17.9 17.1 %collective-permute-start.2 = (bf16[768,256]{1,0:T(8,128)(2,1)S(1)}, bf16[768,256]{1,0:T(8,128)(2,1)S(1)}, u32[]{:S(2)}, u32[]{:S(2)}) collective-permute-start(bf16[768,256]{1,0:T(8,128)(2,1)S(1)} %shard_map.55.rest_0_), channel_id=1, source_target_pairs={{0,12},{1,13},{2,14},{3,15},{4,0},{5,1},{6,2},{7,3},{8,4},{9,5},{1... | collective-permute-start | bytes 1179656 | tf_op jit(solution)/shard_map/ppermute | solution.py:30
  23.4 12.8 %collective-permute-start.3 = (bf16[768,256]{1,0:T(8,128)(2,1)S(1)}, bf16[768,256]{1,0:T(8,128)(2,1)S(1)}, u32[]{:S(2)}, u32[]{:S(2)}) collective-permute-start(bf16[768,256]{1,0:T(8,128)(2,1)S(1)} %shard_map.55.rest_0_), channel_id=1, source_target_pairs={{0,1},{1,2},{2,3},{3,0},{4,5},{5,6},{6,7},{7,4},{8,9},{9,10},{10,1... | collective-permute-start | bytes 1179656 | tf_op jit(solution)/shard_map/ppermute | solution.py:25
  25.4 11.7 %collective-permute-start.4 = (bf16[768,256]{1,0:T(8,128)(2,1)S(1)}, bf16[768,256]{1,0:T(8,128)(2,1)S(1)}, u32[]{:S(2)}, u32[]{:S(2)}) collective-permute-start(bf16[768,256]{1,0:T(8,128)(2,1)S(1)} %shard_map.55.rest_0_), channel_id=1, source_target_pairs={{0,3},{1,0},{2,1},{3,2},{4,7},{5,4},{6,5},{7,6},{8,11},{9,8},{10,9... | collective-permute-start | bytes 1179656 | tf_op jit(solution)/shard_map/ppermute | solution.py:25
  37.1 19.3 %collective-permute-start.5 = (bf16[2,4096,256]{2,1,0:T(8,128)(2,1)}, bf16[2,4096,256]{2,1,0:T(8,128)(2,1)S(1)}, u32[]{:S(2)}, u32[]{:S(2)}) collective-permute-start(bf16[2,4096,256]{2,1,0:T(8,128)(2,1)} %bitcast.3), channel_id=1, source_target_pairs={{0,384},{384,0},{1,385},{385,1},{2,386},{386,2},{3,387},{387,3},{4... | collective-permute-start | bytes 12582920 | tf_op jit(solution)/shard_map/ppermute | solution.py:220
  41.3 29.1 %collective-permute-start.7 = (bf16[1536,256]{1,0:T(8,128)(2,1)S(1)}, bf16[1536,256]{1,0:T(8,128)(2,1)S(1)}, u32[]{:S(2)}, u32[]{:S(2)}) collective-permute-start(bf16[1536,256]{1,0:T(8,128)(2,1)S(1)} %pad_maximum_fusion.5), channel_id=1, source_target_pairs={{0,3},{1,0},{2,1},{3,2},{4,7},{5,4},{6,5},{7,6},{8,11},{9,8},{10,9... | collective-permute-start | bytes 2359304 | tf_op jit(solution)/shard_map/ppermute | solution.py:25
  46.6 9.8 %copy-start = (bf16[1,2,4096,256]{3,2,1,0:T(8,128)(2,1)S(1)}, bf16[1,2,4096,256]{3,2,1,0:T(8,128)(2,1)}, u32[]{:S(2)}) copy-start(bf16[1,2,4096,256]{3,2,1,0:T(8,128)(2,1)} %param.6) | copy-start | bytes 12582916
  46.7 23.7 %collective-permute-start.6 = (bf16[1536,256]{1,0:T(8,128)(2,1)S(1)}, bf16[1536,256]{1,0:T(8,128)(2,1)S(1)}, u32[]{:S(2)}, u32[]{:S(2)}) collective-permute-start(bf16[1536,256]{1,0:T(8,128)(2,1)S(1)} %pad_maximum_fusion.4), channel_id=1, source_target_pairs={{0,1},{1,2},{2,3},{3,0},{4,5},{5,6},{6,7},{7,4},{8,9},{9,10},{10,1... | collective-permute-start | bytes 2359304 | tf_op jit(solution)/shard_map/ppermute | solution.py:25
  49.0 17.4 %collective-permute-start.8 = (bf16[768,256]{1,0:T(8,128)(2,1)S(1)}, bf16[768,256]{1,0:T(8,128)(2,1)S(1)}, u32[]{:S(2)}, u32[]{:S(2)}) collective-permute-start(bf16[768,256]{1,0:T(8,128)(2,1)S(1)} %pad_maximum_fusion.6), channel_id=1, source_target_pairs={{0,4},{1,5},{2,6},{3,7},{4,8},{5,9},{6,10},{7,11},{8,12},{9,13},{1... | collective-permute-start | bytes 1179656 | tf_op jit(solution)/shard_map/ppermute | solution.py:30
  50.9 19.5 %collective-permute-start.9 = (bf16[768,256]{1,0:T(8,128)(2,1)S(1)}, bf16[768,256]{1,0:T(8,128)(2,1)S(1)}, u32[]{:S(2)}, u32[]{:S(2)}) collective-permute-start(bf16[768,256]{1,0:T(8,128)(2,1)S(1)} %pad_maximum_fusion.7), channel_id=1, source_target_pairs={{0,12},{1,13},{2,14},{3,15},{4,0},{5,1},{6,2},{7,3},{8,4},{9,5},{1... | collective-permute-start | bytes 1179656 | tf_op jit(solution)/shard_map/ppermute | solution.py:30
  70.6 31.3 %collective-permute-start.10 = (bf16[1536,256]{1,0:T(8,128)(2,1)S(1)}, bf16[1536,256]{1,0:T(8,128)(2,1)S(1)}, u32[]{:S(2)}, u32[]{:S(2)}) collective-permute-start(bf16[1536,256]{1,0:T(8,128)(2,1)S(1)} %get-tuple-element.78), channel_id=1, source_target_pairs={{0,1},{1,2},{2,3},{3,0},{4,5},{5,6},{6,7},{7,4},{8,9},{9,10},{10,1... | collective-permute-start | bytes 2359304 | tf_op jit(solution)/shard_map/ppermute | solution.py:25
  72.6 29.4 %collective-permute-start.11 = (bf16[1536,256]{1,0:T(8,128)(2,1)S(1)}, bf16[1536,256]{1,0:T(8,128)(2,1)S(1)}, u32[]{:S(2)}, u32[]{:S(2)}) collective-permute-start(bf16[1536,256]{1,0:T(8,128)(2,1)S(1)} %get-tuple-element.77), channel_id=1, source_target_pairs={{0,3},{1,0},{2,1},{3,2},{4,7},{5,4},{6,5},{7,6},{8,11},{9,8},{10,9... | collective-permute-start | bytes 2359304 | tf_op jit(solution)/shard_map/ppermute | solution.py:25
  77.2 24.8 %collective-permute-start.12 = (bf16[768,256]{1,0:T(8,128)(2,1)S(1)}, bf16[768,256]{1,0:T(8,128)(2,1)S(1)}, u32[]{:S(2)}, u32[]{:S(2)}) collective-permute-start(bf16[768,256]{1,0:T(8,128)(2,1)S(1)} %pad_maximum_fusion.8), channel_id=1, source_target_pairs={{0,2},{1,3},{2,0},{3,1},{4,6},{5,7},{6,4},{7,5},{8,10},{9,11},{10,... | collective-permute-start | bytes 1179656 | tf_op jit(solution)/shard_map/ppermute | solution.py:25
  81.3 21.5 %copy-start.3 = (s32[2]{0:T(128)S(1)}, s32[2]{0:T(128)}, u32[]{:S(2)}) copy-start(s32[2]{0:T(128)} %enc_ref.1) | copy-start | bytes 28
  81.3 21.5 %copy-start.4 = (s32[2]{0:T(128)S(1)}, s32[2]{0:T(128)}, u32[]{:S(2)}) copy-start(s32[2]{0:T(128)} %dec_ref.1) | copy-start | bytes 28
  105.1 22.1 %collective-permute-start.13 = (bf16[1024,256]{1,0:T(8,128)(2,1)S(1)}, bf16[1024,256]{1,0:T(8,128)(2,1)S(1)}, u32[]{:S(2)}, u32[]{:S(2)}) collective-permute-start(bf16[1024,256]{1,0:T(8,128)(2,1)S(1)} %get-tuple-element.59), channel_id=1, source_target_pairs={{0,1},{1,2},{2,3},{3,0},{4,5},{5,6},{6,7},{7,4},{8,9},{9,10},{10,1... | collective-permute-start | bytes 1572872 | tf_op jit(solution)/shard_map/ppermute | solution.py:25
  109.5 17.7 %collective-permute-start.14 = (bf16[1024,256]{1,0:T(8,128)(2,1)S(1)}, bf16[1024,256]{1,0:T(8,128)(2,1)S(1)}, u32[]{:S(2)}, u32[]{:S(2)}) collective-permute-start(bf16[1024,256]{1,0:T(8,128)(2,1)S(1)} %get-tuple-element.60), channel_id=1, source_target_pairs={{0,3},{1,0},{2,1},{3,2},{4,7},{5,4},{6,5},{7,6},{8,11},{9,8},{10,9... | collective-permute-start | bytes 1572872 | tf_op jit(solution)/shard_map/ppermute | solution.py:25
  112.1 15.1 %collective-permute-start.15 = (bf16[512,256]{1,0:T(8,128)(2,1)S(1)}, bf16[512,256]{1,0:T(8,128)(2,1)S(1)}, u32[]{:S(2)}, u32[]{:S(2)}) collective-permute-start(bf16[512,256]{1,0:T(8,128)(2,1)S(1)} %get-tuple-element.61), channel_id=1, source_target_pairs={{0,2},{1,3},{2,0},{3,1},{4,6},{5,7},{6,4},{7,5},{8,10},{9,11},{10,... | collective-permute-start | bytes 786440 | tf_op jit(solution)/shard_map/ppermute | solution.py:25
  127.5 17.7 %collective-permute-start.17 = (bf16[1280,256]{1,0:T(8,128)(2,1)S(1)}, bf16[1280,256]{1,0:T(8,128)(2,1)S(1)}, u32[]{:S(2)}, u32[]{:S(2)}) collective-permute-start(bf16[1280,256]{1,0:T(8,128)(2,1)S(1)} %get-tuple-element.67), channel_id=1, source_target_pairs={{0,1},{1,2},{2,3},{3,0},{4,5},{5,6},{6,7},{7,4},{8,9},{9,10},{10,1... | collective-permute-start | bytes 1966088 | tf_op jit(solution)/shard_map/ppermute | solution.py:25
  131.9 15.0 %collective-permute-start.18 = (bf16[1280,256]{1,0:T(8,128)(2,1)S(1)}, bf16[1280,256]{1,0:T(8,128)(2,1)S(1)}, u32[]{:S(2)}, u32[]{:S(2)}) collective-permute-start(bf16[1280,256]{1,0:T(8,128)(2,1)S(1)} %get-tuple-element.68), channel_id=1, source_target_pairs={{0,3},{1,0},{2,1},{3,2},{4,7},{5,4},{6,5},{7,6},{8,11},{9,8},{10,9... | collective-permute-start | bytes 1966088 | tf_op jit(solution)/shard_map/ppermute | solution.py:25
  135.0 26.0 %collective-permute-start.16 = (bf16[512,256]{1,0:T(8,128)(2,1)S(1)}, bf16[512,256]{1,0:T(8,128)(2,1)S(1)}, u32[]{:S(2)}, u32[]{:S(2)}) collective-permute-start(bf16[512,256]{1,0:T(8,128)(2,1)S(1)} %get-tuple-element.62), channel_id=1, source_target_pairs={{0,8},{1,9},{2,10},{3,11},{4,12},{5,13},{6,14},{7,15},{8,0},{9,1},... | collective-permute-start | bytes 786440 | tf_op jit(solution)/shard_map/ppermute | solution.py:30
  147.1 15.1 %collective-permute-start.19 = (bf16[512,256]{1,0:T(8,128)(2,1)S(1)}, bf16[512,256]{1,0:T(8,128)(2,1)S(1)}, u32[]{:S(2)}, u32[]{:S(2)}) collective-permute-start(bf16[512,256]{1,0:T(8,128)(2,1)S(1)} %get-tuple-element.69), channel_id=1, source_target_pairs={{0,4},{1,5},{2,6},{3,7},{4,8},{5,9},{6,10},{7,11},{8,12},{9,13},{1... | collective-permute-start | bytes 786440 | tf_op jit(solution)/shard_map/ppermute | solution.py:30
  149.4 12.7 %collective-permute-start.20 = (bf16[512,256]{1,0:T(8,128)(2,1)S(1)}, bf16[512,256]{1,0:T(8,128)(2,1)S(1)}, u32[]{:S(2)}, u32[]{:S(2)}) collective-permute-start(bf16[512,256]{1,0:T(8,128)(2,1)S(1)} %get-tuple-element.70), channel_id=1, source_target_pairs={{0,12},{1,13},{2,14},{3,15},{4,0},{5,1},{6,2},{7,3},{8,4},{9,5},{1... | collective-permute-start | bytes 786440 | tf_op jit(solution)/shard_map/ppermute | solution.py:30
  154.5 8.6 %collective-permute-start.21 = (bf16[512,256]{1,0:T(8,128)(2,1)S(1)}, bf16[512,256]{1,0:T(8,128)(2,1)S(1)}, u32[]{:S(2)}, u32[]{:S(2)}) collective-permute-start(bf16[512,256]{1,0:T(8,128)(2,1)S(1)} %get-tuple-element.71), channel_id=1, source_target_pairs={{0,1},{1,2},{2,3},{3,0},{4,5},{5,6},{6,7},{7,4},{8,9},{9,10},{10,1... | collective-permute-start | bytes 786440 | tf_op jit(solution)/shard_map/ppermute | solution.py:25
  157.3 7.4 %collective-permute-start.22 = (bf16[512,256]{1,0:T(8,128)(2,1)S(1)}, bf16[512,256]{1,0:T(8,128)(2,1)S(1)}, u32[]{:S(2)}, u32[]{:S(2)}) collective-permute-start(bf16[512,256]{1,0:T(8,128)(2,1)S(1)} %get-tuple-element.72), channel_id=1, source_target_pairs={{0,3},{1,0},{2,1},{3,2},{4,7},{5,4},{6,5},{7,6},{8,11},{9,8},{10,9... | collective-permute-start | bytes 786440 | tf_op jit(solution)/shard_map/ppermute | solution.py:25
  164.8 8.4 %collective-permute-start.23 = (bf16[256,256]{1,0:T(8,128)(2,1)S(1)}, bf16[256,256]{1,0:T(8,128)(2,1)S(1)}, u32[]{:S(2)}, u32[]{:S(2)}) collective-permute-start(bf16[256,256]{1,0:T(8,128)(2,1)S(1)} %shard_map.63), channel_id=1, source_target_pairs={{0,384},{384,0},{1,385},{385,1},{2,386},{386,2},{3,387},{387,3},{4... | collective-permute-start | bytes 393224 | tf_op jit(solution)/shard_map/ppermute | solution.py:286

commit v7 on v6

--- a/solution.py
+++ b/solution.py
@@ -9,6 +9,8 @@
 SIDE = 4
 ROWS = 3 * HS
 HALF = ROWS // 2
+REST = ROWS // 4
+MOST = ROWS - REST
 N = 2 * HS
 F32 = jnp.float32
 BF16 = jnp.bfloat16
@@ -58,28 +60,23 @@
     return pl.ds(pl.multiple_of(index * HS, HS), HS)
 
 
-def assemble(own, cotangent, partner):
-    def body(own_ref, cot_ref, partner_ref, out_ref, sems):
+def local_rows(own, cotangent):
+    def body(own_ref, cot_ref, out_ref):
+        here = slot_rows(lax.axis_index("section"))
+        out_ref[:HS, :] = own_ref[here, :]
+        out_ref[HS:, :] = cot_ref[here, :]
+
+    return call(body, [own, cotangent], [(N, HS)])[0]
+
+
+def assemble(local, partner):
+    def body(local_ref, partner_ref, out_ref):
         sec = lax.axis_index("section")
-        here = slot_rows(sec)
-        copies = [
-            pltpu.make_async_copy(own_ref.at[here, :], out_ref.at[pl.ds(0, HS), :], sems.at[0]),
-            pltpu.make_async_copy(cot_ref.at[here, :], out_ref.at[slot_rows(2 - sec), :], sems.at[1]),
-        ]
-        for copy in copies:
-            copy.start()
-        out_ref[slot_rows(1 + sec), :] = partner_ref[here, :]
-        for copy in copies:
-            copy.wait()
-
-    return pl.pallas_call(
-        body,
-        out_shape=jax.ShapeDtypeStruct((ROWS, HS), BF16),
-        in_specs=[pl.BlockSpec(memory_space=pltpu.HBM)] * 2 + [VMEM],
-        out_specs=VMEM,
-        scratch_shapes=[pltpu.SemaphoreType.DMA((2,))],
-        compiler_params=pltpu.CompilerParams(vmem_limit_bytes=VMEM_LIMIT),
-    )(own, cotangent, partner)
+        out_ref[:HS, :] = local_ref[:HS, :]
+        out_ref[slot_rows(2 - sec), :] = local_ref[HS:, :]
+        out_ref[slot_rows(1 + sec), :] = partner_ref[slot_rows(sec), :]
+
+    return call(body, [local, partner], [(ROWS, HS)])[0]
 
 
 def rows_of(refs, block, low, high):
@@ -210,7 +207,7 @@
 def local(states, proj_weights, out_cotangent, enc_lengths, dec_lengths):
     own = states[0]
     partner = lax.ppermute(own, "section", SWAP)
-    c0 = assemble(own, out_cotangent, partner)
+    c0 = assemble(local_rows(own, out_cotangent), partner)
 
     up1, down1 = shift_y(c0, 1), shift_y(c0, -1)
     right0, left0 = shift_x(c0, 1), shift_x(c0, -1)
@@ -234,8 +231,9 @@
     right1, left1, up2, down2, total = lax.optimization_barrier((right1, left1, up2, down2, total))
 
     last = join(up2[:HALF], down2[:HALF])
-    right2 = shift_x(join(right1[HALF:ROWS], right1[ROWS + HALF :], last), 1)
-    left2 = shift_x(join(left1[HALF:ROWS], left1[ROWS + HALF :], last), -1)
+    right2 = shift_x(join(right1[HALF : HALF + MOST], right1[ROWS + HALF :], down2[HALF : HALF + REST]), 1)
+    left2 = shift_x(join(left1[HALF + REST : ROWS], left1[ROWS + MOST :], last), -1)
+    up3, down3 = shift_y(right1[HALF:ROWS], 1), shift_y(down2[HALF:], -1)
     across2 = shift_x(last, 2)
     total = project(
         [right1, left1, up2, down2],
@@ -246,12 +244,14 @@
         ],
         own_w, other_w, total,
     )
-    right2, left2, across2, total = lax.optimization_barrier((right2, left2, across2, total))
+    right2, left2, across2, up3, down3, total = lax.optimization_barrier(
+        (right2, left2, across2, up3, down3, total)
+    )
     total = project(
-        [right2, left2, across2],
-        [
-            ((-1, 2), [(0, 0, HALF), (1, 0, HALF)]), ((1, 2), [(0, HALF, HALF), (1, HALF, HALF)]),
-            ((2, -1), [(0, ROWS, ROWS)]), ((2, 1), [(1, ROWS, ROWS)]), ((2, 2), [(2, 0, ROWS)]),
+        [right2, left2, across2, up3, down3],
+        [
+            ((-1, 2), [(0, 0, MOST), (1, 0, REST)]), ((1, 2), [(0, MOST, MOST), (1, REST, REST)]),
+            ((2, -1), [(3, 0, HALF), (4, 0, HALF)]), ((2, 1), [(1, 2 * REST, ROWS)]), ((2, 2), [(2, 0, ROWS)]),
         ],
         own_w, other_w, total,
     )

time: 175 us -> 168 us (0.960)
  waiting for transfers between devices: 67 us -> 49.8 us
  starting transfers between devices: 95.7 us -> 106 us
    ppermute x14, waiting for transfers between devices: 45.3 us -> 21 us  [shift_x(): return lax.ppermute(block, 'mp', route)]
    ppermute x7 -> x9, starting transfers between devices: 24.2 us -> 35 us  [shift_y(): return lax.ppermute(block, 'mp', route)]
    ppermute x7 -> x9, waiting for transfers between devices: 19.3 us -> 27.9 us  [shift_y(): return lax.ppermute(block, 'mp', route)]
    ppermute x1, starting transfers between devices: 7.41 us -> 9.58 us  [local(): swapped = lax.ppermute(sent, 'section', SWAP)]
    ppermute x14, starting transfers between devices: 47.6 us -> 45.5 us  [shift_x(): return lax.ppermute(block, 'mp', route)]
    pallas_call x9 -> x11, Pallas kernels: 8.15 us -> 8.2 us  [call(): pl.pallas_call(body, out_shape=out, in_specs=[SMEM] * scalars + [VMEM] *...]
  transfers between devices with their start and end apart: 24 -> 26, of which waited for: 15 -> 13; matrix products, arithmetic and copies ran while one was open for 0% -> 0% of each run, Pallas kernels for 2% -> 2%
where the time goes in v7:
time: 168 us; the launch traced here: 167 us
  starting transfers between devices  106 us (63%)
  waiting for transfers between devices  49.8 us (30%)
  Pallas kernels  8.2 us (5%)
  local copies, waits for them, and re-layouts  2.13 us (1%)
    ppermute x14, starting transfers between devices, shift_x(): return lax.ppermute(block, 'mp', route)  45.5 us
    ppermute x9, starting transfers between devices, shift_y(): return lax.ppermute(block, 'mp', route)  35 us
    ppermute x9, waiting for transfers between devices, shift_y(): return lax.ppermute(block, 'mp', route)  27.9 us
    ppermute x14, waiting for transfers between devices, shift_x(): return lax.ppermute(block, 'mp', route)  21 us
    ppermute x1, starting transfers between devices, local(): partner = lax.ppermute(own, 'section', SWAP)  12.4 us
    ppermute x1, starting transfers between devices, local(): swapped = lax.ppermute(sent, 'section', SWAP)  9.58 us
    pallas_call x11, Pallas kernels, call(): pl.pallas_call(body, out_shape=out, in_specs=[SMEM] * scalars + [VMEM] *...  8.2 us
    ppermute x1, starting transfers between devices, local(): other_w = lax.ppermute(own_w, 'section', SWAP)  3.65 us
  transfers between devices with their start and end apart: 26, of which 13 were waited for; matrix products, arithmetic and copies ran while one was open for 0% of the time, Pallas kernels for 2%

profile of v7, /device:TPU:1, one launch (start us, length us, event | category | flops | bytes accessed | tf_op | source)
XLA Modules:
  0.0 167.1 jit_solution(11731585191285910223)
XLA Ops:
  0.0 12.4 %collective-permute-start = (bf16[512,256]{1,0:T(8,128)(2,1)}, bf16[512,256]{1,0:T(8,128)(2,1)S(1)}, u32[]{:S(2)}, u32[]{:S(2)}) collective-permute-start(bf16[512,256]{1,0:T(8,128)(2,1)} %bitcast.9), channel_id=1, source_target_pairs={{0,384},{384,0},{1,385},{385,1},{2,386},{386,2},{3,387},{387,3},{4... | collective-permute-start | bytes 786440 | tf_op jit(solution)/shard_map/ppermute | solution.py:209
  14.4 1.9 %collective-permute-start.1 = (bf16[768,256]{1,0:T(8,128)(2,1)S(1)}, bf16[768,256]{1,0:T(8,128)(2,1)S(1)}, u32[]{:S(2)}, u32[]{:S(2)}) collective-permute-start(bf16[768,256]{1,0:T(8,128)(2,1)S(1)} %shard_map.56.rest_0_), channel_id=1, source_target_pairs={{0,4},{1,5},{2,6},{3,7},{4,8},{5,9},{6,10},{7,11},{8,12},{9,13},{1... | collective-permute-start | bytes 1179656 | tf_op jit(solution)/shard_map/ppermute | solution.py:32
  16.3 5.5 %collective-permute-start.2 = (bf16[768,256]{1,0:T(8,128)(2,1)S(1)}, bf16[768,256]{1,0:T(8,128)(2,1)S(1)}, u32[]{:S(2)}, u32[]{:S(2)}) collective-permute-start(bf16[768,256]{1,0:T(8,128)(2,1)S(1)} %shard_map.56.rest_0_), channel_id=1, source_target_pairs={{0,12},{1,13},{2,14},{3,15},{4,0},{5,1},{6,2},{7,3},{8,4},{9,5},{1... | collective-permute-start | bytes 1179656 | tf_op jit(solution)/shard_map/ppermute | solution.py:32
  21.8 1.9 %collective-permute-start.3 = (bf16[768,256]{1,0:T(8,128)(2,1)S(1)}, bf16[768,256]{1,0:T(8,128)(2,1)S(1)}, u32[]{:S(2)}, u32[]{:S(2)}) collective-permute-start(bf16[768,256]{1,0:T(8,128)(2,1)S(1)} %shard_map.56.rest_0_), channel_id=1, source_target_pairs={{0,1},{1,2},{2,3},{3,0},{4,5},{5,6},{6,7},{7,4},{8,9},{9,10},{10,1... | collective-permute-start | bytes 1179656 | tf_op jit(solution)/shard_map/ppermute | solution.py:27
  23.7 4.6 %collective-permute-start.4 = (bf16[768,256]{1,0:T(8,128)(2,1)S(1)}, bf16[768,256]{1,0:T(8,128)(2,1)S(1)}, u32[]{:S(2)}, u32[]{:S(2)}) collective-permute-start(bf16[768,256]{1,0:T(8,128)(2,1)S(1)} %shard_map.56.rest_0_), channel_id=1, source_target_pairs={{0,3},{1,0},{2,1},{3,2},{4,7},{5,4},{6,5},{7,6},{8,11},{9,8},{10,9... | collective-permute-start | bytes 1179656 | tf_op jit(solution)/shard_map/ppermute | solution.py:27
  28.3 4.3 %collective-permute-done.1.rest_1_ = bf16[768,256]{1,0:T(8,128)(2,1)S(1)} collective-permute-done((bf16[768,256]{1,0:T(8,128)(2,1)S(1)}, bf16[768,256]{1,0:T(8,128)(2,1)S(1)}, u32[]{:S(2)}, u32[]{:S(2)}) %collective-permute-start.1) | collective-permute-done | bytes 393248 | tf_op jit(solution)/shard_map/ppermute | solution.py:32
  35.9 3.7 %collective-permute-start.5 = (bf16[2,4096,256]{2,1,0:T(8,128)(2,1)}, bf16[2,4096,256]{2,1,0:T(8,128)(2,1)S(1)}, u32[]{:S(2)}, u32[]{:S(2)}) collective-permute-start(bf16[2,4096,256]{2,1,0:T(8,128)(2,1)} %bitcast.3), channel_id=1, source_target_pairs={{0,384},{384,0},{1,385},{385,1},{2,386},{386,2},{3,387},{387,3},{4... | collective-permute-start | bytes 12582920 | tf_op jit(solution)/shard_map/ppermute | solution.py:217
  39.6 5.3 %collective-permute-start.7 = (bf16[1536,256]{1,0:T(8,128)(2,1)S(1)}, bf16[1536,256]{1,0:T(8,128)(2,1)S(1)}, u32[]{:S(2)}, u32[]{:S(2)}) collective-permute-start(bf16[1536,256]{1,0:T(8,128)(2,1)S(1)} %pad_maximum_fusion.1), channel_id=1, source_target_pairs={{0,3},{1,0},{2,1},{3,2},{4,7},{5,4},{6,5},{7,6},{8,11},{9,8},{10,9... | collective-permute-start | bytes 2359304 | tf_op jit(solution)/shard_map/ppermute | solution.py:27
  45.1 2.2 %collective-permute-start.6 = (bf16[1536,256]{1,0:T(8,128)(2,1)S(1)}, bf16[1536,256]{1,0:T(8,128)(2,1)S(1)}, u32[]{:S(2)}, u32[]{:S(2)}) collective-permute-start(bf16[1536,256]{1,0:T(8,128)(2,1)S(1)} %pad_maximum_fusion), channel_id=1, source_target_pairs={{0,1},{1,2},{2,3},{3,0},{4,5},{5,6},{6,7},{7,4},{8,9},{9,10},{10,1... | collective-permute-start | bytes 2359304 | tf_op jit(solution)/shard_map/ppermute | solution.py:27
  47.3 1.9 %collective-permute-start.9 = (bf16[768,256]{1,0:T(8,128)(2,1)S(1)}, bf16[768,256]{1,0:T(8,128)(2,1)S(1)}, u32[]{:S(2)}, u32[]{:S(2)}) collective-permute-start(bf16[768,256]{1,0:T(8,128)(2,1)S(1)} %pad_maximum_fusion.5), channel_id=1, source_target_pairs={{0,12},{1,13},{2,14},{3,15},{4,0},{5,1},{6,2},{7,3},{8,4},{9,5},{1... | collective-permute-start | bytes 1179656 | tf_op jit(solution)/shard_map/ppermute | solution.py:32
  49.3 4.3 %collective-permute-start.8 = (bf16[768,256]{1,0:T(8,128)(2,1)S(1)}, bf16[768,256]{1,0:T(8,128)(2,1)S(1)}, u32[]{:S(2)}, u32[]{:S(2)}) collective-permute-start(bf16[768,256]{1,0:T(8,128)(2,1)S(1)} %pad_maximum_fusion.4), channel_id=1, source_target_pairs={{0,4},{1,5},{2,6},{3,7},{4,8},{5,9},{6,10},{7,11},{8,12},{9,13},{1... | collective-permute-start | bytes 1179656 | tf_op jit(solution)/shard_map/ppermute | solution.py:32
  54.5 11.4 %collective-permute-done.9.rest_3_ = bf16[768,256]{1,0:T(8,128)(2,1)S(1)} collective-permute-done((bf16[768,256]{1,0:T(8,128)(2,1)S(1)}, bf16[768,256]{1,0:T(8,128)(2,1)S(1)}, u32[]{:S(2)}, u32[]{:S(2)}) %collective-permute-start.9) | collective-permute-done | bytes 393248 | tf_op jit(solution)/shard_map/ppermute | solution.py:32
  65.8 4.9 %collective-permute-done.8.rest_2_ = bf16[768,256]{1,0:T(8,128)(2,1)S(1)} collective-permute-done((bf16[768,256]{1,0:T(8,128)(2,1)S(1)}, bf16[768,256]{1,0:T(8,128)(2,1)S(1)}, u32[]{:S(2)}, u32[]{:S(2)}) %collective-permute-start.8) | collective-permute-done | bytes 393248 | tf_op jit(solution)/shard_map/ppermute | solution.py:32
  70.9 4.5 %collective-permute-start.11 = (bf16[1152,256]{1,0:T(8,128)(2,1)S(1)}, bf16[1152,256]{1,0:T(8,128)(2,1)S(1)}, u32[]{:S(2)}, u32[]{:S(2)}) collective-permute-start(bf16[1152,256]{1,0:T(8,128)(2,1)S(1)} %pad_maximum_fusion.3), channel_id=1, source_target_pairs={{0,3},{1,0},{2,1},{3,2},{4,7},{5,4},{6,5},{7,6},{8,11},{9,8},{10,9... | collective-permute-start | bytes 1769480 | tf_op jit(solution)/shard_map/ppermute | solution.py:27
  75.5 1.9 %collective-permute-start.10 = (bf16[1152,256]{1,0:T(8,128)(2,1)S(1)}, bf16[1152,256]{1,0:T(8,128)(2,1)S(1)}, u32[]{:S(2)}, u32[]{:S(2)}) collective-permute-start(bf16[1152,256]{1,0:T(8,128)(2,1)S(1)} %pad_maximum_fusion.2), channel_id=1, source_target_pairs={{0,1},{1,2},{2,3},{3,0},{4,5},{5,6},{6,7},{7,4},{8,9},{9,10},{10,1... | collective-permute-start | bytes 1769480 | tf_op jit(solution)/shard_map/ppermute | solution.py:27
  77.5 3.1 %collective-permute-start.12 = (bf16[768,256]{1,0:T(8,128)(2,1)S(1)}, bf16[768,256]{1,0:T(8,128)(2,1)S(1)}, u32[]{:S(2)}, u32[]{:S(2)}) collective-permute-start(bf16[768,256]{1,0:T(8,128)(2,1)S(1)} %pad_maximum_fusion.6), channel_id=1, source_target_pairs={{0,2},{1,3},{2,0},{3,1},{4,6},{5,7},{6,4},{7,5},{8,10},{9,11},{10,... | collective-permute-start | bytes 1179656 | tf_op jit(solution)/shard_map/ppermute | solution.py:27
  82.5 5.5 %collective-permute-start.14 = (bf16[384,256]{1,0:T(8,128)(2,1)S(1)}, bf16[384,256]{1,0:T(8,128)(2,1)S(1)}, u32[]{:S(2)}, u32[]{:S(2)}) collective-permute-start(bf16[384,256]{1,0:T(8,128)(2,1)S(1)} %get-tuple-element.81), channel_id=1, source_target_pairs={{0,12},{1,13},{2,14},{3,15},{4,0},{5,1},{6,2},{7,3},{8,4},{9,5},{1... | collective-permute-start | bytes 589832 | tf_op jit(solution)/shard_map/ppermute | solution.py:32
  89.0 2.5 %collective-permute-done.13.rest_3_ = bf16[384,256]{1,0:T(8,128)(2,1)S(1)} collective-permute-done((bf16[384,256]{1,0:T(8,128)(2,1)S(1)}, bf16[384,256]{1,0:T(8,128)(2,1)S(1)}, u32[]{:S(2)}, u32[]{:S(2)}) %collective-permute-start.13) | collective-permute-done | bytes 196640 | tf_op jit(solution)/shard_map/ppermute | solution.py:32
  92.1 7.0 %collective-permute-done.12.rest_2_ = bf16[768,256]{1,0:T(8,128)(2,1)S(1)} collective-permute-done((bf16[768,256]{1,0:T(8,128)(2,1)S(1)}, bf16[768,256]{1,0:T(8,128)(2,1)S(1)}, u32[]{:S(2)}, u32[]{:S(2)}) %collective-permute-start.12) | collective-permute-done | bytes 393248 | tf_op jit(solution)/shard_map/ppermute | solution.py:27
  100.0 2.3 %shard_map.60 = (bf16[1024,256]{1,0:T(8,128)(2,1)S(1)}, bf16[1024,256]{1,0:T(8,128)(2,1)S(1)}, bf16[512,256]{1,0:T(8,128)(2,1)S(1)}, bf16[4,256,256]{2,1,0:T(8,128)(2,1)S(1)}) custom-call(s32[2]{0:T(128)S(1)} %copy-done.3, s32[2]{0:T(128)S(1)} %copy-done.4, f32[4,256,256]{2,1,0:T(8,128)S(1)} %shard_map.59.t_ref, bf16[2,4096,256]{2,1,0:T(8,128)(2,1)S(1)} %bitcast.7, ...), custom_call_target="tpu_custom_call" | custom-call | flops 1006632960 | bytes 9437200 | tf_op jit(solution)/shard_map/pallas_call | solution.py:42
  104.2 4.6 %collective-permute-start.16 = (bf16[1024,256]{1,0:T(8,128)(2,1)S(1)}, bf16[1024,256]{1,0:T(8,128)(2,1)S(1)}, u32[]{:S(2)}, u32[]{:S(2)}) collective-permute-start(bf16[1024,256]{1,0:T(8,128)(2,1)S(1)} %get-tuple-element.64), channel_id=1, source_target_pairs={{0,3},{1,0},{2,1},{3,2},{4,7},{5,4},{6,5},{7,6},{8,11},{9,8},{10,9... | collective-permute-start | bytes 1572872 | tf_op jit(solution)/shard_map/ppermute | solution.py:27
  108.8 2.4 %collective-permute-start.17 = (bf16[512,256]{1,0:T(8,128)(2,1)S(1)}, bf16[512,256]{1,0:T(8,128)(2,1)S(1)}, u32[]{:S(2)}, u32[]{:S(2)}) collective-permute-start(bf16[512,256]{1,0:T(8,128)(2,1)S(1)} %get-tuple-element.65), channel_id=1, source_target_pairs={{0,2},{1,3},{2,0},{3,1},{4,6},{5,7},{6,4},{7,5},{8,10},{9,11},{10,... | collective-permute-start | bytes 786440 | tf_op jit(solution)/shard_map/ppermute | solution.py:27
  113.0 7.9 %collective-permute-done.17.refs_5_ = bf16[512,256]{1,0:T(8,128)(2,1)S(1)} collective-permute-done((bf16[512,256]{1,0:T(8,128)(2,1)S(1)}, bf16[512,256]{1,0:T(8,128)(2,1)S(1)}, u32[]{:S(2)}, u32[]{:S(2)}) %collective-permute-start.17) | collective-permute-done | bytes 262176 | tf_op jit(solution)/shard_map/ppermute | solution.py:27
  121.1 4.0 %collective-permute-start.19 = (bf16[1280,256]{1,0:T(8,128)(2,1)S(1)}, bf16[1280,256]{1,0:T(8,128)(2,1)S(1)}, u32[]{:S(2)}, u32[]{:S(2)}) collective-permute-start(bf16[1280,256]{1,0:T(8,128)(2,1)S(1)} %get-tuple-element.71), channel_id=1, source_target_pairs={{0,1},{1,2},{2,3},{3,0},{4,5},{5,6},{6,7},{7,4},{8,9},{9,10},{10,1... | collective-permute-start | bytes 1966088 | tf_op jit(solution)/shard_map/ppermute | solution.py:27
  125.1 2.5 %collective-permute-start.20 = (bf16[1280,256]{1,0:T(8,128)(2,1)S(1)}, bf16[1280,256]{1,0:T(8,128)(2,1)S(1)}, u32[]{:S(2)}, u32[]{:S(2)}) collective-permute-start(bf16[1280,256]{1,0:T(8,128)(2,1)S(1)} %get-tuple-element.72), channel_id=1, source_target_pairs={{0,3},{1,0},{2,1},{3,2},{4,7},{5,4},{6,5},{7,6},{8,11},{9,8},{10,9... | collective-permute-start | bytes 1966088 | tf_op jit(solution)/shard_map/ppermute | solution.py:27
  127.7 6.7 %collective-permute-start.18 = (bf16[512,256]{1,0:T(8,128)(2,1)S(1)}, bf16[512,256]{1,0:T(8,128)(2,1)S(1)}, u32[]{:S(2)}, u32[]{:S(2)}) collective-permute-start(bf16[512,256]{1,0:T(8,128)(2,1)S(1)} %get-tuple-element.66), channel_id=1, source_target_pairs={{0,8},{1,9},{2,10},{3,11},{4,12},{5,13},{6,14},{7,15},{8,0},{9,1},... | collective-permute-start | bytes 786440 | tf_op jit(solution)/shard_map/ppermute | solution.py:32
  134.4 3.7 %collective-permute-done.20.refs_5_ = bf16[1280,256]{1,0:T(8,128)(2,1)S(1)} collective-permute-done((bf16[1280,256]{1,0:T(8,128)(2,1)S(1)}, bf16[1280,256]{1,0:T(8,128)(2,1)S(1)}, u32[]{:S(2)}, u32[]{:S(2)}) %collective-permute-start.20) | collective-permute-done | bytes 655392 | tf_op jit(solution)/shard_map/ppermute | solution.py:27
  140.2 5.5 %collective-permute-start.22 = (bf16[512,256]{1,0:T(8,128)(2,1)S(1)}, bf16[512,256]{1,0:T(8,128)(2,1)S(1)}, u32[]{:S(2)}, u32[]{:S(2)}) collective-permute-start(bf16[512,256]{1,0:T(8,128)(2,1)S(1)} %get-tuple-element.74), channel_id=1, source_target_pairs={{0,12},{1,13},{2,14},{3,15},{4,0},{5,1},{6,2},{7,3},{8,4},{9,5},{1... | collective-permute-start | bytes 786440 | tf_op jit(solution)/shard_map/ppermute | solution.py:32
  145.7 1.9 %collective-permute-start.23 = (bf16[512,256]{1,0:T(8,128)(2,1)S(1)}, bf16[512,256]{1,0:T(8,128)(2,1)S(1)}, u32[]{:S(2)}, u32[]{:S(2)}) collective-permute-start(bf16[512,256]{1,0:T(8,128)(2,1)S(1)} %get-tuple-element.75), channel_id=1, source_target_pairs={{0,1},{1,2},{2,3},{3,0},{4,5},{5,6},{6,7},{7,4},{8,9},{9,10},{10,1... | collective-permute-start | bytes 786440 | tf_op jit(solution)/shard_map/ppermute | solution.py:27
  147.6 4.6 %collective-permute-start.24 = (bf16[512,256]{1,0:T(8,128)(2,1)S(1)}, bf16[512,256]{1,0:T(8,128)(2,1)S(1)}, u32[]{:S(2)}, u32[]{:S(2)}) collective-permute-start(bf16[512,256]{1,0:T(8,128)(2,1)S(1)} %get-tuple-element.76), channel_id=1, source_target_pairs={{0,3},{1,0},{2,1},{3,2},{4,7},{5,4},{6,5},{7,6},{8,11},{9,8},{10,9... | collective-permute-start | bytes 786440 | tf_op jit(solution)/shard_map/ppermute | solution.py:27
  152.2 3.4 %collective-permute-done.22.refs_3_.rest_2_ = bf16[512,256]{1,0:T(8,128)(2,1)S(1)} collective-permute-done((bf16[512,256]{1,0:T(8,128)(2,1)S(1)}, bf16[512,256]{1,0:T(8,128)(2,1)S(1)}, u32[]{:S(2)}, u32[]{:S(2)}) %collective-permute-start.22) | collective-permute-done | bytes 262176 | tf_op jit(solution)/shard_map/ppermute | solution.py:32
  155.8 9.6 %collective-permute-start.25 = (bf16[256,256]{1,0:T(8,128)(2,1)S(1)}, bf16[256,256]{1,0:T(8,128)(2,1)S(1)}, u32[]{:S(2)}, u32[]{:S(2)}) collective-permute-start(bf16[256,256]{1,0:T(8,128)(2,1)S(1)} %shard_map.64), channel_id=1, source_target_pairs={{0,384},{384,0},{1,385},{385,1},{2,386},{386,2},{3,387},{387,3},{4... | collective-permute-start | bytes 393224 | tf_op jit(solution)/shard_map/ppermute | solution.py:286
  (56 shorter events, 18.9 us)
Async XLA Ops:
  0.0 14.3 %collective-permute-start = (bf16[512,256]{1,0:T(8,128)(2,1)}, bf16[512,256]{1,0:T(8,128)(2,1)S(1)}, u32[]{:S(2)}, u32[]{:S(2)}) collective-permute-start(bf16[512,256]{1,0:T(8,128)(2,1)} %bitcast.9), channel_id=1, source_target_pairs={{0,384},{384,0},{1,385},{385,1},{2,386},{386,2},{3,387},{387,3},{4... | collective-permute-start | bytes 786440 | tf_op jit(solution)/shard_map/ppermute | solution.py:209
  12.4 1.0 copy-start.1
  13.4 0.9 copy-start.2
  14.4 18.3 %collective-permute-start.1 = (bf16[768,256]{1,0:T(8,128)(2,1)S(1)}, bf16[768,256]{1,0:T(8,128)(2,1)S(1)}, u32[]{:S(2)}, u32[]{:S(2)}) collective-permute-start(bf16[768,256]{1,0:T(8,128)(2,1)S(1)} %shard_map.56.rest_0_), channel_id=1, source_target_pairs={{0,4},{1,5},{2,6},{3,7},{4,8},{5,9},{6,10},{7,11},{8,12},{9,13},{1... | collective-permute-start | bytes 1179656 | tf_op jit(solution)/shard_map/ppermute | solution.py:32
  16.3 17.1 %collective-permute-start.2 = (bf16[768,256]{1,0:T(8,128)(2,1)S(1)}, bf16[768,256]{1,0:T(8,128)(2,1)S(1)}, u32[]{:S(2)}, u32[]{:S(2)}) collective-permute-start(bf16[768,256]{1,0:T(8,128)(2,1)S(1)} %shard_map.56.rest_0_), channel_id=1, source_target_pairs={{0,12},{1,13},{2,14},{3,15},{4,0},{5,1},{6,2},{7,3},{8,4},{9,5},{1... | collective-permute-start | bytes 1179656 | tf_op jit(solution)/shard_map/ppermute | solution.py:32
  21.8 13.2 %collective-permute-start.3 = (bf16[768,256]{1,0:T(8,128)(2,1)S(1)}, bf16[768,256]{1,0:T(8,128)(2,1)S(1)}, u32[]{:S(2)}, u32[]{:S(2)}) collective-permute-start(bf16[768,256]{1,0:T(8,128)(2,1)S(1)} %shard_map.56.rest_0_), channel_id=1, source_target_pairs={{0,1},{1,2},{2,3},{3,0},{4,5},{5,6},{6,7},{7,4},{8,9},{9,10},{10,1... | collective-permute-start | bytes 1179656 | tf_op jit(solution)/shard_map/ppermute | solution.py:27
  23.7 12.1 %collective-permute-start.4 = (bf16[768,256]{1,0:T(8,128)(2,1)S(1)}, bf16[768,256]{1,0:T(8,128)(2,1)S(1)}, u32[]{:S(2)}, u32[]{:S(2)}) collective-permute-start(bf16[768,256]{1,0:T(8,128)(2,1)S(1)} %shard_map.56.rest_0_), channel_id=1, source_target_pairs={{0,3},{1,0},{2,1},{3,2},{4,7},{5,4},{6,5},{7,6},{8,11},{9,8},{10,9... | collective-permute-start | bytes 1179656 | tf_op jit(solution)/shard_map/ppermute | solution.py:27
  35.9 17.7 %collective-permute-start.5 = (bf16[2,4096,256]{2,1,0:T(8,128)(2,1)}, bf16[2,4096,256]{2,1,0:T(8,128)(2,1)S(1)}, u32[]{:S(2)}, u32[]{:S(2)}) collective-permute-start(bf16[2,4096,256]{2,1,0:T(8,128)(2,1)} %bitcast.3), channel_id=1, source_target_pairs={{0,384},{384,0},{1,385},{385,1},{2,386},{386,2},{3,387},{387,3},{4... | collective-permute-start | bytes 12582920 | tf_op jit(solution)/shard_map/ppermute | solution.py:217
  39.6 31.1 %collective-permute-start.7 = (bf16[1536,256]{1,0:T(8,128)(2,1)S(1)}, bf16[1536,256]{1,0:T(8,128)(2,1)S(1)}, u32[]{:S(2)}, u32[]{:S(2)}) collective-permute-start(bf16[1536,256]{1,0:T(8,128)(2,1)S(1)} %pad_maximum_fusion.1), channel_id=1, source_target_pairs={{0,3},{1,0},{2,1},{3,2},{4,7},{5,4},{6,5},{7,6},{8,11},{9,8},{10,9... | collective-permute-start | bytes 2359304 | tf_op jit(solution)/shard_map/ppermute | solution.py:27
  45.0 8.6 %copy-start = (bf16[1,2,4096,256]{3,2,1,0:T(8,128)(2,1)S(1)}, bf16[1,2,4096,256]{3,2,1,0:T(8,128)(2,1)}, u32[]{:S(2)}) copy-start(bf16[1,2,4096,256]{3,2,1,0:T(8,128)(2,1)} %param.6) | copy-start | bytes 12582916
  45.1 25.6 %collective-permute-start.6 = (bf16[1536,256]{1,0:T(8,128)(2,1)S(1)}, bf16[1536,256]{1,0:T(8,128)(2,1)S(1)}, u32[]{:S(2)}, u32[]{:S(2)}) collective-permute-start(bf16[1536,256]{1,0:T(8,128)(2,1)S(1)} %pad_maximum_fusion), channel_id=1, source_target_pairs={{0,1},{1,2},{2,3},{3,0},{4,5},{5,6},{6,7},{7,4},{8,9},{9,10},{10,1... | collective-permute-start | bytes 2359304 | tf_op jit(solution)/shard_map/ppermute | solution.py:27
  47.3 18.5 %collective-permute-start.9 = (bf16[768,256]{1,0:T(8,128)(2,1)S(1)}, bf16[768,256]{1,0:T(8,128)(2,1)S(1)}, u32[]{:S(2)}, u32[]{:S(2)}) collective-permute-start(bf16[768,256]{1,0:T(8,128)(2,1)S(1)} %pad_maximum_fusion.5), channel_id=1, source_target_pairs={{0,12},{1,13},{2,14},{3,15},{4,0},{5,1},{6,2},{7,3},{8,4},{9,5},{1... | collective-permute-start | bytes 1179656 | tf_op jit(solution)/shard_map/ppermute | solution.py:32
  49.3 21.4 %collective-permute-start.8 = (bf16[768,256]{1,0:T(8,128)(2,1)S(1)}, bf16[768,256]{1,0:T(8,128)(2,1)S(1)}, u32[]{:S(2)}, u32[]{:S(2)}) collective-permute-start(bf16[768,256]{1,0:T(8,128)(2,1)S(1)} %pad_maximum_fusion.4), channel_id=1, source_target_pairs={{0,4},{1,5},{2,6},{3,7},{4,8},{5,9},{6,10},{7,11},{8,12},{9,13},{1... | collective-permute-start | bytes 1179656 | tf_op jit(solution)/shard_map/ppermute | solution.py:32
  70.9 28.2 %collective-permute-start.11 = (bf16[1152,256]{1,0:T(8,128)(2,1)S(1)}, bf16[1152,256]{1,0:T(8,128)(2,1)S(1)}, u32[]{:S(2)}, u32[]{:S(2)}) collective-permute-start(bf16[1152,256]{1,0:T(8,128)(2,1)S(1)} %pad_maximum_fusion.3), channel_id=1, source_target_pairs={{0,3},{1,0},{2,1},{3,2},{4,7},{5,4},{6,5},{7,6},{8,11},{9,8},{10,9... | collective-permute-start | bytes 1769480 | tf_op jit(solution)/shard_map/ppermute | solution.py:27
  75.5 23.6 %collective-permute-start.10 = (bf16[1152,256]{1,0:T(8,128)(2,1)S(1)}, bf16[1152,256]{1,0:T(8,128)(2,1)S(1)}, u32[]{:S(2)}, u32[]{:S(2)}) collective-permute-start(bf16[1152,256]{1,0:T(8,128)(2,1)S(1)} %pad_maximum_fusion.2), channel_id=1, source_target_pairs={{0,1},{1,2},{2,3},{3,0},{4,5},{5,6},{6,7},{7,4},{8,9},{9,10},{10,1... | collective-permute-start | bytes 1769480 | tf_op jit(solution)/shard_map/ppermute | solution.py:27
  77.5 21.6 %collective-permute-start.12 = (bf16[768,256]{1,0:T(8,128)(2,1)S(1)}, bf16[768,256]{1,0:T(8,128)(2,1)S(1)}, u32[]{:S(2)}, u32[]{:S(2)}) collective-permute-start(bf16[768,256]{1,0:T(8,128)(2,1)S(1)} %pad_maximum_fusion.6), channel_id=1, source_target_pairs={{0,2},{1,3},{2,0},{3,1},{4,6},{5,7},{6,4},{7,5},{8,10},{9,11},{10,... | collective-permute-start | bytes 1179656 | tf_op jit(solution)/shard_map/ppermute | solution.py:27
  80.6 10.9 %collective-permute-start.13 = (bf16[384,256]{1,0:T(8,128)(2,1)S(1)}, bf16[384,256]{1,0:T(8,128)(2,1)S(1)}, u32[]{:S(2)}, u32[]{:S(2)}) collective-permute-start(bf16[384,256]{1,0:T(8,128)(2,1)S(1)} %get-tuple-element.77), channel_id=1, source_target_pairs={{0,4},{1,5},{2,6},{3,7},{4,8},{5,9},{6,10},{7,11},{8,12},{9,13},{1... | collective-permute-start | bytes 589832 | tf_op jit(solution)/shard_map/ppermute | solution.py:32
  82.5 9.6 %collective-permute-start.14 = (bf16[384,256]{1,0:T(8,128)(2,1)S(1)}, bf16[384,256]{1,0:T(8,128)(2,1)S(1)}, u32[]{:S(2)}, u32[]{:S(2)}) collective-permute-start(bf16[384,256]{1,0:T(8,128)(2,1)S(1)} %get-tuple-element.81), channel_id=1, source_target_pairs={{0,12},{1,13},{2,14},{3,15},{4,0},{5,1},{6,2},{7,3},{8,4},{9,5},{1... | collective-permute-start | bytes 589832 | tf_op jit(solution)/shard_map/ppermute | solution.py:32
  89.0 11.0 %copy-start.3 = (s32[2]{0:T(128)S(1)}, s32[2]{0:T(128)}, u32[]{:S(2)}) copy-start(s32[2]{0:T(128)} %enc_ref.1) | copy-start | bytes 28
  89.0 11.0 %copy-start.4 = (s32[2]{0:T(128)S(1)}, s32[2]{0:T(128)}, u32[]{:S(2)}) copy-start(s32[2]{0:T(128)} %dec_ref.1) | copy-start | bytes 28
  102.3 18.5 %collective-permute-start.15 = (bf16[1024,256]{1,0:T(8,128)(2,1)S(1)}, bf16[1024,256]{1,0:T(8,128)(2,1)S(1)}, u32[]{:S(2)}, u32[]{:S(2)}) collective-permute-start(bf16[1024,256]{1,0:T(8,128)(2,1)S(1)} %get-tuple-element.63), channel_id=1, source_target_pairs={{0,1},{1,2},{2,3},{3,0},{4,5},{5,6},{6,7},{7,4},{8,9},{9,10},{10,1... | collective-permute-start | bytes 1572872 | tf_op jit(solution)/shard_map/ppermute | solution.py:27
  104.2 16.6 %collective-permute-start.16 = (bf16[1024,256]{1,0:T(8,128)(2,1)S(1)}, bf16[1024,256]{1,0:T(8,128)(2,1)S(1)}, u32[]{:S(2)}, u32[]{:S(2)}) collective-permute-start(bf16[1024,256]{1,0:T(8,128)(2,1)S(1)} %get-tuple-element.64), channel_id=1, source_target_pairs={{0,3},{1,0},{2,1},{3,2},{4,7},{5,4},{6,5},{7,6},{8,11},{9,8},{10,9... | collective-permute-start | bytes 1572872 | tf_op jit(solution)/shard_map/ppermute | solution.py:27
  108.8 12.0 %collective-permute-start.17 = (bf16[512,256]{1,0:T(8,128)(2,1)S(1)}, bf16[512,256]{1,0:T(8,128)(2,1)S(1)}, u32[]{:S(2)}, u32[]{:S(2)}) collective-permute-start(bf16[512,256]{1,0:T(8,128)(2,1)S(1)} %get-tuple-element.65), channel_id=1, source_target_pairs={{0,2},{1,3},{2,0},{3,1},{4,6},{5,7},{6,4},{7,5},{8,10},{9,11},{10,... | collective-permute-start | bytes 786440 | tf_op jit(solution)/shard_map/ppermute | solution.py:27
  121.1 13.3 %collective-permute-start.19 = (bf16[1280,256]{1,0:T(8,128)(2,1)S(1)}, bf16[1280,256]{1,0:T(8,128)(2,1)S(1)}, u32[]{:S(2)}, u32[]{:S(2)}) collective-permute-start(bf16[1280,256]{1,0:T(8,128)(2,1)S(1)} %get-tuple-element.71), channel_id=1, source_target_pairs={{0,1},{1,2},{2,3},{3,0},{4,5},{5,6},{6,7},{7,4},{8,9},{9,10},{10,1... | collective-permute-start | bytes 1966088 | tf_op jit(solution)/shard_map/ppermute | solution.py:27
  125.1 12.9 %collective-permute-start.20 = (bf16[1280,256]{1,0:T(8,128)(2,1)S(1)}, bf16[1280,256]{1,0:T(8,128)(2,1)S(1)}, u32[]{:S(2)}, u32[]{:S(2)}) collective-permute-start(bf16[1280,256]{1,0:T(8,128)(2,1)S(1)} %get-tuple-element.72), channel_id=1, source_target_pairs={{0,3},{1,0},{2,1},{3,2},{4,7},{5,4},{6,5},{7,6},{8,11},{9,8},{10,9... | collective-permute-start | bytes 1966088 | tf_op jit(solution)/shard_map/ppermute | solution.py:27
  127.7 24.6 %collective-permute-start.18 = (bf16[512,256]{1,0:T(8,128)(2,1)S(1)}, bf16[512,256]{1,0:T(8,128)(2,1)S(1)}, u32[]{:S(2)}, u32[]{:S(2)}) collective-permute-start(bf16[512,256]{1,0:T(8,128)(2,1)S(1)} %get-tuple-element.66), channel_id=1, source_target_pairs={{0,8},{1,9},{2,10},{3,11},{4,12},{5,13},{6,14},{7,15},{8,0},{9,1},... | collective-permute-start | bytes 786440 | tf_op jit(solution)/shard_map/ppermute | solution.py:32
  138.3 13.9 %collective-permute-start.21 = (bf16[512,256]{1,0:T(8,128)(2,1)S(1)}, bf16[512,256]{1,0:T(8,128)(2,1)S(1)}, u32[]{:S(2)}, u32[]{:S(2)}) collective-permute-start(bf16[512,256]{1,0:T(8,128)(2,1)S(1)} %get-tuple-element.73), channel_id=1, source_target_pairs={{0,4},{1,5},{2,6},{3,7},{4,8},{5,9},{6,10},{7,11},{8,12},{9,13},{1... | collective-permute-start | bytes 786440 | tf_op jit(solution)/shard_map/ppermute | solution.py:32
  140.2 15.4 %collective-permute-start.22 = (bf16[512,256]{1,0:T(8,128)(2,1)S(1)}, bf16[512,256]{1,0:T(8,128)(2,1)S(1)}, u32[]{:S(2)}, u32[]{:S(2)}) collective-permute-start(bf16[512,256]{1,0:T(8,128)(2,1)S(1)} %get-tuple-element.74), channel_id=1, source_target_pairs={{0,12},{1,13},{2,14},{3,15},{4,0},{5,1},{6,2},{7,3},{8,4},{9,5},{1... | collective-permute-start | bytes 786440 | tf_op jit(solution)/shard_map/ppermute | solution.py:32
  145.7 9.9 %collective-permute-start.23 = (bf16[512,256]{1,0:T(8,128)(2,1)S(1)}, bf16[512,256]{1,0:T(8,128)(2,1)S(1)}, u32[]{:S(2)}, u32[]{:S(2)}) collective-permute-start(bf16[512,256]{1,0:T(8,128)(2,1)S(1)} %get-tuple-element.75), channel_id=1, source_target_pairs={{0,1},{1,2},{2,3},{3,0},{4,5},{5,6},{6,7},{7,4},{8,9},{9,10},{10,1... | collective-permute-start | bytes 786440 | tf_op jit(solution)/shard_map/ppermute | solution.py:27
  147.6 8.0 %collective-permute-start.24 = (bf16[512,256]{1,0:T(8,128)(2,1)S(1)}, bf16[512,256]{1,0:T(8,128)(2,1)S(1)}, u32[]{:S(2)}, u32[]{:S(2)}) collective-permute-start(bf16[512,256]{1,0:T(8,128)(2,1)S(1)} %get-tuple-element.76), channel_id=1, source_target_pairs={{0,3},{1,0},{2,1},{3,2},{4,7},{5,4},{6,5},{7,6},{8,11},{9,8},{10,9... | collective-permute-start | bytes 786440 | tf_op jit(solution)/shard_map/ppermute | solution.py:27
  155.8 10.6 %collective-permute-start.25 = (bf16[256,256]{1,0:T(8,128)(2,1)S(1)}, bf16[256,256]{1,0:T(8,128)(2,1)S(1)}, u32[]{:S(2)}, u32[]{:S(2)}) collective-permute-start(bf16[256,256]{1,0:T(8,128)(2,1)S(1)} %shard_map.64), channel_id=1, source_target_pairs={{0,384},{384,0},{1,385},{385,1},{2,386},{386,2},{3,387},{387,3},{4... | collective-permute-start | bytes 393224 | tf_op jit(solution)/shard_map/ppermute | solution.py:286

commit v8 on v7

--- a/solution.py
+++ b/solution.py
@@ -9,8 +9,10 @@
 SIDE = 4
 ROWS = 3 * HS
 HALF = ROWS // 2
-REST = ROWS // 4
-MOST = ROWS - REST
+D = 192
+E = 96
+MOST = 528
+REST = ROWS - MOST
 N = 2 * HS
 F32 = jnp.float32
 BF16 = jnp.bfloat16
@@ -216,10 +218,10 @@
     )
     other_w = lax.ppermute(own_w, "section", SWAP)
 
-    right1 = shift_x(join(right0[:HALF], up1, down1[:HALF]), 1)
-    left1 = shift_x(join(left0[HALF:], up1[HALF:], down1), -1)
-    up2 = shift_y(join(up1[:HALF], left0[:HALF]), 1)
-    down2 = shift_y(join(down1[HALF:], right0[HALF:]), -1)
+    right1 = shift_x(join(right0[:HALF], up1, down1[: ROWS - D]), 1)
+    left1 = shift_x(join(left0[HALF:], up1[D:], down1), -1)
+    up2 = shift_y(join(up1[:HALF], left0[:D]), 1)
+    down2 = shift_y(join(down1[HALF:], right0[ROWS - D :]), -1)
     total = project(
         [c0, up1, down1, right0, left0],
         [
@@ -231,15 +233,17 @@
     right1, left1, up2, down2, total = lax.optimization_barrier((right1, left1, up2, down2, total))
 
     last = join(up2[:HALF], down2[:HALF])
-    right2 = shift_x(join(right1[HALF : HALF + MOST], right1[ROWS + HALF :], down2[HALF : HALF + REST]), 1)
-    left2 = shift_x(join(left1[HALF + REST : ROWS], left1[ROWS + MOST :], last), -1)
-    up3, down3 = shift_y(right1[HALF:ROWS], 1), shift_y(down2[HALF:], -1)
+    tail, lower = HALF + ROWS, HALF + ROWS - D
+    right2 = shift_x(join(right1[HALF : HALF + MOST], right1[tail : tail + MOST]), 1)
+    left2 = shift_x(join(left1[HALF + MOST - D : lower], left1[lower + MOST :], last[E : ROWS - E]), -1)
+    up3 = shift_y(join(right1[HALF:ROWS], up2[HALF : HALF + E]), 1)
+    down3 = shift_y(join(right1[tail + HALF :], down2[HALF:], left1[lower + ROWS - E :]), -1)
     across2 = shift_x(last, 2)
     total = project(
         [right1, left1, up2, down2],
         [
-            ((-1, -1), [(0, HALF, ROWS)]), ((1, -1), [(0, HALF + ROWS, HALF), (3, HALF, HALF)]),
-            ((-1, 1), [(2, HALF, HALF), (1, HALF, HALF)]), ((1, 1), [(1, ROWS, ROWS)]),
+            ((-1, -1), [(0, HALF, ROWS)]), ((1, -1), [(0, HALF + ROWS, ROWS - D), (3, HALF, D)]),
+            ((-1, 1), [(2, HALF, D), (1, HALF, ROWS - D)]), ((1, 1), [(1, lower, ROWS)]),
             ((0, 2), [(0, 0, HALF), (1, 0, HALF)]), ((2, 0), [(2, 0, HALF), (3, 0, HALF)]),
         ],
         own_w, other_w, total,
@@ -251,7 +255,8 @@
         [right2, left2, across2, up3, down3],
         [
             ((-1, 2), [(0, 0, MOST), (1, 0, REST)]), ((1, 2), [(0, MOST, MOST), (1, REST, REST)]),
-            ((2, -1), [(3, 0, HALF), (4, 0, HALF)]), ((2, 1), [(1, 2 * REST, ROWS)]), ((2, 2), [(2, 0, ROWS)]),
+            ((2, -1), [(3, 0, HALF), (4, 0, HALF)]), ((2, 2), [(2, 0, ROWS)]),
+            ((2, 1), [(3, HALF, E), (1, 2 * REST, ROWS - 2 * E), (4, HALF, E)]),
         ],
         own_w, other_w, total,
     )

time: 168 us -> 167 us (level)
  starting transfers between devices: 106 us -> 98.5 us
  waiting for transfers between devices: 49.8 us -> 56.1 us
    ppermute x14, waiting for transfers between devices: 21 us -> 27.4 us  [shift_x(): return lax.ppermute(block, 'mp', route)]
    ppermute x9, starting transfers between devices: 35 us -> 30.3 us  [shift_y(): return lax.ppermute(block, 'mp', route)]
    ppermute x1, starting transfers between devices: 9.58 us -> 7.33 us  [local(): swapped = lax.ppermute(sent, 'section', SWAP)]
  transfers between devices with their start and end apart: 26 -> 26, of which waited for: 13 -> 16; matrix products, arithmetic and copies ran while one was open for 0% -> 0% of each run, Pallas kernels for 2% -> 2%
where the time goes in v8:
time: 167 us; the launch traced here: 166 us
  starting transfers between devices  98.5 us (59%)
  waiting for transfers between devices  56.1 us (34%)
  Pallas kernels  8.2 us (5%)
  local copies, waits for them, and re-layouts  2.16 us (1%)
    ppermute x14, starting transfers between devices, shift_x(): return lax.ppermute(block, 'mp', route)  44.9 us
    ppermute x9, starting transfers between devices, shift_y(): return lax.ppermute(block, 'mp', route)  30.3 us
    ppermute x9, waiting for transfers between devices, shift_y(): return lax.ppermute(block, 'mp', route)  27.8 us
    ppermute x14, waiting for transfers between devices, shift_x(): return lax.ppermute(block, 'mp', route)  27.4 us
    ppermute x1, starting transfers between devices, local(): partner = lax.ppermute(own, 'section', SWAP)  12.4 us
    pallas_call x11, Pallas kernels, call(): pl.pallas_call(body, out_shape=out, in_specs=[SMEM] * scalars + [VMEM] *...  8.2 us
    ppermute x1, starting transfers between devices, local(): swapped = lax.ppermute(sent, 'section', SWAP)  7.33 us
    ppermute x1, starting transfers between devices, local(): other_w = lax.ppermute(own_w, 'section', SWAP)  3.65 us
  transfers between devices with their start and end apart: 26, of which 16 were waited for; matrix products, arithmetic and copies ran while one was open for 0% of the time, Pallas kernels for 2%

profile of v8, /device:TPU:1, one launch (start us, length us, event | category | flops | bytes accessed | tf_op | source)
XLA Modules:
  0.0 165.9 jit_solution(12462480894736715209)
XLA Ops:
  0.0 12.4 %collective-permute-start = (bf16[512,256]{1,0:T(8,128)(2,1)}, bf16[512,256]{1,0:T(8,128)(2,1)S(1)}, u32[]{:S(2)}, u32[]{:S(2)}) collective-permute-start(bf16[512,256]{1,0:T(8,128)(2,1)} %bitcast.9), channel_id=1, source_target_pairs={{0,384},{384,0},{1,385},{385,1},{2,386},{386,2},{3,387},{387,3},{4... | collective-permute-start | bytes 786440 | tf_op jit(solution)/shard_map/ppermute | solution.py:211
  14.4 1.9 %collective-permute-start.1 = (bf16[768,256]{1,0:T(8,128)(2,1)S(1)}, bf16[768,256]{1,0:T(8,128)(2,1)S(1)}, u32[]{:S(2)}, u32[]{:S(2)}) collective-permute-start(bf16[768,256]{1,0:T(8,128)(2,1)S(1)} %shard_map.56.rest_0_), channel_id=1, source_target_pairs={{0,4},{1,5},{2,6},{3,7},{4,8},{5,9},{6,10},{7,11},{8,12},{9,13},{1... | collective-permute-start | bytes 1179656 | tf_op jit(solution)/shard_map/ppermute | solution.py:34
  16.3 5.5 %collective-permute-start.2 = (bf16[768,256]{1,0:T(8,128)(2,1)S(1)}, bf16[768,256]{1,0:T(8,128)(2,1)S(1)}, u32[]{:S(2)}, u32[]{:S(2)}) collective-permute-start(bf16[768,256]{1,0:T(8,128)(2,1)S(1)} %shard_map.56.rest_0_), channel_id=1, source_target_pairs={{0,12},{1,13},{2,14},{3,15},{4,0},{5,1},{6,2},{7,3},{8,4},{9,5},{1... | collective-permute-start | bytes 1179656 | tf_op jit(solution)/shard_map/ppermute | solution.py:34
  21.8 1.9 %collective-permute-start.3 = (bf16[768,256]{1,0:T(8,128)(2,1)S(1)}, bf16[768,256]{1,0:T(8,128)(2,1)S(1)}, u32[]{:S(2)}, u32[]{:S(2)}) collective-permute-start(bf16[768,256]{1,0:T(8,128)(2,1)S(1)} %shard_map.56.rest_0_), channel_id=1, source_target_pairs={{0,1},{1,2},{2,3},{3,0},{4,5},{5,6},{6,7},{7,4},{8,9},{9,10},{10,1... | collective-permute-start | bytes 1179656 | tf_op jit(solution)/shard_map/ppermute | solution.py:29
  23.7 4.6 %collective-permute-start.4 = (bf16[768,256]{1,0:T(8,128)(2,1)S(1)}, bf16[768,256]{1,0:T(8,128)(2,1)S(1)}, u32[]{:S(2)}, u32[]{:S(2)}) collective-permute-start(bf16[768,256]{1,0:T(8,128)(2,1)S(1)} %shard_map.56.rest_0_), channel_id=1, source_target_pairs={{0,3},{1,0},{2,1},{3,2},{4,7},{5,4},{6,5},{7,6},{8,11},{9,8},{10,9... | collective-permute-start | bytes 1179656 | tf_op jit(solution)/shard_map/ppermute | solution.py:29
  28.3 4.3 %collective-permute-done.1.rest_1_ = bf16[768,256]{1,0:T(8,128)(2,1)S(1)} collective-permute-done((bf16[768,256]{1,0:T(8,128)(2,1)S(1)}, bf16[768,256]{1,0:T(8,128)(2,1)S(1)}, u32[]{:S(2)}, u32[]{:S(2)}) %collective-permute-start.1) | collective-permute-done | bytes 393248 | tf_op jit(solution)/shard_map/ppermute | solution.py:34
  35.9 3.7 %collective-permute-start.5 = (bf16[2,4096,256]{2,1,0:T(8,128)(2,1)}, bf16[2,4096,256]{2,1,0:T(8,128)(2,1)S(1)}, u32[]{:S(2)}, u32[]{:S(2)}) collective-permute-start(bf16[2,4096,256]{2,1,0:T(8,128)(2,1)} %bitcast.3), channel_id=1, source_target_pairs={{0,384},{384,0},{1,385},{385,1},{2,386},{386,2},{3,387},{387,3},{4... | collective-permute-start | bytes 12582920 | tf_op jit(solution)/shard_map/ppermute | solution.py:219
  39.7 5.3 %collective-permute-start.7 = (bf16[1728,256]{1,0:T(8,128)(2,1)S(1)}, bf16[1728,256]{1,0:T(8,128)(2,1)S(1)}, u32[]{:S(2)}, u32[]{:S(2)}) collective-permute-start(bf16[1728,256]{1,0:T(8,128)(2,1)S(1)} %pad_maximum_fusion.1), channel_id=1, source_target_pairs={{0,3},{1,0},{2,1},{3,2},{4,7},{5,4},{6,5},{7,6},{8,11},{9,8},{10,9... | collective-permute-start | bytes 2654216 | tf_op jit(solution)/shard_map/ppermute | solution.py:29
  45.1 2.2 %collective-permute-start.6 = (bf16[1728,256]{1,0:T(8,128)(2,1)S(1)}, bf16[1728,256]{1,0:T(8,128)(2,1)S(1)}, u32[]{:S(2)}, u32[]{:S(2)}) collective-permute-start(bf16[1728,256]{1,0:T(8,128)(2,1)S(1)} %pad_maximum_fusion), channel_id=1, source_target_pairs={{0,1},{1,2},{2,3},{3,0},{4,5},{5,6},{6,7},{7,4},{8,9},{9,10},{10,1... | collective-permute-start | bytes 2654216 | tf_op jit(solution)/shard_map/ppermute | solution.py:29
  49.4 5.5 %collective-permute-start.9 = (bf16[576,256]{1,0:T(8,128)(2,1)S(1)}, bf16[576,256]{1,0:T(8,128)(2,1)S(1)}, u32[]{:S(2)}, u32[]{:S(2)}) collective-permute-start(bf16[576,256]{1,0:T(8,128)(2,1)S(1)} %pad_maximum_fusion.6), channel_id=1, source_target_pairs={{0,12},{1,13},{2,14},{3,15},{4,0},{5,1},{6,2},{7,3},{8,4},{9,5},{1... | collective-permute-start | bytes 884744 | tf_op jit(solution)/shard_map/ppermute | solution.py:34
  55.7 4.4 %collective-permute-done.8.rest_2_ = bf16[576,256]{1,0:T(8,128)(2,1)S(1)} collective-permute-done((bf16[576,256]{1,0:T(8,128)(2,1)S(1)}, bf16[576,256]{1,0:T(8,128)(2,1)S(1)}, u32[]{:S(2)}, u32[]{:S(2)}) %collective-permute-start.8) | collective-permute-done | bytes 294944 | tf_op jit(solution)/shard_map/ppermute | solution.py:34
  60.2 4.5 %collective-permute-done.9.rest_3_ = bf16[576,256]{1,0:T(8,128)(2,1)S(1)} collective-permute-done((bf16[576,256]{1,0:T(8,128)(2,1)S(1)}, bf16[576,256]{1,0:T(8,128)(2,1)S(1)}, u32[]{:S(2)}, u32[]{:S(2)}) %collective-permute-start.9) | collective-permute-done | bytes 294944 | tf_op jit(solution)/shard_map/ppermute | solution.py:34
  64.7 4.7 %collective-permute-done.6.rest_0_ = bf16[1728,256]{1,0:T(8,128)(2,1)S(1)} collective-permute-done((bf16[1728,256]{1,0:T(8,128)(2,1)S(1)}, bf16[1728,256]{1,0:T(8,128)(2,1)S(1)}, u32[]{:S(2)}, u32[]{:S(2)}) %collective-permute-start.6) | collective-permute-done | bytes 884768 | tf_op jit(solution)/shard_map/ppermute | solution.py:29
  71.6 3.4 %collective-permute-start.10 = (bf16[1056,256]{1,0:T(8,128)(2,1)S(1)}, bf16[1056,256]{1,0:T(8,128)(2,1)S(1)}, u32[]{:S(2)}, u32[]{:S(2)}) collective-permute-start(bf16[1056,256]{1,0:T(8,128)(2,1)S(1)} %pad_maximum_fusion.2), channel_id=1, source_target_pairs={{0,1},{1,2},{2,3},{3,0},{4,5},{5,6},{6,7},{7,4},{8,9},{9,10},{10,1... | collective-permute-start | bytes 1622024 | tf_op jit(solution)/shard_map/ppermute | solution.py:29
  77.0 2.1 %collective-permute-start.14 = (bf16[480,256]{1,0:T(8,128)(2,1)S(1)}, bf16[480,256]{1,0:T(8,128)(2,1)S(1)}, u32[]{:S(2)}, u32[]{:S(2)}) collective-permute-start(bf16[480,256]{1,0:T(8,128)(2,1)S(1)} %pad_maximum_fusion.8), channel_id=1, source_target_pairs={{0,12},{1,13},{2,14},{3,15},{4,0},{5,1},{6,2},{7,3},{8,4},{9,5},{1... | collective-permute-start | bytes 737288 | tf_op jit(solution)/shard_map/ppermute | solution.py:34
  79.2 4.0 %collective-permute-start.13 = (bf16[480,256]{1,0:T(8,128)(2,1)S(1)}, bf16[480,256]{1,0:T(8,128)(2,1)S(1)}, u32[]{:S(2)}, u32[]{:S(2)}) collective-permute-start(bf16[480,256]{1,0:T(8,128)(2,1)S(1)} %pad_maximum_fusion.7), channel_id=1, source_target_pairs={{0,4},{1,5},{2,6},{3,7},{4,8},{5,9},{6,10},{7,11},{8,12},{9,13},{1... | collective-permute-start | bytes 737288 | tf_op jit(solution)/shard_map/ppermute | solution.py:34
  84.3 5.8 %collective-permute-done.14.rest_4_ = bf16[480,256]{1,0:T(8,128)(2,1)S(1)} collective-permute-done((bf16[480,256]{1,0:T(8,128)(2,1)S(1)}, bf16[480,256]{1,0:T(8,128)(2,1)S(1)}, u32[]{:S(2)}, u32[]{:S(2)}) %collective-permute-start.14) | collective-permute-done | bytes 245792 | tf_op jit(solution)/shard_map/ppermute | solution.py:34
  90.1 4.0 %collective-permute-done.13.rest_3_ = bf16[480,256]{1,0:T(8,128)(2,1)S(1)} collective-permute-done((bf16[480,256]{1,0:T(8,128)(2,1)S(1)}, bf16[480,256]{1,0:T(8,128)(2,1)S(1)}, u32[]{:S(2)}, u32[]{:S(2)}) %collective-permute-start.13) | collective-permute-done | bytes 245792 | tf_op jit(solution)/shard_map/ppermute | solution.py:34
  96.6 2.3 %shard_map.60 = (bf16[1024,256]{1,0:T(8,128)(2,1)S(1)}, bf16[1024,256]{1,0:T(8,128)(2,1)S(1)}, bf16[512,256]{1,0:T(8,128)(2,1)S(1)}, bf16[4,256,256]{2,1,0:T(8,128)(2,1)S(1)}) custom-call(s32[2]{0:T(128)S(1)} %copy-done.3, s32[2]{0:T(128)S(1)} %copy-done.4, f32[4,256,256]{2,1,0:T(8,128)S(1)} %shard_map.59.t_ref, bf16[2,4096,256]{2,1,0:T(8,128)(2,1)S(1)} %bitcast.7, ...), custom_call_target="tpu_custom_call" | custom-call | flops 1006632960 | bytes 9437200 | tf_op jit(solution)/shard_map/pallas_call | solution.py:44
  99.0 2.6 %collective-permute-start.15 = (bf16[1024,256]{1,0:T(8,128)(2,1)S(1)}, bf16[1024,256]{1,0:T(8,128)(2,1)S(1)}, u32[]{:S(2)}, u32[]{:S(2)}) collective-permute-start(bf16[1024,256]{1,0:T(8,128)(2,1)S(1)} %get-tuple-element.63), channel_id=1, source_target_pairs={{0,1},{1,2},{2,3},{3,0},{4,5},{5,6},{6,7},{7,4},{8,9},{9,10},{10,1... | collective-permute-start | bytes 1572872 | tf_op jit(solution)/shard_map/ppermute | solution.py:29
  101.6 3.9 %collective-permute-start.16 = (bf16[1024,256]{1,0:T(8,128)(2,1)S(1)}, bf16[1024,256]{1,0:T(8,128)(2,1)S(1)}, u32[]{:S(2)}, u32[]{:S(2)}) collective-permute-start(bf16[1024,256]{1,0:T(8,128)(2,1)S(1)} %get-tuple-element.64), channel_id=1, source_target_pairs={{0,3},{1,0},{2,1},{3,2},{4,7},{5,4},{6,5},{7,6},{8,11},{9,8},{10,9... | collective-permute-start | bytes 1572872 | tf_op jit(solution)/shard_map/ppermute | solution.py:29
  105.5 2.2 %collective-permute-start.17 = (bf16[512,256]{1,0:T(8,128)(2,1)S(1)}, bf16[512,256]{1,0:T(8,128)(2,1)S(1)}, u32[]{:S(2)}, u32[]{:S(2)}) collective-permute-start(bf16[512,256]{1,0:T(8,128)(2,1)S(1)} %get-tuple-element.65), channel_id=1, source_target_pairs={{0,2},{1,3},{2,0},{3,1},{4,6},{5,7},{6,4},{7,5},{8,10},{9,11},{10,... | collective-permute-start | bytes 786440 | tf_op jit(solution)/shard_map/ppermute | solution.py:29
  109.4 8.8 %collective-permute-done.17.refs_5_ = bf16[512,256]{1,0:T(8,128)(2,1)S(1)} collective-permute-done((bf16[512,256]{1,0:T(8,128)(2,1)S(1)}, bf16[512,256]{1,0:T(8,128)(2,1)S(1)}, u32[]{:S(2)}, u32[]{:S(2)}) %collective-permute-start.17) | collective-permute-done | bytes 262176 | tf_op jit(solution)/shard_map/ppermute | solution.py:29
  118.4 5.3 %collective-permute-start.19 = (bf16[1280,256]{1,0:T(8,128)(2,1)S(1)}, bf16[1280,256]{1,0:T(8,128)(2,1)S(1)}, u32[]{:S(2)}, u32[]{:S(2)}) collective-permute-start(bf16[1280,256]{1,0:T(8,128)(2,1)S(1)} %get-tuple-element.71), channel_id=1, source_target_pairs={{0,1},{1,2},{2,3},{3,0},{4,5},{5,6},{6,7},{7,4},{8,9},{9,10},{10,1... | collective-permute-start | bytes 1966088 | tf_op jit(solution)/shard_map/ppermute | solution.py:29
  123.8 3.1 %collective-permute-start.20 = (bf16[1280,256]{1,0:T(8,128)(2,1)S(1)}, bf16[1280,256]{1,0:T(8,128)(2,1)S(1)}, u32[]{:S(2)}, u32[]{:S(2)}) collective-permute-start(bf16[1280,256]{1,0:T(8,128)(2,1)S(1)} %get-tuple-element.72), channel_id=1, source_target_pairs={{0,3},{1,0},{2,1},{3,2},{4,7},{5,4},{6,5},{7,6},{8,11},{9,8},{10,9... | collective-permute-start | bytes 1966088 | tf_op jit(solution)/shard_map/ppermute | solution.py:29
  128.8 7.4 %collective-permute-done.19.refs_4_ = bf16[1280,256]{1,0:T(8,128)(2,1)S(1)} collective-permute-done((bf16[1280,256]{1,0:T(8,128)(2,1)S(1)}, bf16[1280,256]{1,0:T(8,128)(2,1)S(1)}, u32[]{:S(2)}, u32[]{:S(2)}) %collective-permute-start.19) | collective-permute-done | bytes 655392 | tf_op jit(solution)/shard_map/ppermute | solution.py:29
  136.2 2.4 %collective-permute-done.20.refs_5_ = bf16[1280,256]{1,0:T(8,128)(2,1)S(1)} collective-permute-done((bf16[1280,256]{1,0:T(8,128)(2,1)S(1)}, bf16[1280,256]{1,0:T(8,128)(2,1)S(1)}, u32[]{:S(2)}, u32[]{:S(2)}) %collective-permute-start.20) | collective-permute-done | bytes 655392 | tf_op jit(solution)/shard_map/ppermute | solution.py:29
  140.8 5.5 %collective-permute-start.22 = (bf16[512,256]{1,0:T(8,128)(2,1)S(1)}, bf16[512,256]{1,0:T(8,128)(2,1)S(1)}, u32[]{:S(2)}, u32[]{:S(2)}) collective-permute-start(bf16[512,256]{1,0:T(8,128)(2,1)S(1)} %get-tuple-element.74), channel_id=1, source_target_pairs={{0,12},{1,13},{2,14},{3,15},{4,0},{5,1},{6,2},{7,3},{8,4},{9,5},{1... | collective-permute-start | bytes 786440 | tf_op jit(solution)/shard_map/ppermute | solution.py:34
  146.3 2.0 %collective-permute-start.23 = (bf16[512,256]{1,0:T(8,128)(2,1)S(1)}, bf16[512,256]{1,0:T(8,128)(2,1)S(1)}, u32[]{:S(2)}, u32[]{:S(2)}) collective-permute-start(bf16[512,256]{1,0:T(8,128)(2,1)S(1)} %get-tuple-element.75), channel_id=1, source_target_pairs={{0,1},{1,2},{2,3},{3,0},{4,5},{5,6},{6,7},{7,4},{8,9},{9,10},{10,1... | collective-permute-start | bytes 786440 | tf_op jit(solution)/shard_map/ppermute | solution.py:29
  148.3 4.5 %collective-permute-start.24 = (bf16[512,256]{1,0:T(8,128)(2,1)S(1)}, bf16[512,256]{1,0:T(8,128)(2,1)S(1)}, u32[]{:S(2)}, u32[]{:S(2)}) collective-permute-start(bf16[512,256]{1,0:T(8,128)(2,1)S(1)} %get-tuple-element.76), channel_id=1, source_target_pairs={{0,3},{1,0},{2,1},{3,2},{4,7},{5,4},{6,5},{7,6},{8,11},{9,8},{10,9... | collective-permute-start | bytes 786440 | tf_op jit(solution)/shard_map/ppermute | solution.py:29
  152.8 3.9 %collective-permute-done.21.refs_2_.rest_1_ = bf16[512,256]{1,0:T(8,128)(2,1)S(1)} collective-permute-done((bf16[512,256]{1,0:T(8,128)(2,1)S(1)}, bf16[512,256]{1,0:T(8,128)(2,1)S(1)}, u32[]{:S(2)}, u32[]{:S(2)}) %collective-permute-start.21) | collective-permute-done | bytes 262176 | tf_op jit(solution)/shard_map/ppermute | solution.py:34
  156.8 7.3 %collective-permute-start.25 = (bf16[256,256]{1,0:T(8,128)(2,1)S(1)}, bf16[256,256]{1,0:T(8,128)(2,1)S(1)}, u32[]{:S(2)}, u32[]{:S(2)}) collective-permute-start(bf16[256,256]{1,0:T(8,128)(2,1)S(1)} %shard_map.64), channel_id=1, source_target_pairs={{0,384},{384,0},{1,385},{385,1},{2,386},{386,2},{3,387},{387,3},{4... | collective-permute-start | bytes 393224 | tf_op jit(solution)/shard_map/ppermute | solution.py:291
  (68 shorter events, 23.8 us)
Async XLA Ops:
  0.0 14.3 %collective-permute-start = (bf16[512,256]{1,0:T(8,128)(2,1)}, bf16[512,256]{1,0:T(8,128)(2,1)S(1)}, u32[]{:S(2)}, u32[]{:S(2)}) collective-permute-start(bf16[512,256]{1,0:T(8,128)(2,1)} %bitcast.9), channel_id=1, source_target_pairs={{0,384},{384,0},{1,385},{385,1},{2,386},{386,2},{3,387},{387,3},{4... | collective-permute-start | bytes 786440 | tf_op jit(solution)/shard_map/ppermute | solution.py:211
  12.4 1.0 copy-start.1
  13.4 0.9 copy-start.2
  14.4 18.3 %collective-permute-start.1 = (bf16[768,256]{1,0:T(8,128)(2,1)S(1)}, bf16[768,256]{1,0:T(8,128)(2,1)S(1)}, u32[]{:S(2)}, u32[]{:S(2)}) collective-permute-start(bf16[768,256]{1,0:T(8,128)(2,1)S(1)} %shard_map.56.rest_0_), channel_id=1, source_target_pairs={{0,4},{1,5},{2,6},{3,7},{4,8},{5,9},{6,10},{7,11},{8,12},{9,13},{1... | collective-permute-start | bytes 1179656 | tf_op jit(solution)/shard_map/ppermute | solution.py:34
  16.3 17.1 %collective-permute-start.2 = (bf16[768,256]{1,0:T(8,128)(2,1)S(1)}, bf16[768,256]{1,0:T(8,128)(2,1)S(1)}, u32[]{:S(2)}, u32[]{:S(2)}) collective-permute-start(bf16[768,256]{1,0:T(8,128)(2,1)S(1)} %shard_map.56.rest_0_), channel_id=1, source_target_pairs={{0,12},{1,13},{2,14},{3,15},{4,0},{5,1},{6,2},{7,3},{8,4},{9,5},{1... | collective-permute-start | bytes 1179656 | tf_op jit(solution)/shard_map/ppermute | solution.py:34
  21.8 13.2 %collective-permute-start.3 = (bf16[768,256]{1,0:T(8,128)(2,1)S(1)}, bf16[768,256]{1,0:T(8,128)(2,1)S(1)}, u32[]{:S(2)}, u32[]{:S(2)}) collective-permute-start(bf16[768,256]{1,0:T(8,128)(2,1)S(1)} %shard_map.56.rest_0_), channel_id=1, source_target_pairs={{0,1},{1,2},{2,3},{3,0},{4,5},{5,6},{6,7},{7,4},{8,9},{9,10},{10,1... | collective-permute-start | bytes 1179656 | tf_op jit(solution)/shard_map/ppermute | solution.py:29
  23.7 12.1 %collective-permute-start.4 = (bf16[768,256]{1,0:T(8,128)(2,1)S(1)}, bf16[768,256]{1,0:T(8,128)(2,1)S(1)}, u32[]{:S(2)}, u32[]{:S(2)}) collective-permute-start(bf16[768,256]{1,0:T(8,128)(2,1)S(1)} %shard_map.56.rest_0_), channel_id=1, source_target_pairs={{0,3},{1,0},{2,1},{3,2},{4,7},{5,4},{6,5},{7,6},{8,11},{9,8},{10,9... | collective-permute-start | bytes 1179656 | tf_op jit(solution)/shard_map/ppermute | solution.py:29
  35.9 19.0 %collective-permute-start.5 = (bf16[2,4096,256]{2,1,0:T(8,128)(2,1)}, bf16[2,4096,256]{2,1,0:T(8,128)(2,1)S(1)}, u32[]{:S(2)}, u32[]{:S(2)}) collective-permute-start(bf16[2,4096,256]{2,1,0:T(8,128)(2,1)} %bitcast.3), channel_id=1, source_target_pairs={{0,384},{384,0},{1,385},{385,1},{2,386},{386,2},{3,387},{387,3},{4... | collective-permute-start | bytes 12582920 | tf_op jit(solution)/shard_map/ppermute | solution.py:219
  39.7 25.1 %collective-permute-start.7 = (bf16[1728,256]{1,0:T(8,128)(2,1)S(1)}, bf16[1728,256]{1,0:T(8,128)(2,1)S(1)}, u32[]{:S(2)}, u32[]{:S(2)}) collective-permute-start(bf16[1728,256]{1,0:T(8,128)(2,1)S(1)} %pad_maximum_fusion.1), channel_id=1, source_target_pairs={{0,3},{1,0},{2,1},{3,2},{4,7},{5,4},{6,5},{7,6},{8,11},{9,8},{10,9... | collective-permute-start | bytes 2654216 | tf_op jit(solution)/shard_map/ppermute | solution.py:29
  45.0 9.9 %copy-start = (bf16[1,2,4096,256]{3,2,1,0:T(8,128)(2,1)S(1)}, bf16[1,2,4096,256]{3,2,1,0:T(8,128)(2,1)}, u32[]{:S(2)}) copy-start(bf16[1,2,4096,256]{3,2,1,0:T(8,128)(2,1)} %param.6) | copy-start | bytes 12582916
  45.1 24.3 %collective-permute-start.6 = (bf16[1728,256]{1,0:T(8,128)(2,1)S(1)}, bf16[1728,256]{1,0:T(8,128)(2,1)S(1)}, u32[]{:S(2)}, u32[]{:S(2)}) collective-permute-start(bf16[1728,256]{1,0:T(8,128)(2,1)S(1)} %pad_maximum_fusion), channel_id=1, source_target_pairs={{0,1},{1,2},{2,3},{3,0},{4,5},{5,6},{6,7},{7,4},{8,9},{9,10},{10,1... | collective-permute-start | bytes 2654216 | tf_op jit(solution)/shard_map/ppermute | solution.py:29
  47.4 12.8 %collective-permute-start.8 = (bf16[576,256]{1,0:T(8,128)(2,1)S(1)}, bf16[576,256]{1,0:T(8,128)(2,1)S(1)}, u32[]{:S(2)}, u32[]{:S(2)}) collective-permute-start(bf16[576,256]{1,0:T(8,128)(2,1)S(1)} %pad_maximum_fusion.5), channel_id=1, source_target_pairs={{0,4},{1,5},{2,6},{3,7},{4,8},{5,9},{6,10},{7,11},{8,12},{9,13},{1... | collective-permute-start | bytes 884744 | tf_op jit(solution)/shard_map/ppermute | solution.py:34
  49.4 15.4 %collective-permute-start.9 = (bf16[576,256]{1,0:T(8,128)(2,1)S(1)}, bf16[576,256]{1,0:T(8,128)(2,1)S(1)}, u32[]{:S(2)}, u32[]{:S(2)}) collective-permute-start(bf16[576,256]{1,0:T(8,128)(2,1)S(1)} %pad_maximum_fusion.6), channel_id=1, source_target_pairs={{0,12},{1,13},{2,14},{3,15},{4,0},{5,1},{6,2},{7,3},{8,4},{9,5},{1... | collective-permute-start | bytes 884744 | tf_op jit(solution)/shard_map/ppermute | solution.py:34
  69.6 24.8 %collective-permute-start.11 = (bf16[1056,256]{1,0:T(8,128)(2,1)S(1)}, bf16[1056,256]{1,0:T(8,128)(2,1)S(1)}, u32[]{:S(2)}, u32[]{:S(2)}) collective-permute-start(bf16[1056,256]{1,0:T(8,128)(2,1)S(1)} %pad_maximum_fusion.3), channel_id=1, source_target_pairs={{0,3},{1,0},{2,1},{3,2},{4,7},{5,4},{6,5},{7,6},{8,11},{9,8},{10,9... | collective-permute-start | bytes 1622024 | tf_op jit(solution)/shard_map/ppermute | solution.py:29
  71.6 24.2 %collective-permute-start.10 = (bf16[1056,256]{1,0:T(8,128)(2,1)S(1)}, bf16[1056,256]{1,0:T(8,128)(2,1)S(1)}, u32[]{:S(2)}, u32[]{:S(2)}) collective-permute-start(bf16[1056,256]{1,0:T(8,128)(2,1)S(1)} %pad_maximum_fusion.2), channel_id=1, source_target_pairs={{0,1},{1,2},{2,3},{3,0},{4,5},{5,6},{6,7},{7,4},{8,9},{9,10},{10,1... | collective-permute-start | bytes 1622024 | tf_op jit(solution)/shard_map/ppermute | solution.py:29
  75.0 19.4 %collective-permute-start.12 = (bf16[768,256]{1,0:T(8,128)(2,1)S(1)}, bf16[768,256]{1,0:T(8,128)(2,1)S(1)}, u32[]{:S(2)}, u32[]{:S(2)}) collective-permute-start(bf16[768,256]{1,0:T(8,128)(2,1)S(1)} %pad_maximum_fusion.4), channel_id=1, source_target_pairs={{0,2},{1,3},{2,0},{3,1},{4,6},{5,7},{6,4},{7,5},{8,10},{9,11},{10,... | collective-permute-start | bytes 1179656 | tf_op jit(solution)/shard_map/ppermute | solution.py:29
  77.0 13.1 %collective-permute-start.14 = (bf16[480,256]{1,0:T(8,128)(2,1)S(1)}, bf16[480,256]{1,0:T(8,128)(2,1)S(1)}, u32[]{:S(2)}, u32[]{:S(2)}) collective-permute-start(bf16[480,256]{1,0:T(8,128)(2,1)S(1)} %pad_maximum_fusion.8), channel_id=1, source_target_pairs={{0,12},{1,13},{2,14},{3,15},{4,0},{5,1},{6,2},{7,3},{8,4},{9,5},{1... | collective-permute-start | bytes 737288 | tf_op jit(solution)/shard_map/ppermute | solution.py:34
  79.2 14.9 %collective-permute-start.13 = (bf16[480,256]{1,0:T(8,128)(2,1)S(1)}, bf16[480,256]{1,0:T(8,128)(2,1)S(1)}, u32[]{:S(2)}, u32[]{:S(2)}) collective-permute-start(bf16[480,256]{1,0:T(8,128)(2,1)S(1)} %pad_maximum_fusion.7), channel_id=1, source_target_pairs={{0,4},{1,5},{2,6},{3,7},{4,8},{5,9},{6,10},{7,11},{8,12},{9,13},{1... | collective-permute-start | bytes 737288 | tf_op jit(solution)/shard_map/ppermute | solution.py:34
  84.2 12.4 %copy-start.3 = (s32[2]{0:T(128)S(1)}, s32[2]{0:T(128)}, u32[]{:S(2)}) copy-start(s32[2]{0:T(128)} %enc_ref.1) | copy-start | bytes 28
  84.3 12.4 %copy-start.4 = (s32[2]{0:T(128)S(1)}, s32[2]{0:T(128)}, u32[]{:S(2)}) copy-start(s32[2]{0:T(128)} %dec_ref.1) | copy-start | bytes 28
  99.0 19.2 %collective-permute-start.15 = (bf16[1024,256]{1,0:T(8,128)(2,1)S(1)}, bf16[1024,256]{1,0:T(8,128)(2,1)S(1)}, u32[]{:S(2)}, u32[]{:S(2)}) collective-permute-start(bf16[1024,256]{1,0:T(8,128)(2,1)S(1)} %get-tuple-element.63), channel_id=1, source_target_pairs={{0,1},{1,2},{2,3},{3,0},{4,5},{5,6},{6,7},{7,4},{8,9},{9,10},{10,1... | collective-permute-start | bytes 1572872 | tf_op jit(solution)/shard_map/ppermute | solution.py:29
  101.6 16.6 %collective-permute-start.16 = (bf16[1024,256]{1,0:T(8,128)(2,1)S(1)}, bf16[1024,256]{1,0:T(8,128)(2,1)S(1)}, u32[]{:S(2)}, u32[]{:S(2)}) collective-permute-start(bf16[1024,256]{1,0:T(8,128)(2,1)S(1)} %get-tuple-element.64), channel_id=1, source_target_pairs={{0,3},{1,0},{2,1},{3,2},{4,7},{5,4},{6,5},{7,6},{8,11},{9,8},{10,9... | collective-permute-start | bytes 1572872 | tf_op jit(solution)/shard_map/ppermute | solution.py:29
  105.5 12.7 %collective-permute-start.17 = (bf16[512,256]{1,0:T(8,128)(2,1)S(1)}, bf16[512,256]{1,0:T(8,128)(2,1)S(1)}, u32[]{:S(2)}, u32[]{:S(2)}) collective-permute-start(bf16[512,256]{1,0:T(8,128)(2,1)S(1)} %get-tuple-element.65), channel_id=1, source_target_pairs={{0,2},{1,3},{2,0},{3,1},{4,6},{5,7},{6,4},{7,5},{8,10},{9,11},{10,... | collective-permute-start | bytes 786440 | tf_op jit(solution)/shard_map/ppermute | solution.py:29
  118.4 17.8 %collective-permute-start.19 = (bf16[1280,256]{1,0:T(8,128)(2,1)S(1)}, bf16[1280,256]{1,0:T(8,128)(2,1)S(1)}, u32[]{:S(2)}, u32[]{:S(2)}) collective-permute-start(bf16[1280,256]{1,0:T(8,128)(2,1)S(1)} %get-tuple-element.71), channel_id=1, source_target_pairs={{0,1},{1,2},{2,3},{3,0},{4,5},{5,6},{6,7},{7,4},{8,9},{9,10},{10,1... | collective-permute-start | bytes 1966088 | tf_op jit(solution)/shard_map/ppermute | solution.py:29
  123.8 14.9 %collective-permute-start.20 = (bf16[1280,256]{1,0:T(8,128)(2,1)S(1)}, bf16[1280,256]{1,0:T(8,128)(2,1)S(1)}, u32[]{:S(2)}, u32[]{:S(2)}) collective-permute-start(bf16[1280,256]{1,0:T(8,128)(2,1)S(1)} %get-tuple-element.72), channel_id=1, source_target_pairs={{0,3},{1,0},{2,1},{3,2},{4,7},{5,4},{6,5},{7,6},{8,11},{9,8},{10,9... | collective-permute-start | bytes 1966088 | tf_op jit(solution)/shard_map/ppermute | solution.py:29
  126.9 25.9 %collective-permute-start.18 = (bf16[512,256]{1,0:T(8,128)(2,1)S(1)}, bf16[512,256]{1,0:T(8,128)(2,1)S(1)}, u32[]{:S(2)}, u32[]{:S(2)}) collective-permute-start(bf16[512,256]{1,0:T(8,128)(2,1)S(1)} %get-tuple-element.66), channel_id=1, source_target_pairs={{0,8},{1,9},{2,10},{3,11},{4,12},{5,13},{6,14},{7,15},{8,0},{9,1},... | collective-permute-start | bytes 786440 | tf_op jit(solution)/shard_map/ppermute | solution.py:34
  138.9 17.8 %collective-permute-start.21 = (bf16[512,256]{1,0:T(8,128)(2,1)S(1)}, bf16[512,256]{1,0:T(8,128)(2,1)S(1)}, u32[]{:S(2)}, u32[]{:S(2)}) collective-permute-start(bf16[512,256]{1,0:T(8,128)(2,1)S(1)} %get-tuple-element.73), channel_id=1, source_target_pairs={{0,4},{1,5},{2,6},{3,7},{4,8},{5,9},{6,10},{7,11},{8,12},{9,13},{1... | collective-permute-start | bytes 786440 | tf_op jit(solution)/shard_map/ppermute | solution.py:34
  140.8 15.9 %collective-permute-start.22 = (bf16[512,256]{1,0:T(8,128)(2,1)S(1)}, bf16[512,256]{1,0:T(8,128)(2,1)S(1)}, u32[]{:S(2)}, u32[]{:S(2)}) collective-permute-start(bf16[512,256]{1,0:T(8,128)(2,1)S(1)} %get-tuple-element.74), channel_id=1, source_target_pairs={{0,12},{1,13},{2,14},{3,15},{4,0},{5,1},{6,2},{7,3},{8,4},{9,5},{1... | collective-permute-start | bytes 786440 | tf_op jit(solution)/shard_map/ppermute | solution.py:34
  146.3 10.4 %collective-permute-start.23 = (bf16[512,256]{1,0:T(8,128)(2,1)S(1)}, bf16[512,256]{1,0:T(8,128)(2,1)S(1)}, u32[]{:S(2)}, u32[]{:S(2)}) collective-permute-start(bf16[512,256]{1,0:T(8,128)(2,1)S(1)} %get-tuple-element.75), channel_id=1, source_target_pairs={{0,1},{1,2},{2,3},{3,0},{4,5},{5,6},{6,7},{7,4},{8,9},{9,10},{10,1... | collective-permute-start | bytes 786440 | tf_op jit(solution)/shard_map/ppermute | solution.py:29
  148.3 8.4 %collective-permute-start.24 = (bf16[512,256]{1,0:T(8,128)(2,1)S(1)}, bf16[512,256]{1,0:T(8,128)(2,1)S(1)}, u32[]{:S(2)}, u32[]{:S(2)}) collective-permute-start(bf16[512,256]{1,0:T(8,128)(2,1)S(1)} %get-tuple-element.76), channel_id=1, source_target_pairs={{0,3},{1,0},{2,1},{3,2},{4,7},{5,4},{6,5},{7,6},{8,11},{9,8},{10,9... | collective-permute-start | bytes 786440 | tf_op jit(solution)/shard_map/ppermute | solution.py:29
  156.8 8.3 %collective-permute-start.25 = (bf16[256,256]{1,0:T(8,128)(2,1)S(1)}, bf16[256,256]{1,0:T(8,128)(2,1)S(1)}, u32[]{:S(2)}, u32[]{:S(2)}) collective-permute-start(bf16[256,256]{1,0:T(8,128)(2,1)S(1)} %shard_map.64), channel_id=1, source_target_pairs={{0,384},{384,0},{1,385},{385,1},{2,386},{386,2},{3,387},{387,3},{4... | collective-permute-start | bytes 393224 | tf_op jit(solution)/shard_map/ppermute | solution.py:291

commit v9 on v8

--- a/solution.py
+++ b/solution.py
@@ -9,9 +9,9 @@
 SIDE = 4
 ROWS = 3 * HS
 HALF = ROWS // 2
-D = 192
+D = 288
 E = 96
-MOST = 528
+MOST = 480
 REST = ROWS - MOST
 N = 2 * HS
 F32 = jnp.float32

time: 167 us -> 168 us (level)
    ppermute x14, waiting for transfers between devices: 27.4 us -> 19.7 us  [shift_x(): return lax.ppermute(block, 'mp', route)]
    ppermute x9, waiting for transfers between devices: 27.8 us -> 35.2 us  [shift_y(): return lax.ppermute(block, 'mp', route)]
    ppermute x9, starting transfers between devices: 30.3 us -> 35.9 us  [shift_y(): return lax.ppermute(block, 'mp', route)]
    ppermute x1, starting transfers between devices: 7.33 us -> 3.96 us  [local(): swapped = lax.ppermute(sent, 'section', SWAP)]
  transfers between devices with their start and end apart: 26 -> 26, of which waited for: 16 -> 14; matrix products, arithmetic and copies ran while one was open for 0% -> 0% of each run, Pallas kernels for 2% -> 2%
where the time goes in v9:
time: 168 us; the launch traced here: 167 us
  starting transfers between devices  99.5 us (59%)
  waiting for transfers between devices  56 us (33%)
  Pallas kernels  8.21 us (5%)
  local copies, waits for them, and re-layouts  2.16 us (1%)
    ppermute x14, starting transfers between devices, shift_x(): return lax.ppermute(block, 'mp', route)  43.6 us
    ppermute x9, starting transfers between devices, shift_y(): return lax.ppermute(block, 'mp', route)  35.9 us
    ppermute x9, waiting for transfers between devices, shift_y(): return lax.ppermute(block, 'mp', route)  35.2 us
    ppermute x14, waiting for transfers between devices, shift_x(): return lax.ppermute(block, 'mp', route)  19.7 us
    ppermute x1, starting transfers between devices, local(): partner = lax.ppermute(own, 'section', SWAP)  12.4 us
    pallas_call x11, Pallas kernels, call(): pl.pallas_call(body, out_shape=out, in_specs=[SMEM] * scalars + [VMEM] *...  8.21 us
    ppermute x1, starting transfers between devices, local(): swapped = lax.ppermute(sent, 'section', SWAP)  3.96 us
    ppermute x1, starting transfers between devices, local(): other_w = lax.ppermute(own_w, 'section', SWAP)  3.65 us
  transfers between devices with their start and end apart: 26, of which 14 were waited for; matrix products, arithmetic and copies ran while one was open for 0% of the time, Pallas kernels for 2%

profile of v9, /device:TPU:1, one launch (start us, length us, event | category | flops | bytes accessed | tf_op | source)
XLA Modules:
  0.0 166.7 jit_solution(3383899545075179060)
XLA Ops:
  0.0 12.4 %collective-permute-start = (bf16[512,256]{1,0:T(8,128)(2,1)}, bf16[512,256]{1,0:T(8,128)(2,1)S(1)}, u32[]{:S(2)}, u32[]{:S(2)}) collective-permute-start(bf16[512,256]{1,0:T(8,128)(2,1)} %bitcast.9), channel_id=1, source_target_pairs={{0,384},{384,0},{1,385},{385,1},{2,386},{386,2},{3,387},{387,3},{4... | collective-permute-start | bytes 786440 | tf_op jit(solution)/shard_map/ppermute | solution.py:211
  14.4 1.9 %collective-permute-start.1 = (bf16[768,256]{1,0:T(8,128)(2,1)S(1)}, bf16[768,256]{1,0:T(8,128)(2,1)S(1)}, u32[]{:S(2)}, u32[]{:S(2)}) collective-permute-start(bf16[768,256]{1,0:T(8,128)(2,1)S(1)} %shard_map.56.rest_0_), channel_id=1, source_target_pairs={{0,4},{1,5},{2,6},{3,7},{4,8},{5,9},{6,10},{7,11},{8,12},{9,13},{1... | collective-permute-start | bytes 1179656 | tf_op jit(solution)/shard_map/ppermute | solution.py:34
  16.3 5.5 %collective-permute-start.2 = (bf16[768,256]{1,0:T(8,128)(2,1)S(1)}, bf16[768,256]{1,0:T(8,128)(2,1)S(1)}, u32[]{:S(2)}, u32[]{:S(2)}) collective-permute-start(bf16[768,256]{1,0:T(8,128)(2,1)S(1)} %shard_map.56.rest_0_), channel_id=1, source_target_pairs={{0,12},{1,13},{2,14},{3,15},{4,0},{5,1},{6,2},{7,3},{8,4},{9,5},{1... | collective-permute-start | bytes 1179656 | tf_op jit(solution)/shard_map/ppermute | solution.py:34
  21.8 1.9 %collective-permute-start.3 = (bf16[768,256]{1,0:T(8,128)(2,1)S(1)}, bf16[768,256]{1,0:T(8,128)(2,1)S(1)}, u32[]{:S(2)}, u32[]{:S(2)}) collective-permute-start(bf16[768,256]{1,0:T(8,128)(2,1)S(1)} %shard_map.56.rest_0_), channel_id=1, source_target_pairs={{0,1},{1,2},{2,3},{3,0},{4,5},{5,6},{6,7},{7,4},{8,9},{9,10},{10,1... | collective-permute-start | bytes 1179656 | tf_op jit(solution)/shard_map/ppermute | solution.py:29
  23.7 4.6 %collective-permute-start.4 = (bf16[768,256]{1,0:T(8,128)(2,1)S(1)}, bf16[768,256]{1,0:T(8,128)(2,1)S(1)}, u32[]{:S(2)}, u32[]{:S(2)}) collective-permute-start(bf16[768,256]{1,0:T(8,128)(2,1)S(1)} %shard_map.56.rest_0_), channel_id=1, source_target_pairs={{0,3},{1,0},{2,1},{3,2},{4,7},{5,4},{6,5},{7,6},{8,11},{9,8},{10,9... | collective-permute-start | bytes 1179656 | tf_op jit(solution)/shard_map/ppermute | solution.py:29
  28.3 4.3 %collective-permute-done.1.rest_1_ = bf16[768,256]{1,0:T(8,128)(2,1)S(1)} collective-permute-done((bf16[768,256]{1,0:T(8,128)(2,1)S(1)}, bf16[768,256]{1,0:T(8,128)(2,1)S(1)}, u32[]{:S(2)}, u32[]{:S(2)}) %collective-permute-start.1) | collective-permute-done | bytes 393248 | tf_op jit(solution)/shard_map/ppermute | solution.py:34
  35.9 3.7 %collective-permute-start.5 = (bf16[2,4096,256]{2,1,0:T(8,128)(2,1)}, bf16[2,4096,256]{2,1,0:T(8,128)(2,1)S(1)}, u32[]{:S(2)}, u32[]{:S(2)}) collective-permute-start(bf16[2,4096,256]{2,1,0:T(8,128)(2,1)} %bitcast.3), channel_id=1, source_target_pairs={{0,384},{384,0},{1,385},{385,1},{2,386},{386,2},{3,387},{387,3},{4... | collective-permute-start | bytes 12582920 | tf_op jit(solution)/shard_map/ppermute | solution.py:219
  39.7 5.3 %collective-permute-start.7 = (bf16[1632,256]{1,0:T(8,128)(2,1)S(1)}, bf16[1632,256]{1,0:T(8,128)(2,1)S(1)}, u32[]{:S(2)}, u32[]{:S(2)}) collective-permute-start(bf16[1632,256]{1,0:T(8,128)(2,1)S(1)} %pad_maximum_fusion.1), channel_id=1, source_target_pairs={{0,3},{1,0},{2,1},{3,2},{4,7},{5,4},{6,5},{7,6},{8,11},{9,8},{10,9... | collective-permute-start | bytes 2506760 | tf_op jit(solution)/shard_map/ppermute | solution.py:29
  45.1 2.2 %collective-permute-start.6 = (bf16[1632,256]{1,0:T(8,128)(2,1)S(1)}, bf16[1632,256]{1,0:T(8,128)(2,1)S(1)}, u32[]{:S(2)}, u32[]{:S(2)}) collective-permute-start(bf16[1632,256]{1,0:T(8,128)(2,1)S(1)} %pad_maximum_fusion), channel_id=1, source_target_pairs={{0,1},{1,2},{2,3},{3,0},{4,5},{5,6},{6,7},{7,4},{8,9},{9,10},{10,1... | collective-permute-start | bytes 2506760 | tf_op jit(solution)/shard_map/ppermute | solution.py:29
  47.4 1.9 %collective-permute-start.8 = (bf16[672,256]{1,0:T(8,128)(2,1)S(1)}, bf16[672,256]{1,0:T(8,128)(2,1)S(1)}, u32[]{:S(2)}, u32[]{:S(2)}) collective-permute-start(bf16[672,256]{1,0:T(8,128)(2,1)S(1)} %pad_maximum_fusion.5), channel_id=1, source_target_pairs={{0,4},{1,5},{2,6},{3,7},{4,8},{5,9},{6,10},{7,11},{8,12},{9,13},{1... | collective-permute-start | bytes 1032200 | tf_op jit(solution)/shard_map/ppermute | solution.py:34
  49.4 5.5 %collective-permute-start.9 = (bf16[672,256]{1,0:T(8,128)(2,1)S(1)}, bf16[672,256]{1,0:T(8,128)(2,1)S(1)}, u32[]{:S(2)}, u32[]{:S(2)}) collective-permute-start(bf16[672,256]{1,0:T(8,128)(2,1)S(1)} %pad_maximum_fusion.6), channel_id=1, source_target_pairs={{0,12},{1,13},{2,14},{3,15},{4,0},{5,1},{6,2},{7,3},{8,4},{9,5},{1... | collective-permute-start | bytes 1032200 | tf_op jit(solution)/shard_map/ppermute | solution.py:34
  55.7 7.0 %collective-permute-done.8.rest_2_ = bf16[672,256]{1,0:T(8,128)(2,1)S(1)} collective-permute-done((bf16[672,256]{1,0:T(8,128)(2,1)S(1)}, bf16[672,256]{1,0:T(8,128)(2,1)S(1)}, u32[]{:S(2)}, u32[]{:S(2)}) %collective-permute-start.8) | collective-permute-done | bytes 344096 | tf_op jit(solution)/shard_map/ppermute | solution.py:34
  62.7 4.0 %collective-permute-done.9.rest_3_ = bf16[672,256]{1,0:T(8,128)(2,1)S(1)} collective-permute-done((bf16[672,256]{1,0:T(8,128)(2,1)S(1)}, bf16[672,256]{1,0:T(8,128)(2,1)S(1)}, u32[]{:S(2)}, u32[]{:S(2)}) %collective-permute-start.9) | collective-permute-done | bytes 344096 | tf_op jit(solution)/shard_map/ppermute | solution.py:34
  68.5 3.0 %collective-permute-start.11 = (bf16[1152,256]{1,0:T(8,128)(2,1)S(1)}, bf16[1152,256]{1,0:T(8,128)(2,1)S(1)}, u32[]{:S(2)}, u32[]{:S(2)}) collective-permute-start(bf16[1152,256]{1,0:T(8,128)(2,1)S(1)} %pad_maximum_fusion.2), channel_id=1, source_target_pairs={{0,3},{1,0},{2,1},{3,2},{4,7},{5,4},{6,5},{7,6},{8,11},{9,8},{10,9... | collective-permute-start | bytes 1769480 | tf_op jit(solution)/shard_map/ppermute | solution.py:29
  71.6 2.3 %collective-permute-start.10 = (bf16[960,256]{1,0:T(8,128)(2,1)S(1)}, bf16[960,256]{1,0:T(8,128)(2,1)S(1)}, u32[]{:S(2)}, u32[]{:S(2)}) collective-permute-start(bf16[960,256]{1,0:T(8,128)(2,1)S(1)} %pad_maximum_fusion.3), channel_id=1, source_target_pairs={{0,1},{1,2},{2,3},{3,0},{4,5},{5,6},{6,7},{7,4},{8,9},{9,10},{10,1... | collective-permute-start | bytes 1474568 | tf_op jit(solution)/shard_map/ppermute | solution.py:29
  74.0 2.7 %collective-permute-start.12 = (bf16[768,256]{1,0:T(8,128)(2,1)S(1)}, bf16[768,256]{1,0:T(8,128)(2,1)S(1)}, u32[]{:S(2)}, u32[]{:S(2)}) collective-permute-start(bf16[768,256]{1,0:T(8,128)(2,1)S(1)} %pad_maximum_fusion.4), channel_id=1, source_target_pairs={{0,2},{1,3},{2,0},{3,1},{4,6},{5,7},{6,4},{7,5},{8,10},{9,11},{10,... | collective-permute-start | bytes 1179656 | tf_op jit(solution)/shard_map/ppermute | solution.py:29
  76.7 4.5 %collective-permute-start.14 = (bf16[480,256]{1,0:T(8,128)(2,1)S(1)}, bf16[480,256]{1,0:T(8,128)(2,1)S(1)}, u32[]{:S(2)}, u32[]{:S(2)}) collective-permute-start(bf16[480,256]{1,0:T(8,128)(2,1)S(1)} %pad_maximum_fusion.8), channel_id=1, source_target_pairs={{0,12},{1,13},{2,14},{3,15},{4,0},{5,1},{6,2},{7,3},{8,4},{9,5},{1... | collective-permute-start | bytes 737288 | tf_op jit(solution)/shard_map/ppermute | solution.py:34
  84.3 6.3 %collective-permute-done.14.rest_4_ = bf16[480,256]{1,0:T(8,128)(2,1)S(1)} collective-permute-done((bf16[480,256]{1,0:T(8,128)(2,1)S(1)}, bf16[480,256]{1,0:T(8,128)(2,1)S(1)}, u32[]{:S(2)}, u32[]{:S(2)}) %collective-permute-start.14) | collective-permute-done | bytes 245792 | tf_op jit(solution)/shard_map/ppermute | solution.py:34
  90.5 5.8 %collective-permute-done.13.rest_3_ = bf16[480,256]{1,0:T(8,128)(2,1)S(1)} collective-permute-done((bf16[480,256]{1,0:T(8,128)(2,1)S(1)}, bf16[480,256]{1,0:T(8,128)(2,1)S(1)}, u32[]{:S(2)}, u32[]{:S(2)}) %collective-permute-start.13) | collective-permute-done | bytes 245792 | tf_op jit(solution)/shard_map/ppermute | solution.py:34
  97.2 2.3 %shard_map.60 = (bf16[1024,256]{1,0:T(8,128)(2,1)S(1)}, bf16[1024,256]{1,0:T(8,128)(2,1)S(1)}, bf16[512,256]{1,0:T(8,128)(2,1)S(1)}, bf16[4,256,256]{2,1,0:T(8,128)(2,1)S(1)}) custom-call(s32[2]{0:T(128)S(1)} %copy-done.3, s32[2]{0:T(128)S(1)} %copy-done.4, f32[4,256,256]{2,1,0:T(8,128)S(1)} %shard_map.59.t_ref, bf16[2,4096,256]{2,1,0:T(8,128)(2,1)S(1)} %bitcast.7, ...), custom_call_target="tpu_custom_call" | custom-call | flops 1006632960 | bytes 9437200 | tf_op jit(solution)/shard_map/pallas_call | solution.py:44
  101.4 4.6 %collective-permute-start.16 = (bf16[1024,256]{1,0:T(8,128)(2,1)S(1)}, bf16[1024,256]{1,0:T(8,128)(2,1)S(1)}, u32[]{:S(2)}, u32[]{:S(2)}) collective-permute-start(bf16[1024,256]{1,0:T(8,128)(2,1)S(1)} %get-tuple-element.64), channel_id=1, source_target_pairs={{0,3},{1,0},{2,1},{3,2},{4,7},{5,4},{6,5},{7,6},{8,11},{9,8},{10,9... | collective-permute-start | bytes 1572872 | tf_op jit(solution)/shard_map/ppermute | solution.py:29
  106.0 2.1 %collective-permute-start.17 = (bf16[512,256]{1,0:T(8,128)(2,1)S(1)}, bf16[512,256]{1,0:T(8,128)(2,1)S(1)}, u32[]{:S(2)}, u32[]{:S(2)}) collective-permute-start(bf16[512,256]{1,0:T(8,128)(2,1)S(1)} %get-tuple-element.65), channel_id=1, source_target_pairs={{0,2},{1,3},{2,0},{3,1},{4,6},{5,7},{6,4},{7,5},{8,10},{9,11},{10,... | collective-permute-start | bytes 786440 | tf_op jit(solution)/shard_map/ppermute | solution.py:29
  109.9 10.2 %collective-permute-done.17.refs_5_ = bf16[512,256]{1,0:T(8,128)(2,1)S(1)} collective-permute-done((bf16[512,256]{1,0:T(8,128)(2,1)S(1)}, bf16[512,256]{1,0:T(8,128)(2,1)S(1)}, u32[]{:S(2)}, u32[]{:S(2)}) %collective-permute-start.17) | collective-permute-done | bytes 262176 | tf_op jit(solution)/shard_map/ppermute | solution.py:29
  120.3 4.4 %collective-permute-start.19 = (bf16[1280,256]{1,0:T(8,128)(2,1)S(1)}, bf16[1280,256]{1,0:T(8,128)(2,1)S(1)}, u32[]{:S(2)}, u32[]{:S(2)}) collective-permute-start(bf16[1280,256]{1,0:T(8,128)(2,1)S(1)} %get-tuple-element.71), channel_id=1, source_target_pairs={{0,1},{1,2},{2,3},{3,0},{4,5},{5,6},{6,7},{7,4},{8,9},{9,10},{10,1... | collective-permute-start | bytes 1966088 | tf_op jit(solution)/shard_map/ppermute | solution.py:29
  124.7 2.1 %collective-permute-start.20 = (bf16[1280,256]{1,0:T(8,128)(2,1)S(1)}, bf16[1280,256]{1,0:T(8,128)(2,1)S(1)}, u32[]{:S(2)}, u32[]{:S(2)}) collective-permute-start(bf16[1280,256]{1,0:T(8,128)(2,1)S(1)} %get-tuple-element.72), channel_id=1, source_target_pairs={{0,3},{1,0},{2,1},{3,2},{4,7},{5,4},{6,5},{7,6},{8,11},{9,8},{10,9... | collective-permute-start | bytes 1966088 | tf_op jit(solution)/shard_map/ppermute | solution.py:29
  126.8 7.3 %collective-permute-start.18 = (bf16[512,256]{1,0:T(8,128)(2,1)S(1)}, bf16[512,256]{1,0:T(8,128)(2,1)S(1)}, u32[]{:S(2)}, u32[]{:S(2)}) collective-permute-start(bf16[512,256]{1,0:T(8,128)(2,1)S(1)} %get-tuple-element.66), channel_id=1, source_target_pairs={{0,8},{1,9},{2,10},{3,11},{4,12},{5,13},{6,14},{7,15},{8,0},{9,1},... | collective-permute-start | bytes 786440 | tf_op jit(solution)/shard_map/ppermute | solution.py:34
  135.7 3.8 %collective-permute-done.20.refs_5_ = bf16[1280,256]{1,0:T(8,128)(2,1)S(1)} collective-permute-done((bf16[1280,256]{1,0:T(8,128)(2,1)S(1)}, bf16[1280,256]{1,0:T(8,128)(2,1)S(1)}, u32[]{:S(2)}, u32[]{:S(2)}) %collective-permute-start.20) | collective-permute-done | bytes 655392 | tf_op jit(solution)/shard_map/ppermute | solution.py:29
  139.8 3.3 %collective-permute-start.21 = (bf16[512,256]{1,0:T(8,128)(2,1)S(1)}, bf16[512,256]{1,0:T(8,128)(2,1)S(1)}, u32[]{:S(2)}, u32[]{:S(2)}) collective-permute-start(bf16[512,256]{1,0:T(8,128)(2,1)S(1)} %get-tuple-element.73), channel_id=1, source_target_pairs={{0,4},{1,5},{2,6},{3,7},{4,8},{5,9},{6,10},{7,11},{8,12},{9,13},{1... | collective-permute-start | bytes 786440 | tf_op jit(solution)/shard_map/ppermute | solution.py:34
  143.1 4.1 %collective-permute-start.22 = (bf16[512,256]{1,0:T(8,128)(2,1)S(1)}, bf16[512,256]{1,0:T(8,128)(2,1)S(1)}, u32[]{:S(2)}, u32[]{:S(2)}) collective-permute-start(bf16[512,256]{1,0:T(8,128)(2,1)S(1)} %get-tuple-element.74), channel_id=1, source_target_pairs={{0,12},{1,13},{2,14},{3,15},{4,0},{5,1},{6,2},{7,3},{8,4},{9,5},{1... | collective-permute-start | bytes 786440 | tf_op jit(solution)/shard_map/ppermute | solution.py:34
  149.2 4.6 %collective-permute-start.24 = (bf16[512,256]{1,0:T(8,128)(2,1)S(1)}, bf16[512,256]{1,0:T(8,128)(2,1)S(1)}, u32[]{:S(2)}, u32[]{:S(2)}) collective-permute-start(bf16[512,256]{1,0:T(8,128)(2,1)S(1)} %get-tuple-element.76), channel_id=1, source_target_pairs={{0,3},{1,0},{2,1},{3,2},{4,7},{5,4},{6,5},{7,6},{8,11},{9,8},{10,9... | collective-permute-start | bytes 786440 | tf_op jit(solution)/shard_map/ppermute | solution.py:29
  153.8 7.1 %collective-permute-done.22.refs_3_.rest_2_ = bf16[512,256]{1,0:T(8,128)(2,1)S(1)} collective-permute-done((bf16[512,256]{1,0:T(8,128)(2,1)S(1)}, bf16[512,256]{1,0:T(8,128)(2,1)S(1)}, u32[]{:S(2)}, u32[]{:S(2)}) %collective-permute-start.22) | collective-permute-done | bytes 262176 | tf_op jit(solution)/shard_map/ppermute | solution.py:34
  161.0 4.0 %collective-permute-start.25 = (bf16[256,256]{1,0:T(8,128)(2,1)S(1)}, bf16[256,256]{1,0:T(8,128)(2,1)S(1)}, u32[]{:S(2)}, u32[]{:S(2)}) collective-permute-start(bf16[256,256]{1,0:T(8,128)(2,1)S(1)} %shard_map.64), channel_id=1, source_target_pairs={{0,384},{384,0},{1,385},{385,1},{2,386},{386,2},{3,387},{387,3},{4... | collective-permute-start | bytes 393224 | tf_op jit(solution)/shard_map/ppermute | solution.py:291
  (68 shorter events, 21.6 us)
Async XLA Ops:
  0.0 14.3 %collective-permute-start = (bf16[512,256]{1,0:T(8,128)(2,1)}, bf16[512,256]{1,0:T(8,128)(2,1)S(1)}, u32[]{:S(2)}, u32[]{:S(2)}) collective-permute-start(bf16[512,256]{1,0:T(8,128)(2,1)} %bitcast.9), channel_id=1, source_target_pairs={{0,384},{384,0},{1,385},{385,1},{2,386},{386,2},{3,387},{387,3},{4... | collective-permute-start | bytes 786440 | tf_op jit(solution)/shard_map/ppermute | solution.py:211
  12.4 1.0 copy-start.1
  13.4 0.9 copy-start.2
  14.4 18.3 %collective-permute-start.1 = (bf16[768,256]{1,0:T(8,128)(2,1)S(1)}, bf16[768,256]{1,0:T(8,128)(2,1)S(1)}, u32[]{:S(2)}, u32[]{:S(2)}) collective-permute-start(bf16[768,256]{1,0:T(8,128)(2,1)S(1)} %shard_map.56.rest_0_), channel_id=1, source_target_pairs={{0,4},{1,5},{2,6},{3,7},{4,8},{5,9},{6,10},{7,11},{8,12},{9,13},{1... | collective-permute-start | bytes 1179656 | tf_op jit(solution)/shard_map/ppermute | solution.py:34
  16.3 17.1 %collective-permute-start.2 = (bf16[768,256]{1,0:T(8,128)(2,1)S(1)}, bf16[768,256]{1,0:T(8,128)(2,1)S(1)}, u32[]{:S(2)}, u32[]{:S(2)}) collective-permute-start(bf16[768,256]{1,0:T(8,128)(2,1)S(1)} %shard_map.56.rest_0_), channel_id=1, source_target_pairs={{0,12},{1,13},{2,14},{3,15},{4,0},{5,1},{6,2},{7,3},{8,4},{9,5},{1... | collective-permute-start | bytes 1179656 | tf_op jit(solution)/shard_map/ppermute | solution.py:34
  21.8 13.2 %collective-permute-start.3 = (bf16[768,256]{1,0:T(8,128)(2,1)S(1)}, bf16[768,256]{1,0:T(8,128)(2,1)S(1)}, u32[]{:S(2)}, u32[]{:S(2)}) collective-permute-start(bf16[768,256]{1,0:T(8,128)(2,1)S(1)} %shard_map.56.rest_0_), channel_id=1, source_target_pairs={{0,1},{1,2},{2,3},{3,0},{4,5},{5,6},{6,7},{7,4},{8,9},{9,10},{10,1... | collective-permute-start | bytes 1179656 | tf_op jit(solution)/shard_map/ppermute | solution.py:29
  23.7 12.1 %collective-permute-start.4 = (bf16[768,256]{1,0:T(8,128)(2,1)S(1)}, bf16[768,256]{1,0:T(8,128)(2,1)S(1)}, u32[]{:S(2)}, u32[]{:S(2)}) collective-permute-start(bf16[768,256]{1,0:T(8,128)(2,1)S(1)} %shard_map.56.rest_0_), channel_id=1, source_target_pairs={{0,3},{1,0},{2,1},{3,2},{4,7},{5,4},{6,5},{7,6},{8,11},{9,8},{10,9... | collective-permute-start | bytes 1179656 | tf_op jit(solution)/shard_map/ppermute | solution.py:29
  35.9 19.0 %collective-permute-start.5 = (bf16[2,4096,256]{2,1,0:T(8,128)(2,1)}, bf16[2,4096,256]{2,1,0:T(8,128)(2,1)S(1)}, u32[]{:S(2)}, u32[]{:S(2)}) collective-permute-start(bf16[2,4096,256]{2,1,0:T(8,128)(2,1)} %bitcast.3), channel_id=1, source_target_pairs={{0,384},{384,0},{1,385},{385,1},{2,386},{386,2},{3,387},{387,3},{4... | collective-permute-start | bytes 12582920 | tf_op jit(solution)/shard_map/ppermute | solution.py:219
  39.7 27.1 %collective-permute-start.7 = (bf16[1632,256]{1,0:T(8,128)(2,1)S(1)}, bf16[1632,256]{1,0:T(8,128)(2,1)S(1)}, u32[]{:S(2)}, u32[]{:S(2)}) collective-permute-start(bf16[1632,256]{1,0:T(8,128)(2,1)S(1)} %pad_maximum_fusion.1), channel_id=1, source_target_pairs={{0,3},{1,0},{2,1},{3,2},{4,7},{5,4},{6,5},{7,6},{8,11},{9,8},{10,9... | collective-permute-start | bytes 2506760 | tf_op jit(solution)/shard_map/ppermute | solution.py:29
  45.0 9.8 %copy-start = (bf16[1,2,4096,256]{3,2,1,0:T(8,128)(2,1)S(1)}, bf16[1,2,4096,256]{3,2,1,0:T(8,128)(2,1)}, u32[]{:S(2)}) copy-start(bf16[1,2,4096,256]{3,2,1,0:T(8,128)(2,1)} %param.6) | copy-start | bytes 12582916
  45.1 23.3 %collective-permute-start.6 = (bf16[1632,256]{1,0:T(8,128)(2,1)S(1)}, bf16[1632,256]{1,0:T(8,128)(2,1)S(1)}, u32[]{:S(2)}, u32[]{:S(2)}) collective-permute-start(bf16[1632,256]{1,0:T(8,128)(2,1)S(1)} %pad_maximum_fusion), channel_id=1, source_target_pairs={{0,1},{1,2},{2,3},{3,0},{4,5},{5,6},{6,7},{7,4},{8,9},{9,10},{10,1... | collective-permute-start | bytes 2506760 | tf_op jit(solution)/shard_map/ppermute | solution.py:29
  47.4 15.3 %collective-permute-start.8 = (bf16[672,256]{1,0:T(8,128)(2,1)S(1)}, bf16[672,256]{1,0:T(8,128)(2,1)S(1)}, u32[]{:S(2)}, u32[]{:S(2)}) collective-permute-start(bf16[672,256]{1,0:T(8,128)(2,1)S(1)} %pad_maximum_fusion.5), channel_id=1, source_target_pairs={{0,4},{1,5},{2,6},{3,7},{4,8},{5,9},{6,10},{7,11},{8,12},{9,13},{1... | collective-permute-start | bytes 1032200 | tf_op jit(solution)/shard_map/ppermute | solution.py:34
  49.4 17.4 %collective-permute-start.9 = (bf16[672,256]{1,0:T(8,128)(2,1)S(1)}, bf16[672,256]{1,0:T(8,128)(2,1)S(1)}, u32[]{:S(2)}, u32[]{:S(2)}) collective-permute-start(bf16[672,256]{1,0:T(8,128)(2,1)S(1)} %pad_maximum_fusion.6), channel_id=1, source_target_pairs={{0,12},{1,13},{2,14},{3,15},{4,0},{5,1},{6,2},{7,3},{8,4},{9,5},{1... | collective-permute-start | bytes 1032200 | tf_op jit(solution)/shard_map/ppermute | solution.py:34
  68.5 27.8 %collective-permute-start.11 = (bf16[1152,256]{1,0:T(8,128)(2,1)S(1)}, bf16[1152,256]{1,0:T(8,128)(2,1)S(1)}, u32[]{:S(2)}, u32[]{:S(2)}) collective-permute-start(bf16[1152,256]{1,0:T(8,128)(2,1)S(1)} %pad_maximum_fusion.2), channel_id=1, source_target_pairs={{0,3},{1,0},{2,1},{3,2},{4,7},{5,4},{6,5},{7,6},{8,11},{9,8},{10,9... | collective-permute-start | bytes 1769480 | tf_op jit(solution)/shard_map/ppermute | solution.py:29
  71.6 24.7 %collective-permute-start.10 = (bf16[960,256]{1,0:T(8,128)(2,1)S(1)}, bf16[960,256]{1,0:T(8,128)(2,1)S(1)}, u32[]{:S(2)}, u32[]{:S(2)}) collective-permute-start(bf16[960,256]{1,0:T(8,128)(2,1)S(1)} %pad_maximum_fusion.3), channel_id=1, source_target_pairs={{0,1},{1,2},{2,3},{3,0},{4,5},{5,6},{6,7},{7,4},{8,9},{9,10},{10,1... | collective-permute-start | bytes 1474568 | tf_op jit(solution)/shard_map/ppermute | solution.py:29
  74.0 22.3 %collective-permute-start.12 = (bf16[768,256]{1,0:T(8,128)(2,1)S(1)}, bf16[768,256]{1,0:T(8,128)(2,1)S(1)}, u32[]{:S(2)}, u32[]{:S(2)}) collective-permute-start(bf16[768,256]{1,0:T(8,128)(2,1)S(1)} %pad_maximum_fusion.4), channel_id=1, source_target_pairs={{0,2},{1,3},{2,0},{3,1},{4,6},{5,7},{6,4},{7,5},{8,10},{9,11},{10,... | collective-permute-start | bytes 1179656 | tf_op jit(solution)/shard_map/ppermute | solution.py:29
  76.7 13.8 %collective-permute-start.14 = (bf16[480,256]{1,0:T(8,128)(2,1)S(1)}, bf16[480,256]{1,0:T(8,128)(2,1)S(1)}, u32[]{:S(2)}, u32[]{:S(2)}) collective-permute-start(bf16[480,256]{1,0:T(8,128)(2,1)S(1)} %pad_maximum_fusion.8), channel_id=1, source_target_pairs={{0,12},{1,13},{2,14},{3,15},{4,0},{5,1},{6,2},{7,3},{8,4},{9,5},{1... | collective-permute-start | bytes 737288 | tf_op jit(solution)/shard_map/ppermute | solution.py:34
  81.3 15.0 %collective-permute-start.13 = (bf16[480,256]{1,0:T(8,128)(2,1)S(1)}, bf16[480,256]{1,0:T(8,128)(2,1)S(1)}, u32[]{:S(2)}, u32[]{:S(2)}) collective-permute-start(bf16[480,256]{1,0:T(8,128)(2,1)S(1)} %pad_maximum_fusion.7), channel_id=1, source_target_pairs={{0,4},{1,5},{2,6},{3,7},{4,8},{5,9},{6,10},{7,11},{8,12},{9,13},{1... | collective-permute-start | bytes 737288 | tf_op jit(solution)/shard_map/ppermute | solution.py:34
  84.2 12.9 %copy-start.3 = (s32[2]{0:T(128)S(1)}, s32[2]{0:T(128)}, u32[]{:S(2)}) copy-start(s32[2]{0:T(128)} %enc_ref.1) | copy-start | bytes 28
  84.2 12.9 %copy-start.4 = (s32[2]{0:T(128)S(1)}, s32[2]{0:T(128)}, u32[]{:S(2)}) copy-start(s32[2]{0:T(128)} %dec_ref.1) | copy-start | bytes 28
  99.5 20.5 %collective-permute-start.15 = (bf16[1024,256]{1,0:T(8,128)(2,1)S(1)}, bf16[1024,256]{1,0:T(8,128)(2,1)S(1)}, u32[]{:S(2)}, u32[]{:S(2)}) collective-permute-start(bf16[1024,256]{1,0:T(8,128)(2,1)S(1)} %get-tuple-element.63), channel_id=1, source_target_pairs={{0,1},{1,2},{2,3},{3,0},{4,5},{5,6},{6,7},{7,4},{8,9},{9,10},{10,1... | collective-permute-start | bytes 1572872 | tf_op jit(solution)/shard_map/ppermute | solution.py:29
  101.4 18.6 %collective-permute-start.16 = (bf16[1024,256]{1,0:T(8,128)(2,1)S(1)}, bf16[1024,256]{1,0:T(8,128)(2,1)S(1)}, u32[]{:S(2)}, u32[]{:S(2)}) collective-permute-start(bf16[1024,256]{1,0:T(8,128)(2,1)S(1)} %get-tuple-element.64), channel_id=1, source_target_pairs={{0,3},{1,0},{2,1},{3,2},{4,7},{5,4},{6,5},{7,6},{8,11},{9,8},{10,9... | collective-permute-start | bytes 1572872 | tf_op jit(solution)/shard_map/ppermute | solution.py:29
  106.0 14.0 %collective-permute-start.17 = (bf16[512,256]{1,0:T(8,128)(2,1)S(1)}, bf16[512,256]{1,0:T(8,128)(2,1)S(1)}, u32[]{:S(2)}, u32[]{:S(2)}) collective-permute-start(bf16[512,256]{1,0:T(8,128)(2,1)S(1)} %get-tuple-element.65), channel_id=1, source_target_pairs={{0,2},{1,3},{2,0},{3,1},{4,6},{5,7},{6,4},{7,5},{8,10},{9,11},{10,... | collective-permute-start | bytes 786440 | tf_op jit(solution)/shard_map/ppermute | solution.py:29
  120.3 15.4 %collective-permute-start.19 = (bf16[1280,256]{1,0:T(8,128)(2,1)S(1)}, bf16[1280,256]{1,0:T(8,128)(2,1)S(1)}, u32[]{:S(2)}, u32[]{:S(2)}) collective-permute-start(bf16[1280,256]{1,0:T(8,128)(2,1)S(1)} %get-tuple-element.71), channel_id=1, source_target_pairs={{0,1},{1,2},{2,3},{3,0},{4,5},{5,6},{6,7},{7,4},{8,9},{9,10},{10,1... | collective-permute-start | bytes 1966088 | tf_op jit(solution)/shard_map/ppermute | solution.py:29
  124.7 14.8 %collective-permute-start.20 = (bf16[1280,256]{1,0:T(8,128)(2,1)S(1)}, bf16[1280,256]{1,0:T(8,128)(2,1)S(1)}, u32[]{:S(2)}, u32[]{:S(2)}) collective-permute-start(bf16[1280,256]{1,0:T(8,128)(2,1)S(1)} %get-tuple-element.72), channel_id=1, source_target_pairs={{0,3},{1,0},{2,1},{3,2},{4,7},{5,4},{6,5},{7,6},{8,11},{9,8},{10,9... | collective-permute-start | bytes 1966088 | tf_op jit(solution)/shard_map/ppermute | solution.py:29
  126.8 26.9 %collective-permute-start.18 = (bf16[512,256]{1,0:T(8,128)(2,1)S(1)}, bf16[512,256]{1,0:T(8,128)(2,1)S(1)}, u32[]{:S(2)}, u32[]{:S(2)}) collective-permute-start(bf16[512,256]{1,0:T(8,128)(2,1)S(1)} %get-tuple-element.66), channel_id=1, source_target_pairs={{0,8},{1,9},{2,10},{3,11},{4,12},{5,13},{6,14},{7,15},{8,0},{9,1},... | collective-permute-start | bytes 786440 | tf_op jit(solution)/shard_map/ppermute | solution.py:34
  139.8 13.9 %collective-permute-start.21 = (bf16[512,256]{1,0:T(8,128)(2,1)S(1)}, bf16[512,256]{1,0:T(8,128)(2,1)S(1)}, u32[]{:S(2)}, u32[]{:S(2)}) collective-permute-start(bf16[512,256]{1,0:T(8,128)(2,1)S(1)} %get-tuple-element.73), channel_id=1, source_target_pairs={{0,4},{1,5},{2,6},{3,7},{4,8},{5,9},{6,10},{7,11},{8,12},{9,13},{1... | collective-permute-start | bytes 786440 | tf_op jit(solution)/shard_map/ppermute | solution.py:34
  143.1 17.7 %collective-permute-start.22 = (bf16[512,256]{1,0:T(8,128)(2,1)S(1)}, bf16[512,256]{1,0:T(8,128)(2,1)S(1)}, u32[]{:S(2)}, u32[]{:S(2)}) collective-permute-start(bf16[512,256]{1,0:T(8,128)(2,1)S(1)} %get-tuple-element.74), channel_id=1, source_target_pairs={{0,12},{1,13},{2,14},{3,15},{4,0},{5,1},{6,2},{7,3},{8,4},{9,5},{1... | collective-permute-start | bytes 786440 | tf_op jit(solution)/shard_map/ppermute | solution.py:34
  147.2 13.6 %collective-permute-start.23 = (bf16[512,256]{1,0:T(8,128)(2,1)S(1)}, bf16[512,256]{1,0:T(8,128)(2,1)S(1)}, u32[]{:S(2)}, u32[]{:S(2)}) collective-permute-start(bf16[512,256]{1,0:T(8,128)(2,1)S(1)} %get-tuple-element.75), channel_id=1, source_target_pairs={{0,1},{1,2},{2,3},{3,0},{4,5},{5,6},{6,7},{7,4},{8,9},{9,10},{10,1... | collective-permute-start | bytes 786440 | tf_op jit(solution)/shard_map/ppermute | solution.py:29
  149.2 11.7 %collective-permute-start.24 = (bf16[512,256]{1,0:T(8,128)(2,1)S(1)}, bf16[512,256]{1,0:T(8,128)(2,1)S(1)}, u32[]{:S(2)}, u32[]{:S(2)}) collective-permute-start(bf16[512,256]{1,0:T(8,128)(2,1)S(1)} %get-tuple-element.76), channel_id=1, source_target_pairs={{0,3},{1,0},{2,1},{3,2},{4,7},{5,4},{6,5},{7,6},{8,11},{9,8},{10,9... | collective-permute-start | bytes 786440 | tf_op jit(solution)/shard_map/ppermute | solution.py:29
  161.0 4.9 %collective-permute-start.25 = (bf16[256,256]{1,0:T(8,128)(2,1)S(1)}, bf16[256,256]{1,0:T(8,128)(2,1)S(1)}, u32[]{:S(2)}, u32[]{:S(2)}) collective-permute-start(bf16[256,256]{1,0:T(8,128)(2,1)S(1)} %shard_map.64), channel_id=1, source_target_pairs={{0,384},{384,0},{1,385},{385,1},{2,386},{386,2},{3,387},{387,3},{4... | collective-permute-start | bytes 393224 | tf_op jit(solution)/shard_map/ppermute | solution.py:291

commit v10 on v8

--- a/solution.py
+++ b/solution.py
@@ -262,16 +262,16 @@
     )
 
     right_a, left_a, across_a, grads = attend(enc_lengths, dec_lengths, total, own_w, other_w)
-    right_a, left_a, across_a = shift_x(right_a, 1), shift_x(left_a, -1), shift_x(across_a, 2)
+    right_a, left_a, across_a = shift_x(right_a, 1), shift_x(left_a, -1), shift_y(across_a, 2)
     far, right_b, left_b, up_c, down_c, right_c, left_c, here = spread(grads, own_w, other_w)
     far, right_b, left_b = add_rows(
         [far, right_b, left_b, right_a, left_a, across_a], [N, 2 * N + HS, 2 * N + HS],
         [
-            (0, 0, [(0, 0), (3, 0), (4, 0), (5, 0)]), (0, HS, [(0, HS), (3, HS), (4, HS), (5, HS)]),
+            (0, 0, [(0, 0), (3, 0), (4, 0)]), (0, HS, [(0, HS), (3, HS), (4, HS)]),
             (1, 0, [(1, 0), (3, N)]), (1, HS, [(1, HS)]),
-            (1, N, [(1, N), (3, N + HS)]), (1, N + HS, [(1, N + HS)]), (1, 2 * N, [(1, 2 * N)]),
+            (1, N, [(1, N), (3, N + HS)]), (1, N + HS, [(1, N + HS)]), (1, 2 * N, [(1, 2 * N), (5, 0)]),
             (2, 0, [(2, 0)]), (2, HS, [(2, HS), (4, N)]),
-            (2, N, [(2, N)]), (2, N + HS, [(2, N + HS), (4, N + HS)]), (2, 2 * N, [(2, 2 * N)]),
+            (2, N, [(2, N)]), (2, N + HS, [(2, N + HS), (4, N + HS)]), (2, 2 * N, [(2, 2 * N), (5, HS)]),
         ],
     )
     far = shift_y(far, 2)

time: 167 us -> 170 us (1.018)
  waiting for transfers between devices: 56.1 us -> 60.4 us
    ppermute x9 -> x10, waiting for transfers between devices: 27.8 us -> 38 us  [shift_y(): return lax.ppermute(block, 'mp', route)]
    ppermute x14 -> x13, waiting for transfers between devices: 27.4 us -> 21.4 us  [shift_x(): return lax.ppermute(block, 'mp', route)]
    ppermute x14 -> x13, starting transfers between devices: 44.9 us -> 41.4 us  [shift_x(): return lax.ppermute(block, 'mp', route)]
    ppermute x9 -> x10, starting transfers between devices: 30.3 us -> 32.7 us  [shift_y(): return lax.ppermute(block, 'mp', route)]
  transfers between devices with their start and end apart: 26 -> 26, of which waited for: 16 -> 17; matrix products, arithmetic and copies ran while one was open for 0% -> 0% of each run, Pallas kernels for 2% -> 2%
where the time goes in v10:
time: 170 us; the launch traced here: 169 us
  starting transfers between devices  96.9 us (57%)
  waiting for transfers between devices  60.4 us (36%)
  Pallas kernels  8.21 us (5%)
  local copies, waits for them, and re-layouts  2.16 us (1%)
    ppermute x13, starting transfers between devices, shift_x(): return lax.ppermute(block, 'mp', route)  41.4 us
    ppermute x10, waiting for transfers between devices, shift_y(): return lax.ppermute(block, 'mp', route)  38 us
    ppermute x10, starting transfers between devices, shift_y(): return lax.ppermute(block, 'mp', route)  32.7 us
    ppermute x13, waiting for transfers between devices, shift_x(): return lax.ppermute(block, 'mp', route)  21.4 us
    ppermute x1, starting transfers between devices, local(): partner = lax.ppermute(own, 'section', SWAP)  12.4 us
    pallas_call x11, Pallas kernels, call(): pl.pallas_call(body, out_shape=out, in_specs=[SMEM] * scalars + [VMEM] *...  8.21 us
    ppermute x1, starting transfers between devices, local(): swapped = lax.ppermute(sent, 'section', SWAP)  6.72 us
    ppermute x1, starting transfers between devices, local(): other_w = lax.ppermute(own_w, 'section', SWAP)  3.65 us
  transfers between devices with their start and end apart: 26, of which 17 were waited for; matrix products, arithmetic and copies ran while one was open for 0% of the time, Pallas kernels for 2%

profile of v10, /device:TPU:1, one launch (start us, length us, event | category | flops | bytes accessed | tf_op | source)
XLA Modules:
  0.0 168.6 jit_solution(12605655473734942662)
XLA Ops:
  0.0 12.4 %collective-permute-start = (bf16[512,256]{1,0:T(8,128)(2,1)}, bf16[512,256]{1,0:T(8,128)(2,1)S(1)}, u32[]{:S(2)}, u32[]{:S(2)}) collective-permute-start(bf16[512,256]{1,0:T(8,128)(2,1)} %bitcast.9), channel_id=1, source_target_pairs={{0,384},{384,0},{1,385},{385,1},{2,386},{386,2},{3,387},{387,3},{4... | collective-permute-start | bytes 786440 | tf_op jit(solution)/shard_map/ppermute | solution.py:211
  14.4 1.9 %collective-permute-start.1 = (bf16[768,256]{1,0:T(8,128)(2,1)S(1)}, bf16[768,256]{1,0:T(8,128)(2,1)S(1)}, u32[]{:S(2)}, u32[]{:S(2)}) collective-permute-start(bf16[768,256]{1,0:T(8,128)(2,1)S(1)} %shard_map.56.rest_0_), channel_id=1, source_target_pairs={{0,4},{1,5},{2,6},{3,7},{4,8},{5,9},{6,10},{7,11},{8,12},{9,13},{1... | collective-permute-start | bytes 1179656 | tf_op jit(solution)/shard_map/ppermute | solution.py:34
  16.3 5.5 %collective-permute-start.2 = (bf16[768,256]{1,0:T(8,128)(2,1)S(1)}, bf16[768,256]{1,0:T(8,128)(2,1)S(1)}, u32[]{:S(2)}, u32[]{:S(2)}) collective-permute-start(bf16[768,256]{1,0:T(8,128)(2,1)S(1)} %shard_map.56.rest_0_), channel_id=1, source_target_pairs={{0,12},{1,13},{2,14},{3,15},{4,0},{5,1},{6,2},{7,3},{8,4},{9,5},{1... | collective-permute-start | bytes 1179656 | tf_op jit(solution)/shard_map/ppermute | solution.py:34
  21.8 1.9 %collective-permute-start.3 = (bf16[768,256]{1,0:T(8,128)(2,1)S(1)}, bf16[768,256]{1,0:T(8,128)(2,1)S(1)}, u32[]{:S(2)}, u32[]{:S(2)}) collective-permute-start(bf16[768,256]{1,0:T(8,128)(2,1)S(1)} %shard_map.56.rest_0_), channel_id=1, source_target_pairs={{0,1},{1,2},{2,3},{3,0},{4,5},{5,6},{6,7},{7,4},{8,9},{9,10},{10,1... | collective-permute-start | bytes 1179656 | tf_op jit(solution)/shard_map/ppermute | solution.py:29
  23.7 4.6 %collective-permute-start.4 = (bf16[768,256]{1,0:T(8,128)(2,1)S(1)}, bf16[768,256]{1,0:T(8,128)(2,1)S(1)}, u32[]{:S(2)}, u32[]{:S(2)}) collective-permute-start(bf16[768,256]{1,0:T(8,128)(2,1)S(1)} %shard_map.56.rest_0_), channel_id=1, source_target_pairs={{0,3},{1,0},{2,1},{3,2},{4,7},{5,4},{6,5},{7,6},{8,11},{9,8},{10,9... | collective-permute-start | bytes 1179656 | tf_op jit(solution)/shard_map/ppermute | solution.py:29
  28.3 4.3 %collective-permute-done.1.rest_1_ = bf16[768,256]{1,0:T(8,128)(2,1)S(1)} collective-permute-done((bf16[768,256]{1,0:T(8,128)(2,1)S(1)}, bf16[768,256]{1,0:T(8,128)(2,1)S(1)}, u32[]{:S(2)}, u32[]{:S(2)}) %collective-permute-start.1) | collective-permute-done | bytes 393248 | tf_op jit(solution)/shard_map/ppermute | solution.py:34
  35.9 3.7 %collective-permute-start.5 = (bf16[2,4096,256]{2,1,0:T(8,128)(2,1)}, bf16[2,4096,256]{2,1,0:T(8,128)(2,1)S(1)}, u32[]{:S(2)}, u32[]{:S(2)}) collective-permute-start(bf16[2,4096,256]{2,1,0:T(8,128)(2,1)} %bitcast.3), channel_id=1, source_target_pairs={{0,384},{384,0},{1,385},{385,1},{2,386},{386,2},{3,387},{387,3},{4... | collective-permute-start | bytes 12582920 | tf_op jit(solution)/shard_map/ppermute | solution.py:219
  39.7 5.3 %collective-permute-start.7 = (bf16[1728,256]{1,0:T(8,128)(2,1)S(1)}, bf16[1728,256]{1,0:T(8,128)(2,1)S(1)}, u32[]{:S(2)}, u32[]{:S(2)}) collective-permute-start(bf16[1728,256]{1,0:T(8,128)(2,1)S(1)} %pad_maximum_fusion.1), channel_id=1, source_target_pairs={{0,3},{1,0},{2,1},{3,2},{4,7},{5,4},{6,5},{7,6},{8,11},{9,8},{10,9... | collective-permute-start | bytes 2654216 | tf_op jit(solution)/shard_map/ppermute | solution.py:29
  45.1 2.2 %collective-permute-start.6 = (bf16[1728,256]{1,0:T(8,128)(2,1)S(1)}, bf16[1728,256]{1,0:T(8,128)(2,1)S(1)}, u32[]{:S(2)}, u32[]{:S(2)}) collective-permute-start(bf16[1728,256]{1,0:T(8,128)(2,1)S(1)} %pad_maximum_fusion), channel_id=1, source_target_pairs={{0,1},{1,2},{2,3},{3,0},{4,5},{5,6},{6,7},{7,4},{8,9},{9,10},{10,1... | collective-permute-start | bytes 2654216 | tf_op jit(solution)/shard_map/ppermute | solution.py:29
  49.4 5.5 %collective-permute-start.9 = (bf16[576,256]{1,0:T(8,128)(2,1)S(1)}, bf16[576,256]{1,0:T(8,128)(2,1)S(1)}, u32[]{:S(2)}, u32[]{:S(2)}) collective-permute-start(bf16[576,256]{1,0:T(8,128)(2,1)S(1)} %pad_maximum_fusion.6), channel_id=1, source_target_pairs={{0,12},{1,13},{2,14},{3,15},{4,0},{5,1},{6,2},{7,3},{8,4},{9,5},{1... | collective-permute-start | bytes 884744 | tf_op jit(solution)/shard_map/ppermute | solution.py:34
  55.7 4.4 %collective-permute-done.8.rest_2_ = bf16[576,256]{1,0:T(8,128)(2,1)S(1)} collective-permute-done((bf16[576,256]{1,0:T(8,128)(2,1)S(1)}, bf16[576,256]{1,0:T(8,128)(2,1)S(1)}, u32[]{:S(2)}, u32[]{:S(2)}) %collective-permute-start.8) | collective-permute-done | bytes 294944 | tf_op jit(solution)/shard_map/ppermute | solution.py:34
  60.2 4.5 %collective-permute-done.9.rest_3_ = bf16[576,256]{1,0:T(8,128)(2,1)S(1)} collective-permute-done((bf16[576,256]{1,0:T(8,128)(2,1)S(1)}, bf16[576,256]{1,0:T(8,128)(2,1)S(1)}, u32[]{:S(2)}, u32[]{:S(2)}) %collective-permute-start.9) | collective-permute-done | bytes 294944 | tf_op jit(solution)/shard_map/ppermute | solution.py:34
  64.7 4.7 %collective-permute-done.6.rest_0_ = bf16[1728,256]{1,0:T(8,128)(2,1)S(1)} collective-permute-done((bf16[1728,256]{1,0:T(8,128)(2,1)S(1)}, bf16[1728,256]{1,0:T(8,128)(2,1)S(1)}, u32[]{:S(2)}, u32[]{:S(2)}) %collective-permute-start.6) | collective-permute-done | bytes 884768 | tf_op jit(solution)/shard_map/ppermute | solution.py:29
  71.6 3.4 %collective-permute-start.10 = (bf16[1056,256]{1,0:T(8,128)(2,1)S(1)}, bf16[1056,256]{1,0:T(8,128)(2,1)S(1)}, u32[]{:S(2)}, u32[]{:S(2)}) collective-permute-start(bf16[1056,256]{1,0:T(8,128)(2,1)S(1)} %pad_maximum_fusion.2), channel_id=1, source_target_pairs={{0,1},{1,2},{2,3},{3,0},{4,5},{5,6},{6,7},{7,4},{8,9},{9,10},{10,1... | collective-permute-start | bytes 1622024 | tf_op jit(solution)/shard_map/ppermute | solution.py:29
  77.0 2.1 %collective-permute-start.14 = (bf16[480,256]{1,0:T(8,128)(2,1)S(1)}, bf16[480,256]{1,0:T(8,128)(2,1)S(1)}, u32[]{:S(2)}, u32[]{:S(2)}) collective-permute-start(bf16[480,256]{1,0:T(8,128)(2,1)S(1)} %pad_maximum_fusion.8), channel_id=1, source_target_pairs={{0,12},{1,13},{2,14},{3,15},{4,0},{5,1},{6,2},{7,3},{8,4},{9,5},{1... | collective-permute-start | bytes 737288 | tf_op jit(solution)/shard_map/ppermute | solution.py:34
  79.2 4.0 %collective-permute-start.13 = (bf16[480,256]{1,0:T(8,128)(2,1)S(1)}, bf16[480,256]{1,0:T(8,128)(2,1)S(1)}, u32[]{:S(2)}, u32[]{:S(2)}) collective-permute-start(bf16[480,256]{1,0:T(8,128)(2,1)S(1)} %pad_maximum_fusion.7), channel_id=1, source_target_pairs={{0,4},{1,5},{2,6},{3,7},{4,8},{5,9},{6,10},{7,11},{8,12},{9,13},{1... | collective-permute-start | bytes 737288 | tf_op jit(solution)/shard_map/ppermute | solution.py:34
  84.3 5.8 %collective-permute-done.14.rest_4_ = bf16[480,256]{1,0:T(8,128)(2,1)S(1)} collective-permute-done((bf16[480,256]{1,0:T(8,128)(2,1)S(1)}, bf16[480,256]{1,0:T(8,128)(2,1)S(1)}, u32[]{:S(2)}, u32[]{:S(2)}) %collective-permute-start.14) | collective-permute-done | bytes 245792 | tf_op jit(solution)/shard_map/ppermute | solution.py:34
  90.1 4.0 %collective-permute-done.13.rest_3_ = bf16[480,256]{1,0:T(8,128)(2,1)S(1)} collective-permute-done((bf16[480,256]{1,0:T(8,128)(2,1)S(1)}, bf16[480,256]{1,0:T(8,128)(2,1)S(1)}, u32[]{:S(2)}, u32[]{:S(2)}) %collective-permute-start.13) | collective-permute-done | bytes 245792 | tf_op jit(solution)/shard_map/ppermute | solution.py:34
  96.6 2.3 %shard_map.60 = (bf16[1024,256]{1,0:T(8,128)(2,1)S(1)}, bf16[1024,256]{1,0:T(8,128)(2,1)S(1)}, bf16[512,256]{1,0:T(8,128)(2,1)S(1)}, bf16[4,256,256]{2,1,0:T(8,128)(2,1)S(1)}) custom-call(s32[2]{0:T(128)S(1)} %copy-done.3, s32[2]{0:T(128)S(1)} %copy-done.4, f32[4,256,256]{2,1,0:T(8,128)S(1)} %shard_map.59.t_ref, bf16[2,4096,256]{2,1,0:T(8,128)(2,1)S(1)} %bitcast.7, ...), custom_call_target="tpu_custom_call" | custom-call | flops 1006632960 | bytes 9437200 | tf_op jit(solution)/shard_map/pallas_call | solution.py:44
  99.0 2.6 %collective-permute-start.15 = (bf16[1024,256]{1,0:T(8,128)(2,1)S(1)}, bf16[1024,256]{1,0:T(8,128)(2,1)S(1)}, u32[]{:S(2)}, u32[]{:S(2)}) collective-permute-start(bf16[1024,256]{1,0:T(8,128)(2,1)S(1)} %get-tuple-element.63), channel_id=1, source_target_pairs={{0,1},{1,2},{2,3},{3,0},{4,5},{5,6},{6,7},{7,4},{8,9},{9,10},{10,1... | collective-permute-start | bytes 1572872 | tf_op jit(solution)/shard_map/ppermute | solution.py:29
  101.6 3.9 %collective-permute-start.16 = (bf16[1024,256]{1,0:T(8,128)(2,1)S(1)}, bf16[1024,256]{1,0:T(8,128)(2,1)S(1)}, u32[]{:S(2)}, u32[]{:S(2)}) collective-permute-start(bf16[1024,256]{1,0:T(8,128)(2,1)S(1)} %get-tuple-element.64), channel_id=1, source_target_pairs={{0,3},{1,0},{2,1},{3,2},{4,7},{5,4},{6,5},{7,6},{8,11},{9,8},{10,9... | collective-permute-start | bytes 1572872 | tf_op jit(solution)/shard_map/ppermute | solution.py:29
  105.5 2.1 %collective-permute-start.17 = (bf16[512,256]{1,0:T(8,128)(2,1)S(1)}, bf16[512,256]{1,0:T(8,128)(2,1)S(1)}, u32[]{:S(2)}, u32[]{:S(2)}) collective-permute-start(bf16[512,256]{1,0:T(8,128)(2,1)S(1)} %get-tuple-element.65), channel_id=1, source_target_pairs={{0,8},{1,9},{2,10},{3,11},{4,12},{5,13},{6,14},{7,15},{8,0},{9,1},... | collective-permute-start | bytes 786440 | tf_op jit(solution)/shard_map/ppermute | solution.py:34
  109.3 14.1 %collective-permute-done.17.refs_5_ = bf16[512,256]{1,0:T(8,128)(2,1)S(1)} collective-permute-done((bf16[512,256]{1,0:T(8,128)(2,1)S(1)}, bf16[512,256]{1,0:T(8,128)(2,1)S(1)}, u32[]{:S(2)}, u32[]{:S(2)}) %collective-permute-start.17) | collective-permute-done | bytes 262176 | tf_op jit(solution)/shard_map/ppermute | solution.py:34
  123.7 2.0 %collective-permute-start.19 = (bf16[1280,256]{1,0:T(8,128)(2,1)S(1)}, bf16[1280,256]{1,0:T(8,128)(2,1)S(1)}, u32[]{:S(2)}, u32[]{:S(2)}) collective-permute-start(bf16[1280,256]{1,0:T(8,128)(2,1)S(1)} %get-tuple-element.71), channel_id=1, source_target_pairs={{0,1},{1,2},{2,3},{3,0},{4,5},{5,6},{6,7},{7,4},{8,9},{9,10},{10,1... | collective-permute-start | bytes 1966088 | tf_op jit(solution)/shard_map/ppermute | solution.py:29
  125.7 4.5 %collective-permute-start.20 = (bf16[1280,256]{1,0:T(8,128)(2,1)S(1)}, bf16[1280,256]{1,0:T(8,128)(2,1)S(1)}, u32[]{:S(2)}, u32[]{:S(2)}) collective-permute-start(bf16[1280,256]{1,0:T(8,128)(2,1)S(1)} %get-tuple-element.72), channel_id=1, source_target_pairs={{0,3},{1,0},{2,1},{3,2},{4,7},{5,4},{6,5},{7,6},{8,11},{9,8},{10,9... | collective-permute-start | bytes 1966088 | tf_op jit(solution)/shard_map/ppermute | solution.py:29
  130.2 2.2 %collective-permute-start.18 = (bf16[512,256]{1,0:T(8,128)(2,1)S(1)}, bf16[512,256]{1,0:T(8,128)(2,1)S(1)}, u32[]{:S(2)}, u32[]{:S(2)}) collective-permute-start(bf16[512,256]{1,0:T(8,128)(2,1)S(1)} %get-tuple-element.66), channel_id=1, source_target_pairs={{0,8},{1,9},{2,10},{3,11},{4,12},{5,13},{6,14},{7,15},{8,0},{9,1},... | collective-permute-start | bytes 786440 | tf_op jit(solution)/shard_map/ppermute | solution.py:34
  132.4 8.4 %collective-permute-done.19.refs_4_ = bf16[1280,256]{1,0:T(8,128)(2,1)S(1)} collective-permute-done((bf16[1280,256]{1,0:T(8,128)(2,1)S(1)}, bf16[1280,256]{1,0:T(8,128)(2,1)S(1)}, u32[]{:S(2)}, u32[]{:S(2)}) %collective-permute-start.19) | collective-permute-done | bytes 655392 | tf_op jit(solution)/shard_map/ppermute | solution.py:29
  143.9 5.5 %collective-permute-start.22 = (bf16[512,256]{1,0:T(8,128)(2,1)S(1)}, bf16[512,256]{1,0:T(8,128)(2,1)S(1)}, u32[]{:S(2)}, u32[]{:S(2)}) collective-permute-start(bf16[512,256]{1,0:T(8,128)(2,1)S(1)} %get-tuple-element.74), channel_id=1, source_target_pairs={{0,12},{1,13},{2,14},{3,15},{4,0},{5,1},{6,2},{7,3},{8,4},{9,5},{1... | collective-permute-start | bytes 786440 | tf_op jit(solution)/shard_map/ppermute | solution.py:34
  149.4 2.0 %collective-permute-start.23 = (bf16[512,256]{1,0:T(8,128)(2,1)S(1)}, bf16[512,256]{1,0:T(8,128)(2,1)S(1)}, u32[]{:S(2)}, u32[]{:S(2)}) collective-permute-start(bf16[512,256]{1,0:T(8,128)(2,1)S(1)} %get-tuple-element.75), channel_id=1, source_target_pairs={{0,1},{1,2},{2,3},{3,0},{4,5},{5,6},{6,7},{7,4},{8,9},{9,10},{10,1... | collective-permute-start | bytes 786440 | tf_op jit(solution)/shard_map/ppermute | solution.py:29
  151.4 5.3 %collective-permute-start.24 = (bf16[512,256]{1,0:T(8,128)(2,1)S(1)}, bf16[512,256]{1,0:T(8,128)(2,1)S(1)}, u32[]{:S(2)}, u32[]{:S(2)}) collective-permute-start(bf16[512,256]{1,0:T(8,128)(2,1)S(1)} %get-tuple-element.76), channel_id=1, source_target_pairs={{0,3},{1,0},{2,1},{3,2},{4,7},{5,4},{6,5},{7,6},{8,11},{9,8},{10,9... | collective-permute-start | bytes 786440 | tf_op jit(solution)/shard_map/ppermute | solution.py:29
  156.7 2.1 %collective-permute-done.23.refs_4_.rest_3_ = bf16[512,256]{1,0:T(8,128)(2,1)S(1)} collective-permute-done((bf16[512,256]{1,0:T(8,128)(2,1)S(1)}, bf16[512,256]{1,0:T(8,128)(2,1)S(1)}, u32[]{:S(2)}, u32[]{:S(2)}) %collective-permute-start.23) | collective-permute-done | bytes 262176 | tf_op jit(solution)/shard_map/ppermute | solution.py:29
  160.1 6.7 %collective-permute-start.25 = (bf16[256,256]{1,0:T(8,128)(2,1)S(1)}, bf16[256,256]{1,0:T(8,128)(2,1)S(1)}, u32[]{:S(2)}, u32[]{:S(2)}) collective-permute-start(bf16[256,256]{1,0:T(8,128)(2,1)S(1)} %shard_map.64), channel_id=1, source_target_pairs={{0,384},{384,0},{1,385},{385,1},{2,386},{386,2},{3,387},{387,3},{4... | collective-permute-start | bytes 393224 | tf_op jit(solution)/shard_map/ppermute | solution.py:291
  (68 shorter events, 24.0 us)
Async XLA Ops:
  0.0 14.3 %collective-permute-start = (bf16[512,256]{1,0:T(8,128)(2,1)}, bf16[512,256]{1,0:T(8,128)(2,1)S(1)}, u32[]{:S(2)}, u32[]{:S(2)}) collective-permute-start(bf16[512,256]{1,0:T(8,128)(2,1)} %bitcast.9), channel_id=1, source_target_pairs={{0,384},{384,0},{1,385},{385,1},{2,386},{386,2},{3,387},{387,3},{4... | collective-permute-start | bytes 786440 | tf_op jit(solution)/shard_map/ppermute | solution.py:211
  12.4 1.0 copy-start.1
  13.4 0.9 copy-start.2
  14.4 18.3 %collective-permute-start.1 = (bf16[768,256]{1,0:T(8,128)(2,1)S(1)}, bf16[768,256]{1,0:T(8,128)(2,1)S(1)}, u32[]{:S(2)}, u32[]{:S(2)}) collective-permute-start(bf16[768,256]{1,0:T(8,128)(2,1)S(1)} %shard_map.56.rest_0_), channel_id=1, source_target_pairs={{0,4},{1,5},{2,6},{3,7},{4,8},{5,9},{6,10},{7,11},{8,12},{9,13},{1... | collective-permute-start | bytes 1179656 | tf_op jit(solution)/shard_map/ppermute | solution.py:34
  16.3 17.1 %collective-permute-start.2 = (bf16[768,256]{1,0:T(8,128)(2,1)S(1)}, bf16[768,256]{1,0:T(8,128)(2,1)S(1)}, u32[]{:S(2)}, u32[]{:S(2)}) collective-permute-start(bf16[768,256]{1,0:T(8,128)(2,1)S(1)} %shard_map.56.rest_0_), channel_id=1, source_target_pairs={{0,12},{1,13},{2,14},{3,15},{4,0},{5,1},{6,2},{7,3},{8,4},{9,5},{1... | collective-permute-start | bytes 1179656 | tf_op jit(solution)/shard_map/ppermute | solution.py:34
  21.8 13.2 %collective-permute-start.3 = (bf16[768,256]{1,0:T(8,128)(2,1)S(1)}, bf16[768,256]{1,0:T(8,128)(2,1)S(1)}, u32[]{:S(2)}, u32[]{:S(2)}) collective-permute-start(bf16[768,256]{1,0:T(8,128)(2,1)S(1)} %shard_map.56.rest_0_), channel_id=1, source_target_pairs={{0,1},{1,2},{2,3},{3,0},{4,5},{5,6},{6,7},{7,4},{8,9},{9,10},{10,1... | collective-permute-start | bytes 1179656 | tf_op jit(solution)/shard_map/ppermute | solution.py:29
  23.7 12.1 %collective-permute-start.4 = (bf16[768,256]{1,0:T(8,128)(2,1)S(1)}, bf16[768,256]{1,0:T(8,128)(2,1)S(1)}, u32[]{:S(2)}, u32[]{:S(2)}) collective-permute-start(bf16[768,256]{1,0:T(8,128)(2,1)S(1)} %shard_map.56.rest_0_), channel_id=1, source_target_pairs={{0,3},{1,0},{2,1},{3,2},{4,7},{5,4},{6,5},{7,6},{8,11},{9,8},{10,9... | collective-permute-start | bytes 1179656 | tf_op jit(solution)/shard_map/ppermute | solution.py:29
  35.9 19.0 %collective-permute-start.5 = (bf16[2,4096,256]{2,1,0:T(8,128)(2,1)}, bf16[2,4096,256]{2,1,0:T(8,128)(2,1)S(1)}, u32[]{:S(2)}, u32[]{:S(2)}) collective-permute-start(bf16[2,4096,256]{2,1,0:T(8,128)(2,1)} %bitcast.3), channel_id=1, source_target_pairs={{0,384},{384,0},{1,385},{385,1},{2,386},{386,2},{3,387},{387,3},{4... | collective-permute-start | bytes 12582920 | tf_op jit(solution)/shard_map/ppermute | solution.py:219
  39.7 25.1 %collective-permute-start.7 = (bf16[1728,256]{1,0:T(8,128)(2,1)S(1)}, bf16[1728,256]{1,0:T(8,128)(2,1)S(1)}, u32[]{:S(2)}, u32[]{:S(2)}) collective-permute-start(bf16[1728,256]{1,0:T(8,128)(2,1)S(1)} %pad_maximum_fusion.1), channel_id=1, source_target_pairs={{0,3},{1,0},{2,1},{3,2},{4,7},{5,4},{6,5},{7,6},{8,11},{9,8},{10,9... | collective-permute-start | bytes 2654216 | tf_op jit(solution)/shard_map/ppermute | solution.py:29
  45.0 9.9 %copy-start = (bf16[1,2,4096,256]{3,2,1,0:T(8,128)(2,1)S(1)}, bf16[1,2,4096,256]{3,2,1,0:T(8,128)(2,1)}, u32[]{:S(2)}) copy-start(bf16[1,2,4096,256]{3,2,1,0:T(8,128)(2,1)} %param.6) | copy-start | bytes 12582916
  45.1 24.3 %collective-permute-start.6 = (bf16[1728,256]{1,0:T(8,128)(2,1)S(1)}, bf16[1728,256]{1,0:T(8,128)(2,1)S(1)}, u32[]{:S(2)}, u32[]{:S(2)}) collective-permute-start(bf16[1728,256]{1,0:T(8,128)(2,1)S(1)} %pad_maximum_fusion), channel_id=1, source_target_pairs={{0,1},{1,2},{2,3},{3,0},{4,5},{5,6},{6,7},{7,4},{8,9},{9,10},{10,1... | collective-permute-start | bytes 2654216 | tf_op jit(solution)/shard_map/ppermute | solution.py:29
  47.4 12.8 %collective-permute-start.8 = (bf16[576,256]{1,0:T(8,128)(2,1)S(1)}, bf16[576,256]{1,0:T(8,128)(2,1)S(1)}, u32[]{:S(2)}, u32[]{:S(2)}) collective-permute-start(bf16[576,256]{1,0:T(8,128)(2,1)S(1)} %pad_maximum_fusion.5), channel_id=1, source_target_pairs={{0,4},{1,5},{2,6},{3,7},{4,8},{5,9},{6,10},{7,11},{8,12},{9,13},{1... | collective-permute-start | bytes 884744 | tf_op jit(solution)/shard_map/ppermute | solution.py:34
  49.4 15.4 %collective-permute-start.9 = (bf16[576,256]{1,0:T(8,128)(2,1)S(1)}, bf16[576,256]{1,0:T(8,128)(2,1)S(1)}, u32[]{:S(2)}, u32[]{:S(2)}) collective-permute-start(bf16[576,256]{1,0:T(8,128)(2,1)S(1)} %pad_maximum_fusion.6), channel_id=1, source_target_pairs={{0,12},{1,13},{2,14},{3,15},{4,0},{5,1},{6,2},{7,3},{8,4},{9,5},{1... | collective-permute-start | bytes 884744 | tf_op jit(solution)/shard_map/ppermute | solution.py:34
  69.6 24.8 %collective-permute-start.11 = (bf16[1056,256]{1,0:T(8,128)(2,1)S(1)}, bf16[1056,256]{1,0:T(8,128)(2,1)S(1)}, u32[]{:S(2)}, u32[]{:S(2)}) collective-permute-start(bf16[1056,256]{1,0:T(8,128)(2,1)S(1)} %pad_maximum_fusion.3), channel_id=1, source_target_pairs={{0,3},{1,0},{2,1},{3,2},{4,7},{5,4},{6,5},{7,6},{8,11},{9,8},{10,9... | collective-permute-start | bytes 1622024 | tf_op jit(solution)/shard_map/ppermute | solution.py:29
  71.6 24.2 %collective-permute-start.10 = (bf16[1056,256]{1,0:T(8,128)(2,1)S(1)}, bf16[1056,256]{1,0:T(8,128)(2,1)S(1)}, u32[]{:S(2)}, u32[]{:S(2)}) collective-permute-start(bf16[1056,256]{1,0:T(8,128)(2,1)S(1)} %pad_maximum_fusion.2), channel_id=1, source_target_pairs={{0,1},{1,2},{2,3},{3,0},{4,5},{5,6},{6,7},{7,4},{8,9},{9,10},{10,1... | collective-permute-start | bytes 1622024 | tf_op jit(solution)/shard_map/ppermute | solution.py:29
  75.0 19.4 %collective-permute-start.12 = (bf16[768,256]{1,0:T(8,128)(2,1)S(1)}, bf16[768,256]{1,0:T(8,128)(2,1)S(1)}, u32[]{:S(2)}, u32[]{:S(2)}) collective-permute-start(bf16[768,256]{1,0:T(8,128)(2,1)S(1)} %pad_maximum_fusion.4), channel_id=1, source_target_pairs={{0,2},{1,3},{2,0},{3,1},{4,6},{5,7},{6,4},{7,5},{8,10},{9,11},{10,... | collective-permute-start | bytes 1179656 | tf_op jit(solution)/shard_map/ppermute | solution.py:29
  77.0 13.1 %collective-permute-start.14 = (bf16[480,256]{1,0:T(8,128)(2,1)S(1)}, bf16[480,256]{1,0:T(8,128)(2,1)S(1)}, u32[]{:S(2)}, u32[]{:S(2)}) collective-permute-start(bf16[480,256]{1,0:T(8,128)(2,1)S(1)} %pad_maximum_fusion.8), channel_id=1, source_target_pairs={{0,12},{1,13},{2,14},{3,15},{4,0},{5,1},{6,2},{7,3},{8,4},{9,5},{1... | collective-permute-start | bytes 737288 | tf_op jit(solution)/shard_map/ppermute | solution.py:34
  79.2 14.9 %collective-permute-start.13 = (bf16[480,256]{1,0:T(8,128)(2,1)S(1)}, bf16[480,256]{1,0:T(8,128)(2,1)S(1)}, u32[]{:S(2)}, u32[]{:S(2)}) collective-permute-start(bf16[480,256]{1,0:T(8,128)(2,1)S(1)} %pad_maximum_fusion.7), channel_id=1, source_target_pairs={{0,4},{1,5},{2,6},{3,7},{4,8},{5,9},{6,10},{7,11},{8,12},{9,13},{1... | collective-permute-start | bytes 737288 | tf_op jit(solution)/shard_map/ppermute | solution.py:34
  84.2 12.4 %copy-start.3 = (s32[2]{0:T(128)S(1)}, s32[2]{0:T(128)}, u32[]{:S(2)}) copy-start(s32[2]{0:T(128)} %enc_ref.1) | copy-start | bytes 28
  84.3 12.4 %copy-start.4 = (s32[2]{0:T(128)S(1)}, s32[2]{0:T(128)}, u32[]{:S(2)}) copy-start(s32[2]{0:T(128)} %dec_ref.1) | copy-start | bytes 28
  99.0 24.5 %collective-permute-start.15 = (bf16[1024,256]{1,0:T(8,128)(2,1)S(1)}, bf16[1024,256]{1,0:T(8,128)(2,1)S(1)}, u32[]{:S(2)}, u32[]{:S(2)}) collective-permute-start(bf16[1024,256]{1,0:T(8,128)(2,1)S(1)} %get-tuple-element.63), channel_id=1, source_target_pairs={{0,1},{1,2},{2,3},{3,0},{4,5},{5,6},{6,7},{7,4},{8,9},{9,10},{10,1... | collective-permute-start | bytes 1572872 | tf_op jit(solution)/shard_map/ppermute | solution.py:29
  101.6 21.9 %collective-permute-start.16 = (bf16[1024,256]{1,0:T(8,128)(2,1)S(1)}, bf16[1024,256]{1,0:T(8,128)(2,1)S(1)}, u32[]{:S(2)}, u32[]{:S(2)}) collective-permute-start(bf16[1024,256]{1,0:T(8,128)(2,1)S(1)} %get-tuple-element.64), channel_id=1, source_target_pairs={{0,3},{1,0},{2,1},{3,2},{4,7},{5,4},{6,5},{7,6},{8,11},{9,8},{10,9... | collective-permute-start | bytes 1572872 | tf_op jit(solution)/shard_map/ppermute | solution.py:29
  105.5 18.0 %collective-permute-start.17 = (bf16[512,256]{1,0:T(8,128)(2,1)S(1)}, bf16[512,256]{1,0:T(8,128)(2,1)S(1)}, u32[]{:S(2)}, u32[]{:S(2)}) collective-permute-start(bf16[512,256]{1,0:T(8,128)(2,1)S(1)} %get-tuple-element.65), channel_id=1, source_target_pairs={{0,8},{1,9},{2,10},{3,11},{4,12},{5,13},{6,14},{7,15},{8,0},{9,1},... | collective-permute-start | bytes 786440 | tf_op jit(solution)/shard_map/ppermute | solution.py:34
  123.7 17.1 %collective-permute-start.19 = (bf16[1280,256]{1,0:T(8,128)(2,1)S(1)}, bf16[1280,256]{1,0:T(8,128)(2,1)S(1)}, u32[]{:S(2)}, u32[]{:S(2)}) collective-permute-start(bf16[1280,256]{1,0:T(8,128)(2,1)S(1)} %get-tuple-element.71), channel_id=1, source_target_pairs={{0,1},{1,2},{2,3},{3,0},{4,5},{5,6},{6,7},{7,4},{8,9},{9,10},{10,1... | collective-permute-start | bytes 1966088 | tf_op jit(solution)/shard_map/ppermute | solution.py:29
  125.7 16.0 %collective-permute-start.20 = (bf16[1280,256]{1,0:T(8,128)(2,1)S(1)}, bf16[1280,256]{1,0:T(8,128)(2,1)S(1)}, u32[]{:S(2)}, u32[]{:S(2)}) collective-permute-start(bf16[1280,256]{1,0:T(8,128)(2,1)S(1)} %get-tuple-element.72), channel_id=1, source_target_pairs={{0,3},{1,0},{2,1},{3,2},{4,7},{5,4},{6,5},{7,6},{8,11},{9,8},{10,9... | collective-permute-start | bytes 1966088 | tf_op jit(solution)/shard_map/ppermute | solution.py:29
  130.2 26.4 %collective-permute-start.18 = (bf16[512,256]{1,0:T(8,128)(2,1)S(1)}, bf16[512,256]{1,0:T(8,128)(2,1)S(1)}, u32[]{:S(2)}, u32[]{:S(2)}) collective-permute-start(bf16[512,256]{1,0:T(8,128)(2,1)S(1)} %get-tuple-element.66), channel_id=1, source_target_pairs={{0,8},{1,9},{2,10},{3,11},{4,12},{5,13},{6,14},{7,15},{8,0},{9,1},... | collective-permute-start | bytes 786440 | tf_op jit(solution)/shard_map/ppermute | solution.py:34
  142.0 14.7 %collective-permute-start.21 = (bf16[512,256]{1,0:T(8,128)(2,1)S(1)}, bf16[512,256]{1,0:T(8,128)(2,1)S(1)}, u32[]{:S(2)}, u32[]{:S(2)}) collective-permute-start(bf16[512,256]{1,0:T(8,128)(2,1)S(1)} %get-tuple-element.73), channel_id=1, source_target_pairs={{0,4},{1,5},{2,6},{3,7},{4,8},{5,9},{6,10},{7,11},{8,12},{9,13},{1... | collective-permute-start | bytes 786440 | tf_op jit(solution)/shard_map/ppermute | solution.py:34
  143.9 12.8 %collective-permute-start.22 = (bf16[512,256]{1,0:T(8,128)(2,1)S(1)}, bf16[512,256]{1,0:T(8,128)(2,1)S(1)}, u32[]{:S(2)}, u32[]{:S(2)}) collective-permute-start(bf16[512,256]{1,0:T(8,128)(2,1)S(1)} %get-tuple-element.74), channel_id=1, source_target_pairs={{0,12},{1,13},{2,14},{3,15},{4,0},{5,1},{6,2},{7,3},{8,4},{9,5},{1... | collective-permute-start | bytes 786440 | tf_op jit(solution)/shard_map/ppermute | solution.py:34
  149.4 9.4 %collective-permute-start.23 = (bf16[512,256]{1,0:T(8,128)(2,1)S(1)}, bf16[512,256]{1,0:T(8,128)(2,1)S(1)}, u32[]{:S(2)}, u32[]{:S(2)}) collective-permute-start(bf16[512,256]{1,0:T(8,128)(2,1)S(1)} %get-tuple-element.75), channel_id=1, source_target_pairs={{0,1},{1,2},{2,3},{3,0},{4,5},{5,6},{6,7},{7,4},{8,9},{9,10},{10,1... | collective-permute-start | bytes 786440 | tf_op jit(solution)/shard_map/ppermute | solution.py:29
  151.4 8.6 %collective-permute-start.24 = (bf16[512,256]{1,0:T(8,128)(2,1)S(1)}, bf16[512,256]{1,0:T(8,128)(2,1)S(1)}, u32[]{:S(2)}, u32[]{:S(2)}) collective-permute-start(bf16[512,256]{1,0:T(8,128)(2,1)S(1)} %get-tuple-element.76), channel_id=1, source_target_pairs={{0,3},{1,0},{2,1},{3,2},{4,7},{5,4},{6,5},{7,6},{8,11},{9,8},{10,9... | collective-permute-start | bytes 786440 | tf_op jit(solution)/shard_map/ppermute | solution.py:29
  160.1 7.7 %collective-permute-start.25 = (bf16[256,256]{1,0:T(8,128)(2,1)S(1)}, bf16[256,256]{1,0:T(8,128)(2,1)S(1)}, u32[]{:S(2)}, u32[]{:S(2)}) collective-permute-start(bf16[256,256]{1,0:T(8,128)(2,1)S(1)} %shard_map.64), channel_id=1, source_target_pairs={{0,384},{384,0},{1,385},{385,1},{2,386},{386,2},{3,387},{387,3},{4... | collective-permute-start | bytes 393224 | tf_op jit(solution)/shard_map/ppermute | solution.py:291

commit v11 on v8

--- a/solution.py
+++ b/solution.py
@@ -230,7 +230,7 @@
         ],
         own_w, other_w, None,
     )
-    right1, left1, up2, down2, total = lax.optimization_barrier((right1, left1, up2, down2, total))
+    left1, up2, down2, total = lax.optimization_barrier((left1, up2, down2, total))
 
     last = join(up2[:HALF], down2[:HALF])
     tail, lower = HALF + ROWS, HALF + ROWS - D

time: 167 us -> 165 us (0.988)
  waiting for transfers between devices: 56.1 us -> 51.9 us
  starting transfers between devices: 98.5 us -> 101 us
    ppermute x9, waiting for transfers between devices: 27.8 us -> 17.7 us  [shift_y(): return lax.ppermute(block, 'mp', route)]
    ppermute x14, waiting for transfers between devices: 27.4 us -> 33.2 us  [shift_x(): return lax.ppermute(block, 'mp', route)]
    ppermute x9, starting transfers between devices: 30.3 us -> 32 us  [shift_y(): return lax.ppermute(block, 'mp', route)]
  transfers between devices with their start and end apart: 26 -> 26, of which waited for: 16 -> 14; matrix products, arithmetic and copies ran while one was open for 0% -> 0% of each run, Pallas kernels for 2% -> 2%
where the time goes in v11:
time: 165 us; the launch traced here: 164 us
  starting transfers between devices  101 us (61%)
  waiting for transfers between devices  51.9 us (31%)
  Pallas kernels  8.2 us (5%)
  local copies, waits for them, and re-layouts  2.15 us (1%)
    ppermute x14, starting transfers between devices, shift_x(): return lax.ppermute(block, 'mp', route)  44.9 us
    ppermute x14, waiting for transfers between devices, shift_x(): return lax.ppermute(block, 'mp', route)  33.2 us
    ppermute x9, starting transfers between devices, shift_y(): return lax.ppermute(block, 'mp', route)  32 us
    ppermute x9, waiting for transfers between devices, shift_y(): return lax.ppermute(block, 'mp', route)  17.7 us
    ppermute x1, starting transfers between devices, local(): partner = lax.ppermute(own, 'section', SWAP)  12.4 us
    pallas_call x11, Pallas kernels, call(): pl.pallas_call(body, out_shape=out, in_specs=[SMEM] * scalars + [VMEM] *...  8.2 us
    ppermute x1, starting transfers between devices, local(): swapped = lax.ppermute(sent, 'section', SWAP)  7.79 us
    ppermute x1, starting transfers between devices, local(): other_w = lax.ppermute(own_w, 'section', SWAP)  3.65 us
  transfers between devices with their start and end apart: 26, of which 14 were waited for; matrix products, arithmetic and copies ran while one was open for 0% of the time, Pallas kernels for 2%

profile of v11, /device:TPU:1, one launch (start us, length us, event | category | flops | bytes accessed | tf_op | source)
XLA Modules:
  0.0 164.1 jit_solution(13069716767341696980)
XLA Ops:
  0.0 12.4 %collective-permute-start = (bf16[512,256]{1,0:T(8,128)(2,1)}, bf16[512,256]{1,0:T(8,128)(2,1)S(1)}, u32[]{:S(2)}, u32[]{:S(2)}) collective-permute-start(bf16[512,256]{1,0:T(8,128)(2,1)} %bitcast.9), channel_id=1, source_target_pairs={{0,384},{384,0},{1,385},{385,1},{2,386},{386,2},{3,387},{387,3},{4... | collective-permute-start | bytes 786440 | tf_op jit(solution)/shard_map/ppermute | solution.py:211
  14.4 1.9 %collective-permute-start.1 = (bf16[768,256]{1,0:T(8,128)(2,1)S(1)}, bf16[768,256]{1,0:T(8,128)(2,1)S(1)}, u32[]{:S(2)}, u32[]{:S(2)}) collective-permute-start(bf16[768,256]{1,0:T(8,128)(2,1)S(1)} %shard_map.56.rest_0_), channel_id=1, source_target_pairs={{0,4},{1,5},{2,6},{3,7},{4,8},{5,9},{6,10},{7,11},{8,12},{9,13},{1... | collective-permute-start | bytes 1179656 | tf_op jit(solution)/shard_map/ppermute | solution.py:34
  16.3 5.5 %collective-permute-start.2 = (bf16[768,256]{1,0:T(8,128)(2,1)S(1)}, bf16[768,256]{1,0:T(8,128)(2,1)S(1)}, u32[]{:S(2)}, u32[]{:S(2)}) collective-permute-start(bf16[768,256]{1,0:T(8,128)(2,1)S(1)} %shard_map.56.rest_0_), channel_id=1, source_target_pairs={{0,12},{1,13},{2,14},{3,15},{4,0},{5,1},{6,2},{7,3},{8,4},{9,5},{1... | collective-permute-start | bytes 1179656 | tf_op jit(solution)/shard_map/ppermute | solution.py:34
  21.8 1.9 %collective-permute-start.3 = (bf16[768,256]{1,0:T(8,128)(2,1)S(1)}, bf16[768,256]{1,0:T(8,128)(2,1)S(1)}, u32[]{:S(2)}, u32[]{:S(2)}) collective-permute-start(bf16[768,256]{1,0:T(8,128)(2,1)S(1)} %shard_map.56.rest_0_), channel_id=1, source_target_pairs={{0,1},{1,2},{2,3},{3,0},{4,5},{5,6},{6,7},{7,4},{8,9},{9,10},{10,1... | collective-permute-start | bytes 1179656 | tf_op jit(solution)/shard_map/ppermute | solution.py:29
  23.7 4.6 %collective-permute-start.4 = (bf16[768,256]{1,0:T(8,128)(2,1)S(1)}, bf16[768,256]{1,0:T(8,128)(2,1)S(1)}, u32[]{:S(2)}, u32[]{:S(2)}) collective-permute-start(bf16[768,256]{1,0:T(8,128)(2,1)S(1)} %shard_map.56.rest_0_), channel_id=1, source_target_pairs={{0,3},{1,0},{2,1},{3,2},{4,7},{5,4},{6,5},{7,6},{8,11},{9,8},{10,9... | collective-permute-start | bytes 1179656 | tf_op jit(solution)/shard_map/ppermute | solution.py:29
  28.3 4.3 %collective-permute-done.1.rest_1_ = bf16[768,256]{1,0:T(8,128)(2,1)S(1)} collective-permute-done((bf16[768,256]{1,0:T(8,128)(2,1)S(1)}, bf16[768,256]{1,0:T(8,128)(2,1)S(1)}, u32[]{:S(2)}, u32[]{:S(2)}) %collective-permute-start.1) | collective-permute-done | bytes 393248 | tf_op jit(solution)/shard_map/ppermute | solution.py:34
  35.9 3.7 %collective-permute-start.5 = (bf16[2,4096,256]{2,1,0:T(8,128)(2,1)}, bf16[2,4096,256]{2,1,0:T(8,128)(2,1)S(1)}, u32[]{:S(2)}, u32[]{:S(2)}) collective-permute-start(bf16[2,4096,256]{2,1,0:T(8,128)(2,1)} %bitcast.3), channel_id=1, source_target_pairs={{0,384},{384,0},{1,385},{385,1},{2,386},{386,2},{3,387},{387,3},{4... | collective-permute-start | bytes 12582920 | tf_op jit(solution)/shard_map/ppermute | solution.py:219
  39.6 1.9 %collective-permute-start.6 = (bf16[1728,256]{1,0:T(8,128)(2,1)S(1)}, bf16[1728,256]{1,0:T(8,128)(2,1)S(1)}, u32[]{:S(2)}, u32[]{:S(2)}) collective-permute-start(bf16[1728,256]{1,0:T(8,128)(2,1)S(1)} %pad_maximum_fusion), channel_id=1, source_target_pairs={{0,1},{1,2},{2,3},{3,0},{4,5},{5,6},{6,7},{7,4},{8,9},{9,10},{10,1... | collective-permute-start | bytes 2654216 | tf_op jit(solution)/shard_map/ppermute | solution.py:29
  41.7 5.3 %collective-permute-start.8 = (bf16[1728,256]{1,0:T(8,128)(2,1)S(1)}, bf16[1728,256]{1,0:T(8,128)(2,1)S(1)}, u32[]{:S(2)}, u32[]{:S(2)}) collective-permute-start(bf16[1728,256]{1,0:T(8,128)(2,1)S(1)} %pad_maximum_fusion.1), channel_id=1, source_target_pairs={{0,3},{1,0},{2,1},{3,2},{4,7},{5,4},{6,5},{7,6},{8,11},{9,8},{10,9... | collective-permute-start | bytes 2654216 | tf_op jit(solution)/shard_map/ppermute | solution.py:29
  47.1 2.2 %collective-permute-start.10 = (bf16[576,256]{1,0:T(8,128)(2,1)S(1)}, bf16[576,256]{1,0:T(8,128)(2,1)S(1)}, u32[]{:S(2)}, u32[]{:S(2)}) collective-permute-start(bf16[576,256]{1,0:T(8,128)(2,1)S(1)} %pad_maximum_fusion.6), channel_id=1, source_target_pairs={{0,12},{1,13},{2,14},{3,15},{4,0},{5,1},{6,2},{7,3},{8,4},{9,5},{1... | collective-permute-start | bytes 884744 | tf_op jit(solution)/shard_map/ppermute | solution.py:34
  49.4 4.3 %collective-permute-start.9 = (bf16[576,256]{1,0:T(8,128)(2,1)S(1)}, bf16[576,256]{1,0:T(8,128)(2,1)S(1)}, u32[]{:S(2)}, u32[]{:S(2)}) collective-permute-start(bf16[576,256]{1,0:T(8,128)(2,1)S(1)} %pad_maximum_fusion.5), channel_id=1, source_target_pairs={{0,4},{1,5},{2,6},{3,7},{4,8},{5,9},{6,10},{7,11},{8,12},{9,13},{1... | collective-permute-start | bytes 884744 | tf_op jit(solution)/shard_map/ppermute | solution.py:34
  53.6 11.3 %collective-permute-done.6.rest_0_ = bf16[1728,256]{1,0:T(8,128)(2,1)S(1)} collective-permute-done((bf16[1728,256]{1,0:T(8,128)(2,1)S(1)}, bf16[1728,256]{1,0:T(8,128)(2,1)S(1)}, u32[]{:S(2)}, u32[]{:S(2)}) %collective-permute-start.6) | collective-permute-done | bytes 884768 | tf_op jit(solution)/shard_map/ppermute | solution.py:29
  65.1 1.9 %collective-permute-start.7 = (bf16[1056,256]{1,0:T(8,128)(2,1)S(1)}, bf16[1056,256]{1,0:T(8,128)(2,1)S(1)}, u32[]{:S(2)}, u32[]{:S(2)}) collective-permute-start(bf16[1056,256]{1,0:T(8,128)(2,1)S(1)} %pad_maximum_fusion.2), channel_id=1, source_target_pairs={{0,1},{1,2},{2,3},{3,0},{4,5},{5,6},{6,7},{7,4},{8,9},{9,10},{10,1... | collective-permute-start | bytes 1622024 | tf_op jit(solution)/shard_map/ppermute | solution.py:29
  68.1 4.7 %collective-permute-start.11 = (bf16[1056,256]{1,0:T(8,128)(2,1)S(1)}, bf16[1056,256]{1,0:T(8,128)(2,1)S(1)}, u32[]{:S(2)}, u32[]{:S(2)}) collective-permute-start(bf16[1056,256]{1,0:T(8,128)(2,1)S(1)} %pad_maximum_fusion.3), channel_id=1, source_target_pairs={{0,3},{1,0},{2,1},{3,2},{4,7},{5,4},{6,5},{7,6},{8,11},{9,8},{10,9... | collective-permute-start | bytes 1622024 | tf_op jit(solution)/shard_map/ppermute | solution.py:29
  76.8 4.3 %collective-permute-start.13 = (bf16[480,256]{1,0:T(8,128)(2,1)S(1)}, bf16[480,256]{1,0:T(8,128)(2,1)S(1)}, u32[]{:S(2)}, u32[]{:S(2)}) collective-permute-start(bf16[480,256]{1,0:T(8,128)(2,1)S(1)} %pad_maximum_fusion.7), channel_id=1, source_target_pairs={{0,4},{1,5},{2,6},{3,7},{4,8},{5,9},{6,10},{7,11},{8,12},{9,13},{1... | collective-permute-start | bytes 737288 | tf_op jit(solution)/shard_map/ppermute | solution.py:34
  82.1 4.6 %collective-permute-done.14.rest_4_ = bf16[480,256]{1,0:T(8,128)(2,1)S(1)} collective-permute-done((bf16[480,256]{1,0:T(8,128)(2,1)S(1)}, bf16[480,256]{1,0:T(8,128)(2,1)S(1)}, u32[]{:S(2)}, u32[]{:S(2)}) %collective-permute-start.14) | collective-permute-done | bytes 245792 | tf_op jit(solution)/shard_map/ppermute | solution.py:34
  86.7 6.1 %collective-permute-done.13.rest_3_ = bf16[480,256]{1,0:T(8,128)(2,1)S(1)} collective-permute-done((bf16[480,256]{1,0:T(8,128)(2,1)S(1)}, bf16[480,256]{1,0:T(8,128)(2,1)S(1)}, u32[]{:S(2)}, u32[]{:S(2)}) %collective-permute-start.13) | collective-permute-done | bytes 245792 | tf_op jit(solution)/shard_map/ppermute | solution.py:34
  93.7 2.3 %shard_map.60 = (bf16[1024,256]{1,0:T(8,128)(2,1)S(1)}, bf16[1024,256]{1,0:T(8,128)(2,1)S(1)}, bf16[512,256]{1,0:T(8,128)(2,1)S(1)}, bf16[4,256,256]{2,1,0:T(8,128)(2,1)S(1)}) custom-call(s32[2]{0:T(128)S(1)} %copy-done.5, s32[2]{0:T(128)S(1)} %copy-done.6, f32[4,256,256]{2,1,0:T(8,128)S(1)} %shard_map.59.t_ref, bf16[2,4096,256]{2,1,0:T(8,128)(2,1)S(1)} %bitcast.7, ...), custom_call_target="tpu_custom_call" | custom-call | flops 1006632960 | bytes 9437200 | tf_op jit(solution)/shard_map/pallas_call | solution.py:44
  96.0 2.6 %collective-permute-start.15 = (bf16[1024,256]{1,0:T(8,128)(2,1)S(1)}, bf16[1024,256]{1,0:T(8,128)(2,1)S(1)}, u32[]{:S(2)}, u32[]{:S(2)}) collective-permute-start(bf16[1024,256]{1,0:T(8,128)(2,1)S(1)} %get-tuple-element.61), channel_id=1, source_target_pairs={{0,1},{1,2},{2,3},{3,0},{4,5},{5,6},{6,7},{7,4},{8,9},{9,10},{10,1... | collective-permute-start | bytes 1572872 | tf_op jit(solution)/shard_map/ppermute | solution.py:29
  98.6 3.9 %collective-permute-start.16 = (bf16[1024,256]{1,0:T(8,128)(2,1)S(1)}, bf16[1024,256]{1,0:T(8,128)(2,1)S(1)}, u32[]{:S(2)}, u32[]{:S(2)}) collective-permute-start(bf16[1024,256]{1,0:T(8,128)(2,1)S(1)} %get-tuple-element.62), channel_id=1, source_target_pairs={{0,3},{1,0},{2,1},{3,2},{4,7},{5,4},{6,5},{7,6},{8,11},{9,8},{10,9... | collective-permute-start | bytes 1572872 | tf_op jit(solution)/shard_map/ppermute | solution.py:29
  102.5 3.1 %collective-permute-start.17 = (bf16[512,256]{1,0:T(8,128)(2,1)S(1)}, bf16[512,256]{1,0:T(8,128)(2,1)S(1)}, u32[]{:S(2)}, u32[]{:S(2)}) collective-permute-start(bf16[512,256]{1,0:T(8,128)(2,1)S(1)} %get-tuple-element.63), channel_id=1, source_target_pairs={{0,2},{1,3},{2,0},{3,1},{4,6},{5,7},{6,4},{7,5},{8,10},{9,11},{10,... | collective-permute-start | bytes 786440 | tf_op jit(solution)/shard_map/ppermute | solution.py:29
  107.4 10.0 %collective-permute-done.17.refs_5_ = bf16[512,256]{1,0:T(8,128)(2,1)S(1)} collective-permute-done((bf16[512,256]{1,0:T(8,128)(2,1)S(1)}, bf16[512,256]{1,0:T(8,128)(2,1)S(1)}, u32[]{:S(2)}, u32[]{:S(2)}) %collective-permute-start.17) | collective-permute-done | bytes 262176 | tf_op jit(solution)/shard_map/ppermute | solution.py:29
  117.6 4.4 %collective-permute-start.19 = (bf16[1280,256]{1,0:T(8,128)(2,1)S(1)}, bf16[1280,256]{1,0:T(8,128)(2,1)S(1)}, u32[]{:S(2)}, u32[]{:S(2)}) collective-permute-start(bf16[1280,256]{1,0:T(8,128)(2,1)S(1)} %get-tuple-element.69), channel_id=1, source_target_pairs={{0,1},{1,2},{2,3},{3,0},{4,5},{5,6},{6,7},{7,4},{8,9},{9,10},{10,1... | collective-permute-start | bytes 1966088 | tf_op jit(solution)/shard_map/ppermute | solution.py:29
  122.1 2.1 %collective-permute-start.20 = (bf16[1280,256]{1,0:T(8,128)(2,1)S(1)}, bf16[1280,256]{1,0:T(8,128)(2,1)S(1)}, u32[]{:S(2)}, u32[]{:S(2)}) collective-permute-start(bf16[1280,256]{1,0:T(8,128)(2,1)S(1)} %get-tuple-element.70), channel_id=1, source_target_pairs={{0,3},{1,0},{2,1},{3,2},{4,7},{5,4},{6,5},{7,6},{8,11},{9,8},{10,9... | collective-permute-start | bytes 1966088 | tf_op jit(solution)/shard_map/ppermute | solution.py:29
  124.2 4.6 %collective-permute-start.18 = (bf16[512,256]{1,0:T(8,128)(2,1)S(1)}, bf16[512,256]{1,0:T(8,128)(2,1)S(1)}, u32[]{:S(2)}, u32[]{:S(2)}) collective-permute-start(bf16[512,256]{1,0:T(8,128)(2,1)S(1)} %get-tuple-element.64), channel_id=1, source_target_pairs={{0,8},{1,9},{2,10},{3,11},{4,12},{5,13},{6,14},{7,15},{8,0},{9,1},... | collective-permute-start | bytes 786440 | tf_op jit(solution)/shard_map/ppermute | solution.py:34
  128.8 4.9 %collective-permute-done.19.refs_4_ = bf16[1280,256]{1,0:T(8,128)(2,1)S(1)} collective-permute-done((bf16[1280,256]{1,0:T(8,128)(2,1)S(1)}, bf16[1280,256]{1,0:T(8,128)(2,1)S(1)}, u32[]{:S(2)}, u32[]{:S(2)}) %collective-permute-start.19) | collective-permute-done | bytes 655392 | tf_op jit(solution)/shard_map/ppermute | solution.py:29
  133.7 3.2 %collective-permute-done.20.refs_5_ = bf16[1280,256]{1,0:T(8,128)(2,1)S(1)} collective-permute-done((bf16[1280,256]{1,0:T(8,128)(2,1)S(1)}, bf16[1280,256]{1,0:T(8,128)(2,1)S(1)}, u32[]{:S(2)}, u32[]{:S(2)}) %collective-permute-start.20) | collective-permute-done | bytes 655392 | tf_op jit(solution)/shard_map/ppermute | solution.py:29
  139.1 5.5 %collective-permute-start.22 = (bf16[512,256]{1,0:T(8,128)(2,1)S(1)}, bf16[512,256]{1,0:T(8,128)(2,1)S(1)}, u32[]{:S(2)}, u32[]{:S(2)}) collective-permute-start(bf16[512,256]{1,0:T(8,128)(2,1)S(1)} %get-tuple-element.72), channel_id=1, source_target_pairs={{0,12},{1,13},{2,14},{3,15},{4,0},{5,1},{6,2},{7,3},{8,4},{9,5},{1... | collective-permute-start | bytes 786440 | tf_op jit(solution)/shard_map/ppermute | solution.py:34
  144.6 2.0 %collective-permute-start.23 = (bf16[512,256]{1,0:T(8,128)(2,1)S(1)}, bf16[512,256]{1,0:T(8,128)(2,1)S(1)}, u32[]{:S(2)}, u32[]{:S(2)}) collective-permute-start(bf16[512,256]{1,0:T(8,128)(2,1)S(1)} %get-tuple-element.73), channel_id=1, source_target_pairs={{0,1},{1,2},{2,3},{3,0},{4,5},{5,6},{6,7},{7,4},{8,9},{9,10},{10,1... | collective-permute-start | bytes 786440 | tf_op jit(solution)/shard_map/ppermute | solution.py:29
  146.6 4.5 %collective-permute-start.24 = (bf16[512,256]{1,0:T(8,128)(2,1)S(1)}, bf16[512,256]{1,0:T(8,128)(2,1)S(1)}, u32[]{:S(2)}, u32[]{:S(2)}) collective-permute-start(bf16[512,256]{1,0:T(8,128)(2,1)S(1)} %get-tuple-element.74), channel_id=1, source_target_pairs={{0,3},{1,0},{2,1},{3,2},{4,7},{5,4},{6,5},{7,6},{8,11},{9,8},{10,9... | collective-permute-start | bytes 786440 | tf_op jit(solution)/shard_map/ppermute | solution.py:29
  151.1 2.0 %collective-permute-done.22.refs_3_.rest_2_ = bf16[512,256]{1,0:T(8,128)(2,1)S(1)} collective-permute-done((bf16[512,256]{1,0:T(8,128)(2,1)S(1)}, bf16[512,256]{1,0:T(8,128)(2,1)S(1)}, u32[]{:S(2)}, u32[]{:S(2)}) %collective-permute-start.22) | collective-permute-done | bytes 262176 | tf_op jit(solution)/shard_map/ppermute | solution.py:34
  154.5 7.8 %collective-permute-start.25 = (bf16[256,256]{1,0:T(8,128)(2,1)S(1)}, bf16[256,256]{1,0:T(8,128)(2,1)S(1)}, u32[]{:S(2)}, u32[]{:S(2)}) collective-permute-start(bf16[256,256]{1,0:T(8,128)(2,1)S(1)} %shard_map.64), channel_id=1, source_target_pairs={{0,384},{384,0},{1,385},{385,1},{2,386},{386,2},{3,387},{387,3},{4... | collective-permute-start | bytes 393224 | tf_op jit(solution)/shard_map/ppermute | solution.py:291
  (74 shorter events, 19.6 us)
Async XLA Ops:
  0.0 14.3 %collective-permute-start = (bf16[512,256]{1,0:T(8,128)(2,1)}, bf16[512,256]{1,0:T(8,128)(2,1)S(1)}, u32[]{:S(2)}, u32[]{:S(2)}) collective-permute-start(bf16[512,256]{1,0:T(8,128)(2,1)} %bitcast.9), channel_id=1, source_target_pairs={{0,384},{384,0},{1,385},{385,1},{2,386},{386,2},{3,387},{387,3},{4... | collective-permute-start | bytes 786440 | tf_op jit(solution)/shard_map/ppermute | solution.py:211
  14.4 18.3 %collective-permute-start.1 = (bf16[768,256]{1,0:T(8,128)(2,1)S(1)}, bf16[768,256]{1,0:T(8,128)(2,1)S(1)}, u32[]{:S(2)}, u32[]{:S(2)}) collective-permute-start(bf16[768,256]{1,0:T(8,128)(2,1)S(1)} %shard_map.56.rest_0_), channel_id=1, source_target_pairs={{0,4},{1,5},{2,6},{3,7},{4,8},{5,9},{6,10},{7,11},{8,12},{9,13},{1... | collective-permute-start | bytes 1179656 | tf_op jit(solution)/shard_map/ppermute | solution.py:34
  16.3 17.1 %collective-permute-start.2 = (bf16[768,256]{1,0:T(8,128)(2,1)S(1)}, bf16[768,256]{1,0:T(8,128)(2,1)S(1)}, u32[]{:S(2)}, u32[]{:S(2)}) collective-permute-start(bf16[768,256]{1,0:T(8,128)(2,1)S(1)} %shard_map.56.rest_0_), channel_id=1, source_target_pairs={{0,12},{1,13},{2,14},{3,15},{4,0},{5,1},{6,2},{7,3},{8,4},{9,5},{1... | collective-permute-start | bytes 1179656 | tf_op jit(solution)/shard_map/ppermute | solution.py:34
  21.8 13.2 %collective-permute-start.3 = (bf16[768,256]{1,0:T(8,128)(2,1)S(1)}, bf16[768,256]{1,0:T(8,128)(2,1)S(1)}, u32[]{:S(2)}, u32[]{:S(2)}) collective-permute-start(bf16[768,256]{1,0:T(8,128)(2,1)S(1)} %shard_map.56.rest_0_), channel_id=1, source_target_pairs={{0,1},{1,2},{2,3},{3,0},{4,5},{5,6},{6,7},{7,4},{8,9},{9,10},{10,1... | collective-permute-start | bytes 1179656 | tf_op jit(solution)/shard_map/ppermute | solution.py:29
  23.7 12.1 %collective-permute-start.4 = (bf16[768,256]{1,0:T(8,128)(2,1)S(1)}, bf16[768,256]{1,0:T(8,128)(2,1)S(1)}, u32[]{:S(2)}, u32[]{:S(2)}) collective-permute-start(bf16[768,256]{1,0:T(8,128)(2,1)S(1)} %shard_map.56.rest_0_), channel_id=1, source_target_pairs={{0,3},{1,0},{2,1},{3,2},{4,7},{5,4},{6,5},{7,6},{8,11},{9,8},{10,9... | collective-permute-start | bytes 1179656 | tf_op jit(solution)/shard_map/ppermute | solution.py:29
  35.9 31.1 %collective-permute-start.5 = (bf16[2,4096,256]{2,1,0:T(8,128)(2,1)}, bf16[2,4096,256]{2,1,0:T(8,128)(2,1)S(1)}, u32[]{:S(2)}, u32[]{:S(2)}) collective-permute-start(bf16[2,4096,256]{2,1,0:T(8,128)(2,1)} %bitcast.3), channel_id=1, source_target_pairs={{0,384},{384,0},{1,385},{385,1},{2,386},{386,2},{3,387},{387,3},{4... | collective-permute-start | bytes 12582920 | tf_op jit(solution)/shard_map/ppermute | solution.py:219
  39.6 25.3 %collective-permute-start.6 = (bf16[1728,256]{1,0:T(8,128)(2,1)S(1)}, bf16[1728,256]{1,0:T(8,128)(2,1)S(1)}, u32[]{:S(2)}, u32[]{:S(2)}) collective-permute-start(bf16[1728,256]{1,0:T(8,128)(2,1)S(1)} %pad_maximum_fusion), channel_id=1, source_target_pairs={{0,1},{1,2},{2,3},{3,0},{4,5},{5,6},{6,7},{7,4},{8,9},{9,10},{10,1... | collective-permute-start | bytes 2654216 | tf_op jit(solution)/shard_map/ppermute | solution.py:29
  41.7 26.2 %collective-permute-start.8 = (bf16[1728,256]{1,0:T(8,128)(2,1)S(1)}, bf16[1728,256]{1,0:T(8,128)(2,1)S(1)}, u32[]{:S(2)}, u32[]{:S(2)}) collective-permute-start(bf16[1728,256]{1,0:T(8,128)(2,1)S(1)} %pad_maximum_fusion.1), channel_id=1, source_target_pairs={{0,3},{1,0},{2,1},{3,2},{4,7},{5,4},{6,5},{7,6},{8,11},{9,8},{10,9... | collective-permute-start | bytes 2654216 | tf_op jit(solution)/shard_map/ppermute | solution.py:29
  47.1 19.9 %copy-start = (bf16[1,2,4096,256]{3,2,1,0:T(8,128)(2,1)S(1)}, bf16[1,2,4096,256]{3,2,1,0:T(8,128)(2,1)}, u32[]{:S(2)}) copy-start(bf16[1,2,4096,256]{3,2,1,0:T(8,128)(2,1)} %param.6) | copy-start | bytes 12582916
  47.1 20.7 %collective-permute-start.10 = (bf16[576,256]{1,0:T(8,128)(2,1)S(1)}, bf16[576,256]{1,0:T(8,128)(2,1)S(1)}, u32[]{:S(2)}, u32[]{:S(2)}) collective-permute-start(bf16[576,256]{1,0:T(8,128)(2,1)S(1)} %pad_maximum_fusion.6), channel_id=1, source_target_pairs={{0,12},{1,13},{2,14},{3,15},{4,0},{5,1},{6,2},{7,3},{8,4},{9,5},{1... | collective-permute-start | bytes 884744 | tf_op jit(solution)/shard_map/ppermute | solution.py:34
  49.4 18.5 %collective-permute-start.9 = (bf16[576,256]{1,0:T(8,128)(2,1)S(1)}, bf16[576,256]{1,0:T(8,128)(2,1)S(1)}, u32[]{:S(2)}, u32[]{:S(2)}) collective-permute-start(bf16[576,256]{1,0:T(8,128)(2,1)S(1)} %pad_maximum_fusion.5), channel_id=1, source_target_pairs={{0,4},{1,5},{2,6},{3,7},{4,8},{5,9},{6,10},{7,11},{8,12},{9,13},{1... | collective-permute-start | bytes 884744 | tf_op jit(solution)/shard_map/ppermute | solution.py:34
  65.1 17.1 %collective-permute-start.7 = (bf16[1056,256]{1,0:T(8,128)(2,1)S(1)}, bf16[1056,256]{1,0:T(8,128)(2,1)S(1)}, u32[]{:S(2)}, u32[]{:S(2)}) collective-permute-start(bf16[1056,256]{1,0:T(8,128)(2,1)S(1)} %pad_maximum_fusion.2), channel_id=1, source_target_pairs={{0,1},{1,2},{2,3},{3,0},{4,5},{5,6},{6,7},{7,4},{8,9},{9,10},{10,1... | collective-permute-start | bytes 1622024 | tf_op jit(solution)/shard_map/ppermute | solution.py:29
  68.0 6.8 %slice-start = ((bf16[1728,256]{1,0:T(8,128)(2,1)}), bf16[192,256]{1,0:T(8,128)(2,1)S(1)}, s32[]{:S(2)}) async-start(bf16[1728,256]{1,0:T(8,128)(2,1)} %copy-done.1), calls=%async_computation | async-start | bytes 196608 | tf_op jit(solution)/shard_map/slice | solution.py:240
  68.0 8.8 %slice-start.1 = ((bf16[1728,256]{1,0:T(8,128)(2,1)}), bf16[384,256]{1,0:T(8,128)(2,1)S(1)}, s32[]{:S(2)}) async-start(bf16[1728,256]{1,0:T(8,128)(2,1)} %copy-done.1), calls=%async_computation.1 | async-start | bytes 393216 | tf_op jit(solution)/shard_map/slice | solution.py:239
  68.0 13.0 %copy-start.2 = (bf16[1728,256]{1,0:T(8,128)(2,1)S(1)}, bf16[1728,256]{1,0:T(8,128)(2,1)}, u32[]{:S(2)}) copy-start(bf16[1728,256]{1,0:T(8,128)(2,1)} %copy-done.1) | copy-start | bytes 2654212
  68.1 24.7 %collective-permute-start.11 = (bf16[1056,256]{1,0:T(8,128)(2,1)S(1)}, bf16[1056,256]{1,0:T(8,128)(2,1)S(1)}, u32[]{:S(2)}, u32[]{:S(2)}) collective-permute-start(bf16[1056,256]{1,0:T(8,128)(2,1)S(1)} %pad_maximum_fusion.3), channel_id=1, source_target_pairs={{0,3},{1,0},{2,1},{3,2},{4,7},{5,4},{6,5},{7,6},{8,11},{9,8},{10,9... | collective-permute-start | bytes 1622024 | tf_op jit(solution)/shard_map/ppermute | solution.py:29
  72.9 19.9 %collective-permute-start.12 = (bf16[768,256]{1,0:T(8,128)(2,1)S(1)}, bf16[768,256]{1,0:T(8,128)(2,1)S(1)}, u32[]{:S(2)}, u32[]{:S(2)}) collective-permute-start(bf16[768,256]{1,0:T(8,128)(2,1)S(1)} %pad_maximum_fusion.4), channel_id=1, source_target_pairs={{0,2},{1,3},{2,0},{3,1},{4,6},{5,7},{6,4},{7,5},{8,10},{9,11},{10,... | collective-permute-start | bytes 1179656 | tf_op jit(solution)/shard_map/ppermute | solution.py:29
  74.8 11.8 %collective-permute-start.14 = (bf16[480,256]{1,0:T(8,128)(2,1)S(1)}, bf16[480,256]{1,0:T(8,128)(2,1)S(1)}, u32[]{:S(2)}, u32[]{:S(2)}) collective-permute-start(bf16[480,256]{1,0:T(8,128)(2,1)S(1)} %pad_maximum_fusion.8), channel_id=1, source_target_pairs={{0,12},{1,13},{2,14},{3,15},{4,0},{5,1},{6,2},{7,3},{8,4},{9,5},{1... | collective-permute-start | bytes 737288 | tf_op jit(solution)/shard_map/ppermute | solution.py:34
  76.8 16.0 %collective-permute-start.13 = (bf16[480,256]{1,0:T(8,128)(2,1)S(1)}, bf16[480,256]{1,0:T(8,128)(2,1)S(1)}, u32[]{:S(2)}, u32[]{:S(2)}) collective-permute-start(bf16[480,256]{1,0:T(8,128)(2,1)S(1)} %pad_maximum_fusion.7), channel_id=1, source_target_pairs={{0,4},{1,5},{2,6},{3,7},{4,8},{5,9},{6,10},{7,11},{8,12},{9,13},{1... | collective-permute-start | bytes 737288 | tf_op jit(solution)/shard_map/ppermute | solution.py:34
  82.1 11.6 %copy-start.5 = (s32[2]{0:T(128)S(1)}, s32[2]{0:T(128)}, u32[]{:S(2)}) copy-start(s32[2]{0:T(128)} %enc_ref.1) | copy-start | bytes 28
  82.1 11.6 %copy-start.6 = (s32[2]{0:T(128)S(1)}, s32[2]{0:T(128)}, u32[]{:S(2)}) copy-start(s32[2]{0:T(128)} %dec_ref.1) | copy-start | bytes 28
  96.0 21.4 %collective-permute-start.15 = (bf16[1024,256]{1,0:T(8,128)(2,1)S(1)}, bf16[1024,256]{1,0:T(8,128)(2,1)S(1)}, u32[]{:S(2)}, u32[]{:S(2)}) collective-permute-start(bf16[1024,256]{1,0:T(8,128)(2,1)S(1)} %get-tuple-element.61), channel_id=1, source_target_pairs={{0,1},{1,2},{2,3},{3,0},{4,5},{5,6},{6,7},{7,4},{8,9},{9,10},{10,1... | collective-permute-start | bytes 1572872 | tf_op jit(solution)/shard_map/ppermute | solution.py:29
  98.6 18.8 %collective-permute-start.16 = (bf16[1024,256]{1,0:T(8,128)(2,1)S(1)}, bf16[1024,256]{1,0:T(8,128)(2,1)S(1)}, u32[]{:S(2)}, u32[]{:S(2)}) collective-permute-start(bf16[1024,256]{1,0:T(8,128)(2,1)S(1)} %get-tuple-element.62), channel_id=1, source_target_pairs={{0,3},{1,0},{2,1},{3,2},{4,7},{5,4},{6,5},{7,6},{8,11},{9,8},{10,9... | collective-permute-start | bytes 1572872 | tf_op jit(solution)/shard_map/ppermute | solution.py:29
  102.5 14.9 %collective-permute-start.17 = (bf16[512,256]{1,0:T(8,128)(2,1)S(1)}, bf16[512,256]{1,0:T(8,128)(2,1)S(1)}, u32[]{:S(2)}, u32[]{:S(2)}) collective-permute-start(bf16[512,256]{1,0:T(8,128)(2,1)S(1)} %get-tuple-element.63), channel_id=1, source_target_pairs={{0,2},{1,3},{2,0},{3,1},{4,6},{5,7},{6,4},{7,5},{8,10},{9,11},{10,... | collective-permute-start | bytes 786440 | tf_op jit(solution)/shard_map/ppermute | solution.py:29
  117.6 16.1 %collective-permute-start.19 = (bf16[1280,256]{1,0:T(8,128)(2,1)S(1)}, bf16[1280,256]{1,0:T(8,128)(2,1)S(1)}, u32[]{:S(2)}, u32[]{:S(2)}) collective-permute-start(bf16[1280,256]{1,0:T(8,128)(2,1)S(1)} %get-tuple-element.69), channel_id=1, source_target_pairs={{0,1},{1,2},{2,3},{3,0},{4,5},{5,6},{6,7},{7,4},{8,9},{9,10},{10,1... | collective-permute-start | bytes 1966088 | tf_op jit(solution)/shard_map/ppermute | solution.py:29
  122.1 14.9 %collective-permute-start.20 = (bf16[1280,256]{1,0:T(8,128)(2,1)S(1)}, bf16[1280,256]{1,0:T(8,128)(2,1)S(1)}, u32[]{:S(2)}, u32[]{:S(2)}) collective-permute-start(bf16[1280,256]{1,0:T(8,128)(2,1)S(1)} %get-tuple-element.70), channel_id=1, source_target_pairs={{0,3},{1,0},{2,1},{3,2},{4,7},{5,4},{6,5},{7,6},{8,11},{9,8},{10,9... | collective-permute-start | bytes 1966088 | tf_op jit(solution)/shard_map/ppermute | solution.py:29
  124.2 26.9 %collective-permute-start.18 = (bf16[512,256]{1,0:T(8,128)(2,1)S(1)}, bf16[512,256]{1,0:T(8,128)(2,1)S(1)}, u32[]{:S(2)}, u32[]{:S(2)}) collective-permute-start(bf16[512,256]{1,0:T(8,128)(2,1)S(1)} %get-tuple-element.64), channel_id=1, source_target_pairs={{0,8},{1,9},{2,10},{3,11},{4,12},{5,13},{6,14},{7,15},{8,0},{9,1},... | collective-permute-start | bytes 786440 | tf_op jit(solution)/shard_map/ppermute | solution.py:34
  137.2 13.9 %collective-permute-start.21 = (bf16[512,256]{1,0:T(8,128)(2,1)S(1)}, bf16[512,256]{1,0:T(8,128)(2,1)S(1)}, u32[]{:S(2)}, u32[]{:S(2)}) collective-permute-start(bf16[512,256]{1,0:T(8,128)(2,1)S(1)} %get-tuple-element.71), channel_id=1, source_target_pairs={{0,4},{1,5},{2,6},{3,7},{4,8},{5,9},{6,10},{7,11},{8,12},{9,13},{1... | collective-permute-start | bytes 786440 | tf_op jit(solution)/shard_map/ppermute | solution.py:34
  139.1 14.0 %collective-permute-start.22 = (bf16[512,256]{1,0:T(8,128)(2,1)S(1)}, bf16[512,256]{1,0:T(8,128)(2,1)S(1)}, u32[]{:S(2)}, u32[]{:S(2)}) collective-permute-start(bf16[512,256]{1,0:T(8,128)(2,1)S(1)} %get-tuple-element.72), channel_id=1, source_target_pairs={{0,12},{1,13},{2,14},{3,15},{4,0},{5,1},{6,2},{7,3},{8,4},{9,5},{1... | collective-permute-start | bytes 786440 | tf_op jit(solution)/shard_map/ppermute | solution.py:34
  144.6 8.6 %collective-permute-start.23 = (bf16[512,256]{1,0:T(8,128)(2,1)S(1)}, bf16[512,256]{1,0:T(8,128)(2,1)S(1)}, u32[]{:S(2)}, u32[]{:S(2)}) collective-permute-start(bf16[512,256]{1,0:T(8,128)(2,1)S(1)} %get-tuple-element.73), channel_id=1, source_target_pairs={{0,1},{1,2},{2,3},{3,0},{4,5},{5,6},{6,7},{7,4},{8,9},{9,10},{10,1... | collective-permute-start | bytes 786440 | tf_op jit(solution)/shard_map/ppermute | solution.py:29
  146.6 7.8 %collective-permute-start.24 = (bf16[512,256]{1,0:T(8,128)(2,1)S(1)}, bf16[512,256]{1,0:T(8,128)(2,1)S(1)}, u32[]{:S(2)}, u32[]{:S(2)}) collective-permute-start(bf16[512,256]{1,0:T(8,128)(2,1)S(1)} %get-tuple-element.74), channel_id=1, source_target_pairs={{0,3},{1,0},{2,1},{3,2},{4,7},{5,4},{6,5},{7,6},{8,11},{9,8},{10,9... | collective-permute-start | bytes 786440 | tf_op jit(solution)/shard_map/ppermute | solution.py:29
  154.5 8.8 %collective-permute-start.25 = (bf16[256,256]{1,0:T(8,128)(2,1)S(1)}, bf16[256,256]{1,0:T(8,128)(2,1)S(1)}, u32[]{:S(2)}, u32[]{:S(2)}) collective-permute-start(bf16[256,256]{1,0:T(8,128)(2,1)S(1)} %shard_map.64), channel_id=1, source_target_pairs={{0,384},{384,0},{1,385},{385,1},{2,386},{386,2},{3,387},{387,3},{4... | collective-permute-start | bytes 393224 | tf_op jit(solution)/shard_map/ppermute | solution.py:291
  (3 other events, 4.8 us)

commit v12 on v11

--- a/solution.py
+++ b/solution.py
@@ -10,8 +10,8 @@
 ROWS = 3 * HS
 HALF = ROWS // 2
 D = 192
-E = 96
-MOST = 528
+E = 48
+MOST = 576
 REST = ROWS - MOST
 N = 2 * HS
 F32 = jnp.float32

time: 165 us -> 165 us (level)
  no operation moved by 1% of the time
where the time goes in v12:
time: 165 us; the launch traced here: 164 us
  starting transfers between devices  101 us (61%)
  waiting for transfers between devices  52.2 us (32%)
  Pallas kernels  8.21 us (5%)
  local copies, waits for them, and re-layouts  2.15 us (1%)
    ppermute x14, starting transfers between devices, shift_x(): return lax.ppermute(block, 'mp', route)  45.8 us
    ppermute x14, waiting for transfers between devices, shift_x(): return lax.ppermute(block, 'mp', route)  34.3 us
    ppermute x9, starting transfers between devices, shift_y(): return lax.ppermute(block, 'mp', route)  31 us
    ppermute x9, waiting for transfers between devices, shift_y(): return lax.ppermute(block, 'mp', route)  16.9 us
    ppermute x1, starting transfers between devices, local(): partner = lax.ppermute(own, 'section', SWAP)  12.4 us
    pallas_call x11, Pallas kernels, call(): pl.pallas_call(body, out_shape=out, in_specs=[SMEM] * scalars + [VMEM] *...  8.21 us
    ppermute x1, starting transfers between devices, local(): swapped = lax.ppermute(sent, 'section', SWAP)  7.79 us
    ppermute x1, starting transfers between devices, local(): other_w = lax.ppermute(own_w, 'section', SWAP)  3.65 us
  transfers between devices with their start and end apart: 26, of which 14 were waited for; matrix products, arithmetic and copies ran while one was open for 0% of the time, Pallas kernels for 2%

profile of v12, /device:TPU:1, one launch (start us, length us, event | category | flops | bytes accessed | tf_op | source)
XLA Modules:
  0.0 164.1 jit_solution(103075690943992946)
XLA Ops:
  0.0 12.4 %collective-permute-start = (bf16[512,256]{1,0:T(8,128)(2,1)}, bf16[512,256]{1,0:T(8,128)(2,1)S(1)}, u32[]{:S(2)}, u32[]{:S(2)}) collective-permute-start(bf16[512,256]{1,0:T(8,128)(2,1)} %bitcast.9), channel_id=1, source_target_pairs={{0,384},{384,0},{1,385},{385,1},{2,386},{386,2},{3,387},{387,3},{4... | collective-permute-start | bytes 786440 | tf_op jit(solution)/shard_map/ppermute | solution.py:211
  14.4 1.9 %collective-permute-start.1 = (bf16[768,256]{1,0:T(8,128)(2,1)S(1)}, bf16[768,256]{1,0:T(8,128)(2,1)S(1)}, u32[]{:S(2)}, u32[]{:S(2)}) collective-permute-start(bf16[768,256]{1,0:T(8,128)(2,1)S(1)} %shard_map.56.rest_0_), channel_id=1, source_target_pairs={{0,4},{1,5},{2,6},{3,7},{4,8},{5,9},{6,10},{7,11},{8,12},{9,13},{1... | collective-permute-start | bytes 1179656 | tf_op jit(solution)/shard_map/ppermute | solution.py:34
  16.3 5.5 %collective-permute-start.2 = (bf16[768,256]{1,0:T(8,128)(2,1)S(1)}, bf16[768,256]{1,0:T(8,128)(2,1)S(1)}, u32[]{:S(2)}, u32[]{:S(2)}) collective-permute-start(bf16[768,256]{1,0:T(8,128)(2,1)S(1)} %shard_map.56.rest_0_), channel_id=1, source_target_pairs={{0,12},{1,13},{2,14},{3,15},{4,0},{5,1},{6,2},{7,3},{8,4},{9,5},{1... | collective-permute-start | bytes 1179656 | tf_op jit(solution)/shard_map/ppermute | solution.py:34
  21.8 1.9 %collective-permute-start.3 = (bf16[768,256]{1,0:T(8,128)(2,1)S(1)}, bf16[768,256]{1,0:T(8,128)(2,1)S(1)}, u32[]{:S(2)}, u32[]{:S(2)}) collective-permute-start(bf16[768,256]{1,0:T(8,128)(2,1)S(1)} %shard_map.56.rest_0_), channel_id=1, source_target_pairs={{0,1},{1,2},{2,3},{3,0},{4,5},{5,6},{6,7},{7,4},{8,9},{9,10},{10,1... | collective-permute-start | bytes 1179656 | tf_op jit(solution)/shard_map/ppermute | solution.py:29
  23.7 4.6 %collective-permute-start.4 = (bf16[768,256]{1,0:T(8,128)(2,1)S(1)}, bf16[768,256]{1,0:T(8,128)(2,1)S(1)}, u32[]{:S(2)}, u32[]{:S(2)}) collective-permute-start(bf16[768,256]{1,0:T(8,128)(2,1)S(1)} %shard_map.56.rest_0_), channel_id=1, source_target_pairs={{0,3},{1,0},{2,1},{3,2},{4,7},{5,4},{6,5},{7,6},{8,11},{9,8},{10,9... | collective-permute-start | bytes 1179656 | tf_op jit(solution)/shard_map/ppermute | solution.py:29
  28.3 4.3 %collective-permute-done.1.rest_1_ = bf16[768,256]{1,0:T(8,128)(2,1)S(1)} collective-permute-done((bf16[768,256]{1,0:T(8,128)(2,1)S(1)}, bf16[768,256]{1,0:T(8,128)(2,1)S(1)}, u32[]{:S(2)}, u32[]{:S(2)}) %collective-permute-start.1) | collective-permute-done | bytes 393248 | tf_op jit(solution)/shard_map/ppermute | solution.py:34
  35.9 3.7 %collective-permute-start.5 = (bf16[2,4096,256]{2,1,0:T(8,128)(2,1)}, bf16[2,4096,256]{2,1,0:T(8,128)(2,1)S(1)}, u32[]{:S(2)}, u32[]{:S(2)}) collective-permute-start(bf16[2,4096,256]{2,1,0:T(8,128)(2,1)} %bitcast.3), channel_id=1, source_target_pairs={{0,384},{384,0},{1,385},{385,1},{2,386},{386,2},{3,387},{387,3},{4... | collective-permute-start | bytes 12582920 | tf_op jit(solution)/shard_map/ppermute | solution.py:219
  39.6 1.9 %collective-permute-start.6 = (bf16[1728,256]{1,0:T(8,128)(2,1)S(1)}, bf16[1728,256]{1,0:T(8,128)(2,1)S(1)}, u32[]{:S(2)}, u32[]{:S(2)}) collective-permute-start(bf16[1728,256]{1,0:T(8,128)(2,1)S(1)} %pad_maximum_fusion), channel_id=1, source_target_pairs={{0,1},{1,2},{2,3},{3,0},{4,5},{5,6},{6,7},{7,4},{8,9},{9,10},{10,1... | collective-permute-start | bytes 2654216 | tf_op jit(solution)/shard_map/ppermute | solution.py:29
  41.7 5.3 %collective-permute-start.8 = (bf16[1728,256]{1,0:T(8,128)(2,1)S(1)}, bf16[1728,256]{1,0:T(8,128)(2,1)S(1)}, u32[]{:S(2)}, u32[]{:S(2)}) collective-permute-start(bf16[1728,256]{1,0:T(8,128)(2,1)S(1)} %pad_maximum_fusion.1), channel_id=1, source_target_pairs={{0,3},{1,0},{2,1},{3,2},{4,7},{5,4},{6,5},{7,6},{8,11},{9,8},{10,9... | collective-permute-start | bytes 2654216 | tf_op jit(solution)/shard_map/ppermute | solution.py:29
  47.1 2.2 %collective-permute-start.10 = (bf16[576,256]{1,0:T(8,128)(2,1)S(1)}, bf16[576,256]{1,0:T(8,128)(2,1)S(1)}, u32[]{:S(2)}, u32[]{:S(2)}) collective-permute-start(bf16[576,256]{1,0:T(8,128)(2,1)S(1)} %pad_maximum_fusion.6), channel_id=1, source_target_pairs={{0,12},{1,13},{2,14},{3,15},{4,0},{5,1},{6,2},{7,3},{8,4},{9,5},{1... | collective-permute-start | bytes 884744 | tf_op jit(solution)/shard_map/ppermute | solution.py:34
  49.4 4.3 %collective-permute-start.9 = (bf16[576,256]{1,0:T(8,128)(2,1)S(1)}, bf16[576,256]{1,0:T(8,128)(2,1)S(1)}, u32[]{:S(2)}, u32[]{:S(2)}) collective-permute-start(bf16[576,256]{1,0:T(8,128)(2,1)S(1)} %pad_maximum_fusion.5), channel_id=1, source_target_pairs={{0,4},{1,5},{2,6},{3,7},{4,8},{5,9},{6,10},{7,11},{8,12},{9,13},{1... | collective-permute-start | bytes 884744 | tf_op jit(solution)/shard_map/ppermute | solution.py:34
  53.6 11.3 %collective-permute-done.6.rest_0_ = bf16[1728,256]{1,0:T(8,128)(2,1)S(1)} collective-permute-done((bf16[1728,256]{1,0:T(8,128)(2,1)S(1)}, bf16[1728,256]{1,0:T(8,128)(2,1)S(1)}, u32[]{:S(2)}, u32[]{:S(2)}) %collective-permute-start.6) | collective-permute-done | bytes 884768 | tf_op jit(solution)/shard_map/ppermute | solution.py:29
  65.1 1.9 %collective-permute-start.7 = (bf16[1152,256]{1,0:T(8,128)(2,1)S(1)}, bf16[1152,256]{1,0:T(8,128)(2,1)S(1)}, u32[]{:S(2)}, u32[]{:S(2)}) collective-permute-start(bf16[1152,256]{1,0:T(8,128)(2,1)S(1)} %pad_maximum_fusion.2), channel_id=1, source_target_pairs={{0,1},{1,2},{2,3},{3,0},{4,5},{5,6},{6,7},{7,4},{8,9},{9,10},{10,1... | collective-permute-start | bytes 1769480 | tf_op jit(solution)/shard_map/ppermute | solution.py:29
  68.1 4.7 %collective-permute-start.11 = (bf16[1056,256]{1,0:T(8,128)(2,1)S(1)}, bf16[1056,256]{1,0:T(8,128)(2,1)S(1)}, u32[]{:S(2)}, u32[]{:S(2)}) collective-permute-start(bf16[1056,256]{1,0:T(8,128)(2,1)S(1)} %pad_maximum_fusion.3), channel_id=1, source_target_pairs={{0,3},{1,0},{2,1},{3,2},{4,7},{5,4},{6,5},{7,6},{8,11},{9,8},{10,9... | collective-permute-start | bytes 1622024 | tf_op jit(solution)/shard_map/ppermute | solution.py:29
  76.8 4.3 %collective-permute-start.13 = (bf16[432,256]{1,0:T(8,128)(2,1)S(1)}, bf16[432,256]{1,0:T(8,128)(2,1)S(1)}, u32[]{:S(2)}, u32[]{:S(2)}) collective-permute-start(bf16[432,256]{1,0:T(8,128)(2,1)S(1)} %pad_maximum_fusion.7), channel_id=1, source_target_pairs={{0,4},{1,5},{2,6},{3,7},{4,8},{5,9},{6,10},{7,11},{8,12},{9,13},{1... | collective-permute-start | bytes 663560 | tf_op jit(solution)/shard_map/ppermute | solution.py:34
  82.9 2.7 %collective-permute-done.14.rest_4_ = bf16[432,256]{1,0:T(8,128)(2,1)S(1)} collective-permute-done((bf16[432,256]{1,0:T(8,128)(2,1)S(1)}, bf16[432,256]{1,0:T(8,128)(2,1)S(1)}, u32[]{:S(2)}, u32[]{:S(2)}) %collective-permute-start.14) | collective-permute-done | bytes 221216 | tf_op jit(solution)/shard_map/ppermute | solution.py:34
  85.6 6.1 %collective-permute-done.13.rest_3_ = bf16[432,256]{1,0:T(8,128)(2,1)S(1)} collective-permute-done((bf16[432,256]{1,0:T(8,128)(2,1)S(1)}, bf16[432,256]{1,0:T(8,128)(2,1)S(1)}, u32[]{:S(2)}, u32[]{:S(2)}) %collective-permute-start.13) | collective-permute-done | bytes 221216 | tf_op jit(solution)/shard_map/ppermute | solution.py:34
  92.6 2.3 %shard_map.60 = (bf16[1024,256]{1,0:T(8,128)(2,1)S(1)}, bf16[1024,256]{1,0:T(8,128)(2,1)S(1)}, bf16[512,256]{1,0:T(8,128)(2,1)S(1)}, bf16[4,256,256]{2,1,0:T(8,128)(2,1)S(1)}) custom-call(s32[2]{0:T(128)S(1)} %copy-done.5, s32[2]{0:T(128)S(1)} %copy-done.6, f32[4,256,256]{2,1,0:T(8,128)S(1)} %shard_map.59.t_ref, bf16[2,4096,256]{2,1,0:T(8,128)(2,1)S(1)} %bitcast.7, ...), custom_call_target="tpu_custom_call" | custom-call | flops 1006632960 | bytes 9437200 | tf_op jit(solution)/shard_map/pallas_call | solution.py:44
  95.0 3.2 %collective-permute-start.15 = (bf16[1024,256]{1,0:T(8,128)(2,1)S(1)}, bf16[1024,256]{1,0:T(8,128)(2,1)S(1)}, u32[]{:S(2)}, u32[]{:S(2)}) collective-permute-start(bf16[1024,256]{1,0:T(8,128)(2,1)S(1)} %get-tuple-element.61), channel_id=1, source_target_pairs={{0,1},{1,2},{2,3},{3,0},{4,5},{5,6},{6,7},{7,4},{8,9},{9,10},{10,1... | collective-permute-start | bytes 1572872 | tf_op jit(solution)/shard_map/ppermute | solution.py:29
  98.2 4.2 %collective-permute-start.16 = (bf16[1024,256]{1,0:T(8,128)(2,1)S(1)}, bf16[1024,256]{1,0:T(8,128)(2,1)S(1)}, u32[]{:S(2)}, u32[]{:S(2)}) collective-permute-start(bf16[1024,256]{1,0:T(8,128)(2,1)S(1)} %get-tuple-element.62), channel_id=1, source_target_pairs={{0,3},{1,0},{2,1},{3,2},{4,7},{5,4},{6,5},{7,6},{8,11},{9,8},{10,9... | collective-permute-start | bytes 1572872 | tf_op jit(solution)/shard_map/ppermute | solution.py:29
  102.4 3.1 %collective-permute-start.17 = (bf16[512,256]{1,0:T(8,128)(2,1)S(1)}, bf16[512,256]{1,0:T(8,128)(2,1)S(1)}, u32[]{:S(2)}, u32[]{:S(2)}) collective-permute-start(bf16[512,256]{1,0:T(8,128)(2,1)S(1)} %get-tuple-element.63), channel_id=1, source_target_pairs={{0,2},{1,3},{2,0},{3,1},{4,6},{5,7},{6,4},{7,5},{8,10},{9,11},{10,... | collective-permute-start | bytes 786440 | tf_op jit(solution)/shard_map/ppermute | solution.py:29
  107.2 10.2 %collective-permute-done.17.refs_5_ = bf16[512,256]{1,0:T(8,128)(2,1)S(1)} collective-permute-done((bf16[512,256]{1,0:T(8,128)(2,1)S(1)}, bf16[512,256]{1,0:T(8,128)(2,1)S(1)}, u32[]{:S(2)}, u32[]{:S(2)}) %collective-permute-start.17) | collective-permute-done | bytes 262176 | tf_op jit(solution)/shard_map/ppermute | solution.py:29
  117.7 4.4 %collective-permute-start.19 = (bf16[1280,256]{1,0:T(8,128)(2,1)S(1)}, bf16[1280,256]{1,0:T(8,128)(2,1)S(1)}, u32[]{:S(2)}, u32[]{:S(2)}) collective-permute-start(bf16[1280,256]{1,0:T(8,128)(2,1)S(1)} %get-tuple-element.69), channel_id=1, source_target_pairs={{0,1},{1,2},{2,3},{3,0},{4,5},{5,6},{6,7},{7,4},{8,9},{9,10},{10,1... | collective-permute-start | bytes 1966088 | tf_op jit(solution)/shard_map/ppermute | solution.py:29
  122.1 2.1 %collective-permute-start.20 = (bf16[1280,256]{1,0:T(8,128)(2,1)S(1)}, bf16[1280,256]{1,0:T(8,128)(2,1)S(1)}, u32[]{:S(2)}, u32[]{:S(2)}) collective-permute-start(bf16[1280,256]{1,0:T(8,128)(2,1)S(1)} %get-tuple-element.70), channel_id=1, source_target_pairs={{0,3},{1,0},{2,1},{3,2},{4,7},{5,4},{6,5},{7,6},{8,11},{9,8},{10,9... | collective-permute-start | bytes 1966088 | tf_op jit(solution)/shard_map/ppermute | solution.py:29
  124.2 3.5 %collective-permute-start.18 = (bf16[512,256]{1,0:T(8,128)(2,1)S(1)}, bf16[512,256]{1,0:T(8,128)(2,1)S(1)}, u32[]{:S(2)}, u32[]{:S(2)}) collective-permute-start(bf16[512,256]{1,0:T(8,128)(2,1)S(1)} %get-tuple-element.64), channel_id=1, source_target_pairs={{0,8},{1,9},{2,10},{3,11},{4,12},{5,13},{6,14},{7,15},{8,0},{9,1},... | collective-permute-start | bytes 786440 | tf_op jit(solution)/shard_map/ppermute | solution.py:34
  127.7 6.1 %collective-permute-done.19.refs_4_ = bf16[1280,256]{1,0:T(8,128)(2,1)S(1)} collective-permute-done((bf16[1280,256]{1,0:T(8,128)(2,1)S(1)}, bf16[1280,256]{1,0:T(8,128)(2,1)S(1)}, u32[]{:S(2)}, u32[]{:S(2)}) %collective-permute-start.19) | collective-permute-done | bytes 655392 | tf_op jit(solution)/shard_map/ppermute | solution.py:29
  133.8 3.1 %collective-permute-done.20.refs_5_ = bf16[1280,256]{1,0:T(8,128)(2,1)S(1)} collective-permute-done((bf16[1280,256]{1,0:T(8,128)(2,1)S(1)}, bf16[1280,256]{1,0:T(8,128)(2,1)S(1)}, u32[]{:S(2)}, u32[]{:S(2)}) %collective-permute-start.20) | collective-permute-done | bytes 655392 | tf_op jit(solution)/shard_map/ppermute | solution.py:29
  139.1 5.5 %collective-permute-start.22 = (bf16[512,256]{1,0:T(8,128)(2,1)S(1)}, bf16[512,256]{1,0:T(8,128)(2,1)S(1)}, u32[]{:S(2)}, u32[]{:S(2)}) collective-permute-start(bf16[512,256]{1,0:T(8,128)(2,1)S(1)} %get-tuple-element.72), channel_id=1, source_target_pairs={{0,12},{1,13},{2,14},{3,15},{4,0},{5,1},{6,2},{7,3},{8,4},{9,5},{1... | collective-permute-start | bytes 786440 | tf_op jit(solution)/shard_map/ppermute | solution.py:34
  144.6 2.2 %collective-permute-start.23 = (bf16[512,256]{1,0:T(8,128)(2,1)S(1)}, bf16[512,256]{1,0:T(8,128)(2,1)S(1)}, u32[]{:S(2)}, u32[]{:S(2)}) collective-permute-start(bf16[512,256]{1,0:T(8,128)(2,1)S(1)} %get-tuple-element.73), channel_id=1, source_target_pairs={{0,1},{1,2},{2,3},{3,0},{4,5},{5,6},{6,7},{7,4},{8,9},{9,10},{10,1... | collective-permute-start | bytes 786440 | tf_op jit(solution)/shard_map/ppermute | solution.py:29
  146.8 4.3 %collective-permute-start.24 = (bf16[512,256]{1,0:T(8,128)(2,1)S(1)}, bf16[512,256]{1,0:T(8,128)(2,1)S(1)}, u32[]{:S(2)}, u32[]{:S(2)}) collective-permute-start(bf16[512,256]{1,0:T(8,128)(2,1)S(1)} %get-tuple-element.74), channel_id=1, source_target_pairs={{0,3},{1,0},{2,1},{3,2},{4,7},{5,4},{6,5},{7,6},{8,11},{9,8},{10,9... | collective-permute-start | bytes 786440 | tf_op jit(solution)/shard_map/ppermute | solution.py:29
  151.1 3.0 %collective-permute-done.21.refs_2_.rest_1_ = bf16[512,256]{1,0:T(8,128)(2,1)S(1)} collective-permute-done((bf16[512,256]{1,0:T(8,128)(2,1)S(1)}, bf16[512,256]{1,0:T(8,128)(2,1)S(1)}, u32[]{:S(2)}, u32[]{:S(2)}) %collective-permute-start.21) | collective-permute-done | bytes 262176 | tf_op jit(solution)/shard_map/ppermute | solution.py:34
  154.5 7.8 %collective-permute-start.25 = (bf16[256,256]{1,0:T(8,128)(2,1)S(1)}, bf16[256,256]{1,0:T(8,128)(2,1)S(1)}, u32[]{:S(2)}, u32[]{:S(2)}) collective-permute-start(bf16[256,256]{1,0:T(8,128)(2,1)S(1)} %shard_map.64), channel_id=1, source_target_pairs={{0,384},{384,0},{1,385},{385,1},{2,386},{386,2},{3,387},{387,3},{4... | collective-permute-start | bytes 393224 | tf_op jit(solution)/shard_map/ppermute | solution.py:291
  (74 shorter events, 19.4 us)
Async XLA Ops:
  0.0 14.3 %collective-permute-start = (bf16[512,256]{1,0:T(8,128)(2,1)}, bf16[512,256]{1,0:T(8,128)(2,1)S(1)}, u32[]{:S(2)}, u32[]{:S(2)}) collective-permute-start(bf16[512,256]{1,0:T(8,128)(2,1)} %bitcast.9), channel_id=1, source_target_pairs={{0,384},{384,0},{1,385},{385,1},{2,386},{386,2},{3,387},{387,3},{4... | collective-permute-start | bytes 786440 | tf_op jit(solution)/shard_map/ppermute | solution.py:211
  14.4 18.3 %collective-permute-start.1 = (bf16[768,256]{1,0:T(8,128)(2,1)S(1)}, bf16[768,256]{1,0:T(8,128)(2,1)S(1)}, u32[]{:S(2)}, u32[]{:S(2)}) collective-permute-start(bf16[768,256]{1,0:T(8,128)(2,1)S(1)} %shard_map.56.rest_0_), channel_id=1, source_target_pairs={{0,4},{1,5},{2,6},{3,7},{4,8},{5,9},{6,10},{7,11},{8,12},{9,13},{1... | collective-permute-start | bytes 1179656 | tf_op jit(solution)/shard_map/ppermute | solution.py:34
  16.3 17.1 %collective-permute-start.2 = (bf16[768,256]{1,0:T(8,128)(2,1)S(1)}, bf16[768,256]{1,0:T(8,128)(2,1)S(1)}, u32[]{:S(2)}, u32[]{:S(2)}) collective-permute-start(bf16[768,256]{1,0:T(8,128)(2,1)S(1)} %shard_map.56.rest_0_), channel_id=1, source_target_pairs={{0,12},{1,13},{2,14},{3,15},{4,0},{5,1},{6,2},{7,3},{8,4},{9,5},{1... | collective-permute-start | bytes 1179656 | tf_op jit(solution)/shard_map/ppermute | solution.py:34
  21.8 13.2 %collective-permute-start.3 = (bf16[768,256]{1,0:T(8,128)(2,1)S(1)}, bf16[768,256]{1,0:T(8,128)(2,1)S(1)}, u32[]{:S(2)}, u32[]{:S(2)}) collective-permute-start(bf16[768,256]{1,0:T(8,128)(2,1)S(1)} %shard_map.56.rest_0_), channel_id=1, source_target_pairs={{0,1},{1,2},{2,3},{3,0},{4,5},{5,6},{6,7},{7,4},{8,9},{9,10},{10,1... | collective-permute-start | bytes 1179656 | tf_op jit(solution)/shard_map/ppermute | solution.py:29
  23.7 12.1 %collective-permute-start.4 = (bf16[768,256]{1,0:T(8,128)(2,1)S(1)}, bf16[768,256]{1,0:T(8,128)(2,1)S(1)}, u32[]{:S(2)}, u32[]{:S(2)}) collective-permute-start(bf16[768,256]{1,0:T(8,128)(2,1)S(1)} %shard_map.56.rest_0_), channel_id=1, source_target_pairs={{0,3},{1,0},{2,1},{3,2},{4,7},{5,4},{6,5},{7,6},{8,11},{9,8},{10,9... | collective-permute-start | bytes 1179656 | tf_op jit(solution)/shard_map/ppermute | solution.py:29
  35.9 31.1 %collective-permute-start.5 = (bf16[2,4096,256]{2,1,0:T(8,128)(2,1)}, bf16[2,4096,256]{2,1,0:T(8,128)(2,1)S(1)}, u32[]{:S(2)}, u32[]{:S(2)}) collective-permute-start(bf16[2,4096,256]{2,1,0:T(8,128)(2,1)} %bitcast.3), channel_id=1, source_target_pairs={{0,384},{384,0},{1,385},{385,1},{2,386},{386,2},{3,387},{387,3},{4... | collective-permute-start | bytes 12582920 | tf_op jit(solution)/shard_map/ppermute | solution.py:219
  39.6 25.3 %collective-permute-start.6 = (bf16[1728,256]{1,0:T(8,128)(2,1)S(1)}, bf16[1728,256]{1,0:T(8,128)(2,1)S(1)}, u32[]{:S(2)}, u32[]{:S(2)}) collective-permute-start(bf16[1728,256]{1,0:T(8,128)(2,1)S(1)} %pad_maximum_fusion), channel_id=1, source_target_pairs={{0,1},{1,2},{2,3},{3,0},{4,5},{5,6},{6,7},{7,4},{8,9},{9,10},{10,1... | collective-permute-start | bytes 2654216 | tf_op jit(solution)/shard_map/ppermute | solution.py:29
  41.7 26.2 %collective-permute-start.8 = (bf16[1728,256]{1,0:T(8,128)(2,1)S(1)}, bf16[1728,256]{1,0:T(8,128)(2,1)S(1)}, u32[]{:S(2)}, u32[]{:S(2)}) collective-permute-start(bf16[1728,256]{1,0:T(8,128)(2,1)S(1)} %pad_maximum_fusion.1), channel_id=1, source_target_pairs={{0,3},{1,0},{2,1},{3,2},{4,7},{5,4},{6,5},{7,6},{8,11},{9,8},{10,9... | collective-permute-start | bytes 2654216 | tf_op jit(solution)/shard_map/ppermute | solution.py:29
  47.1 19.9 %copy-start = (bf16[1,2,4096,256]{3,2,1,0:T(8,128)(2,1)S(1)}, bf16[1,2,4096,256]{3,2,1,0:T(8,128)(2,1)}, u32[]{:S(2)}) copy-start(bf16[1,2,4096,256]{3,2,1,0:T(8,128)(2,1)} %param.6) | copy-start | bytes 12582916
  47.1 20.7 %collective-permute-start.10 = (bf16[576,256]{1,0:T(8,128)(2,1)S(1)}, bf16[576,256]{1,0:T(8,128)(2,1)S(1)}, u32[]{:S(2)}, u32[]{:S(2)}) collective-permute-start(bf16[576,256]{1,0:T(8,128)(2,1)S(1)} %pad_maximum_fusion.6), channel_id=1, source_target_pairs={{0,12},{1,13},{2,14},{3,15},{4,0},{5,1},{6,2},{7,3},{8,4},{9,5},{1... | collective-permute-start | bytes 884744 | tf_op jit(solution)/shard_map/ppermute | solution.py:34
  49.4 18.5 %collective-permute-start.9 = (bf16[576,256]{1,0:T(8,128)(2,1)S(1)}, bf16[576,256]{1,0:T(8,128)(2,1)S(1)}, u32[]{:S(2)}, u32[]{:S(2)}) collective-permute-start(bf16[576,256]{1,0:T(8,128)(2,1)S(1)} %pad_maximum_fusion.5), channel_id=1, source_target_pairs={{0,4},{1,5},{2,6},{3,7},{4,8},{5,9},{6,10},{7,11},{8,12},{9,13},{1... | collective-permute-start | bytes 884744 | tf_op jit(solution)/shard_map/ppermute | solution.py:34
  65.1 17.9 %collective-permute-start.7 = (bf16[1152,256]{1,0:T(8,128)(2,1)S(1)}, bf16[1152,256]{1,0:T(8,128)(2,1)S(1)}, u32[]{:S(2)}, u32[]{:S(2)}) collective-permute-start(bf16[1152,256]{1,0:T(8,128)(2,1)S(1)} %pad_maximum_fusion.2), channel_id=1, source_target_pairs={{0,1},{1,2},{2,3},{3,0},{4,5},{5,6},{6,7},{7,4},{8,9},{9,10},{10,1... | collective-permute-start | bytes 1769480 | tf_op jit(solution)/shard_map/ppermute | solution.py:29
  67.9 6.9 %slice-start = ((bf16[1728,256]{1,0:T(8,128)(2,1)}), bf16[192,256]{1,0:T(8,128)(2,1)S(1)}, s32[]{:S(2)}) async-start(bf16[1728,256]{1,0:T(8,128)(2,1)} %copy-done.1), calls=%async_computation | async-start | bytes 196608 | tf_op jit(solution)/shard_map/slice | solution.py:240
  68.0 8.8 %slice-start.1 = ((bf16[1728,256]{1,0:T(8,128)(2,1)}), bf16[384,256]{1,0:T(8,128)(2,1)S(1)}, s32[]{:S(2)}) async-start(bf16[1728,256]{1,0:T(8,128)(2,1)} %copy-done.1), calls=%async_computation.1 | async-start | bytes 393216 | tf_op jit(solution)/shard_map/slice | solution.py:239
  68.0 13.1 %copy-start.2 = (bf16[1728,256]{1,0:T(8,128)(2,1)S(1)}, bf16[1728,256]{1,0:T(8,128)(2,1)}, u32[]{:S(2)}) copy-start(bf16[1728,256]{1,0:T(8,128)(2,1)} %copy-done.1) | copy-start | bytes 2654212
  68.1 23.6 %collective-permute-start.11 = (bf16[1056,256]{1,0:T(8,128)(2,1)S(1)}, bf16[1056,256]{1,0:T(8,128)(2,1)S(1)}, u32[]{:S(2)}, u32[]{:S(2)}) collective-permute-start(bf16[1056,256]{1,0:T(8,128)(2,1)S(1)} %pad_maximum_fusion.3), channel_id=1, source_target_pairs={{0,3},{1,0},{2,1},{3,2},{4,7},{5,4},{6,5},{7,6},{8,11},{9,8},{10,9... | collective-permute-start | bytes 1622024 | tf_op jit(solution)/shard_map/ppermute | solution.py:29
  72.9 18.9 %collective-permute-start.12 = (bf16[768,256]{1,0:T(8,128)(2,1)S(1)}, bf16[768,256]{1,0:T(8,128)(2,1)S(1)}, u32[]{:S(2)}, u32[]{:S(2)}) collective-permute-start(bf16[768,256]{1,0:T(8,128)(2,1)S(1)} %pad_maximum_fusion.4), channel_id=1, source_target_pairs={{0,2},{1,3},{2,0},{3,1},{4,6},{5,7},{6,4},{7,5},{8,10},{9,11},{10,... | collective-permute-start | bytes 1179656 | tf_op jit(solution)/shard_map/ppermute | solution.py:29
  74.8 10.8 %collective-permute-start.14 = (bf16[432,256]{1,0:T(8,128)(2,1)S(1)}, bf16[432,256]{1,0:T(8,128)(2,1)S(1)}, u32[]{:S(2)}, u32[]{:S(2)}) collective-permute-start(bf16[432,256]{1,0:T(8,128)(2,1)S(1)} %pad_maximum_fusion.8), channel_id=1, source_target_pairs={{0,12},{1,13},{2,14},{3,15},{4,0},{5,1},{6,2},{7,3},{8,4},{9,5},{1... | collective-permute-start | bytes 663560 | tf_op jit(solution)/shard_map/ppermute | solution.py:34
  76.8 14.9 %collective-permute-start.13 = (bf16[432,256]{1,0:T(8,128)(2,1)S(1)}, bf16[432,256]{1,0:T(8,128)(2,1)S(1)}, u32[]{:S(2)}, u32[]{:S(2)}) collective-permute-start(bf16[432,256]{1,0:T(8,128)(2,1)S(1)} %pad_maximum_fusion.7), channel_id=1, source_target_pairs={{0,4},{1,5},{2,6},{3,7},{4,8},{5,9},{6,10},{7,11},{8,12},{9,13},{1... | collective-permute-start | bytes 663560 | tf_op jit(solution)/shard_map/ppermute | solution.py:34
  82.1 10.5 %copy-start.5 = (s32[2]{0:T(128)S(1)}, s32[2]{0:T(128)}, u32[]{:S(2)}) copy-start(s32[2]{0:T(128)} %enc_ref.1) | copy-start | bytes 28
  82.1 10.5 %copy-start.6 = (s32[2]{0:T(128)S(1)}, s32[2]{0:T(128)}, u32[]{:S(2)}) copy-start(s32[2]{0:T(128)} %dec_ref.1) | copy-start | bytes 28
  95.0 22.5 %collective-permute-start.15 = (bf16[1024,256]{1,0:T(8,128)(2,1)S(1)}, bf16[1024,256]{1,0:T(8,128)(2,1)S(1)}, u32[]{:S(2)}, u32[]{:S(2)}) collective-permute-start(bf16[1024,256]{1,0:T(8,128)(2,1)S(1)} %get-tuple-element.61), channel_id=1, source_target_pairs={{0,1},{1,2},{2,3},{3,0},{4,5},{5,6},{6,7},{7,4},{8,9},{9,10},{10,1... | collective-permute-start | bytes 1572872 | tf_op jit(solution)/shard_map/ppermute | solution.py:29
  98.2 19.2 %collective-permute-start.16 = (bf16[1024,256]{1,0:T(8,128)(2,1)S(1)}, bf16[1024,256]{1,0:T(8,128)(2,1)S(1)}, u32[]{:S(2)}, u32[]{:S(2)}) collective-permute-start(bf16[1024,256]{1,0:T(8,128)(2,1)S(1)} %get-tuple-element.62), channel_id=1, source_target_pairs={{0,3},{1,0},{2,1},{3,2},{4,7},{5,4},{6,5},{7,6},{8,11},{9,8},{10,9... | collective-permute-start | bytes 1572872 | tf_op jit(solution)/shard_map/ppermute | solution.py:29
  102.4 15.0 %collective-permute-start.17 = (bf16[512,256]{1,0:T(8,128)(2,1)S(1)}, bf16[512,256]{1,0:T(8,128)(2,1)S(1)}, u32[]{:S(2)}, u32[]{:S(2)}) collective-permute-start(bf16[512,256]{1,0:T(8,128)(2,1)S(1)} %get-tuple-element.63), channel_id=1, source_target_pairs={{0,2},{1,3},{2,0},{3,1},{4,6},{5,7},{6,4},{7,5},{8,10},{9,11},{10,... | collective-permute-start | bytes 786440 | tf_op jit(solution)/shard_map/ppermute | solution.py:29
  117.7 16.1 %collective-permute-start.19 = (bf16[1280,256]{1,0:T(8,128)(2,1)S(1)}, bf16[1280,256]{1,0:T(8,128)(2,1)S(1)}, u32[]{:S(2)}, u32[]{:S(2)}) collective-permute-start(bf16[1280,256]{1,0:T(8,128)(2,1)S(1)} %get-tuple-element.69), channel_id=1, source_target_pairs={{0,1},{1,2},{2,3},{3,0},{4,5},{5,6},{6,7},{7,4},{8,9},{9,10},{10,1... | collective-permute-start | bytes 1966088 | tf_op jit(solution)/shard_map/ppermute | solution.py:29
  122.1 14.9 %collective-permute-start.20 = (bf16[1280,256]{1,0:T(8,128)(2,1)S(1)}, bf16[1280,256]{1,0:T(8,128)(2,1)S(1)}, u32[]{:S(2)}, u32[]{:S(2)}) collective-permute-start(bf16[1280,256]{1,0:T(8,128)(2,1)S(1)} %get-tuple-element.70), channel_id=1, source_target_pairs={{0,3},{1,0},{2,1},{3,2},{4,7},{5,4},{6,5},{7,6},{8,11},{9,8},{10,9... | collective-permute-start | bytes 1966088 | tf_op jit(solution)/shard_map/ppermute | solution.py:29
  124.2 26.9 %collective-permute-start.18 = (bf16[512,256]{1,0:T(8,128)(2,1)S(1)}, bf16[512,256]{1,0:T(8,128)(2,1)S(1)}, u32[]{:S(2)}, u32[]{:S(2)}) collective-permute-start(bf16[512,256]{1,0:T(8,128)(2,1)S(1)} %get-tuple-element.64), channel_id=1, source_target_pairs={{0,8},{1,9},{2,10},{3,11},{4,12},{5,13},{6,14},{7,15},{8,0},{9,1},... | collective-permute-start | bytes 786440 | tf_op jit(solution)/shard_map/ppermute | solution.py:34
  137.2 16.9 %collective-permute-start.21 = (bf16[512,256]{1,0:T(8,128)(2,1)S(1)}, bf16[512,256]{1,0:T(8,128)(2,1)S(1)}, u32[]{:S(2)}, u32[]{:S(2)}) collective-permute-start(bf16[512,256]{1,0:T(8,128)(2,1)S(1)} %get-tuple-element.71), channel_id=1, source_target_pairs={{0,4},{1,5},{2,6},{3,7},{4,8},{5,9},{6,10},{7,11},{8,12},{9,13},{1... | collective-permute-start | bytes 786440 | tf_op jit(solution)/shard_map/ppermute | solution.py:34
  139.1 15.0 %collective-permute-start.22 = (bf16[512,256]{1,0:T(8,128)(2,1)S(1)}, bf16[512,256]{1,0:T(8,128)(2,1)S(1)}, u32[]{:S(2)}, u32[]{:S(2)}) collective-permute-start(bf16[512,256]{1,0:T(8,128)(2,1)S(1)} %get-tuple-element.72), channel_id=1, source_target_pairs={{0,12},{1,13},{2,14},{3,15},{4,0},{5,1},{6,2},{7,3},{8,4},{9,5},{1... | collective-permute-start | bytes 786440 | tf_op jit(solution)/shard_map/ppermute | solution.py:34
  144.6 9.5 %collective-permute-start.23 = (bf16[512,256]{1,0:T(8,128)(2,1)S(1)}, bf16[512,256]{1,0:T(8,128)(2,1)S(1)}, u32[]{:S(2)}, u32[]{:S(2)}) collective-permute-start(bf16[512,256]{1,0:T(8,128)(2,1)S(1)} %get-tuple-element.73), channel_id=1, source_target_pairs={{0,1},{1,2},{2,3},{3,0},{4,5},{5,6},{6,7},{7,4},{8,9},{9,10},{10,1... | collective-permute-start | bytes 786440 | tf_op jit(solution)/shard_map/ppermute | solution.py:29
  146.8 7.6 %collective-permute-start.24 = (bf16[512,256]{1,0:T(8,128)(2,1)S(1)}, bf16[512,256]{1,0:T(8,128)(2,1)S(1)}, u32[]{:S(2)}, u32[]{:S(2)}) collective-permute-start(bf16[512,256]{1,0:T(8,128)(2,1)S(1)} %get-tuple-element.74), channel_id=1, source_target_pairs={{0,3},{1,0},{2,1},{3,2},{4,7},{5,4},{6,5},{7,6},{8,11},{9,8},{10,9... | collective-permute-start | bytes 786440 | tf_op jit(solution)/shard_map/ppermute | solution.py:29
  154.5 8.8 %collective-permute-start.25 = (bf16[256,256]{1,0:T(8,128)(2,1)S(1)}, bf16[256,256]{1,0:T(8,128)(2,1)S(1)}, u32[]{:S(2)}, u32[]{:S(2)}) collective-permute-start(bf16[256,256]{1,0:T(8,128)(2,1)S(1)} %shard_map.64), channel_id=1, source_target_pairs={{0,384},{384,0},{1,385},{385,1},{2,386},{386,2},{3,387},{387,3},{4... | collective-permute-start | bytes 393224 | tf_op jit(solution)/shard_map/ppermute | solution.py:291
  (3 other events, 4.8 us)
